TPU v7x, 128 devices: a whole 4x4x4 slice. The times are simulated.
128 devices in a mesh: pas: 32 (over y, z, core), tp: 4 (over x).
Axes of the slice: x: 4, y: 4, z: 4, core: 2. Of those that a mesh axis runs over, the one named last changes fastest.
Arguments:
- passage_hidden: bfloat16 [32768, 8192], P('pas', 'tp'), may hold values from -6 to 6
- kv_weight: bfloat16 [1024, 8192], P('pas', 'tp'), may hold values from -0.0625 to 0.0625
- queries: bfloat16 [16384, 4096], P('pas', 'tp'), may hold values from -600 to 600
- query_kv: bfloat16 [16384, 1024], P('pas', 'tp'), may hold values from -6 to 6
- out_grad: bfloat16 [16384, 4096], P('pas', 'tp'), may hold values from -6 to 6
- source_device: int32 [128, 8], P('pas'), may hold values from 0 to 31, all different within a row; in each aligned block of 4 rows (0 to 3, 4 to 7, ...) at most 2 rows name the same one
- source_slot: int32 [128, 8], P('pas'), may hold values from 0 to 7
Outputs:
- query_grad: bfloat16 [16384, 4096], P('pas', 'tp')
- query_kv_grad: bfloat16 [16384, 1024], P('pas', 'tp')
- weight_grad: float32 [1024, 8192], P('pas', 'tp')
Inputs may be any that keep to these rules, and one draw needn't show every extreme that they name: `source_device`: each query names 8 different owners; among the 4 queries of one index of pas no owner is named more than 2 times, and one owner exactly 2 times.
All inputs are finite; a program needn't handle non-finite values.
Results may differ from a plain program's by a relative error of at most 0.0095.
Values may be sent and summed in bfloat16 or wider, within the bound.
No kernel may reach another device: no remote copies, remote signals or barrier semaphores. Data moves between devices by JAX's collectives and lax.ppermute only.
A program may use at most 128 MiB of HBM per device.

v0:
```python
import functools
import math

import jax
import jax.numpy as jnp
from jax import lax
from jax.experimental import pallas as pl
from jax.experimental.pallas import tpu as pltpu
from jax.sharding import PartitionSpec as P

HD = 128
PLEN = 128
BF = jnp.bfloat16
F32 = jnp.float32
NT = (((1,), (1,)), ((), ()))
TN = (((0,), (0,)), ((), ()))
SIDE = 4
OUT_ROWS = 32
CHUNKS = 4


def device_at(y, z, core):
    return (y * SIDE + z) * 2 + core


def ring_pairs(order, k):
    pairs = []
    for y in range(SIDE):
        for z in range(SIDE):
            for core in range(2):
                if (order + core) % 2 == 0:
                    to = device_at(y, (z + k) % SIDE, core)
                else:
                    to = device_at((y + k) % SIDE, z, core)
                pairs.append((device_at(y, z, core), to))
    return pairs


def send_first(x, k):
    return lax.ppermute(x, "pas", ring_pairs(0, k))


def send_second(x, k):
    return lax.ppermute(x, "pas", ring_pairs(1, k))


def send_tp(x, k):
    return lax.ppermute(x, "tp", [(i, (i + k) % SIDE) for i in range(SIDE)])


def swap_cores(x):
    return lax.ppermute(x, "pas", [(i, i ^ 1) for i in range(2 * SIDE * SIDE)])


def ring_gather(x, send):
    left = send(x, 1)
    right = send(x, -1)
    return [x, left, send(x, 2), right]


def ring_gather_halves(x, send):
    half = x.shape[0] // 2
    left = send(x, 1)
    right = send(x, -1)
    return [x, left, send(left[:half], 1), send(right[half:], -1), right]


def here():
    pas = lax.axis_index("pas")
    return pas // (2 * SIDE), (pas // 2) % SIDE, pas % 2, lax.axis_index("tp")


def here_in_kernel():
    pas = lax.axis_index("pas")
    return (
        lax.div(pas, 2 * SIDE),
        lax.rem(lax.div(pas, 2), SIDE),
        lax.rem(pas, 2),
        lax.axis_index("tp"),
    )


def ring_mod(n):
    return lax.rem(n + 2 * SIDE, SIDE)


def project_kernel(chunks, h_ref, *rest):
    n_out = chunks * SIDE
    pieces = rest[: 2 * SIDE]
    outs = rest[2 * SIDE : 2 * SIDE + n_out]
    weights, result, w_sem, out_sem = rest[2 * SIDE + n_out :]
    step = pl.program_id(0)
    y, z, core, tp = here_in_kernel()
    head_rows = weights.shape[1]
    chunk = h_ref.shape[0] // chunks

    @pl.when(step == 0)
    def _():
        for src in range(2):
            which = core if src == 0 else 1 - core
            first = jnp.where(which == 0, z, y)
            second = jnp.where(which == 0, y, z)
            for jb in range(SIDE):
                for ja in range(SIDE):
                    a = ring_mod(first - ja)
                    b = ring_mod(second - jb)
                    place = ring_mod(jnp.where(which == 0, b, a) - tp)
                    part = jnp.where(which == 0, a, b) * 2 + which
                    pltpu.make_async_copy(
                        pieces[SIDE * src + jb].at[pl.ds(ja * OUT_ROWS, OUT_ROWS)],
                        weights.at[place, pl.ds(pl.multiple_of(part * OUT_ROWS, OUT_ROWS), OUT_ROWS)],
                        w_sem.at[place, part],
                    ).start()

    for n in range(2 * SIDE):
        pltpu.make_async_copy(
            pieces[0].at[pl.ds(0, OUT_ROWS)],
            weights.at[step, pl.ds(n * OUT_ROWS, OUT_ROWS)],
            w_sem.at[step, n],
        ).wait()
    result[step] = lax.dot_general(
        h_ref[...], weights[step], NT, preferred_element_type=F32
    )
    for j in range(SIDE):

        @pl.when(step == j)
        def _():
            for n in range(chunks):
                pltpu.make_async_copy(
                    result.at[j, pl.ds(n * chunk, chunk)],
                    outs[n * SIDE + j],
                    out_sem.at[n * SIDE + j],
                ).start()

    @pl.when(step == SIDE - 1)
    def _():
        for j in range(SIDE):
            for n in range(chunks):
                pltpu.make_async_copy(
                    result.at[j, pl.ds(n * chunk, chunk)],
                    outs[n * SIDE + j],
                    out_sem.at[n * SIDE + j],
                ).wait()


def project(hidden, pieces, chunks):
    rows, depth = hidden.shape
    columns = 2 * SIDE * SIDE * OUT_ROWS
    head = columns // SIDE
    hbm = pl.BlockSpec(memory_space=pl.ANY)
    return pl.pallas_call(
        functools.partial(project_kernel, chunks),
        out_shape=[jax.ShapeDtypeStruct((rows // chunks, head), F32)] * (chunks * SIDE),
        grid=(SIDE,),
        in_specs=[pl.BlockSpec((rows, depth), lambda i: (0, 0))] + [hbm] * (2 * SIDE),
        out_specs=[hbm] * (chunks * SIDE),
        scratch_shapes=[
            pltpu.VMEM((SIDE, head, depth), BF),
            pltpu.VMEM((SIDE, rows, head), F32),
            pltpu.SemaphoreType.DMA((SIDE, 2 * SIDE)),
            pltpu.SemaphoreType.DMA((chunks * SIDE,)),
        ],
        compiler_params=pltpu.CompilerParams(vmem_limit_bytes=40 * 2**20),
        cost_estimate=pl.CostEstimate(
            flops=2 * rows * columns * depth,
            bytes_accessed=2 * rows * depth + 2 * columns * depth + 4 * rows * columns,
            transcendentals=0,
        ),
        name="project",
    )(hidden, *pieces)


def reduce_heads(parts):
    down, up = parts[0][3], parts[1][1]
    for first, second in ((2, 2), (1, 3), (0, 0)):
        down = send_tp(down, 1) + parts[0][first]
        up = send_tp(up, -1) + parts[1][second]
    return jnp.concatenate([down.astype(BF), up.astype(BF)], axis=0)


def weight_kernel(*refs):
    mine, theirs = refs[:5], refs[5:10]
    h_mine, h_theirs = refs[10:12]
    outs = refs[12 : 12 + SIDE]
    left, result = refs[12 + SIDE :]
    y, z, core, tp = here_in_kernel()
    rows = mine[0].shape[1]

    @pl.when(pl.program_id(0) == 0)
    def _():
        for half, refs_of in enumerate((mine, theirs)):
            at = 0
            for piece in refs_of:
                left[pl.ds(at, piece.shape[0]), half * rows : (half + 1) * rows] = piece[...]
                at += piece.shape[0]

    result[...] = jnp.dot(
        left[:, :rows], h_mine[...], preferred_element_type=F32
    ) + jnp.dot(left[:, rows:], h_theirs[...], preferred_element_type=F32)

    def block(ja, jb):
        a_z, a_y = ring_mod(z + ja), ring_mod(y + ja)
        b_z, b_y = ring_mod(z + jb), ring_mod(y + jb)
        y_of = jnp.where(core == 0, b_y, a_y)
        z_of = jnp.where(core == 0, a_z, b_z)
        at = ring_mod(tp - y_of) * SIDE * OUT_ROWS + z_of * OUT_ROWS
        return result[pl.ds(pl.multiple_of(at, OUT_ROWS), OUT_ROWS), :]

    for jb in range(SIDE):
        outs[0][jb] = block(0, jb)
    for ja in range(1, SIDE):
        for jb in range(SIDE):
            outs[ja][jb] = block(ja, jb).astype(BF)


def weight_product(mine, theirs, h_mine, h_theirs):
    rows, depth = h_mine.shape
    tile = 512
    heads_rows = SIDE * SIDE * OUT_ROWS
    whole = pl.BlockSpec(memory_space=pltpu.VMEM)
    out = pl.BlockSpec((SIDE, OUT_ROWS, tile), lambda i: (0, 0, i))
    return pl.pallas_call(
        weight_kernel,
        out_shape=[jax.ShapeDtypeStruct((SIDE, OUT_ROWS, depth), F32)]
        + [jax.ShapeDtypeStruct((SIDE, OUT_ROWS, depth), BF)] * (SIDE - 1),
        grid=(depth // tile,),
        in_specs=[whole] * 10 + [pl.BlockSpec((rows, tile), lambda i: (0, i))] * 2,
        out_specs=[out] * SIDE,
        scratch_shapes=[
            pltpu.VMEM((heads_rows, 2 * rows), BF),
            pltpu.VMEM((heads_rows, tile), F32),
        ],
        compiler_params=pltpu.CompilerParams(vmem_limit_bytes=40 * 2**20),
        cost_estimate=pl.CostEstimate(
            flops=4 * heads_rows * rows * depth,
            bytes_accessed=4 * rows * depth + 4 * heads_rows * depth,
            transcendentals=0,
        ),
        name="weight_product",
    )(*mine, *theirs, h_mine, h_theirs)


def reduce_owners(blocks):
    own, one, two, three = blocks
    left = send_first(one, 1)
    right = send_first(three, -1)
    far = send_first(two, 2)
    total = (own + left.astype(F32)) + (right.astype(F32) + far.astype(F32))
    low = total[1:].astype(BF)
    left = send_second(low[0], 1)
    right = send_second(low[2], -1)
    far = send_second(low[1], 2)
    return (total[0] + left.astype(F32)) + (right.astype(F32) + far.astype(F32))


def attention_kernel(
    n_src, buf_of, row_of, q_ref, do_ref, own_ref, *rest
):
    srcs = rest[:n_src]
    dq_ref, down_ref = rest[n_src : n_src + 2]
    outs = rest[n_src + 2 : 2 * n_src + 2]
    kv, stage, q_st, do_st, p_t, ds_t, in_sem, out_sem = rest[2 * n_src + 2 :]
    step = pl.program_id(0)
    steps = pl.num_programs(0)
    group = q_ref.shape[1] // HD
    retrieved = in_sem.shape[1]
    rows = retrieved * PLEN
    keys = rows + own_ref.shape[0]
    slot = lax.rem(step, 2)
    scaling = HD ** (-0.5)

    def fetch(query, into):
        @pl.loop(0, retrieved)
        def _(j):
            at = query * retrieved + j
            for b in range(n_src):

                @pl.when(buf_of[at] == b)
                def _():
                    pltpu.make_async_copy(
                        srcs[b].at[row_of[at]],
                        kv.at[into, pl.ds(pl.multiple_of(j * PLEN, PLEN), PLEN)],
                        in_sem.at[into, j],
                    ).start()

    @pl.when(step == 0)
    def _():
        fetch(0, 0)

    @pl.when(step + 1 < steps)
    def _():
        fetch(step + 1, 1 - slot)

    for g in range(group):
        q_st[pl.ds(g * HD, HD), :] = q_ref[:, g * HD : (g + 1) * HD]
        do_st[pl.ds(g * HD, HD), :] = do_ref[:, g * HD : (g + 1) * HD]
    kv[slot, pl.ds(rows, keys - rows), :] = own_ref[...]
    for j in range(retrieved):
        pltpu.make_async_copy(
            srcs[0].at[0], kv.at[slot, pl.ds(j * PLEN, PLEN)], in_sem.at[slot, j]
        ).wait()

    k_all = kv[slot, :, :HD]
    v_all = kv[slot, :, HD:]
    width = 2 * HD
    key_at = lax.broadcasted_iota(jnp.int32, (keys - rows, width), 0)
    tok_at = lax.broadcasted_iota(jnp.int32, (keys - rows, width), 1) % HD
    visible = key_at <= tok_at
    for g in range(0, group, 2):
        cols = pl.ds(g * HD, width)
        s = lax.dot_general(k_all, q_st[cols, :], NT, preferred_element_type=F32)
        s = jnp.concatenate(
            [s[:rows], jnp.where(visible, s[rows:], F32(-1e30))], axis=0
        )
        largest = jnp.max(s, axis=0, keepdims=True)
        e = jnp.exp2((s - largest) * F32(scaling * math.log2(math.e)))
        w = e * (1.0 / jnp.sum(e, axis=0, keepdims=True))
        w_low = w.astype(BF)
        p_t[:, cols] = w_low
        gw = lax.dot_general(v_all, do_st[cols, :], NT, preferred_element_type=F32)
        delta = jnp.sum(w_low.astype(F32) * gw, axis=0, keepdims=True)
        ds_t[:, cols] = (w * (gw - delta)).astype(BF)
    d_v = jnp.dot(p_t[...], do_st[...], preferred_element_type=F32)
    d_k = jnp.dot(ds_t[...], q_st[...], preferred_element_type=F32) * F32(scaling)
    dq_t = lax.dot_general(k_all, ds_t[...], TN, preferred_element_type=F32) * F32(scaling)
    for g in range(group):
        dq_ref[:, g * HD : (g + 1) * HD] = dq_t[:, g * HD : (g + 1) * HD].T.astype(BF)

    down_ref[:, :HD] = d_k[rows:].astype(BF)
    down_ref[:, HD:] = d_v[rows:].astype(BF)

    def sent(at_slot, j):
        return pltpu.make_async_copy(
            stage.at[at_slot, pl.ds(j * PLEN, PLEN)], outs[0].at[0], out_sem.at[at_slot, j]
        )

    @pl.when(step >= 2)
    def _():
        for j in range(retrieved):
            sent(slot, j).wait()

    stage[slot, :, :HD] = d_k[:rows].astype(BF)
    stage[slot, :, HD:] = d_v[:rows].astype(BF)

    @pl.loop(0, retrieved)
    def _(j):
        at = step * retrieved + j
        for b in range(n_src):

            @pl.when(buf_of[at] == b)
            def _():
                pltpu.make_async_copy(
                    stage.at[slot, pl.ds(pl.multiple_of(j * PLEN, PLEN), PLEN)],
                    outs[b].at[row_of[at]],
                    out_sem.at[slot, j],
                ).start()

    @pl.when(step == steps - 1)
    def _():
        for j in range(retrieved):
            if steps > 1:
                sent(1 - slot, j).wait()
            sent(slot, j).wait()


def attention(queries, out_grad, query_kv, sources, out_blocks, buf_of, row_of, n_query):
    rows, width = queries.shape
    qlen = rows // n_query
    retrieved = buf_of.shape[0] // n_query
    keys = retrieved * PLEN + qlen
    local = query_kv.shape[1]
    block = lambda w: pl.BlockSpec((qlen, w), lambda i, *_: (i, 0))
    hbm = pl.BlockSpec(memory_space=pl.ANY)
    return pl.pallas_call(
        functools.partial(attention_kernel, len(sources)),
        out_shape=(
            jax.ShapeDtypeStruct((rows, width), BF),
            jax.ShapeDtypeStruct((rows, local), BF),
        )
        + tuple(jax.ShapeDtypeStruct((n, PLEN, local), BF) for n in out_blocks),
        grid_spec=pltpu.PrefetchScalarGridSpec(
            num_scalar_prefetch=2,
            grid=(n_query,),
            in_specs=[block(width), block(width), block(local)] + [hbm] * len(sources),
            out_specs=(block(width), block(local)) + (hbm,) * len(sources),
            scratch_shapes=[
                pltpu.VMEM((2, keys, local), BF),
                pltpu.VMEM((2, retrieved * PLEN, local), BF),
                pltpu.VMEM((width, HD), BF),
                pltpu.VMEM((width, HD), BF),
                pltpu.VMEM((keys, width), BF),
                pltpu.VMEM((keys, width), BF),
                pltpu.SemaphoreType.DMA((2, retrieved)),
                pltpu.SemaphoreType.DMA((2, retrieved)),
            ],
        ),
        compiler_params=pltpu.CompilerParams(vmem_limit_bytes=48 * 2**20),
        cost_estimate=pl.CostEstimate(
            flops=10 * n_query * keys * qlen * width,
            bytes_accessed=8 * rows * width + 4 * n_query * keys * local,
            transcendentals=n_query * keys * width,
        ),
        name="attention",
    )(buf_of, row_of, queries, out_grad, query_kv, *sources)


def pick_kernel(slot_of, *rest):
    ring, outs, sem = rest[:SIDE], rest[SIDE : 2 * SIDE], rest[2 * SIDE]
    n = outs[0].shape[0]
    copies = []
    for k in range(SIDE):
        for m in range(n):
            place = jnp.maximum(slot_of[k * n + m], 0)
            copies.append(
                pltpu.make_async_copy(
                    ring[(m // 2) % SIDE].at[place], outs[k].at[m], sem.at[k * n + m]
                )
            )
    for copy in copies:
        copy.start()
    for copy in copies:
        copy.wait()


def pick(slot_of, ring):
    n = slot_of.shape[0] // SIDE
    hbm = pl.BlockSpec(memory_space=pl.ANY)
    shape = jax.ShapeDtypeStruct((n,) + ring[0].shape[1:], BF)
    return pl.pallas_call(
        pick_kernel,
        out_shape=[shape] * SIDE,
        grid_spec=pltpu.PrefetchScalarGridSpec(
            num_scalar_prefetch=1,
            in_specs=[hbm] * SIDE,
            out_specs=[pl.BlockSpec(memory_space=pltpu.VMEM)] * SIDE,
            scratch_shapes=[pltpu.SemaphoreType.DMA((SIDE * n,))],
        ),
        compiler_params=pltpu.CompilerParams(vmem_limit_bytes=24 * 2**20),
        cost_estimate=pl.CostEstimate(
            flops=0, bytes_accessed=4 * SIDE * n * PLEN * 2 * HD, transcendentals=0
        ),
        name="pick",
    )(slot_of, *ring)


def add_blocks_kernel(slot_of, *rest):
    parts, outs, total = rest[: 2 * SIDE], rest[2 * SIDE : 3 * SIDE], rest[3 * SIDE]
    n = parts[0].shape[0]
    total[...] = jnp.zeros_like(total)
    for p, part in enumerate(parts):

        @pl.loop(0, n)
        def _(m):
            place = slot_of[p * n + m]

            @pl.when(place >= 0)
            def _():
                total[lax.div(m, 2), place] += part[m].astype(F32)

    outs[0][...] = total[0]
    for j in range(1, SIDE):
        outs[j][...] = total[j].astype(BF)


def add_blocks(slot_of, parts, passages):
    shape = (passages,) + parts[0].shape[1:]
    whole = pl.BlockSpec(memory_space=pltpu.VMEM)
    return pl.pallas_call(
        add_blocks_kernel,
        out_shape=[jax.ShapeDtypeStruct(shape, F32)]
        + [jax.ShapeDtypeStruct(shape, BF)] * (SIDE - 1),
        grid_spec=pltpu.PrefetchScalarGridSpec(
            num_scalar_prefetch=1,
            in_specs=[whole] * (2 * SIDE),
            out_specs=[whole] * SIDE,
            scratch_shapes=[pltpu.VMEM((SIDE,) + shape, F32)],
        ),
        compiler_params=pltpu.CompilerParams(vmem_limit_bytes=32 * 2**20),
        cost_estimate=pl.CostEstimate(
            flops=8 * parts[0].size, bytes_accessed=32 * parts[0].size, transcendentals=0
        ),
        name="add_blocks",
    )(slot_of, *parts)


def add_owners_kernel(own_ref, left_ref, far_ref, right_ref, mine_ref, theirs_ref, turned):
    core = lax.rem(lax.axis_index("pas"), 2)
    for p in range(own_ref.shape[0]):
        total = (own_ref[p] + left_ref[p].astype(F32)) + (
            far_ref[p].astype(F32) + right_ref[p].astype(F32)
        )
        turned[:, p * PLEN : (p + 1) * PLEN] = total.T.astype(BF)
    for z in range(SIDE):
        for ref, which in ((mine_ref, core), (theirs_ref, 1 - core)):
            at = pl.multiple_of(z * 2 * OUT_ROWS + which * OUT_ROWS, OUT_ROWS)
            ref[z * OUT_ROWS : (z + 1) * OUT_ROWS, :] = turned[pl.ds(at, OUT_ROWS), :]


def add_owners(parts):
    passages, length, width = parts[0].shape
    half = jax.ShapeDtypeStruct((width // 2, passages * length), BF)
    whole = pl.BlockSpec(memory_space=pltpu.VMEM)
    return pl.pallas_call(
        add_owners_kernel,
        out_shape=(half, half),
        in_specs=[whole] * SIDE,
        out_specs=(whole, whole),
        scratch_shapes=[pltpu.VMEM((width, passages * length), BF)],
        compiler_params=pltpu.CompilerParams(vmem_limit_bytes=32 * 2**20),
        cost_estimate=pl.CostEstimate(
            flops=4 * parts[0].size, bytes_accessed=12 * parts[0].size, transcendentals=0
        ),
        name="add_owners",
    )(*parts)


def requests(source_device, source_slot, owners, capacity):
    flat_device = source_device.reshape(-1)
    flat_slot = source_slot.reshape(-1)
    owner_hits = (flat_device[:, None] == jnp.arange(owners, dtype=jnp.int32)[None, :]).astype(
        jnp.int32
    )
    at = jnp.arange(flat_device.shape[0])
    earlier_same = jnp.logical_and(
        flat_device[:, None] == flat_device[None, :], at[None, :] < at[:, None]
    )
    ranking = jnp.sum(earlier_same.astype(jnp.int32), axis=1)
    slot_hits = (ranking[:, None] == jnp.arange(capacity, dtype=jnp.int32)[None, :]).astype(
        jnp.int32
    )
    placed = owner_hits[:, :, None] * slot_hits[:, None, :]
    table = jnp.sum(placed * (flat_slot + 1)[:, None, None], axis=0) - 1
    return flat_device, ranking, table


def ring_steps(y, z, core, to_y, to_z):
    back_y, back_z = (y - to_y) % SIDE, (z - to_z) % SIDE
    return jnp.where(core == 0, back_z, back_y), jnp.where(core == 0, back_y, back_z)


def own_places(flat_device, ranking, capacity):
    y, z, core, _ = here()
    owner_core = flat_device % 2
    ja, jb = ring_steps(
        y, z, owner_core, flat_device // (2 * SIDE), (flat_device // 2) % SIDE
    )
    block = ja * capacity + ranking
    same = owner_core == core
    return jnp.where(same, jb, SIDE), jnp.where(same, block, jb * SIDE * capacity + block)


def slots_served(tables, owners, capacity):
    y, z, core, _ = here()
    n = jnp.arange(SIDE * 2 * SIDE * capacity, dtype=jnp.int32)
    ja = (n // capacity) % SIDE
    owner = jnp.where(core == 0, device_at(y, (z - ja) % SIDE, 0), device_at((y - ja) % SIDE, z, 0))
    asks = n // (capacity * SIDE)
    at = (asks * owners + owner + core) * capacity + n % capacity
    return tables.reshape(-1)[at]


def per_device(passage_hidden, kv_weight, queries, query_kv, out_grad, source_device, source_slot):
    owners = lax.axis_size("pas")
    rows_local = passage_hidden.shape[0]
    local_width = query_kv.shape[1]
    passages_here = rows_local // PLEN
    queries_here = source_device.shape[0]
    capacity = 2

    flat_device, ranking, table = requests(source_device, source_slot, owners, capacity)
    shards = ring_gather(kv_weight, send_first)
    shards = ring_gather(jnp.concatenate(shards, axis=0), send_second)
    partial = project(passage_hidden, shards + [swap_cores(s) for s in shards], CHUNKS)
    partial, table = lax.optimization_barrier((partial, table))
    pair = jnp.concatenate([table, swap_cores(table)], axis=0)
    tables = jnp.stack([pair] + [send_second(pair, -k) for k in range(1, SIDE)])
    hidden_theirs = swap_cores(passage_hidden)
    buf_of, row_of = own_places(flat_device, ranking, capacity)
    served = slots_served(tables, owners, capacity)

    quarters = [partial[n * SIDE : (n + 1) * SIDE] for n in range(CHUNKS)]
    own = [reduce_heads(quarters[n : n + 2]) for n in range(0, CHUNKS, 2)]
    own = jnp.concatenate(own, axis=0).reshape(passages_here, PLEN, local_width)
    wanted = pick(served, ring_gather(own, send_first))
    got = [wanted[0]] + [send_second(wanted[k], k) for k in range(1, SIDE)]
    half = got[0].shape[0] // 2
    sources = got + [swap_cores(jnp.concatenate([g[half:] for g in got], axis=0))]
    grad_queries, own_grads, *grads = attention(
        queries,
        out_grad,
        query_kv,
        sources,
        [half] * SIDE + [SIDE * half],
        buf_of,
        row_of,
        queries_here,
    )
    mine, theirs = grads[:SIDE], swap_cores(grads[SIDE])
    theirs = [theirs[k * half : (k + 1) * half] for k in range(SIDE)]
    parts = [mine[0], theirs[0]]
    for k in range(1, SIDE):
        parts += [send_second(mine[k], -k), send_second(theirs[k], -k)]
    sums = add_blocks(served, parts, passages_here)
    mine, theirs = add_owners([sums[0]] + [send_first(sums[j], -j) for j in range(1, SIDE)])
    mine_heads = ring_gather_halves(mine, send_tp)
    theirs_heads = ring_gather_halves(swap_cores(theirs), send_tp)
    blocks = weight_product(mine_heads, theirs_heads, passage_hidden, hidden_theirs)
    return grad_queries, own_grads, reduce_owners(blocks)


def solution(mesh):
    in_specs = (
        P("pas", "tp"),
        P("pas", "tp"),
        P("pas", "tp"),
        P("pas", "tp"),
        P("pas", "tp"),
        P("pas", None),
        P("pas", None),
    )
    out_specs = (P("pas", "tp"), P("pas", "tp"), P("pas", "tp"))
    return jax.shard_map(
        per_device, mesh=mesh, in_specs=in_specs, out_specs=out_specs, check_vma=False
    )
```

profile of v0, /device:TPU:0, one launch (start us, length us, event | category | flops | bytes accessed | tf_op | source)
XLA Modules:
  0.0 284.7 jit_solution(11008444613688383169)
XLA Ops:
  0.6 4.0 %collective-permute-start.1 = (bf16[32,2048]{1,0:T(8,128)(2,1)}, bf16[32,2048]{1,0:T(8,128)(2,1)S(1)}, u32[]{:S(2)}, u32[]{:S(2)}) collective-permute-start(bf16[32,2048]{1,0:T(8,128)(2,1)} %param.8), channel_id=1, source_target_pairs={{0,16},{4,68},{8,24},{12,76},{16,0},{20,84},{24,8},{28,92},{32,48}... | collective-permute-start | bytes 393224 | tf_op jit(solution)/shard_map/ppermute | solution.py:40
  5.7 2.2 collective-permute-start.2
  11.1 3.1 %collective-permute-start.5 = (bf16[128,2048]{1,0:T(8,128)(2,1)S(1)}, bf16[128,2048]{1,0:T(8,128)(2,1)S(1)}, u32[]{:S(2)}, u32[]{:S(2)}) collective-permute-start(bf16[128,2048]{1,0:T(8,128)(2,1)S(1)} %constant_dynamic-update-slice_fusion.rest_0_), channel_id=1, source_target_pairs={{0,96},{4,28},{8,104},{12,4},{16,112},{20,12},{24,120},{28,20},{32... | collective-permute-start | bytes 1572872 | tf_op jit(solution)/shard_map/ppermute | solution.py:44
  17.3 9.2 %collective-permute-done.5.rest_3_ = bf16[128,2048]{1,0:T(8,128)(2,1)S(1)} collective-permute-done((bf16[128,2048]{1,0:T(8,128)(2,1)S(1)}, bf16[128,2048]{1,0:T(8,128)(2,1)S(1)}, u32[]{:S(2)}, u32[]{:S(2)}) %collective-permute-start.5) | collective-permute-done | bytes 524320 | tf_op jit(solution)/shard_map/ppermute | solution.py:44
  27.0 3.5 %collective-permute-done.3.rest_1_ = bf16[128,2048]{1,0:T(8,128)(2,1)S(1)} collective-permute-done((bf16[128,2048]{1,0:T(8,128)(2,1)S(1)}, bf16[128,2048]{1,0:T(8,128)(2,1)S(1)}, u32[]{:S(2)}, u32[]{:S(2)}) %collective-permute-start.3) | collective-permute-done | bytes 524320 | tf_op jit(solution)/shard_map/ppermute | solution.py:44
  32.4 2.2 copy-done
  34.6 12.8 %project.1 = (f32[256,256]{1,0:T(8,128)S(1)}, f32[256,256]{1,0:T(8,128)S(1)}, f32[256,256]{1,0:T(8,128)S(1)}, f32[256,256]{1,0:T(8,128)S(1)}, f32[256,256]{1,0:T...) custom-call(bf16[1024,2048]{1,0:T(8,128)(2,1)S(1)} %copy-done, ...), custom_call_target="tpu_custom_call" | custom-call | flops 4294967296 | bytes 12582912 | tf_op jit(solution)/shard_map/project/pallas_call | solution.py:151
  51.0 3.0 %collective-permute-start.23 = (f32[256,256]{1,0:T(8,128)S(1)}, f32[256,256]{1,0:T(8,128)S(1)}, u32[]{:S(2)}, u32[]{:S(2)}) collective-permute-start(f32[256,256]{1,0:T(8,128)S(1)} %get-tuple-element.86), channel_id=1, source_target_pairs={{0,3},{1,0},{2,1},{3,2},{4,7},{5,4},{6,5},{7,6},{8,11},{9,8},{10,9... | collective-permute-start | bytes 786440 | tf_op jit(solution)/shard_map/ppermute | solution.py:48
  53.9 3.9 %collective-permute-done.14 = f32[256,256]{1,0:T(8,128)S(1)} collective-permute-done((f32[256,256]{1,0:T(8,128)S(1)}, f32[256,256]{1,0:T(8,128)S(1)}, u32[]{:S(2)}, u32[]{:S(2)}) %collective-permute-start.14) | collective-permute-done | bytes 262176 | tf_op jit(solution)/shard_map/ppermute | solution.py:48
  58.3 3.0 %collective-permute-start.18 = (f32[256,256]{1,0:T(8,128)S(1)}, f32[256,256]{1,0:T(8,128)S(1)}, u32[]{:S(2)}, u32[]{:S(2)}) collective-permute-start(f32[256,256]{1,0:T(8,128)S(1)} %add.263), channel_id=1, source_target_pairs={{0,3},{1,0},{2,1},{3,2},{4,7},{5,4},{6,5},{7,6},{8,11},{9,8},{10,9... | collective-permute-start | bytes 786440 | tf_op jit(solution)/shard_map/ppermute | solution.py:48
  61.3 2.2 collective-permute-done.20
  63.9 3.0 %collective-permute-start.24 = (f32[256,256]{1,0:T(8,128)S(1)}, f32[256,256]{1,0:T(8,128)S(1)}, u32[]{:S(2)}, u32[]{:S(2)}) collective-permute-start(f32[256,256]{1,0:T(8,128)S(1)} %add.269), channel_id=1, source_target_pairs={{0,3},{1,0},{2,1},{3,2},{4,7},{5,4},{6,5},{7,6},{8,11},{9,8},{10,9... | collective-permute-start | bytes 786440 | tf_op jit(solution)/shard_map/ppermute | solution.py:48
  66.9 2.2 collective-permute-done.15
  69.5 3.0 %collective-permute-start.19 = (f32[256,256]{1,0:T(8,128)S(1)}, f32[256,256]{1,0:T(8,128)S(1)}, u32[]{:S(2)}, u32[]{:S(2)}) collective-permute-start(f32[256,256]{1,0:T(8,128)S(1)} %add.264), channel_id=1, source_target_pairs={{0,3},{1,0},{2,1},{3,2},{4,7},{5,4},{6,5},{7,6},{8,11},{9,8},{10,9... | collective-permute-start | bytes 786440 | tf_op jit(solution)/shard_map/ppermute | solution.py:48
  72.5 2.2 collective-permute-done.21
  75.1 3.0 %collective-permute-start.25 = (f32[256,256]{1,0:T(8,128)S(1)}, f32[256,256]{1,0:T(8,128)S(1)}, u32[]{:S(2)}, u32[]{:S(2)}) collective-permute-start(f32[256,256]{1,0:T(8,128)S(1)} %add.270), channel_id=1, source_target_pairs={{0,3},{1,0},{2,1},{3,2},{4,7},{5,4},{6,5},{7,6},{8,11},{9,8},{10,9... | collective-permute-start | bytes 786440 | tf_op jit(solution)/shard_map/ppermute | solution.py:48
  78.1 2.2 collective-permute-done.16
  80.7 4.5 %collective-permute-done.22 = f32[256,256]{1,0:T(8,128)S(1)} collective-permute-done((f32[256,256]{1,0:T(8,128)S(1)}, f32[256,256]{1,0:T(8,128)S(1)}, u32[]{:S(2)}, u32[]{:S(2)}) %collective-permute-start.22) | collective-permute-done | bytes 262176 | tf_op jit(solution)/shard_map/ppermute | solution.py:48
  85.3 3.2 %collective-permute-start.28 = (bf16[8,128,256]{2,1,0:T(8,128)(2,1)S(1)}, bf16[8,128,256]{2,1,0:T(8,128)(2,1)S(1)}, u32[]{:S(2)}, u32[]{:S(2)}) collective-permute-start(bf16[8,128,256]{2,1,0:T(8,128)(2,1)S(1)} %bitcast.19), channel_id=1, source_target_pairs={{0,24},{4,100},{8,0},{12,108},{16,8},{20,116},{24,16},{28,124},{32... | collective-permute-start | bytes 1572872 | tf_op jit(solution)/shard_map/ppermute | solution.py:40
  90.9 2.7 collective-permute-start.12
  96.1 3.1 %collective-permute-done.11 = s32[64,2]{0,1:T(2,128)S(1)} collective-permute-done((s32[64,2]{0,1:T(2,128)S(1)}, s32[64,2]{0,1:T(2,128)S(1)}, u32[]{:S(2)}, u32[]{:S(2)}) %collective-permute-start.11) | collective-permute-done | bytes 544 | tf_op jit(solution)/shard_map/ppermute | solution.py:44
  100.8 3.7 %collective-permute-done.26.rest_1_ = bf16[8,128,256]{2,1,0:T(8,128)(2,1)S(1)} collective-permute-done((bf16[8,128,256]{2,1,0:T(8,128)(2,1)S(1)}, bf16[8,128,256]{2,1,0:T(8,128)(2,1)S(1)}, u32[]{:S(2)}, u32[]{:S(2)}) %collective-permute-start.26) | collective-permute-done | bytes 524320 | tf_op jit(solution)/shard_map/ppermute | solution.py:40
  104.5 7.7 %pick.1 = (bf16[16,128,256]{2,1,0:T(8,128)(2,1)S(1)}, bf16[16,128,256]{2,1,0:T(8,128)(2,1)S(1)}, bf16[16,128,256]{2,1,0:T(8,128)(2,1)S(1)}, bf16[16,128,256]{2,1,0:T(8,128)(2,1)S(1)}) custom-call(s32[64]{0:T(128)S(1)} %gather_fusion, bf16[8,128,256]{2,1,0:T(8,128)(2,1)S(1)} %bitcast.22, bf16[8,128,256]{2,1,0:T(8,128)(2,1)S(1)} %collective-permute-done.26.rest_1_, ...), custom_call_target="tpu_custom_call" | custom-call | bytes 8388608 | tf_op jit(solution)/shard_map/pick/pallas_call | solution.py:429
  112.3 2.7 collective-permute-start.30
  115.6 23.9 %collective-permute-done.29.rest_1_ = bf16[16,128,256]{2,1,0:T(8,128)(2,1)S(1)} collective-permute-done((bf16[16,128,256]{2,1,0:T(8,128)(2,1)S(1)}, bf16[16,128,256]{2,1,0:T(8,128)(2,1)S(1)}, u32[]{:S(2)}, u32[]{:S(2)}) %collective-permute-start.29) | collective-permute-done | bytes 1048608 | tf_op jit(solution)/shard_map/ppermute | solution.py:44
  143.9 2.2 collective-permute-done.32.rest_4_
  147.5 27.3 %attention.1 = (bf16[512,1024]{1,0:T(8,128)(2,1)}, bf16[512,256]{1,0:T(8,128)(2,1)}, bf16[8,128,256]{2,1,0:T(8,128)(2,1)S(1)}, bf16[8,128,256]{2,1,0:T(8,128)(2,...) custom-call(s32[32]{0:T(128)S(1)} %compare_select_fusion.16.buf_of, ...), custom_call_target="tpu_custom_call" | custom-call | flops 6039797760 | bytes 8912896 | tf_op jit(solution)/shard_map/attention/pallas_call | solution.py:374
  174.9 2.2 collective-permute-start.34
  180.8 8.6 %collective-permute-done.34.rest_2_ = bf16[8,128,256]{2,1,0:T(8,128)(2,1)S(1)} collective-permute-done((bf16[8,128,256]{2,1,0:T(8,128)(2,1)S(1)}, bf16[8,128,256]{2,1,0:T(8,128)(2,1)S(1)}, u32[]{:S(2)}, u32[]{:S(2)}) %collective-permute-start.34) | collective-permute-done | bytes 524320 | tf_op jit(solution)/shard_map/ppermute | solution.py:44
  189.4 3.7 %collective-permute-start.35 = (bf16[8,128,256]{2,1,0:T(8,128)(2,1)S(1)}, bf16[8,128,256]{2,1,0:T(8,128)(2,1)S(1)}, u32[]{:S(2)}, u32[]{:S(2)}) collective-permute-start(bf16[8,128,256]{2,1,0:T(8,128)(2,1)S(1)} %get-tuple-element.118), channel_id=1, source_target_pairs={{0,96},{4,28},{8,104},{12,4},{16,112},{20,12},{24,120},{28,20},{32... | collective-permute-start | bytes 1572872 | tf_op jit(solution)/shard_map/ppermute | solution.py:44
  193.1 5.6 %collective-permute-done.39.rest_7_ = bf16[8,128,256]{2,1,0:T(8,128)(2,1)S(1)} collective-permute-done((bf16[8,128,256]{2,1,0:T(8,128)(2,1)S(1)}, bf16[8,128,256]{2,1,0:T(8,128)(2,1)S(1)}, u32[]{:S(2)}, u32[]{:S(2)}) %collective-permute-start.39) | collective-permute-done | bytes 524320 | tf_op jit(solution)/shard_map/ppermute | solution.py:44
  198.7 6.0 %collective-permute-done.37.rest_5_ = bf16[8,128,256]{2,1,0:T(8,128)(2,1)S(1)} collective-permute-done((bf16[8,128,256]{2,1,0:T(8,128)(2,1)S(1)}, bf16[8,128,256]{2,1,0:T(8,128)(2,1)S(1)}, u32[]{:S(2)}, u32[]{:S(2)}) %collective-permute-start.37) | collective-permute-done | bytes 524320 | tf_op jit(solution)/shard_map/ppermute | solution.py:44
  204.6 2.1 collective-permute-done.35.rest_3_
  206.7 2.4 add_blocks.1
  211.2 7.2 %collective-permute-done.40.left_ref = bf16[8,128,256]{2,1,0:T(8,128)(2,1)S(1)} collective-permute-done((bf16[8,128,256]{2,1,0:T(8,128)(2,1)S(1)}, bf16[8,128,256]{2,1,0:T(8,128)(2,1)S(1)}, u32[]{:S(2)}, u32[]{:S(2)}) %collective-permute-start.40) | collective-permute-done | bytes 524320 | tf_op jit(solution)/shard_map/ppermute | solution.py:40
  218.4 2.5 collective-permute-done.41.far_ref
  220.9 5.5 %collective-permute-done.42.right_ref = bf16[8,128,256]{2,1,0:T(8,128)(2,1)S(1)} collective-permute-done((bf16[8,128,256]{2,1,0:T(8,128)(2,1)S(1)}, bf16[8,128,256]{2,1,0:T(8,128)(2,1)S(1)}, u32[]{:S(2)}, u32[]{:S(2)}) %collective-permute-start.42) | collective-permute-done | bytes 524320 | tf_op jit(solution)/shard_map/ppermute | solution.py:40
  226.9 3.0 %collective-permute-start.45 = (bf16[128,1024]{1,0:T(8,128)(2,1)S(1)}, bf16[128,1024]{1,0:T(8,128)(2,1)S(1)}, u32[]{:S(2)}, u32[]{:S(2)}) collective-permute-start(bf16[128,1024]{1,0:T(8,128)(2,1)S(1)} %get-tuple-element.105.refs_0_), channel_id=1, source_target_pairs={{0,3},{1,0},{2,1},{3,2},{4,7},{5,4},{6,5},{7,6},{8,11},{9,8},{10,9... | collective-permute-start | bytes 786440 | tf_op jit(solution)/shard_map/ppermute | solution.py:48
  229.9 3.2 %collective-permute-start.50 = (bf16[128,1024]{1,0:T(8,128)(2,1)S(1)}, bf16[128,1024]{1,0:T(8,128)(2,1)S(1)}, u32[]{:S(2)}, u32[]{:S(2)}) collective-permute-start(bf16[128,1024]{1,0:T(8,128)(2,1)S(1)} %collective-permute-done.47.refs_5_), channel_id=1, source_target_pairs={{0,3},{1,0},{2,1},{3,2},{4,7},{5,4},{6,5},{7,6},{8,11},{9,8},{10,9... | collective-permute-start | bytes 786440 | tf_op jit(solution)/shard_map/ppermute | solution.py:48
  233.2 3.4 %collective-permute-done.45.refs_4_ = bf16[128,1024]{1,0:T(8,128)(2,1)S(1)} collective-permute-done((bf16[128,1024]{1,0:T(8,128)(2,1)S(1)}, bf16[128,1024]{1,0:T(8,128)(2,1)S(1)}, u32[]{:S(2)}, u32[]{:S(2)}) %collective-permute-start.45) | collective-permute-done | bytes 262176 | tf_op jit(solution)/shard_map/ppermute | solution.py:48
  236.6 3.8 %collective-permute-start.46 = (bf16[64,1024]{1,0:T(8,128)(2,1)S(1)}, bf16[64,1024]{1,0:T(8,128)(2,1)S(1)}, u32[]{:S(2)}, u32[]{:S(2)}) collective-permute-start(bf16[64,1024]{1,0:T(8,128)(2,1)S(1)} %slice.79), channel_id=1, source_target_pairs={{0,3},{1,0},{2,1},{3,2},{4,7},{5,4},{6,5},{7,6},{8,11},{9,8},{10,9... | collective-permute-start | bytes 393224 | tf_op jit(solution)/shard_map/ppermute | solution.py:48
  242.2 3.8 %collective-permute-start.51 = (bf16[64,1024]{1,0:T(8,128)(2,1)S(1)}, bf16[64,1024]{1,0:T(8,128)(2,1)S(1)}, u32[]{:S(2)}, u32[]{:S(2)}) collective-permute-start(bf16[64,1024]{1,0:T(8,128)(2,1)S(1)} %slice.81), channel_id=1, source_target_pairs={{0,3},{1,0},{2,1},{3,2},{4,7},{5,4},{6,5},{7,6},{8,11},{9,8},{10,9... | collective-permute-start | bytes 393224 | tf_op jit(solution)/shard_map/ppermute | solution.py:48
  248.5 3.7 %collective-permute-done.49.refs_7_ = bf16[64,1024]{1,0:T(8,128)(2,1)S(1)} collective-permute-done((bf16[64,1024]{1,0:T(8,128)(2,1)S(1)}, bf16[64,1024]{1,0:T(8,128)(2,1)S(1)}, u32[]{:S(2)}, u32[]{:S(2)}) %collective-permute-start.49) | collective-permute-done | bytes 131104 | tf_op jit(solution)/shard_map/ppermute | solution.py:48
  252.2 6.4 %weight_product.1 = (f32[4,32,2048]{2,1,0:T(8,128)S(1)}, bf16[4,32,2048]{2,1,0:T(8,128)(2,1)S(1)}, bf16[4,32,2048]{2,1,0:T(8,128)(2,1)S(1)}, bf16[4,32,2048]{2,1,0:T(8,128)(2,1)S(1)}) custom-call(bf16[128,1024]{1,0:T(8,128)(2,1)S(1)} %get-tuple-element.105.refs_0_, bf16[128,1024]{1,0:T(8,128)(2,1)S(1)} %collective-permute-done.43.refs_1_, ...), custom_call_target="tpu_custom_call" | custom-call | flops 4294967296 | bytes 12582912 | tf_op jit(solution)/shard_map/weight_product/pallas_call | solution.py:222
  258.7 3.2 %collective-permute-start.54 = (bf16[4,32,2048]{2,1,0:T(8,128)(2,1)S(1)}, bf16[4,32,2048]{2,1,0:T(8,128)(2,1)S(1)}, u32[]{:S(2)}, u32[]{:S(2)}) collective-permute-start(bf16[4,32,2048]{2,1,0:T(8,128)(2,1)S(1)} %get-tuple-element.109), channel_id=1, source_target_pairs={{0,24},{4,100},{8,0},{12,108},{16,8},{20,116},{24,16},{28,124},{32... | collective-permute-start | bytes 1572872 | tf_op jit(solution)/shard_map/ppermute | solution.py:40
  261.9 12.8 %collective-permute-done.53 = bf16[4,32,2048]{2,1,0:T(8,128)(2,1)S(1)} collective-permute-done((bf16[4,32,2048]{2,1,0:T(8,128)(2,1)S(1)}, bf16[4,32,2048]{2,1,0:T(8,128)(2,1)S(1)}, u32[]{:S(2)}, u32[]{:S(2)}) %collective-permute-start.53) | collective-permute-done | bytes 524320 | tf_op jit(solution)/shard_map/ppermute | solution.py:40
  275.1 3.8 %collective-permute-start.58 = (bf16[32,2048]{1,0:T(8,128)(2,1)S(1)}, bf16[32,2048]{1,0:T(8,128)(2,1)S(1)}, u32[]{:S(2)}, u32[]{:S(2)}) collective-permute-start(bf16[32,2048]{1,0:T(8,128)(2,1)S(1)} %get-tuple-element.121), channel_id=1, source_target_pairs={{0,64},{4,20},{8,72},{12,28},{16,80},{20,4},{24,88},{28,12},{32,96... | collective-permute-start | bytes 393224 | tf_op jit(solution)/shard_map/ppermute | solution.py:44
  278.9 2.3 collective-permute-done.56
  (141 shorter events, 42.9 us)
Async XLA Ops:
  0.6 10.4 %collective-permute-start.1 = (bf16[32,2048]{1,0:T(8,128)(2,1)}, bf16[32,2048]{1,0:T(8,128)(2,1)S(1)}, u32[]{:S(2)}, u32[]{:S(2)}) collective-permute-start(bf16[32,2048]{1,0:T(8,128)(2,1)} %param.8), channel_id=1, source_target_pairs={{0,16},{4,68},{8,24},{12,76},{16,0},{20,84},{24,8},{28,92},{32,48}... | collective-permute-start | bytes 393224 | tf_op jit(solution)/shard_map/ppermute | solution.py:40
  4.7 6.4 %collective-permute-start = (bf16[32,2048]{1,0:T(8,128)(2,1)}, bf16[32,2048]{1,0:T(8,128)(2,1)S(1)}, u32[]{:S(2)}, u32[]{:S(2)}) collective-permute-start(bf16[32,2048]{1,0:T(8,128)(2,1)} %param.8), channel_id=1, source_target_pairs={{0,8},{4,36},{8,16},{12,44},{16,24},{20,52},{24,0},{28,60},{32,40}... | collective-permute-start | bytes 393224 | tf_op jit(solution)/shard_map/ppermute | solution.py:40
  5.7 5.4 %collective-permute-start.2 = (bf16[32,2048]{1,0:T(8,128)(2,1)}, bf16[32,2048]{1,0:T(8,128)(2,1)S(1)}, u32[]{:S(2)}, u32[]{:S(2)}) collective-permute-start(bf16[32,2048]{1,0:T(8,128)(2,1)} %param.8), channel_id=1, source_target_pairs={{0,24},{4,100},{8,0},{12,108},{16,8},{20,116},{24,16},{28,124},{32... | collective-permute-start | bytes 393224 | tf_op jit(solution)/shard_map/ppermute | solution.py:40
  11.1 15.4 %collective-permute-start.5 = (bf16[128,2048]{1,0:T(8,128)(2,1)S(1)}, bf16[128,2048]{1,0:T(8,128)(2,1)S(1)}, u32[]{:S(2)}, u32[]{:S(2)}) collective-permute-start(bf16[128,2048]{1,0:T(8,128)(2,1)S(1)} %constant_dynamic-update-slice_fusion.rest_0_), channel_id=1, source_target_pairs={{0,96},{4,28},{8,104},{12,4},{16,112},{20,12},{24,120},{28,20},{32... | collective-permute-start | bytes 1572872 | tf_op jit(solution)/shard_map/ppermute | solution.py:44
  14.2 12.3 %collective-permute-start.4 = (bf16[128,2048]{1,0:T(8,128)(2,1)S(1)}, bf16[128,2048]{1,0:T(8,128)(2,1)S(1)}, u32[]{:S(2)}, u32[]{:S(2)}) collective-permute-start(bf16[128,2048]{1,0:T(8,128)(2,1)S(1)} %constant_dynamic-update-slice_fusion.rest_0_), channel_id=1, source_target_pairs={{0,64},{4,20},{8,72},{12,28},{16,80},{20,4},{24,88},{28,12},{32,96... | collective-permute-start | bytes 1572872 | tf_op jit(solution)/shard_map/ppermute | solution.py:44
  14.9 15.6 %collective-permute-start.3 = (bf16[128,2048]{1,0:T(8,128)(2,1)S(1)}, bf16[128,2048]{1,0:T(8,128)(2,1)S(1)}, u32[]{:S(2)}, u32[]{:S(2)}) collective-permute-start(bf16[128,2048]{1,0:T(8,128)(2,1)S(1)} %constant_dynamic-update-slice_fusion.rest_0_), channel_id=1, source_target_pairs={{0,32},{4,12},{8,40},{12,20},{16,48},{20,28},{24,56},{28,4},{32,64... | collective-permute-start | bytes 1572872 | tf_op jit(solution)/shard_map/ppermute | solution.py:44
  17.2 13.4 %collective-permute-start.6 = (bf16[128,2048]{1,0:T(8,128)(2,1)S(1)}, bf16[128,2048]{1,0:T(8,128)(2,1)S(1)}, u32[]{:S(2)}, u32[]{:S(2)}) collective-permute-start(bf16[128,2048]{1,0:T(8,128)(2,1)S(1)} %constant_dynamic-update-slice_fusion.rest_0_), channel_id=1, source_target_pairs={{0,4},{4,0},{8,12},{12,8},{16,20},{20,16},{24,28},{28,24},{32,36},... | collective-permute-start | bytes 1572872 | tf_op jit(solution)/shard_map/ppermute | solution.py:52
  47.4 10.4 %collective-permute-start.14 = (f32[256,256]{1,0:T(8,128)S(1)}, f32[256,256]{1,0:T(8,128)S(1)}, u32[]{:S(2)}, u32[]{:S(2)}) collective-permute-start(f32[256,256]{1,0:T(8,128)S(1)} %get-tuple-element.74), channel_id=1, source_target_pairs={{0,1},{1,2},{2,3},{3,0},{4,5},{5,6},{6,7},{7,4},{8,9},{9,10},{10,1... | collective-permute-start | bytes 786440 | tf_op jit(solution)/shard_map/ppermute | solution.py:48
  49.0 9.3 %collective-permute-start.17 = (f32[256,256]{1,0:T(8,128)S(1)}, f32[256,256]{1,0:T(8,128)S(1)}, u32[]{:S(2)}, u32[]{:S(2)}) collective-permute-start(f32[256,256]{1,0:T(8,128)S(1)} %get-tuple-element.78), channel_id=1, source_target_pairs={{0,3},{1,0},{2,1},{3,2},{4,7},{5,4},{6,5},{7,6},{8,11},{9,8},{10,9... | collective-permute-start | bytes 786440 | tf_op jit(solution)/shard_map/ppermute | solution.py:48
  50.7 12.7 %collective-permute-start.20 = (f32[256,256]{1,0:T(8,128)S(1)}, f32[256,256]{1,0:T(8,128)S(1)}, u32[]{:S(2)}, u32[]{:S(2)}) collective-permute-start(f32[256,256]{1,0:T(8,128)S(1)} %get-tuple-element.82), channel_id=1, source_target_pairs={{0,1},{1,2},{2,3},{3,0},{4,5},{5,6},{6,7},{7,4},{8,9},{9,10},{10,1... | collective-permute-start | bytes 786440 | tf_op jit(solution)/shard_map/ppermute | solution.py:48
  51.0 12.8 %collective-permute-start.23 = (f32[256,256]{1,0:T(8,128)S(1)}, f32[256,256]{1,0:T(8,128)S(1)}, u32[]{:S(2)}, u32[]{:S(2)}) collective-permute-start(f32[256,256]{1,0:T(8,128)S(1)} %get-tuple-element.86), channel_id=1, source_target_pairs={{0,3},{1,0},{2,1},{3,2},{4,7},{5,4},{6,5},{7,6},{8,11},{9,8},{10,9... | collective-permute-start | bytes 786440 | tf_op jit(solution)/shard_map/ppermute | solution.py:48
  57.9 11.2 %collective-permute-start.15 = (f32[256,256]{1,0:T(8,128)S(1)}, f32[256,256]{1,0:T(8,128)S(1)}, u32[]{:S(2)}, u32[]{:S(2)}) collective-permute-start(f32[256,256]{1,0:T(8,128)S(1)} %add.260), channel_id=1, source_target_pairs={{0,1},{1,2},{2,3},{3,0},{4,5},{5,6},{6,7},{7,4},{8,9},{9,10},{10,1... | collective-permute-start | bytes 786440 | tf_op jit(solution)/shard_map/ppermute | solution.py:48
  58.3 11.2 %collective-permute-start.18 = (f32[256,256]{1,0:T(8,128)S(1)}, f32[256,256]{1,0:T(8,128)S(1)}, u32[]{:S(2)}, u32[]{:S(2)}) collective-permute-start(f32[256,256]{1,0:T(8,128)S(1)} %add.263), channel_id=1, source_target_pairs={{0,3},{1,0},{2,1},{3,2},{4,7},{5,4},{6,5},{7,6},{8,11},{9,8},{10,9... | collective-permute-start | bytes 786440 | tf_op jit(solution)/shard_map/ppermute | solution.py:48
  63.5 11.2 %collective-permute-start.21 = (f32[256,256]{1,0:T(8,128)S(1)}, f32[256,256]{1,0:T(8,128)S(1)}, u32[]{:S(2)}, u32[]{:S(2)}) collective-permute-start(f32[256,256]{1,0:T(8,128)S(1)} %add.266), channel_id=1, source_target_pairs={{0,1},{1,2},{2,3},{3,0},{4,5},{5,6},{6,7},{7,4},{8,9},{9,10},{10,1... | collective-permute-start | bytes 786440 | tf_op jit(solution)/shard_map/ppermute | solution.py:48
  63.9 11.2 %collective-permute-start.24 = (f32[256,256]{1,0:T(8,128)S(1)}, f32[256,256]{1,0:T(8,128)S(1)}, u32[]{:S(2)}, u32[]{:S(2)}) collective-permute-start(f32[256,256]{1,0:T(8,128)S(1)} %add.269), channel_id=1, source_target_pairs={{0,3},{1,0},{2,1},{3,2},{4,7},{5,4},{6,5},{7,6},{8,11},{9,8},{10,9... | collective-permute-start | bytes 786440 | tf_op jit(solution)/shard_map/ppermute | solution.py:48
  69.1 11.2 %collective-permute-start.16 = (f32[256,256]{1,0:T(8,128)S(1)}, f32[256,256]{1,0:T(8,128)S(1)}, u32[]{:S(2)}, u32[]{:S(2)}) collective-permute-start(f32[256,256]{1,0:T(8,128)S(1)} %add.261), channel_id=1, source_target_pairs={{0,1},{1,2},{2,3},{3,0},{4,5},{5,6},{6,7},{7,4},{8,9},{9,10},{10,1... | collective-permute-start | bytes 786440 | tf_op jit(solution)/shard_map/ppermute | solution.py:48
  69.5 11.1 %collective-permute-start.19 = (f32[256,256]{1,0:T(8,128)S(1)}, f32[256,256]{1,0:T(8,128)S(1)}, u32[]{:S(2)}, u32[]{:S(2)}) collective-permute-start(f32[256,256]{1,0:T(8,128)S(1)} %add.264), channel_id=1, source_target_pairs={{0,3},{1,0},{2,1},{3,2},{4,7},{5,4},{6,5},{7,6},{8,11},{9,8},{10,9... | collective-permute-start | bytes 786440 | tf_op jit(solution)/shard_map/ppermute | solution.py:48
  74.7 10.4 %collective-permute-start.22 = (f32[256,256]{1,0:T(8,128)S(1)}, f32[256,256]{1,0:T(8,128)S(1)}, u32[]{:S(2)}, u32[]{:S(2)}) collective-permute-start(f32[256,256]{1,0:T(8,128)S(1)} %add.267), channel_id=1, source_target_pairs={{0,1},{1,2},{2,3},{3,0},{4,5},{5,6},{6,7},{7,4},{8,9},{9,10},{10,1... | collective-permute-start | bytes 786440 | tf_op jit(solution)/shard_map/ppermute | solution.py:48
  75.1 10.0 %collective-permute-start.25 = (f32[256,256]{1,0:T(8,128)S(1)}, f32[256,256]{1,0:T(8,128)S(1)}, u32[]{:S(2)}, u32[]{:S(2)}) collective-permute-start(f32[256,256]{1,0:T(8,128)S(1)} %add.270), channel_id=1, source_target_pairs={{0,3},{1,0},{2,1},{3,2},{4,7},{5,4},{6,5},{7,6},{8,11},{9,8},{10,9... | collective-permute-start | bytes 786440 | tf_op jit(solution)/shard_map/ppermute | solution.py:48
  85.3 15.6 %collective-permute-start.28 = (bf16[8,128,256]{2,1,0:T(8,128)(2,1)S(1)}, bf16[8,128,256]{2,1,0:T(8,128)(2,1)S(1)}, u32[]{:S(2)}, u32[]{:S(2)}) collective-permute-start(bf16[8,128,256]{2,1,0:T(8,128)(2,1)S(1)} %bitcast.19), channel_id=1, source_target_pairs={{0,24},{4,100},{8,0},{12,108},{16,8},{20,116},{24,16},{28,124},{32... | collective-permute-start | bytes 1572872 | tf_op jit(solution)/shard_map/ppermute | solution.py:40
  88.5 12.3 %collective-permute-start.27 = (bf16[8,128,256]{2,1,0:T(8,128)(2,1)S(1)}, bf16[8,128,256]{2,1,0:T(8,128)(2,1)S(1)}, u32[]{:S(2)}, u32[]{:S(2)}) collective-permute-start(bf16[8,128,256]{2,1,0:T(8,128)(2,1)S(1)} %bitcast.20), channel_id=1, source_target_pairs={{0,16},{4,68},{8,24},{12,76},{16,0},{20,84},{24,8},{28,92},{32,48}... | collective-permute-start | bytes 1572872 | tf_op jit(solution)/shard_map/ppermute | solution.py:40
  88.5 16.0 %collective-permute-start.26 = (bf16[8,128,256]{2,1,0:T(8,128)(2,1)S(1)}, bf16[8,128,256]{2,1,0:T(8,128)(2,1)S(1)}, u32[]{:S(2)}, u32[]{:S(2)}) collective-permute-start(bf16[8,128,256]{2,1,0:T(8,128)(2,1)S(1)} %bitcast.21), channel_id=1, source_target_pairs={{0,8},{4,36},{8,16},{12,44},{16,24},{20,52},{24,0},{28,60},{32,40}... | collective-permute-start | bytes 1572872 | tf_op jit(solution)/shard_map/ppermute | solution.py:40
  112.2 27.3 %collective-permute-start.29 = (bf16[16,128,256]{2,1,0:T(8,128)(2,1)S(1)}, bf16[16,128,256]{2,1,0:T(8,128)(2,1)S(1)}, u32[]{:S(2)}, u32[]{:S(2)}) collective-permute-start(bf16[16,128,256]{2,1,0:T(8,128)(2,1)S(1)} %get-tuple-element.91), channel_id=1, source_target_pairs={{0,32},{4,12},{8,40},{12,20},{16,48},{20,28},{24,56},{28,4},{32,64... | collective-permute-start | bytes 3145736 | tf_op jit(solution)/shard_map/ppermute | solution.py:44
  112.3 27.3 %collective-permute-start.30 = (bf16[16,128,256]{2,1,0:T(8,128)(2,1)S(1)}, bf16[16,128,256]{2,1,0:T(8,128)(2,1)S(1)}, u32[]{:S(2)}, u32[]{:S(2)}) collective-permute-start(bf16[16,128,256]{2,1,0:T(8,128)(2,1)S(1)} %get-tuple-element.92), channel_id=1, source_target_pairs={{0,64},{4,20},{8,72},{12,28},{16,80},{20,4},{24,88},{28,12},{32,96... | collective-permute-start | bytes 3145736 | tf_op jit(solution)/shard_map/ppermute | solution.py:44
  114.9 25.5 %collective-permute-start.31 = (bf16[16,128,256]{2,1,0:T(8,128)(2,1)S(1)}, bf16[16,128,256]{2,1,0:T(8,128)(2,1)S(1)}, u32[]{:S(2)}, u32[]{:S(2)}) collective-permute-start(bf16[16,128,256]{2,1,0:T(8,128)(2,1)S(1)} %get-tuple-element.93), channel_id=1, source_target_pairs={{0,96},{4,28},{8,104},{12,4},{16,112},{20,12},{24,120},{28,20},{32... | collective-permute-start | bytes 3145736 | tf_op jit(solution)/shard_map/ppermute | solution.py:44
  143.9 102.2 %collective-permute-start.52 = (bf16[1024,2048]{1,0:T(8,128)(2,1)S(1)}, bf16[1024,2048]{1,0:T(8,128)(2,1)S(1)}, u32[]{:S(2)}, u32[]{:S(2)}) collective-permute-start(bf16[1024,2048]{1,0:T(8,128)(2,1)S(1)} %copy-done.1), channel_id=1, source_target_pairs={{0,4},{4,0},{8,12},{12,8},{16,20},{20,16},{24,28},{28,24},{32,36},... | collective-permute-start | bytes 12582920 | tf_op jit(solution)/shard_map/ppermute | solution.py:52
  174.9 14.6 %collective-permute-start.34 = (bf16[8,128,256]{2,1,0:T(8,128)(2,1)S(1)}, bf16[8,128,256]{2,1,0:T(8,128)(2,1)S(1)}, u32[]{:S(2)}, u32[]{:S(2)}) collective-permute-start(bf16[8,128,256]{2,1,0:T(8,128)(2,1)S(1)} %get-tuple-element.98), channel_id=1, source_target_pairs={{0,96},{4,28},{8,104},{12,4},{16,112},{20,12},{24,120},{28,20},{32... | collective-permute-start | bytes 1572872 | tf_op jit(solution)/shard_map/ppermute | solution.py:44
  177.1 12.4 %collective-permute-start.36 = (bf16[8,128,256]{2,1,0:T(8,128)(2,1)S(1)}, bf16[8,128,256]{2,1,0:T(8,128)(2,1)S(1)}, u32[]{:S(2)}, u32[]{:S(2)}) collective-permute-start(bf16[8,128,256]{2,1,0:T(8,128)(2,1)S(1)} %get-tuple-element.99), channel_id=1, source_target_pairs={{0,64},{4,20},{8,72},{12,28},{16,80},{20,4},{24,88},{28,12},{32,96... | collective-permute-start | bytes 1572872 | tf_op jit(solution)/shard_map/ppermute | solution.py:44
  177.1 16.0 %collective-permute-start.38 = (bf16[8,128,256]{2,1,0:T(8,128)(2,1)S(1)}, bf16[8,128,256]{2,1,0:T(8,128)(2,1)S(1)}, u32[]{:S(2)}, u32[]{:S(2)}) collective-permute-start(bf16[8,128,256]{2,1,0:T(8,128)(2,1)S(1)} %get-tuple-element.100), channel_id=1, source_target_pairs={{0,32},{4,12},{8,40},{12,20},{16,48},{20,28},{24,56},{28,4},{32,64... | collective-permute-start | bytes 1572872 | tf_op jit(solution)/shard_map/ppermute | solution.py:44
  179.4 19.3 %collective-permute-start.39 = (bf16[8,128,256]{2,1,0:T(8,128)(2,1)S(1)}, bf16[8,128,256]{2,1,0:T(8,128)(2,1)S(1)}, u32[]{:S(2)}, u32[]{:S(2)}) collective-permute-start(bf16[8,128,256]{2,1,0:T(8,128)(2,1)S(1)} %get-tuple-element.116), channel_id=1, source_target_pairs={{0,32},{4,12},{8,40},{12,20},{16,48},{20,28},{24,56},{28,4},{32,64... | collective-permute-start | bytes 1572872 | tf_op jit(solution)/shard_map/ppermute | solution.py:44
  189.4 15.2 %collective-permute-start.37 = (bf16[8,128,256]{2,1,0:T(8,128)(2,1)S(1)}, bf16[8,128,256]{2,1,0:T(8,128)(2,1)S(1)}, u32[]{:S(2)}, u32[]{:S(2)}) collective-permute-start(bf16[8,128,256]{2,1,0:T(8,128)(2,1)S(1)} %get-tuple-element.117), channel_id=1, source_target_pairs={{0,64},{4,20},{8,72},{12,28},{16,80},{20,4},{24,88},{28,12},{32,96... | collective-permute-start | bytes 1572872 | tf_op jit(solution)/shard_map/ppermute | solution.py:44
  189.4 17.3 %collective-permute-start.35 = (bf16[8,128,256]{2,1,0:T(8,128)(2,1)S(1)}, bf16[8,128,256]{2,1,0:T(8,128)(2,1)S(1)}, u32[]{:S(2)}, u32[]{:S(2)}) collective-permute-start(bf16[8,128,256]{2,1,0:T(8,128)(2,1)S(1)} %get-tuple-element.118), channel_id=1, source_target_pairs={{0,96},{4,28},{8,104},{12,4},{16,112},{20,12},{24,120},{28,20},{32... | collective-permute-start | bytes 1572872 | tf_op jit(solution)/shard_map/ppermute | solution.py:44
  209.1 9.3 %collective-permute-start.40 = (bf16[8,128,256]{2,1,0:T(8,128)(2,1)S(1)}, bf16[8,128,256]{2,1,0:T(8,128)(2,1)S(1)}, u32[]{:S(2)}, u32[]{:S(2)}) collective-permute-start(bf16[8,128,256]{2,1,0:T(8,128)(2,1)S(1)} %get-tuple-element.102), channel_id=1, source_target_pairs={{0,24},{4,100},{8,0},{12,108},{16,8},{20,116},{24,16},{28,124},{32... | collective-permute-start | bytes 1572872 | tf_op jit(solution)/shard_map/ppermute | solution.py:40
  210.1 10.8 %collective-permute-start.41 = (bf16[8,128,256]{2,1,0:T(8,128)(2,1)S(1)}, bf16[8,128,256]{2,1,0:T(8,128)(2,1)S(1)}, u32[]{:S(2)}, u32[]{:S(2)}) collective-permute-start(bf16[8,128,256]{2,1,0:T(8,128)(2,1)S(1)} %get-tuple-element.103), channel_id=1, source_target_pairs={{0,16},{4,68},{8,24},{12,76},{16,0},{20,84},{24,8},{28,92},{32,48}... | collective-permute-start | bytes 1572872 | tf_op jit(solution)/shard_map/ppermute | solution.py:40
  210.1 16.3 %collective-permute-start.42 = (bf16[8,128,256]{2,1,0:T(8,128)(2,1)S(1)}, bf16[8,128,256]{2,1,0:T(8,128)(2,1)S(1)}, u32[]{:S(2)}, u32[]{:S(2)}) collective-permute-start(bf16[8,128,256]{2,1,0:T(8,128)(2,1)S(1)} %get-tuple-element.104), channel_id=1, source_target_pairs={{0,8},{4,36},{8,16},{12,44},{16,24},{20,52},{24,0},{28,60},{32,40}... | collective-permute-start | bytes 1572872 | tf_op jit(solution)/shard_map/ppermute | solution.py:40
  226.9 9.6 %collective-permute-start.45 = (bf16[128,1024]{1,0:T(8,128)(2,1)S(1)}, bf16[128,1024]{1,0:T(8,128)(2,1)S(1)}, u32[]{:S(2)}, u32[]{:S(2)}) collective-permute-start(bf16[128,1024]{1,0:T(8,128)(2,1)S(1)} %get-tuple-element.105.refs_0_), channel_id=1, source_target_pairs={{0,3},{1,0},{2,1},{3,2},{4,7},{5,4},{6,5},{7,6},{8,11},{9,8},{10,9... | collective-permute-start | bytes 786440 | tf_op jit(solution)/shard_map/ppermute | solution.py:48
  229.9 10.4 %collective-permute-start.43 = (bf16[128,1024]{1,0:T(8,128)(2,1)S(1)}, bf16[128,1024]{1,0:T(8,128)(2,1)S(1)}, u32[]{:S(2)}, u32[]{:S(2)}) collective-permute-start(bf16[128,1024]{1,0:T(8,128)(2,1)S(1)} %get-tuple-element.105.refs_0_), channel_id=1, source_target_pairs={{0,1},{1,2},{2,3},{3,0},{4,5},{5,6},{6,7},{7,4},{8,9},{9,10},{10,1... | collective-permute-start | bytes 786440 | tf_op jit(solution)/shard_map/ppermute | solution.py:48
  229.9 12.2 %collective-permute-start.50 = (bf16[128,1024]{1,0:T(8,128)(2,1)S(1)}, bf16[128,1024]{1,0:T(8,128)(2,1)S(1)}, u32[]{:S(2)}, u32[]{:S(2)}) collective-permute-start(bf16[128,1024]{1,0:T(8,128)(2,1)S(1)} %collective-permute-done.47.refs_5_), channel_id=1, source_target_pairs={{0,3},{1,0},{2,1},{3,2},{4,7},{5,4},{6,5},{7,6},{8,11},{9,8},{10,9... | collective-permute-start | bytes 786440 | tf_op jit(solution)/shard_map/ppermute | solution.py:48
  233.2 12.8 %collective-permute-start.48 = (bf16[128,1024]{1,0:T(8,128)(2,1)S(1)}, bf16[128,1024]{1,0:T(8,128)(2,1)S(1)}, u32[]{:S(2)}, u32[]{:S(2)}) collective-permute-start(bf16[128,1024]{1,0:T(8,128)(2,1)S(1)} %collective-permute-done.47.refs_5_), channel_id=1, source_target_pairs={{0,1},{1,2},{2,3},{3,0},{4,5},{5,6},{6,7},{7,4},{8,9},{9,10},{10,1... | collective-permute-start | bytes 786440 | tf_op jit(solution)/shard_map/ppermute | solution.py:48
  236.6 9.5 %collective-permute-start.46 = (bf16[64,1024]{1,0:T(8,128)(2,1)S(1)}, bf16[64,1024]{1,0:T(8,128)(2,1)S(1)}, u32[]{:S(2)}, u32[]{:S(2)}) collective-permute-start(bf16[64,1024]{1,0:T(8,128)(2,1)S(1)} %slice.79), channel_id=1, source_target_pairs={{0,3},{1,0},{2,1},{3,2},{4,7},{5,4},{6,5},{7,6},{8,11},{9,8},{10,9... | collective-permute-start | bytes 393224 | tf_op jit(solution)/shard_map/ppermute | solution.py:48
  240.3 7.6 %collective-permute-start.44 = (bf16[64,1024]{1,0:T(8,128)(2,1)S(1)}, bf16[64,1024]{1,0:T(8,128)(2,1)S(1)}, u32[]{:S(2)}, u32[]{:S(2)}) collective-permute-start(bf16[64,1024]{1,0:T(8,128)(2,1)S(1)} %slice.78), channel_id=1, source_target_pairs={{0,1},{1,2},{2,3},{3,0},{4,5},{5,6},{6,7},{7,4},{8,9},{9,10},{10,1... | collective-permute-start | bytes 393224 | tf_op jit(solution)/shard_map/ppermute | solution.py:48
  242.2 6.3 %collective-permute-start.51 = (bf16[64,1024]{1,0:T(8,128)(2,1)S(1)}, bf16[64,1024]{1,0:T(8,128)(2,1)S(1)}, u32[]{:S(2)}, u32[]{:S(2)}) collective-permute-start(bf16[64,1024]{1,0:T(8,128)(2,1)S(1)} %slice.81), channel_id=1, source_target_pairs={{0,3},{1,0},{2,1},{3,2},{4,7},{5,4},{6,5},{7,6},{8,11},{9,8},{10,9... | collective-permute-start | bytes 393224 | tf_op jit(solution)/shard_map/ppermute | solution.py:48
  246.0 6.2 %collective-permute-start.49 = (bf16[64,1024]{1,0:T(8,128)(2,1)S(1)}, bf16[64,1024]{1,0:T(8,128)(2,1)S(1)}, u32[]{:S(2)}, u32[]{:S(2)}) collective-permute-start(bf16[64,1024]{1,0:T(8,128)(2,1)S(1)} %slice.80), channel_id=1, source_target_pairs={{0,1},{1,2},{2,3},{3,0},{4,5},{5,6},{6,7},{7,4},{8,9},{9,10},{10,1... | collective-permute-start | bytes 393224 | tf_op jit(solution)/shard_map/ppermute | solution.py:48
  258.6 16.1 %collective-permute-start.53 = (bf16[4,32,2048]{2,1,0:T(8,128)(2,1)S(1)}, bf16[4,32,2048]{2,1,0:T(8,128)(2,1)S(1)}, u32[]{:S(2)}, u32[]{:S(2)}) collective-permute-start(bf16[4,32,2048]{2,1,0:T(8,128)(2,1)S(1)} %get-tuple-element.108), channel_id=1, source_target_pairs={{0,8},{4,36},{8,16},{12,44},{16,24},{20,52},{24,0},{28,60},{32,40}... | collective-permute-start | bytes 1572872 | tf_op jit(solution)/shard_map/ppermute | solution.py:40
  258.7 16.0 %collective-permute-start.54 = (bf16[4,32,2048]{2,1,0:T(8,128)(2,1)S(1)}, bf16[4,32,2048]{2,1,0:T(8,128)(2,1)S(1)}, u32[]{:S(2)}, u32[]{:S(2)}) collective-permute-start(bf16[4,32,2048]{2,1,0:T(8,128)(2,1)S(1)} %get-tuple-element.109), channel_id=1, source_target_pairs={{0,24},{4,100},{8,0},{12,108},{16,8},{20,116},{24,16},{28,124},{32... | collective-permute-start | bytes 1572872 | tf_op jit(solution)/shard_map/ppermute | solution.py:40
  261.9 12.8 %collective-permute-start.55 = (bf16[4,32,2048]{2,1,0:T(8,128)(2,1)S(1)}, bf16[4,32,2048]{2,1,0:T(8,128)(2,1)S(1)}, u32[]{:S(2)}, u32[]{:S(2)}) collective-permute-start(bf16[4,32,2048]{2,1,0:T(8,128)(2,1)S(1)} %get-tuple-element.110), channel_id=1, source_target_pairs={{0,16},{4,68},{8,24},{12,76},{16,0},{20,84},{24,8},{28,92},{32,48}... | collective-permute-start | bytes 1572872 | tf_op jit(solution)/shard_map/ppermute | solution.py:40
  275.0 6.2 %collective-permute-start.56 = (bf16[32,2048]{1,0:T(8,128)(2,1)S(1)}, bf16[32,2048]{1,0:T(8,128)(2,1)S(1)}, u32[]{:S(2)}, u32[]{:S(2)}) collective-permute-start(bf16[32,2048]{1,0:T(8,128)(2,1)S(1)} %get-tuple-element.120), channel_id=1, source_target_pairs={{0,32},{4,12},{8,40},{12,20},{16,48},{20,28},{24,56},{28,4},{32,64... | collective-permute-start | bytes 393224 | tf_op jit(solution)/shard_map/ppermute | solution.py:44
  275.1 8.2 %collective-permute-start.58 = (bf16[32,2048]{1,0:T(8,128)(2,1)S(1)}, bf16[32,2048]{1,0:T(8,128)(2,1)S(1)}, u32[]{:S(2)}, u32[]{:S(2)}) collective-permute-start(bf16[32,2048]{1,0:T(8,128)(2,1)S(1)} %get-tuple-element.121), channel_id=1, source_target_pairs={{0,64},{4,20},{8,72},{12,28},{16,80},{20,4},{24,88},{28,12},{32,96... | collective-permute-start | bytes 393224 | tf_op jit(solution)/shard_map/ppermute | solution.py:44
  (20 other events, 73.8 us)
where the time goes:
time: 285 us
  waiting for transfers between devices  139 us (49%)
  starting transfers between devices  75 us (26%)
  Pallas kernels  56.9 us (20%)
  local copies, waits for them, and re-layouts  9.82 us (3%)
  other arithmetic  2.99 us (1%)
    ppermute x18, waiting for transfers between devices, send_second(): return lax.ppermute(x, 'pas', ring_pairs(1, k))  70.3 us
    ppermute x20, starting transfers between devices, send_tp(): return lax.ppermute(x, 'tp', [(i, (i + k) % SIDE) for i in range(SIDE)])  33.9 us
    ppermute x12, waiting for transfers between devices, send_first(): return lax.ppermute(x, 'pas', ring_pairs(0, k))  33.6 us
    ppermute x20, waiting for transfers between devices, send_tp(): return lax.ppermute(x, 'tp', [(i, (i + k) % SIDE) for i in range(SIDE)])  28.6 us
    pallas_call x1, Pallas kernels, attention(): pl.pallas_call(functools.partial(attention_kernel, len(sources)), out_sha...  27.3 us
    ppermute x18, starting transfers between devices, send_second(): return lax.ppermute(x, 'pas', ring_pairs(1, k))  23.5 us
    ppermute x12, starting transfers between devices, send_first(): return lax.ppermute(x, 'pas', ring_pairs(0, k))  16.9 us
    pallas_call x1, Pallas kernels, project(): pl.pallas_call(functools.partial(project_kernel, chunks), out_shape=[jax....  12.8 us
  transfers between devices with their start and end apart: 59, of which 37 were waited for; matrix products, arithmetic and copies ran while one was open for 2% of the time, Pallas kernels for 11%

commit v1 on v0

--- a/solution.py
+++ b/solution.py
@@ -16,7 +16,6 @@
 TN = (((0,), (0,)), ((), ()))
 SIDE = 4
 OUT_ROWS = 32
-CHUNKS = 4
 
 
 def device_at(y, z, core):
@@ -84,18 +83,22 @@
     return lax.rem(n + 2 * SIDE, SIDE)
 
 
-def project_kernel(chunks, h_ref, *rest):
-    n_out = chunks * SIDE
-    pieces = rest[: 2 * SIDE]
-    outs = rest[2 * SIDE : 2 * SIDE + n_out]
-    weights, result, w_sem, out_sem = rest[2 * SIDE + n_out :]
+def project_kernel(h_ref, *rest):
+    pieces, outs = rest[: 2 * SIDE], rest[2 * SIDE : 6 * SIDE]
+    weights, rows, h_sem = rest[6 * SIDE :]
     step = pl.program_id(0)
     y, z, core, tp = here_in_kernel()
-    head_rows = weights.shape[1]
-    chunk = h_ref.shape[0] // chunks
+    block = rows.shape[1]
+    head = weights.shape[0] // SIDE
+
+    def hidden_copy(i):
+        at = pl.ds(pl.multiple_of(i * block, block), block)
+        return pltpu.make_async_copy(h_ref.at[at], rows.at[i], h_sem.at[i])
 
     @pl.when(step == 0)
     def _():
+        for i in range(rows.shape[0]):
+            hidden_copy(i).start()
         for src in range(2):
             which = core if src == 0 else 1 - core
             first = jnp.where(which == 0, z, y)
@@ -105,65 +108,42 @@
                     a = ring_mod(first - ja)
                     b = ring_mod(second - jb)
                     place = ring_mod(jnp.where(which == 0, b, a) - tp)
-                    part = jnp.where(which == 0, a, b) * 2 + which
-                    pltpu.make_async_copy(
-                        pieces[SIDE * src + jb].at[pl.ds(ja * OUT_ROWS, OUT_ROWS)],
-                        weights.at[place, pl.ds(pl.multiple_of(part * OUT_ROWS, OUT_ROWS), OUT_ROWS)],
-                        w_sem.at[place, part],
-                    ).start()
-
-    for n in range(2 * SIDE):
-        pltpu.make_async_copy(
-            pieces[0].at[pl.ds(0, OUT_ROWS)],
-            weights.at[step, pl.ds(n * OUT_ROWS, OUT_ROWS)],
-            w_sem.at[step, n],
-        ).wait()
-    result[step] = lax.dot_general(
-        h_ref[...], weights[step], NT, preferred_element_type=F32
-    )
-    for j in range(SIDE):
-
-        @pl.when(step == j)
+                    part = (place * SIDE + jnp.where(which == 0, a, b)) * 2 + which
+                    weights[pl.ds(pl.multiple_of(part * OUT_ROWS, OUT_ROWS), OUT_ROWS), :] = pieces[
+                        SIDE * src + jb
+                    ][ja * OUT_ROWS : (ja + 1) * OUT_ROWS, :]
+
+    hidden_copy(step).wait()
+    product = lax.dot_general(rows[step], weights[...], NT, preferred_element_type=F32)
+    for i in range(4):
+
+        @pl.when(step == i)
         def _():
-            for n in range(chunks):
-                pltpu.make_async_copy(
-                    result.at[j, pl.ds(n * chunk, chunk)],
-                    outs[n * SIDE + j],
-                    out_sem.at[n * SIDE + j],
-                ).start()
-
-    @pl.when(step == SIDE - 1)
-    def _():
-        for j in range(SIDE):
-            for n in range(chunks):
-                pltpu.make_async_copy(
-                    result.at[j, pl.ds(n * chunk, chunk)],
-                    outs[n * SIDE + j],
-                    out_sem.at[n * SIDE + j],
-                ).wait()
-
-
-def project(hidden, pieces, chunks):
+            for j in range(SIDE):
+                outs[i * SIDE + j][...] = product[:, j * head : (j + 1) * head]
+
+
+def project(hidden, pieces):
     rows, depth = hidden.shape
+    block = rows // 4
     columns = 2 * SIDE * SIDE * OUT_ROWS
     head = columns // SIDE
-    hbm = pl.BlockSpec(memory_space=pl.ANY)
+    whole = pl.BlockSpec(memory_space=pltpu.VMEM)
     return pl.pallas_call(
-        functools.partial(project_kernel, chunks),
-        out_shape=[jax.ShapeDtypeStruct((rows // chunks, head), F32)] * (chunks * SIDE),
-        grid=(SIDE,),
-        in_specs=[pl.BlockSpec((rows, depth), lambda i: (0, 0))] + [hbm] * (2 * SIDE),
-        out_specs=[hbm] * (chunks * SIDE),
+        project_kernel,
+        out_shape=[jax.ShapeDtypeStruct((block, head), F32)] * (4 * SIDE),
+        grid=(4,),
+        in_specs=[pl.BlockSpec(memory_space=pltpu.HBM)] + [whole] * (2 * SIDE),
+        out_specs=[whole] * (4 * SIDE),
         scratch_shapes=[
-            pltpu.VMEM((SIDE, head, depth), BF),
-            pltpu.VMEM((SIDE, rows, head), F32),
-            pltpu.SemaphoreType.DMA((SIDE, 2 * SIDE)),
-            pltpu.SemaphoreType.DMA((chunks * SIDE,)),
+            pltpu.VMEM((columns, depth), BF),
+            pltpu.VMEM((4, block, depth), BF),
+            pltpu.SemaphoreType.DMA((4,)),
         ],
-        compiler_params=pltpu.CompilerParams(vmem_limit_bytes=40 * 2**20),
+        compiler_params=pltpu.CompilerParams(vmem_limit_bytes=28 * 2**20),
         cost_estimate=pl.CostEstimate(
             flops=2 * rows * columns * depth,
-            bytes_accessed=2 * rows * depth + 2 * columns * depth + 4 * rows * columns,
+            bytes_accessed=2 * (rows + columns) * depth + 4 * rows * columns,
             transcendentals=0,
         ),
         name="project",
@@ -171,10 +151,10 @@
 
 
 def reduce_heads(parts):
-    down, up = parts[0][3], parts[1][1]
+    down, up = parts[3], parts[SIDE + 1]
     for first, second in ((2, 2), (1, 3), (0, 0)):
-        down = send_tp(down, 1) + parts[0][first]
-        up = send_tp(up, -1) + parts[1][second]
+        down = send_tp(down, 1) + parts[first]
+        up = send_tp(up, -1) + parts[SIDE + second]
     return jnp.concatenate([down.astype(BF), up.astype(BF)], axis=0)
 
 
@@ -206,11 +186,11 @@
         at = ring_mod(tp - y_of) * SIDE * OUT_ROWS + z_of * OUT_ROWS
         return result[pl.ds(pl.multiple_of(at, OUT_ROWS), OUT_ROWS), :]
 
-    for jb in range(SIDE):
-        outs[0][jb] = block(0, jb)
-    for ja in range(1, SIDE):
+    tile = result.shape[1]
+    columns = pl.ds(pl.multiple_of(pl.program_id(0) * tile, tile), tile)
+    for ja in range(SIDE):
         for jb in range(SIDE):
-            outs[ja][jb] = block(ja, jb).astype(BF)
+            outs[ja][jb, :, columns] = block(ja, jb).astype(outs[ja].dtype)
 
 
 def weight_product(mine, theirs, h_mine, h_theirs):
@@ -218,14 +198,13 @@
     tile = 512
     heads_rows = SIDE * SIDE * OUT_ROWS
     whole = pl.BlockSpec(memory_space=pltpu.VMEM)
-    out = pl.BlockSpec((SIDE, OUT_ROWS, tile), lambda i: (0, 0, i))
     return pl.pallas_call(
         weight_kernel,
         out_shape=[jax.ShapeDtypeStruct((SIDE, OUT_ROWS, depth), F32)]
         + [jax.ShapeDtypeStruct((SIDE, OUT_ROWS, depth), BF)] * (SIDE - 1),
         grid=(depth // tile,),
         in_specs=[whole] * 10 + [pl.BlockSpec((rows, tile), lambda i: (0, i))] * 2,
-        out_specs=[out] * SIDE,
+        out_specs=[whole] * SIDE,
         scratch_shapes=[
             pltpu.VMEM((heads_rows, 2 * rows), BF),
             pltpu.VMEM((heads_rows, tile), F32),
@@ -254,54 +233,42 @@
 
 
 def attention_kernel(
-    n_src, buf_of, row_of, q_ref, do_ref, own_ref, *rest
+    n_src, n_dst, taken_by, out_buf, out_row, q_ref, do_ref, own_ref, *rest
 ):
     srcs = rest[:n_src]
     dq_ref, down_ref = rest[n_src : n_src + 2]
-    outs = rest[n_src + 2 : 2 * n_src + 2]
-    kv, stage, q_st, do_st, p_t, ds_t, in_sem, out_sem = rest[2 * n_src + 2 :]
+    outs = rest[n_src + 2 : n_src + n_dst + 2]
+    keys_at, values_at, q_st, do_st, p_t, ds_t = rest[n_src + n_dst + 2 :]
     step = pl.program_id(0)
-    steps = pl.num_programs(0)
     group = q_ref.shape[1] // HD
-    retrieved = in_sem.shape[1]
-    rows = retrieved * PLEN
-    keys = rows + own_ref.shape[0]
-    slot = lax.rem(step, 2)
+    keys = keys_at.shape[1]
+    rows = keys - own_ref.shape[0]
+    retrieved = rows // PLEN
     scaling = HD ** (-0.5)
 
-    def fetch(query, into):
-        @pl.loop(0, retrieved)
-        def _(j):
-            at = query * retrieved + j
-            for b in range(n_src):
-
-                @pl.when(buf_of[at] == b)
-                def _():
-                    pltpu.make_async_copy(
-                        srcs[b].at[row_of[at]],
-                        kv.at[into, pl.ds(pl.multiple_of(j * PLEN, PLEN), PLEN)],
-                        in_sem.at[into, j],
-                    ).start()
+    slots = taken_by.shape[0] // n_src
 
     @pl.when(step == 0)
     def _():
-        fetch(0, 0)
-
-    @pl.when(step + 1 < steps)
-    def _():
-        fetch(step + 1, 1 - slot)
+        for b in range(n_src):
+            for m in range(slots):
+                to = taken_by[b * slots + m]
+                at = m if b < SIDE else slots + m
+
+                @pl.when(to >= 0)
+                def _():
+                    query = lax.div(to, retrieved)
+                    into = pl.ds(pl.multiple_of(lax.rem(to, retrieved) * PLEN, PLEN), PLEN)
+                    keys_at[query, into, :] = srcs[b][at, :, :HD]
+                    values_at[query, into, :] = srcs[b][at, :, HD:]
 
     for g in range(group):
         q_st[pl.ds(g * HD, HD), :] = q_ref[:, g * HD : (g + 1) * HD]
         do_st[pl.ds(g * HD, HD), :] = do_ref[:, g * HD : (g + 1) * HD]
-    kv[slot, pl.ds(rows, keys - rows), :] = own_ref[...]
-    for j in range(retrieved):
-        pltpu.make_async_copy(
-            srcs[0].at[0], kv.at[slot, pl.ds(j * PLEN, PLEN)], in_sem.at[slot, j]
-        ).wait()
-
-    k_all = kv[slot, :, :HD]
-    v_all = kv[slot, :, HD:]
+    keys_at[step, pl.ds(rows, keys - rows), :] = own_ref[:, :HD]
+    values_at[step, pl.ds(rows, keys - rows), :] = own_ref[:, HD:]
+    k_all = keys_at[step]
+    v_all = values_at[step]
     width = 2 * HD
     key_at = lax.broadcasted_iota(jnp.int32, (keys - rows, width), 0)
     tok_at = lax.broadcasted_iota(jnp.int32, (keys - rows, width), 1) % HD
@@ -329,115 +296,79 @@
     down_ref[:, :HD] = d_k[rows:].astype(BF)
     down_ref[:, HD:] = d_v[rows:].astype(BF)
 
-    def sent(at_slot, j):
-        return pltpu.make_async_copy(
-            stage.at[at_slot, pl.ds(j * PLEN, PLEN)], outs[0].at[0], out_sem.at[at_slot, j]
-        )
-
-    @pl.when(step >= 2)
-    def _():
-        for j in range(retrieved):
-            sent(slot, j).wait()
-
-    stage[slot, :, :HD] = d_k[:rows].astype(BF)
-    stage[slot, :, HD:] = d_v[:rows].astype(BF)
-
-    @pl.loop(0, retrieved)
-    def _(j):
+    for j in range(retrieved):
         at = step * retrieved + j
-        for b in range(n_src):
-
-            @pl.when(buf_of[at] == b)
+        part = slice(j * PLEN, (j + 1) * PLEN)
+        for b in range(n_dst):
+
+            @pl.when(out_buf[at] == b)
             def _():
-                pltpu.make_async_copy(
-                    stage.at[slot, pl.ds(pl.multiple_of(j * PLEN, PLEN), PLEN)],
-                    outs[b].at[row_of[at]],
-                    out_sem.at[slot, j],
-                ).start()
-
-    @pl.when(step == steps - 1)
-    def _():
-        for j in range(retrieved):
-            if steps > 1:
-                sent(1 - slot, j).wait()
-            sent(slot, j).wait()
-
-
-def attention(queries, out_grad, query_kv, sources, out_blocks, buf_of, row_of, n_query):
+                outs[b][out_row[at], :, :HD] = d_k[part].astype(BF)
+                outs[b][out_row[at], :, HD:] = d_v[part].astype(BF)
+
+
+def attention(queries, out_grad, query_kv, sources, out_blocks, places, n_query):
     rows, width = queries.shape
     qlen = rows // n_query
-    retrieved = buf_of.shape[0] // n_query
+    retrieved = places[1].shape[0] // n_query
     keys = retrieved * PLEN + qlen
     local = query_kv.shape[1]
     block = lambda w: pl.BlockSpec((qlen, w), lambda i, *_: (i, 0))
-    hbm = pl.BlockSpec(memory_space=pl.ANY)
+    whole = pl.BlockSpec(memory_space=pltpu.VMEM)
     return pl.pallas_call(
-        functools.partial(attention_kernel, len(sources)),
+        functools.partial(attention_kernel, len(sources), len(out_blocks)),
         out_shape=(
             jax.ShapeDtypeStruct((rows, width), BF),
             jax.ShapeDtypeStruct((rows, local), BF),
         )
         + tuple(jax.ShapeDtypeStruct((n, PLEN, local), BF) for n in out_blocks),
         grid_spec=pltpu.PrefetchScalarGridSpec(
-            num_scalar_prefetch=2,
+            num_scalar_prefetch=3,
             grid=(n_query,),
-            in_specs=[block(width), block(width), block(local)] + [hbm] * len(sources),
-            out_specs=(block(width), block(local)) + (hbm,) * len(sources),
+            in_specs=[block(width), block(width), block(local)] + [whole] * len(sources),
+            out_specs=(block(width), block(local)) + (whole,) * len(out_blocks),
             scratch_shapes=[
-                pltpu.VMEM((2, keys, local), BF),
-                pltpu.VMEM((2, retrieved * PLEN, local), BF),
+                pltpu.VMEM((n_query, keys, HD), BF),
+                pltpu.VMEM((n_query, keys, HD), BF),
                 pltpu.VMEM((width, HD), BF),
                 pltpu.VMEM((width, HD), BF),
                 pltpu.VMEM((keys, width), BF),
                 pltpu.VMEM((keys, width), BF),
-                pltpu.SemaphoreType.DMA((2, retrieved)),
-                pltpu.SemaphoreType.DMA((2, retrieved)),
             ],
         ),
-        compiler_params=pltpu.CompilerParams(vmem_limit_bytes=48 * 2**20),
+        compiler_params=pltpu.CompilerParams(vmem_limit_bytes=44 * 2**20),
         cost_estimate=pl.CostEstimate(
             flops=10 * n_query * keys * qlen * width,
             bytes_accessed=8 * rows * width + 4 * n_query * keys * local,
             transcendentals=n_query * keys * width,
         ),
         name="attention",
-    )(buf_of, row_of, queries, out_grad, query_kv, *sources)
+    )(*places, queries, out_grad, query_kv, *sources)
 
 
 def pick_kernel(slot_of, *rest):
-    ring, outs, sem = rest[:SIDE], rest[SIDE : 2 * SIDE], rest[2 * SIDE]
+    ring, outs = rest[:SIDE], rest[SIDE:]
     n = outs[0].shape[0]
-    copies = []
     for k in range(SIDE):
         for m in range(n):
-            place = jnp.maximum(slot_of[k * n + m], 0)
-            copies.append(
-                pltpu.make_async_copy(
-                    ring[(m // 2) % SIDE].at[place], outs[k].at[m], sem.at[k * n + m]
-                )
-            )
-    for copy in copies:
-        copy.start()
-    for copy in copies:
-        copy.wait()
+            outs[k][m] = ring[(m // 2) % SIDE][jnp.maximum(slot_of[k * n + m], 0)]
 
 
 def pick(slot_of, ring):
     n = slot_of.shape[0] // SIDE
-    hbm = pl.BlockSpec(memory_space=pl.ANY)
+    whole = pl.BlockSpec(memory_space=pltpu.VMEM)
     shape = jax.ShapeDtypeStruct((n,) + ring[0].shape[1:], BF)
     return pl.pallas_call(
         pick_kernel,
         out_shape=[shape] * SIDE,
         grid_spec=pltpu.PrefetchScalarGridSpec(
             num_scalar_prefetch=1,
-            in_specs=[hbm] * SIDE,
-            out_specs=[pl.BlockSpec(memory_space=pltpu.VMEM)] * SIDE,
-            scratch_shapes=[pltpu.SemaphoreType.DMA((SIDE * n,))],
-        ),
-        compiler_params=pltpu.CompilerParams(vmem_limit_bytes=24 * 2**20),
+            in_specs=[whole] * SIDE,
+            out_specs=[whole] * SIDE,
+        ),
+        compiler_params=pltpu.CompilerParams(vmem_limit_bytes=16 * 2**20),
         cost_estimate=pl.CostEstimate(
-            flops=0, bytes_accessed=4 * SIDE * n * PLEN * 2 * HD, transcendentals=0
+            flops=0, bytes_accessed=8 * SIDE * n * PLEN * HD, transcendentals=0
         ),
         name="pick",
     )(slot_of, *ring)
@@ -544,9 +475,14 @@
     ja, jb = ring_steps(
         y, z, owner_core, flat_device // (2 * SIDE), (flat_device // 2) % SIDE
     )
+    n = SIDE * capacity
     block = ja * capacity + ranking
     same = owner_core == core
-    return jnp.where(same, jb, SIDE), jnp.where(same, block, jb * SIDE * capacity + block)
+    named = jnp.where(same, jb, SIDE + jb) * n + block
+    at = jnp.arange(2 * SIDE * n, dtype=jnp.int32)[:, None]
+    request = jnp.arange(named.shape[0], dtype=jnp.int32)[None, :]
+    taken_by = jnp.max(jnp.where(named[None, :] == at, request, -1), axis=1)
+    return taken_by, jnp.where(same, jb, SIDE), jnp.where(same, block, jb * n + block)
 
 
 def slots_served(tables, owners, capacity):
@@ -568,31 +504,29 @@
     capacity = 2
 
     flat_device, ranking, table = requests(source_device, source_slot, owners, capacity)
-    shards = ring_gather(kv_weight, send_first)
-    shards = ring_gather(jnp.concatenate(shards, axis=0), send_second)
-    partial = project(passage_hidden, shards + [swap_cores(s) for s in shards], CHUNKS)
-    partial, table = lax.optimization_barrier((partial, table))
+    shards = jnp.concatenate(ring_gather(kv_weight, send_first), axis=0)
+    shards, table = lax.optimization_barrier((shards, table))
+    weights = ring_gather(shards, send_second)
+    weights = weights + [swap_cores(w) for w in weights]
     pair = jnp.concatenate([table, swap_cores(table)], axis=0)
     tables = jnp.stack([pair] + [send_second(pair, -k) for k in range(1, SIDE)])
-    hidden_theirs = swap_cores(passage_hidden)
-    buf_of, row_of = own_places(flat_device, ranking, capacity)
+    places = own_places(flat_device, ranking, capacity)
     served = slots_served(tables, owners, capacity)
 
-    quarters = [partial[n * SIDE : (n + 1) * SIDE] for n in range(CHUNKS)]
-    own = [reduce_heads(quarters[n : n + 2]) for n in range(0, CHUNKS, 2)]
+    parts = project(passage_hidden, weights)
+    own = [reduce_heads(parts[n : n + 2 * SIDE]) for n in (0, 2 * SIDE)]
     own = jnp.concatenate(own, axis=0).reshape(passages_here, PLEN, local_width)
     wanted = pick(served, ring_gather(own, send_first))
-    got = [wanted[0]] + [send_second(wanted[k], k) for k in range(1, SIDE)]
-    half = got[0].shape[0] // 2
-    sources = got + [swap_cores(jnp.concatenate([g[half:] for g in got], axis=0))]
+    got = [wanted[0]] + [send_second(wanted[k], k) for k in (1, 2, 3)]
+    hidden_theirs = swap_cores(passage_hidden)
+    half = SIDE * capacity
     grad_queries, own_grads, *grads = attention(
         queries,
         out_grad,
         query_kv,
-        sources,
+        got + [swap_cores(g) for g in got],
         [half] * SIDE + [SIDE * half],
-        buf_of,
-        row_of,
+        places,
         queries_here,
     )
     mine, theirs = grads[:SIDE], swap_cores(grads[SIDE])

time: 285 us -> 269 us (0.944)
  Pallas kernels: 56.9 us -> 42.7 us
  local copies, waits for them, and re-layouts: 9.82 us -> 5.82 us
    pallas_call x2, Pallas kernels: 40 us -> 32.9 us  [the longest x1 26.5 us: attention(): pl.pallas_call(functools.partial(attention_kernel, len(sources), len(out_...]
    pallas_call x1, Pallas kernels: 7.66 us -> 0.81 us  [pick(): pl.pallas_call(pick_kernel, out_shape=[shape] * SIDE, grid_spec=pltpu.Pre...]
    ppermute x9 -> x12, waiting for transfers between devices: 6.33 us -> 11.7 us  [swap_cores(): return lax.ppermute(x, 'pas', [(i, i ^ 1) for i in range(2 * SIDE * SIDE)])]
    ppermute x18, waiting for transfers between devices: 70.3 us -> 65.6 us  [send_second(): return lax.ppermute(x, 'pas', ring_pairs(1, k))]
    unnamed x21 -> x18, local copies, waits for them, and re-layouts: 7.51 us -> 3.65 us
  transfers between devices with their start and end apart: 59 -> 62, of which waited for: 37 -> 38; matrix products, arithmetic and copies ran while one was open for 2% -> 2% of each run, Pallas kernels for 11% -> 11%
where the time goes in v1:
time: 269 us
  waiting for transfers between devices  139 us (52%)
  starting transfers between devices  75.8 us (28%)
  Pallas kernels  42.7 us (16%)
  local copies, waits for them, and re-layouts  5.82 us (2%)
  other arithmetic  4.44 us (2%)
    ppermute x18, waiting for transfers between devices, send_second(): return lax.ppermute(x, 'pas', ring_pairs(1, k))  65.6 us
    ppermute x20, starting transfers between devices, send_tp(): return lax.ppermute(x, 'tp', [(i, (i + k) % SIDE) for i in range(SIDE)])  33.9 us
    ppermute x12, waiting for transfers between devices, send_first(): return lax.ppermute(x, 'pas', ring_pairs(0, k))  32.9 us
    ppermute x20, waiting for transfers between devices, send_tp(): return lax.ppermute(x, 'tp', [(i, (i + k) % SIDE) for i in range(SIDE)])  28.6 us
    pallas_call x1, Pallas kernels, attention(): pl.pallas_call(functools.partial(attention_kernel, len(sources), len(out_...  26.5 us
    ppermute x18, starting transfers between devices, send_second(): return lax.ppermute(x, 'pas', ring_pairs(1, k))  23.2 us
    ppermute x12, starting transfers between devices, send_first(): return lax.ppermute(x, 'pas', ring_pairs(0, k))  16.9 us
    ppermute x12, waiting for transfers between devices, swap_cores(): return lax.ppermute(x, 'pas', [(i, i ^ 1) for i in range(2 * SIDE * SIDE)])  11.7 us
  transfers between devices with their start and end apart: 62, of which 38 were waited for; matrix products, arithmetic and copies ran while one was open for 2% of the time, Pallas kernels for 11%

profile of v1, /device:TPU:0, one launch (start us, length us, event | category | flops | bytes accessed | tf_op | source)
XLA Modules:
  0.0 268.6 jit_solution(5235466323722491266)
XLA Ops:
  0.6 4.0 %collective-permute-start.1 = (bf16[32,2048]{1,0:T(8,128)(2,1)}, bf16[32,2048]{1,0:T(8,128)(2,1)S(1)}, u32[]{:S(2)}, u32[]{:S(2)}) collective-permute-start(bf16[32,2048]{1,0:T(8,128)(2,1)} %param.8), channel_id=1, source_target_pairs={{0,16},{4,68},{8,24},{12,76},{16,0},{20,84},{24,8},{28,92},{32,48}... | collective-permute-start | bytes 393224 | tf_op jit(solution)/shard_map/ppermute | solution.py:39
  5.7 2.2 collective-permute-start.2
  12.0 3.1 %collective-permute-start.9 = (bf16[128,2048]{1,0:T(8,128)(2,1)S(1)}, bf16[128,2048]{1,0:T(8,128)(2,1)S(1)}, u32[]{:S(2)}, u32[]{:S(2)}) collective-permute-start(bf16[128,2048]{1,0:T(8,128)(2,1)S(1)} %pad_maximum_fusion.rest_0_), channel_id=1, source_target_pairs={{0,96},{4,28},{8,104},{12,4},{16,112},{20,12},{24,120},{28,20},{32... | collective-permute-start | bytes 1572872 | tf_op jit(solution)/shard_map/ppermute | solution.py:43
  16.7 10.7 %collective-permute-done.9.rest_3_ = bf16[128,2048]{1,0:T(8,128)(2,1)S(1)} collective-permute-done((bf16[128,2048]{1,0:T(8,128)(2,1)S(1)}, bf16[128,2048]{1,0:T(8,128)(2,1)S(1)}, u32[]{:S(2)}, u32[]{:S(2)}) %collective-permute-start.9) | collective-permute-done | bytes 524320 | tf_op jit(solution)/shard_map/ppermute | solution.py:43
  27.9 3.5 %collective-permute-done.7.rest_1_ = bf16[128,2048]{1,0:T(8,128)(2,1)S(1)} collective-permute-done((bf16[128,2048]{1,0:T(8,128)(2,1)S(1)}, bf16[128,2048]{1,0:T(8,128)(2,1)S(1)}, u32[]{:S(2)}, u32[]{:S(2)}) %collective-permute-start.7) | collective-permute-done | bytes 524320 | tf_op jit(solution)/shard_map/ppermute | solution.py:43
  33.3 2.2 copy-done
  35.5 6.3 %project.1 = (f32[256,256]{1,0:T(8,128)S(1)}, f32[256,256]{1,0:T(8,128)S(1)}, f32[256,256]{1,0:T(8,128)S(1)}, f32[256,256]{1,0:T(8,128)S(1)}, f32[256,256]{1,0:T...) custom-call(bf16[1024,2048]{1,0:T(8,128)(2,1)S(1)} %copy-done, ...), custom_call_target="tpu_custom_call" | custom-call | flops 4294967296 | bytes 12582912 | tf_op jit(solution)/shard_map/project/pallas_call | solution.py:132
  45.4 3.0 %collective-permute-start.23 = (f32[256,256]{1,0:T(8,128)S(1)}, f32[256,256]{1,0:T(8,128)S(1)}, u32[]{:S(2)}, u32[]{:S(2)}) collective-permute-start(f32[256,256]{1,0:T(8,128)S(1)} %get-tuple-element.56), channel_id=1, source_target_pairs={{0,3},{1,0},{2,1},{3,2},{4,7},{5,4},{6,5},{7,6},{8,11},{9,8},{10,9... | collective-permute-start | bytes 786440 | tf_op jit(solution)/shard_map/ppermute | solution.py:47
  48.4 3.9 %collective-permute-done.14 = f32[256,256]{1,0:T(8,128)S(1)} collective-permute-done((f32[256,256]{1,0:T(8,128)S(1)}, f32[256,256]{1,0:T(8,128)S(1)}, u32[]{:S(2)}, u32[]{:S(2)}) %collective-permute-start.14) | collective-permute-done | bytes 262176 | tf_op jit(solution)/shard_map/ppermute | solution.py:47
  52.7 3.0 %collective-permute-start.18 = (f32[256,256]{1,0:T(8,128)S(1)}, f32[256,256]{1,0:T(8,128)S(1)}, u32[]{:S(2)}, u32[]{:S(2)}) collective-permute-start(f32[256,256]{1,0:T(8,128)S(1)} %add.308), channel_id=1, source_target_pairs={{0,3},{1,0},{2,1},{3,2},{4,7},{5,4},{6,5},{7,6},{8,11},{9,8},{10,9... | collective-permute-start | bytes 786440 | tf_op jit(solution)/shard_map/ppermute | solution.py:47
  55.7 2.2 collective-permute-done.20
  58.3 3.0 %collective-permute-start.24 = (f32[256,256]{1,0:T(8,128)S(1)}, f32[256,256]{1,0:T(8,128)S(1)}, u32[]{:S(2)}, u32[]{:S(2)}) collective-permute-start(f32[256,256]{1,0:T(8,128)S(1)} %add.314), channel_id=1, source_target_pairs={{0,3},{1,0},{2,1},{3,2},{4,7},{5,4},{6,5},{7,6},{8,11},{9,8},{10,9... | collective-permute-start | bytes 786440 | tf_op jit(solution)/shard_map/ppermute | solution.py:47
  61.4 2.2 collective-permute-done.15
  64.0 3.0 %collective-permute-start.19 = (f32[256,256]{1,0:T(8,128)S(1)}, f32[256,256]{1,0:T(8,128)S(1)}, u32[]{:S(2)}, u32[]{:S(2)}) collective-permute-start(f32[256,256]{1,0:T(8,128)S(1)} %add.309), channel_id=1, source_target_pairs={{0,3},{1,0},{2,1},{3,2},{4,7},{5,4},{6,5},{7,6},{8,11},{9,8},{10,9... | collective-permute-start | bytes 786440 | tf_op jit(solution)/shard_map/ppermute | solution.py:47
  67.0 2.2 collective-permute-done.21
  69.6 3.0 %collective-permute-start.25 = (f32[256,256]{1,0:T(8,128)S(1)}, f32[256,256]{1,0:T(8,128)S(1)}, u32[]{:S(2)}, u32[]{:S(2)}) collective-permute-start(f32[256,256]{1,0:T(8,128)S(1)} %add.315), channel_id=1, source_target_pairs={{0,3},{1,0},{2,1},{3,2},{4,7},{5,4},{6,5},{7,6},{8,11},{9,8},{10,9... | collective-permute-start | bytes 786440 | tf_op jit(solution)/shard_map/ppermute | solution.py:47
  72.6 2.2 collective-permute-done.16
  75.1 4.5 %collective-permute-done.22 = f32[256,256]{1,0:T(8,128)S(1)} collective-permute-done((f32[256,256]{1,0:T(8,128)S(1)}, f32[256,256]{1,0:T(8,128)S(1)}, u32[]{:S(2)}, u32[]{:S(2)}) %collective-permute-start.22) | collective-permute-done | bytes 262176 | tf_op jit(solution)/shard_map/ppermute | solution.py:47
  79.7 3.3 %collective-permute-start.28 = (bf16[8,128,256]{2,1,0:T(8,128)(2,1)S(1)}, bf16[8,128,256]{2,1,0:T(8,128)(2,1)S(1)}, u32[]{:S(2)}, u32[]{:S(2)}) collective-permute-start(bf16[8,128,256]{2,1,0:T(8,128)(2,1)S(1)} %bitcast.19), channel_id=1, source_target_pairs={{0,24},{4,100},{8,0},{12,108},{16,8},{20,116},{24,16},{28,124},{32... | collective-permute-start | bytes 1572872 | tf_op jit(solution)/shard_map/ppermute | solution.py:39
  85.4 2.7 %collective-permute-start.5 = (s32[64,2]{0,1:T(2,128)S(1)}, s32[64,2]{0,1:T(2,128)S(1)}, u32[]{:S(2)}, u32[]{:S(2)}) collective-permute-start(s32[64,2]{0,1:T(2,128)S(1)} %pad_add_fusion.1), channel_id=1, source_target_pairs={{0,64},{4,20},{8,72},{12,28},{16,80},{20,4},{24,88},{28,12},{32,96... | collective-permute-start | bytes 1544 | tf_op jit(solution)/shard_map/ppermute | solution.py:43
  88.2 2.1 collective-permute-done.6
  90.7 3.1 %collective-permute-done.4 = s32[64,2]{0,1:T(2,128)S(1)} collective-permute-done((s32[64,2]{0,1:T(2,128)S(1)}, s32[64,2]{0,1:T(2,128)S(1)}, u32[]{:S(2)}, u32[]{:S(2)}) %collective-permute-start.4) | collective-permute-done | bytes 544 | tf_op jit(solution)/shard_map/ppermute | solution.py:43
  95.4 3.7 %collective-permute-done.26.rest_1_ = bf16[8,128,256]{2,1,0:T(8,128)(2,1)S(1)} collective-permute-done((bf16[8,128,256]{2,1,0:T(8,128)(2,1)S(1)}, bf16[8,128,256]{2,1,0:T(8,128)(2,1)S(1)}, u32[]{:S(2)}, u32[]{:S(2)}) %collective-permute-start.26) | collective-permute-done | bytes 524320 | tf_op jit(solution)/shard_map/ppermute | solution.py:39
  100.0 2.7 collective-permute-start.30
  103.2 24.0 %collective-permute-done.29.rest_1_ = bf16[16,128,256]{2,1,0:T(8,128)(2,1)S(1)} collective-permute-done((bf16[16,128,256]{2,1,0:T(8,128)(2,1)S(1)}, bf16[16,128,256]{2,1,0:T(8,128)(2,1)S(1)}, u32[]{:S(2)}, u32[]{:S(2)}) %collective-permute-start.29) | collective-permute-done | bytes 1048608 | tf_op jit(solution)/shard_map/ppermute | solution.py:43
  129.9 3.0 %collective-permute-done.34.rest_6_ = bf16[16,128,256]{2,1,0:T(8,128)(2,1)S(1)} collective-permute-done((bf16[16,128,256]{2,1,0:T(8,128)(2,1)S(1)}, bf16[16,128,256]{2,1,0:T(8,128)(2,1)S(1)}, u32[]{:S(2)}, u32[]{:S(2)}) %collective-permute-start.34) | collective-permute-done | bytes 1048608 | tf_op jit(solution)/shard_map/ppermute | solution.py:51
  132.9 3.0 %collective-permute-done.35.rest_7_ = bf16[16,128,256]{2,1,0:T(8,128)(2,1)S(1)} collective-permute-done((bf16[16,128,256]{2,1,0:T(8,128)(2,1)S(1)}, bf16[16,128,256]{2,1,0:T(8,128)(2,1)S(1)}, u32[]{:S(2)}, u32[]{:S(2)}) %collective-permute-start.35) | collective-permute-done | bytes 1048608 | tf_op jit(solution)/shard_map/ppermute | solution.py:51
  136.9 26.5 %attention.1 = (bf16[512,1024]{1,0:T(8,128)(2,1)}, bf16[512,256]{1,0:T(8,128)(2,1)}, bf16[8,128,256]{2,1,0:T(8,128)(2,1)S(1)}, bf16[8,128,256]{2,1,0:T(8,128)(2,...) custom-call(s32[64]{0:T(128)S(1)} %select_reduce_fusion.taken_by, ...), custom_call_target="tpu_custom_call" | custom-call | flops 6039797760 | bytes 8912896 | tf_op jit(solution)/shard_map/attention/pallas_call | solution.py:318
  165.6 2.2 collective-permute-done.36
  168.3 4.4 %collective-permute-done.37.rest_2_ = bf16[8,128,256]{2,1,0:T(8,128)(2,1)S(1)} collective-permute-done((bf16[8,128,256]{2,1,0:T(8,128)(2,1)S(1)}, bf16[8,128,256]{2,1,0:T(8,128)(2,1)S(1)}, u32[]{:S(2)}, u32[]{:S(2)}) %collective-permute-start.37) | collective-permute-done | bytes 524320 | tf_op jit(solution)/shard_map/ppermute | solution.py:43
  174.4 6.6 %collective-permute-start.38 = (bf16[8,128,256]{2,1,0:T(8,128)(2,1)S(1)}, bf16[8,128,256]{2,1,0:T(8,128)(2,1)S(1)}, u32[]{:S(2)}, u32[]{:S(2)}) collective-permute-start(bf16[8,128,256]{2,1,0:T(8,128)(2,1)S(1)} %get-tuple-element.89), channel_id=1, source_target_pairs={{0,96},{4,28},{8,104},{12,4},{16,112},{20,12},{24,120},{28,20},{32... | collective-permute-start | bytes 1572872 | tf_op jit(solution)/shard_map/ppermute | solution.py:43
  181.0 4.5 %collective-permute-done.42.rest_7_ = bf16[8,128,256]{2,1,0:T(8,128)(2,1)S(1)} collective-permute-done((bf16[8,128,256]{2,1,0:T(8,128)(2,1)S(1)}, bf16[8,128,256]{2,1,0:T(8,128)(2,1)S(1)}, u32[]{:S(2)}, u32[]{:S(2)}) %collective-permute-start.42) | collective-permute-done | bytes 524320 | tf_op jit(solution)/shard_map/ppermute | solution.py:43
  185.5 5.7 %collective-permute-done.40.rest_5_ = bf16[8,128,256]{2,1,0:T(8,128)(2,1)S(1)} collective-permute-done((bf16[8,128,256]{2,1,0:T(8,128)(2,1)S(1)}, bf16[8,128,256]{2,1,0:T(8,128)(2,1)S(1)}, u32[]{:S(2)}, u32[]{:S(2)}) %collective-permute-start.40) | collective-permute-done | bytes 524320 | tf_op jit(solution)/shard_map/ppermute | solution.py:43
  191.2 2.4 add_blocks.1
  195.7 7.2 %collective-permute-done.43.left_ref = bf16[8,128,256]{2,1,0:T(8,128)(2,1)S(1)} collective-permute-done((bf16[8,128,256]{2,1,0:T(8,128)(2,1)S(1)}, bf16[8,128,256]{2,1,0:T(8,128)(2,1)S(1)}, u32[]{:S(2)}, u32[]{:S(2)}) %collective-permute-start.43) | collective-permute-done | bytes 524320 | tf_op jit(solution)/shard_map/ppermute | solution.py:39
  202.8 2.5 collective-permute-done.44.far_ref
  205.3 5.5 %collective-permute-done.45.right_ref = bf16[8,128,256]{2,1,0:T(8,128)(2,1)S(1)} collective-permute-done((bf16[8,128,256]{2,1,0:T(8,128)(2,1)S(1)}, bf16[8,128,256]{2,1,0:T(8,128)(2,1)S(1)}, u32[]{:S(2)}, u32[]{:S(2)}) %collective-permute-start.45) | collective-permute-done | bytes 524320 | tf_op jit(solution)/shard_map/ppermute | solution.py:39
  211.4 3.0 %collective-permute-start.48 = (bf16[128,1024]{1,0:T(8,128)(2,1)S(1)}, bf16[128,1024]{1,0:T(8,128)(2,1)S(1)}, u32[]{:S(2)}, u32[]{:S(2)}) collective-permute-start(bf16[128,1024]{1,0:T(8,128)(2,1)S(1)} %get-tuple-element.75.refs_0_), channel_id=1, source_target_pairs={{0,3},{1,0},{2,1},{3,2},{4,7},{5,4},{6,5},{7,6},{8,11},{9,8},{10,9... | collective-permute-start | bytes 786440 | tf_op jit(solution)/shard_map/ppermute | solution.py:47
  214.3 3.2 %collective-permute-start.53 = (bf16[128,1024]{1,0:T(8,128)(2,1)S(1)}, bf16[128,1024]{1,0:T(8,128)(2,1)S(1)}, u32[]{:S(2)}, u32[]{:S(2)}) collective-permute-start(bf16[128,1024]{1,0:T(8,128)(2,1)S(1)} %collective-permute-done.50.refs_5_), channel_id=1, source_target_pairs={{0,3},{1,0},{2,1},{3,2},{4,7},{5,4},{6,5},{7,6},{8,11},{9,8},{10,9... | collective-permute-start | bytes 786440 | tf_op jit(solution)/shard_map/ppermute | solution.py:47
  217.6 3.4 %collective-permute-done.48.refs_4_ = bf16[128,1024]{1,0:T(8,128)(2,1)S(1)} collective-permute-done((bf16[128,1024]{1,0:T(8,128)(2,1)S(1)}, bf16[128,1024]{1,0:T(8,128)(2,1)S(1)}, u32[]{:S(2)}, u32[]{:S(2)}) %collective-permute-start.48) | collective-permute-done | bytes 262176 | tf_op jit(solution)/shard_map/ppermute | solution.py:47
  221.0 3.8 %collective-permute-start.49 = (bf16[64,1024]{1,0:T(8,128)(2,1)S(1)}, bf16[64,1024]{1,0:T(8,128)(2,1)S(1)}, u32[]{:S(2)}, u32[]{:S(2)}) collective-permute-start(bf16[64,1024]{1,0:T(8,128)(2,1)S(1)} %slice.60), channel_id=1, source_target_pairs={{0,3},{1,0},{2,1},{3,2},{4,7},{5,4},{6,5},{7,6},{8,11},{9,8},{10,9... | collective-permute-start | bytes 393224 | tf_op jit(solution)/shard_map/ppermute | solution.py:47
  226.6 3.8 %collective-permute-start.54 = (bf16[64,1024]{1,0:T(8,128)(2,1)S(1)}, bf16[64,1024]{1,0:T(8,128)(2,1)S(1)}, u32[]{:S(2)}, u32[]{:S(2)}) collective-permute-start(bf16[64,1024]{1,0:T(8,128)(2,1)S(1)} %slice.62), channel_id=1, source_target_pairs={{0,3},{1,0},{2,1},{3,2},{4,7},{5,4},{6,5},{7,6},{8,11},{9,8},{10,9... | collective-permute-start | bytes 393224 | tf_op jit(solution)/shard_map/ppermute | solution.py:47
  232.9 3.7 %collective-permute-done.52.refs_7_ = bf16[64,1024]{1,0:T(8,128)(2,1)S(1)} collective-permute-done((bf16[64,1024]{1,0:T(8,128)(2,1)S(1)}, bf16[64,1024]{1,0:T(8,128)(2,1)S(1)}, u32[]{:S(2)}, u32[]{:S(2)}) %collective-permute-start.52) | collective-permute-done | bytes 131104 | tf_op jit(solution)/shard_map/ppermute | solution.py:47
  236.6 6.2 %weight_product.1 = (f32[4,32,2048]{2,1,0:T(8,128)S(1)}, bf16[4,32,2048]{2,1,0:T(8,128)(2,1)S(1)}, bf16[4,32,2048]{2,1,0:T(8,128)(2,1)S(1)}, bf16[4,32,2048]{2,1,0:T(8,128)(2,1)S(1)}) custom-call(bf16[128,1024]{1,0:T(8,128)(2,1)S(1)} %get-tuple-element.75.refs_0_, bf16[128,1024]{1,0:T(8,128)(2,1)S(1)} %collective-permute-done.46.refs_1_, ...), custom_call_target="tpu_custom_call" | custom-call | flops 4294967296 | bytes 12582912 | tf_op jit(solution)/shard_map/weight_product/pallas_call | solution.py:201
  242.9 3.2 %collective-permute-start.57 = (bf16[4,32,2048]{2,1,0:T(8,128)(2,1)S(1)}, bf16[4,32,2048]{2,1,0:T(8,128)(2,1)S(1)}, u32[]{:S(2)}, u32[]{:S(2)}) collective-permute-start(bf16[4,32,2048]{2,1,0:T(8,128)(2,1)S(1)} %get-tuple-element.79), channel_id=1, source_target_pairs={{0,24},{4,100},{8,0},{12,108},{16,8},{20,116},{24,16},{28,124},{32... | collective-permute-start | bytes 1572872 | tf_op jit(solution)/shard_map/ppermute | solution.py:39
  246.1 12.8 %collective-permute-done.56 = bf16[4,32,2048]{2,1,0:T(8,128)(2,1)S(1)} collective-permute-done((bf16[4,32,2048]{2,1,0:T(8,128)(2,1)S(1)}, bf16[4,32,2048]{2,1,0:T(8,128)(2,1)S(1)}, u32[]{:S(2)}, u32[]{:S(2)}) %collective-permute-start.56) | collective-permute-done | bytes 524320 | tf_op jit(solution)/shard_map/ppermute | solution.py:39
  259.3 2.4 collective-permute-start.61
  262.5 4.3 %collective-permute-done.59 = bf16[32,2048]{1,0:T(8,128)(2,1)S(1)} collective-permute-done((bf16[32,2048]{1,0:T(8,128)(2,1)S(1)}, bf16[32,2048]{1,0:T(8,128)(2,1)S(1)}, u32[]{:S(2)}, u32[]{:S(2)}) %collective-permute-start.59) | collective-permute-done | bytes 131104 | tf_op jit(solution)/shard_map/ppermute | solution.py:43
  (141 shorter events, 38.6 us)
Async XLA Ops:
  0.6 9.6 %collective-permute-start.1 = (bf16[32,2048]{1,0:T(8,128)(2,1)}, bf16[32,2048]{1,0:T(8,128)(2,1)S(1)}, u32[]{:S(2)}, u32[]{:S(2)}) collective-permute-start(bf16[32,2048]{1,0:T(8,128)(2,1)} %param.8), channel_id=1, source_target_pairs={{0,16},{4,68},{8,24},{12,76},{16,0},{20,84},{24,8},{28,92},{32,48}... | collective-permute-start | bytes 393224 | tf_op jit(solution)/shard_map/ppermute | solution.py:39
  4.7 6.4 %collective-permute-start = (bf16[32,2048]{1,0:T(8,128)(2,1)}, bf16[32,2048]{1,0:T(8,128)(2,1)S(1)}, u32[]{:S(2)}, u32[]{:S(2)}) collective-permute-start(bf16[32,2048]{1,0:T(8,128)(2,1)} %param.8), channel_id=1, source_target_pairs={{0,8},{4,36},{8,16},{12,44},{16,24},{20,52},{24,0},{28,60},{32,40}... | collective-permute-start | bytes 393224 | tf_op jit(solution)/shard_map/ppermute | solution.py:39
  12.0 15.4 %collective-permute-start.9 = (bf16[128,2048]{1,0:T(8,128)(2,1)S(1)}, bf16[128,2048]{1,0:T(8,128)(2,1)S(1)}, u32[]{:S(2)}, u32[]{:S(2)}) collective-permute-start(bf16[128,2048]{1,0:T(8,128)(2,1)S(1)} %pad_maximum_fusion.rest_0_), channel_id=1, source_target_pairs={{0,96},{4,28},{8,104},{12,4},{16,112},{20,12},{24,120},{28,20},{32... | collective-permute-start | bytes 1572872 | tf_op jit(solution)/shard_map/ppermute | solution.py:43
  15.1 12.3 %collective-permute-start.8 = (bf16[128,2048]{1,0:T(8,128)(2,1)S(1)}, bf16[128,2048]{1,0:T(8,128)(2,1)S(1)}, u32[]{:S(2)}, u32[]{:S(2)}) collective-permute-start(bf16[128,2048]{1,0:T(8,128)(2,1)S(1)} %pad_maximum_fusion.rest_0_), channel_id=1, source_target_pairs={{0,64},{4,20},{8,72},{12,28},{16,80},{20,4},{24,88},{28,12},{32,96... | collective-permute-start | bytes 1572872 | tf_op jit(solution)/shard_map/ppermute | solution.py:43
  15.7 15.7 %collective-permute-start.7 = (bf16[128,2048]{1,0:T(8,128)(2,1)S(1)}, bf16[128,2048]{1,0:T(8,128)(2,1)S(1)}, u32[]{:S(2)}, u32[]{:S(2)}) collective-permute-start(bf16[128,2048]{1,0:T(8,128)(2,1)S(1)} %pad_maximum_fusion.rest_0_), channel_id=1, source_target_pairs={{0,32},{4,12},{8,40},{12,20},{16,48},{20,28},{24,56},{28,4},{32,64... | collective-permute-start | bytes 1572872 | tf_op jit(solution)/shard_map/ppermute | solution.py:43
  16.7 14.7 %collective-permute-start.10 = (bf16[128,2048]{1,0:T(8,128)(2,1)S(1)}, bf16[128,2048]{1,0:T(8,128)(2,1)S(1)}, u32[]{:S(2)}, u32[]{:S(2)}) collective-permute-start(bf16[128,2048]{1,0:T(8,128)(2,1)S(1)} %pad_maximum_fusion.rest_0_), channel_id=1, source_target_pairs={{0,4},{4,0},{8,12},{12,8},{16,20},{20,16},{24,28},{28,24},{32,36},... | collective-permute-start | bytes 1572872 | tf_op jit(solution)/shard_map/ppermute | solution.py:51
  41.9 10.4 %collective-permute-start.14 = (f32[256,256]{1,0:T(8,128)S(1)}, f32[256,256]{1,0:T(8,128)S(1)}, u32[]{:S(2)}, u32[]{:S(2)}) collective-permute-start(f32[256,256]{1,0:T(8,128)S(1)} %get-tuple-element.44), channel_id=1, source_target_pairs={{0,1},{1,2},{2,3},{3,0},{4,5},{5,6},{6,7},{7,4},{8,9},{9,10},{10,1... | collective-permute-start | bytes 786440 | tf_op jit(solution)/shard_map/ppermute | solution.py:47
  43.4 9.3 %collective-permute-start.17 = (f32[256,256]{1,0:T(8,128)S(1)}, f32[256,256]{1,0:T(8,128)S(1)}, u32[]{:S(2)}, u32[]{:S(2)}) collective-permute-start(f32[256,256]{1,0:T(8,128)S(1)} %get-tuple-element.48), channel_id=1, source_target_pairs={{0,3},{1,0},{2,1},{3,2},{4,7},{5,4},{6,5},{7,6},{8,11},{9,8},{10,9... | collective-permute-start | bytes 786440 | tf_op jit(solution)/shard_map/ppermute | solution.py:47
  45.2 12.7 %collective-permute-start.20 = (f32[256,256]{1,0:T(8,128)S(1)}, f32[256,256]{1,0:T(8,128)S(1)}, u32[]{:S(2)}, u32[]{:S(2)}) collective-permute-start(f32[256,256]{1,0:T(8,128)S(1)} %get-tuple-element.52), channel_id=1, source_target_pairs={{0,1},{1,2},{2,3},{3,0},{4,5},{5,6},{6,7},{7,4},{8,9},{9,10},{10,1... | collective-permute-start | bytes 786440 | tf_op jit(solution)/shard_map/ppermute | solution.py:47
  45.4 12.9 %collective-permute-start.23 = (f32[256,256]{1,0:T(8,128)S(1)}, f32[256,256]{1,0:T(8,128)S(1)}, u32[]{:S(2)}, u32[]{:S(2)}) collective-permute-start(f32[256,256]{1,0:T(8,128)S(1)} %get-tuple-element.56), channel_id=1, source_target_pairs={{0,3},{1,0},{2,1},{3,2},{4,7},{5,4},{6,5},{7,6},{8,11},{9,8},{10,9... | collective-permute-start | bytes 786440 | tf_op jit(solution)/shard_map/ppermute | solution.py:47
  52.3 11.2 %collective-permute-start.15 = (f32[256,256]{1,0:T(8,128)S(1)}, f32[256,256]{1,0:T(8,128)S(1)}, u32[]{:S(2)}, u32[]{:S(2)}) collective-permute-start(f32[256,256]{1,0:T(8,128)S(1)} %add.305), channel_id=1, source_target_pairs={{0,1},{1,2},{2,3},{3,0},{4,5},{5,6},{6,7},{7,4},{8,9},{9,10},{10,1... | collective-permute-start | bytes 786440 | tf_op jit(solution)/shard_map/ppermute | solution.py:47
  52.7 11.2 %collective-permute-start.18 = (f32[256,256]{1,0:T(8,128)S(1)}, f32[256,256]{1,0:T(8,128)S(1)}, u32[]{:S(2)}, u32[]{:S(2)}) collective-permute-start(f32[256,256]{1,0:T(8,128)S(1)} %add.308), channel_id=1, source_target_pairs={{0,3},{1,0},{2,1},{3,2},{4,7},{5,4},{6,5},{7,6},{8,11},{9,8},{10,9... | collective-permute-start | bytes 786440 | tf_op jit(solution)/shard_map/ppermute | solution.py:47
  57.9 11.2 %collective-permute-start.21 = (f32[256,256]{1,0:T(8,128)S(1)}, f32[256,256]{1,0:T(8,128)S(1)}, u32[]{:S(2)}, u32[]{:S(2)}) collective-permute-start(f32[256,256]{1,0:T(8,128)S(1)} %add.311), channel_id=1, source_target_pairs={{0,1},{1,2},{2,3},{3,0},{4,5},{5,6},{6,7},{7,4},{8,9},{9,10},{10,1... | collective-permute-start | bytes 786440 | tf_op jit(solution)/shard_map/ppermute | solution.py:47
  58.3 11.2 %collective-permute-start.24 = (f32[256,256]{1,0:T(8,128)S(1)}, f32[256,256]{1,0:T(8,128)S(1)}, u32[]{:S(2)}, u32[]{:S(2)}) collective-permute-start(f32[256,256]{1,0:T(8,128)S(1)} %add.314), channel_id=1, source_target_pairs={{0,3},{1,0},{2,1},{3,2},{4,7},{5,4},{6,5},{7,6},{8,11},{9,8},{10,9... | collective-permute-start | bytes 786440 | tf_op jit(solution)/shard_map/ppermute | solution.py:47
  63.6 11.2 %collective-permute-start.16 = (f32[256,256]{1,0:T(8,128)S(1)}, f32[256,256]{1,0:T(8,128)S(1)}, u32[]{:S(2)}, u32[]{:S(2)}) collective-permute-start(f32[256,256]{1,0:T(8,128)S(1)} %add.306), channel_id=1, source_target_pairs={{0,1},{1,2},{2,3},{3,0},{4,5},{5,6},{6,7},{7,4},{8,9},{9,10},{10,1... | collective-permute-start | bytes 786440 | tf_op jit(solution)/shard_map/ppermute | solution.py:47
  64.0 11.1 %collective-permute-start.19 = (f32[256,256]{1,0:T(8,128)S(1)}, f32[256,256]{1,0:T(8,128)S(1)}, u32[]{:S(2)}, u32[]{:S(2)}) collective-permute-start(f32[256,256]{1,0:T(8,128)S(1)} %add.309), channel_id=1, source_target_pairs={{0,3},{1,0},{2,1},{3,2},{4,7},{5,4},{6,5},{7,6},{8,11},{9,8},{10,9... | collective-permute-start | bytes 786440 | tf_op jit(solution)/shard_map/ppermute | solution.py:47
  69.2 10.4 %collective-permute-start.22 = (f32[256,256]{1,0:T(8,128)S(1)}, f32[256,256]{1,0:T(8,128)S(1)}, u32[]{:S(2)}, u32[]{:S(2)}) collective-permute-start(f32[256,256]{1,0:T(8,128)S(1)} %add.312), channel_id=1, source_target_pairs={{0,1},{1,2},{2,3},{3,0},{4,5},{5,6},{6,7},{7,4},{8,9},{9,10},{10,1... | collective-permute-start | bytes 786440 | tf_op jit(solution)/shard_map/ppermute | solution.py:47
  69.6 10.0 %collective-permute-start.25 = (f32[256,256]{1,0:T(8,128)S(1)}, f32[256,256]{1,0:T(8,128)S(1)}, u32[]{:S(2)}, u32[]{:S(2)}) collective-permute-start(f32[256,256]{1,0:T(8,128)S(1)} %add.315), channel_id=1, source_target_pairs={{0,3},{1,0},{2,1},{3,2},{4,7},{5,4},{6,5},{7,6},{8,11},{9,8},{10,9... | collective-permute-start | bytes 786440 | tf_op jit(solution)/shard_map/ppermute | solution.py:47
  79.7 15.6 %collective-permute-start.28 = (bf16[8,128,256]{2,1,0:T(8,128)(2,1)S(1)}, bf16[8,128,256]{2,1,0:T(8,128)(2,1)S(1)}, u32[]{:S(2)}, u32[]{:S(2)}) collective-permute-start(bf16[8,128,256]{2,1,0:T(8,128)(2,1)S(1)} %bitcast.19), channel_id=1, source_target_pairs={{0,24},{4,100},{8,0},{12,108},{16,8},{20,116},{24,16},{28,124},{32... | collective-permute-start | bytes 1572872 | tf_op jit(solution)/shard_map/ppermute | solution.py:39
  83.0 12.3 %collective-permute-start.27 = (bf16[8,128,256]{2,1,0:T(8,128)(2,1)S(1)}, bf16[8,128,256]{2,1,0:T(8,128)(2,1)S(1)}, u32[]{:S(2)}, u32[]{:S(2)}) collective-permute-start(bf16[8,128,256]{2,1,0:T(8,128)(2,1)S(1)} %bitcast.20), channel_id=1, source_target_pairs={{0,16},{4,68},{8,24},{12,76},{16,0},{20,84},{24,8},{28,92},{32,48}... | collective-permute-start | bytes 1572872 | tf_op jit(solution)/shard_map/ppermute | solution.py:39
  83.0 16.0 %collective-permute-start.26 = (bf16[8,128,256]{2,1,0:T(8,128)(2,1)S(1)}, bf16[8,128,256]{2,1,0:T(8,128)(2,1)S(1)}, u32[]{:S(2)}, u32[]{:S(2)}) collective-permute-start(bf16[8,128,256]{2,1,0:T(8,128)(2,1)S(1)} %bitcast.21), channel_id=1, source_target_pairs={{0,8},{4,36},{8,16},{12,44},{16,24},{20,52},{24,0},{28,60},{32,40}... | collective-permute-start | bytes 1572872 | tf_op jit(solution)/shard_map/ppermute | solution.py:39
  99.9 27.3 %collective-permute-start.29 = (bf16[16,128,256]{2,1,0:T(8,128)(2,1)S(1)}, bf16[16,128,256]{2,1,0:T(8,128)(2,1)S(1)}, u32[]{:S(2)}, u32[]{:S(2)}) collective-permute-start(bf16[16,128,256]{2,1,0:T(8,128)(2,1)S(1)} %get-tuple-element.61), channel_id=1, source_target_pairs={{0,32},{4,12},{8,40},{12,20},{16,48},{20,28},{24,56},{28,4},{32,64... | collective-permute-start | bytes 3145736 | tf_op jit(solution)/shard_map/ppermute | solution.py:43
  100.0 27.2 %collective-permute-start.30 = (bf16[16,128,256]{2,1,0:T(8,128)(2,1)S(1)}, bf16[16,128,256]{2,1,0:T(8,128)(2,1)S(1)}, u32[]{:S(2)}, u32[]{:S(2)}) collective-permute-start(bf16[16,128,256]{2,1,0:T(8,128)(2,1)S(1)} %get-tuple-element.62), channel_id=1, source_target_pairs={{0,64},{4,20},{8,72},{12,28},{16,80},{20,4},{24,88},{28,12},{32,96... | collective-permute-start | bytes 3145736 | tf_op jit(solution)/shard_map/ppermute | solution.py:43
  102.6 25.5 %collective-permute-start.31 = (bf16[16,128,256]{2,1,0:T(8,128)(2,1)S(1)}, bf16[16,128,256]{2,1,0:T(8,128)(2,1)S(1)}, u32[]{:S(2)}, u32[]{:S(2)}) collective-permute-start(bf16[16,128,256]{2,1,0:T(8,128)(2,1)S(1)} %get-tuple-element.63), channel_id=1, source_target_pairs={{0,96},{4,28},{8,104},{12,4},{16,112},{20,12},{24,120},{28,20},{32... | collective-permute-start | bytes 3145736 | tf_op jit(solution)/shard_map/ppermute | solution.py:43
  103.2 26.2 %collective-permute-start.32 = (bf16[16,128,256]{2,1,0:T(8,128)(2,1)S(1)}, bf16[16,128,256]{2,1,0:T(8,128)(2,1)S(1)}, u32[]{:S(2)}, u32[]{:S(2)}) collective-permute-start(bf16[16,128,256]{2,1,0:T(8,128)(2,1)S(1)} %get-tuple-element.60.rest_0_), channel_id=1, source_target_pairs={{0,4},{4,0},{8,12},{12,8},{16,20},{20,16},{24,28},{28,24},{32,36},... | collective-permute-start | bytes 3145736 | tf_op jit(solution)/shard_map/ppermute | solution.py:51
  128.1 7.8 %collective-permute-start.35 = (bf16[16,128,256]{2,1,0:T(8,128)(2,1)S(1)}, bf16[16,128,256]{2,1,0:T(8,128)(2,1)S(1)}, u32[]{:S(2)}, u32[]{:S(2)}) collective-permute-start(bf16[16,128,256]{2,1,0:T(8,128)(2,1)S(1)} %collective-permute-done.31.rest_3_), channel_id=1, source_target_pairs={{0,4},{4,0},{8,12},{12,8},{16,20},{20,16},{24,28},{28,24},{32,36},... | collective-permute-start | bytes 3145736 | tf_op jit(solution)/shard_map/ppermute | solution.py:51
  128.1 102.4 %collective-permute-start.55 = (bf16[1024,2048]{1,0:T(8,128)(2,1)}, bf16[1024,2048]{1,0:T(8,128)(2,1)S(1)}, u32[]{:S(2)}, u32[]{:S(2)}) collective-permute-start(bf16[1024,2048]{1,0:T(8,128)(2,1)} %refs_10_.1), channel_id=1, source_target_pairs={{0,4},{4,0},{8,12},{12,8},{16,20},{20,16},{24,28},{28,24},{32,36},... | collective-permute-start | bytes 12582920 | tf_op jit(solution)/shard_map/ppermute | solution.py:51
  163.6 9.2 %collective-permute-start.37 = (bf16[8,128,256]{2,1,0:T(8,128)(2,1)S(1)}, bf16[8,128,256]{2,1,0:T(8,128)(2,1)S(1)}, u32[]{:S(2)}, u32[]{:S(2)}) collective-permute-start(bf16[8,128,256]{2,1,0:T(8,128)(2,1)S(1)} %get-tuple-element.68), channel_id=1, source_target_pairs={{0,96},{4,28},{8,104},{12,4},{16,112},{20,12},{24,120},{28,20},{32... | collective-permute-start | bytes 1572872 | tf_op jit(solution)/shard_map/ppermute | solution.py:43
  163.6 10.8 %collective-permute-start.39 = (bf16[8,128,256]{2,1,0:T(8,128)(2,1)S(1)}, bf16[8,128,256]{2,1,0:T(8,128)(2,1)S(1)}, u32[]{:S(2)}, u32[]{:S(2)}) collective-permute-start(bf16[8,128,256]{2,1,0:T(8,128)(2,1)S(1)} %get-tuple-element.69), channel_id=1, source_target_pairs={{0,64},{4,20},{8,72},{12,28},{16,80},{20,4},{24,88},{28,12},{32,96... | collective-permute-start | bytes 1572872 | tf_op jit(solution)/shard_map/ppermute | solution.py:43
  163.6 17.4 %collective-permute-start.41 = (bf16[8,128,256]{2,1,0:T(8,128)(2,1)S(1)}, bf16[8,128,256]{2,1,0:T(8,128)(2,1)S(1)}, u32[]{:S(2)}, u32[]{:S(2)}) collective-permute-start(bf16[8,128,256]{2,1,0:T(8,128)(2,1)S(1)} %get-tuple-element.70), channel_id=1, source_target_pairs={{0,32},{4,12},{8,40},{12,20},{16,48},{20,28},{24,56},{28,4},{32,64... | collective-permute-start | bytes 1572872 | tf_op jit(solution)/shard_map/ppermute | solution.py:43
  168.0 17.5 %collective-permute-start.42 = (bf16[8,128,256]{2,1,0:T(8,128)(2,1)S(1)}, bf16[8,128,256]{2,1,0:T(8,128)(2,1)S(1)}, u32[]{:S(2)}, u32[]{:S(2)}) collective-permute-start(bf16[8,128,256]{2,1,0:T(8,128)(2,1)S(1)} %get-tuple-element.87), channel_id=1, source_target_pairs={{0,32},{4,12},{8,40},{12,20},{16,48},{20,28},{24,56},{28,4},{32,64... | collective-permute-start | bytes 1572872 | tf_op jit(solution)/shard_map/ppermute | solution.py:43
  172.7 18.4 %collective-permute-start.40 = (bf16[8,128,256]{2,1,0:T(8,128)(2,1)S(1)}, bf16[8,128,256]{2,1,0:T(8,128)(2,1)S(1)}, u32[]{:S(2)}, u32[]{:S(2)}) collective-permute-start(bf16[8,128,256]{2,1,0:T(8,128)(2,1)S(1)} %get-tuple-element.88), channel_id=1, source_target_pairs={{0,64},{4,20},{8,72},{12,28},{16,80},{20,4},{24,88},{28,12},{32,96... | collective-permute-start | bytes 1572872 | tf_op jit(solution)/shard_map/ppermute | solution.py:43
  174.4 16.8 %collective-permute-start.38 = (bf16[8,128,256]{2,1,0:T(8,128)(2,1)S(1)}, bf16[8,128,256]{2,1,0:T(8,128)(2,1)S(1)}, u32[]{:S(2)}, u32[]{:S(2)}) collective-permute-start(bf16[8,128,256]{2,1,0:T(8,128)(2,1)S(1)} %get-tuple-element.89), channel_id=1, source_target_pairs={{0,96},{4,28},{8,104},{12,4},{16,112},{20,12},{24,120},{28,20},{32... | collective-permute-start | bytes 1572872 | tf_op jit(solution)/shard_map/ppermute | solution.py:43
  193.6 9.3 %collective-permute-start.43 = (bf16[8,128,256]{2,1,0:T(8,128)(2,1)S(1)}, bf16[8,128,256]{2,1,0:T(8,128)(2,1)S(1)}, u32[]{:S(2)}, u32[]{:S(2)}) collective-permute-start(bf16[8,128,256]{2,1,0:T(8,128)(2,1)S(1)} %get-tuple-element.72), channel_id=1, source_target_pairs={{0,24},{4,100},{8,0},{12,108},{16,8},{20,116},{24,16},{28,124},{32... | collective-permute-start | bytes 1572872 | tf_op jit(solution)/shard_map/ppermute | solution.py:39
  194.6 10.8 %collective-permute-start.44 = (bf16[8,128,256]{2,1,0:T(8,128)(2,1)S(1)}, bf16[8,128,256]{2,1,0:T(8,128)(2,1)S(1)}, u32[]{:S(2)}, u32[]{:S(2)}) collective-permute-start(bf16[8,128,256]{2,1,0:T(8,128)(2,1)S(1)} %get-tuple-element.73), channel_id=1, source_target_pairs={{0,16},{4,68},{8,24},{12,76},{16,0},{20,84},{24,8},{28,92},{32,48}... | collective-permute-start | bytes 1572872 | tf_op jit(solution)/shard_map/ppermute | solution.py:39
  194.6 16.3 %collective-permute-start.45 = (bf16[8,128,256]{2,1,0:T(8,128)(2,1)S(1)}, bf16[8,128,256]{2,1,0:T(8,128)(2,1)S(1)}, u32[]{:S(2)}, u32[]{:S(2)}) collective-permute-start(bf16[8,128,256]{2,1,0:T(8,128)(2,1)S(1)} %get-tuple-element.74), channel_id=1, source_target_pairs={{0,8},{4,36},{8,16},{12,44},{16,24},{20,52},{24,0},{28,60},{32,40}... | collective-permute-start | bytes 1572872 | tf_op jit(solution)/shard_map/ppermute | solution.py:39
  211.4 9.6 %collective-permute-start.48 = (bf16[128,1024]{1,0:T(8,128)(2,1)S(1)}, bf16[128,1024]{1,0:T(8,128)(2,1)S(1)}, u32[]{:S(2)}, u32[]{:S(2)}) collective-permute-start(bf16[128,1024]{1,0:T(8,128)(2,1)S(1)} %get-tuple-element.75.refs_0_), channel_id=1, source_target_pairs={{0,3},{1,0},{2,1},{3,2},{4,7},{5,4},{6,5},{7,6},{8,11},{9,8},{10,9... | collective-permute-start | bytes 786440 | tf_op jit(solution)/shard_map/ppermute | solution.py:47
  214.3 10.4 %collective-permute-start.46 = (bf16[128,1024]{1,0:T(8,128)(2,1)S(1)}, bf16[128,1024]{1,0:T(8,128)(2,1)S(1)}, u32[]{:S(2)}, u32[]{:S(2)}) collective-permute-start(bf16[128,1024]{1,0:T(8,128)(2,1)S(1)} %get-tuple-element.75.refs_0_), channel_id=1, source_target_pairs={{0,1},{1,2},{2,3},{3,0},{4,5},{5,6},{6,7},{7,4},{8,9},{9,10},{10,1... | collective-permute-start | bytes 786440 | tf_op jit(solution)/shard_map/ppermute | solution.py:47
  214.3 12.2 %collective-permute-start.53 = (bf16[128,1024]{1,0:T(8,128)(2,1)S(1)}, bf16[128,1024]{1,0:T(8,128)(2,1)S(1)}, u32[]{:S(2)}, u32[]{:S(2)}) collective-permute-start(bf16[128,1024]{1,0:T(8,128)(2,1)S(1)} %collective-permute-done.50.refs_5_), channel_id=1, source_target_pairs={{0,3},{1,0},{2,1},{3,2},{4,7},{5,4},{6,5},{7,6},{8,11},{9,8},{10,9... | collective-permute-start | bytes 786440 | tf_op jit(solution)/shard_map/ppermute | solution.py:47
  217.6 12.8 %collective-permute-start.51 = (bf16[128,1024]{1,0:T(8,128)(2,1)S(1)}, bf16[128,1024]{1,0:T(8,128)(2,1)S(1)}, u32[]{:S(2)}, u32[]{:S(2)}) collective-permute-start(bf16[128,1024]{1,0:T(8,128)(2,1)S(1)} %collective-permute-done.50.refs_5_), channel_id=1, source_target_pairs={{0,1},{1,2},{2,3},{3,0},{4,5},{5,6},{6,7},{7,4},{8,9},{9,10},{10,1... | collective-permute-start | bytes 786440 | tf_op jit(solution)/shard_map/ppermute | solution.py:47
  221.0 9.5 %collective-permute-start.49 = (bf16[64,1024]{1,0:T(8,128)(2,1)S(1)}, bf16[64,1024]{1,0:T(8,128)(2,1)S(1)}, u32[]{:S(2)}, u32[]{:S(2)}) collective-permute-start(bf16[64,1024]{1,0:T(8,128)(2,1)S(1)} %slice.60), channel_id=1, source_target_pairs={{0,3},{1,0},{2,1},{3,2},{4,7},{5,4},{6,5},{7,6},{8,11},{9,8},{10,9... | collective-permute-start | bytes 393224 | tf_op jit(solution)/shard_map/ppermute | solution.py:47
  224.8 7.6 %collective-permute-start.47 = (bf16[64,1024]{1,0:T(8,128)(2,1)S(1)}, bf16[64,1024]{1,0:T(8,128)(2,1)S(1)}, u32[]{:S(2)}, u32[]{:S(2)}) collective-permute-start(bf16[64,1024]{1,0:T(8,128)(2,1)S(1)} %slice.59), channel_id=1, source_target_pairs={{0,1},{1,2},{2,3},{3,0},{4,5},{5,6},{6,7},{7,4},{8,9},{9,10},{10,1... | collective-permute-start | bytes 393224 | tf_op jit(solution)/shard_map/ppermute | solution.py:47
  226.6 6.3 %collective-permute-start.54 = (bf16[64,1024]{1,0:T(8,128)(2,1)S(1)}, bf16[64,1024]{1,0:T(8,128)(2,1)S(1)}, u32[]{:S(2)}, u32[]{:S(2)}) collective-permute-start(bf16[64,1024]{1,0:T(8,128)(2,1)S(1)} %slice.62), channel_id=1, source_target_pairs={{0,3},{1,0},{2,1},{3,2},{4,7},{5,4},{6,5},{7,6},{8,11},{9,8},{10,9... | collective-permute-start | bytes 393224 | tf_op jit(solution)/shard_map/ppermute | solution.py:47
  242.8 16.1 %collective-permute-start.56 = (bf16[4,32,2048]{2,1,0:T(8,128)(2,1)S(1)}, bf16[4,32,2048]{2,1,0:T(8,128)(2,1)S(1)}, u32[]{:S(2)}, u32[]{:S(2)}) collective-permute-start(bf16[4,32,2048]{2,1,0:T(8,128)(2,1)S(1)} %get-tuple-element.78), channel_id=1, source_target_pairs={{0,8},{4,36},{8,16},{12,44},{16,24},{20,52},{24,0},{28,60},{32,40}... | collective-permute-start | bytes 1572872 | tf_op jit(solution)/shard_map/ppermute | solution.py:39
  242.9 16.0 %collective-permute-start.57 = (bf16[4,32,2048]{2,1,0:T(8,128)(2,1)S(1)}, bf16[4,32,2048]{2,1,0:T(8,128)(2,1)S(1)}, u32[]{:S(2)}, u32[]{:S(2)}) collective-permute-start(bf16[4,32,2048]{2,1,0:T(8,128)(2,1)S(1)} %get-tuple-element.79), channel_id=1, source_target_pairs={{0,24},{4,100},{8,0},{12,108},{16,8},{20,116},{24,16},{28,124},{32... | collective-permute-start | bytes 1572872 | tf_op jit(solution)/shard_map/ppermute | solution.py:39
  246.1 12.8 %collective-permute-start.58 = (bf16[4,32,2048]{2,1,0:T(8,128)(2,1)S(1)}, bf16[4,32,2048]{2,1,0:T(8,128)(2,1)S(1)}, u32[]{:S(2)}, u32[]{:S(2)}) collective-permute-start(bf16[4,32,2048]{2,1,0:T(8,128)(2,1)S(1)} %get-tuple-element.80), channel_id=1, source_target_pairs={{0,16},{4,68},{8,24},{12,76},{16,0},{20,84},{24,8},{28,92},{32,48}... | collective-permute-start | bytes 1572872 | tf_op jit(solution)/shard_map/ppermute | solution.py:39
  259.2 7.7 %collective-permute-start.59 = (bf16[32,2048]{1,0:T(8,128)(2,1)S(1)}, bf16[32,2048]{1,0:T(8,128)(2,1)S(1)}, u32[]{:S(2)}, u32[]{:S(2)}) collective-permute-start(bf16[32,2048]{1,0:T(8,128)(2,1)S(1)} %get-tuple-element.91), channel_id=1, source_target_pairs={{0,32},{4,12},{8,40},{12,20},{16,48},{20,28},{24,56},{28,4},{32,64... | collective-permute-start | bytes 393224 | tf_op jit(solution)/shard_map/ppermute | solution.py:43
  259.3 7.6 %collective-permute-start.61 = (bf16[32,2048]{1,0:T(8,128)(2,1)S(1)}, bf16[32,2048]{1,0:T(8,128)(2,1)S(1)}, u32[]{:S(2)}, u32[]{:S(2)}) collective-permute-start(bf16[32,2048]{1,0:T(8,128)(2,1)S(1)} %get-tuple-element.92), channel_id=1, source_target_pairs={{0,64},{4,20},{8,72},{12,28},{16,80},{20,4},{24,88},{28,12},{32,96... | collective-permute-start | bytes 393224 | tf_op jit(solution)/shard_map/ppermute | solution.py:43
  (23 other events, 272.9 us)

commit v2 on v1

--- a/solution.py
+++ b/solution.py
@@ -83,39 +83,39 @@
     return lax.rem(n + 2 * SIDE, SIDE)
 
 
-def project_kernel(h_ref, *rest):
-    pieces, outs = rest[: 2 * SIDE], rest[2 * SIDE : 6 * SIDE]
-    weights, rows, h_sem = rest[6 * SIDE :]
+def gather_rows(pieces, weights):
+    y, z, core, tp = here_in_kernel()
+    for src in range(2):
+        which = core if src == 0 else 1 - core
+        first = jnp.where(which == 0, z, y)
+        second = jnp.where(which == 0, y, z)
+        for jb in range(SIDE):
+            for ja in range(SIDE):
+                a = ring_mod(first - ja)
+                b = ring_mod(second - jb)
+                place = ring_mod(jnp.where(which == 0, b, a) - tp)
+                part = (place * SIDE + jnp.where(which == 0, a, b)) * 2 + which
+                weights[pl.ds(pl.multiple_of(part * OUT_ROWS, OUT_ROWS), OUT_ROWS), :] = pieces[
+                    SIDE * src + jb
+                ][ja * OUT_ROWS : (ja + 1) * OUT_ROWS, :]
+
+
+def project_kernel(first, n_in, h_ref, *rest):
+    outs = rest[n_in : n_in + 2 * SIDE]
     step = pl.program_id(0)
-    y, z, core, tp = here_in_kernel()
-    block = rows.shape[1]
-    head = weights.shape[0] // SIDE
-
-    def hidden_copy(i):
-        at = pl.ds(pl.multiple_of(i * block, block), block)
-        return pltpu.make_async_copy(h_ref.at[at], rows.at[i], h_sem.at[i])
-
-    @pl.when(step == 0)
-    def _():
-        for i in range(rows.shape[0]):
-            hidden_copy(i).start()
-        for src in range(2):
-            which = core if src == 0 else 1 - core
-            first = jnp.where(which == 0, z, y)
-            second = jnp.where(which == 0, y, z)
-            for jb in range(SIDE):
-                for ja in range(SIDE):
-                    a = ring_mod(first - ja)
-                    b = ring_mod(second - jb)
-                    place = ring_mod(jnp.where(which == 0, b, a) - tp)
-                    part = (place * SIDE + jnp.where(which == 0, a, b)) * 2 + which
-                    weights[pl.ds(pl.multiple_of(part * OUT_ROWS, OUT_ROWS), OUT_ROWS), :] = pieces[
-                        SIDE * src + jb
-                    ][ja * OUT_ROWS : (ja + 1) * OUT_ROWS, :]
-
-    hidden_copy(step).wait()
-    product = lax.dot_general(rows[step], weights[...], NT, preferred_element_type=F32)
-    for i in range(4):
+    if first == 0:
+        weights = rest[n_in + 2 * SIDE]
+
+        @pl.when(step == 0)
+        def _():
+            gather_rows(rest[:n_in], weights)
+
+    else:
+        weights = rest[0]
+    block, head = outs[0].shape
+    at = pl.ds(pl.multiple_of((first + step) * block, block), block)
+    product = lax.dot_general(h_ref[at, :], weights[...], NT, preferred_element_type=F32)
+    for i in range(2):
 
         @pl.when(step == i)
         def _():
@@ -123,27 +123,25 @@
                 outs[i * SIDE + j][...] = product[:, j * head : (j + 1) * head]
 
 
-def project(hidden, pieces):
+def project(hidden, pieces, first):
     rows, depth = hidden.shape
     block = rows // 4
     columns = 2 * SIDE * SIDE * OUT_ROWS
     head = columns // SIDE
     whole = pl.BlockSpec(memory_space=pltpu.VMEM)
+    outs = [jax.ShapeDtypeStruct((block, head), F32)] * (2 * SIDE)
+    if first == 0:
+        outs += [jax.ShapeDtypeStruct((columns, depth), BF)]
     return pl.pallas_call(
-        project_kernel,
-        out_shape=[jax.ShapeDtypeStruct((block, head), F32)] * (4 * SIDE),
-        grid=(4,),
-        in_specs=[pl.BlockSpec(memory_space=pltpu.HBM)] + [whole] * (2 * SIDE),
-        out_specs=[whole] * (4 * SIDE),
-        scratch_shapes=[
-            pltpu.VMEM((columns, depth), BF),
-            pltpu.VMEM((4, block, depth), BF),
-            pltpu.SemaphoreType.DMA((4,)),
-        ],
-        compiler_params=pltpu.CompilerParams(vmem_limit_bytes=28 * 2**20),
+        functools.partial(project_kernel, first, len(pieces)),
+        out_shape=outs,
+        grid=(2,),
+        in_specs=[whole] * (1 + len(pieces)),
+        out_specs=[whole] * len(outs),
+        compiler_params=pltpu.CompilerParams(vmem_limit_bytes=20 * 2**20),
         cost_estimate=pl.CostEstimate(
-            flops=2 * rows * columns * depth,
-            bytes_accessed=2 * (rows + columns) * depth + 4 * rows * columns,
+            flops=rows * columns * depth,
+            bytes_accessed=(rows + 2 * columns) * depth + 2 * rows * columns,
             transcendentals=0,
         ),
         name="project",
@@ -253,14 +251,13 @@
         for b in range(n_src):
             for m in range(slots):
                 to = taken_by[b * slots + m]
-                at = m if b < SIDE else slots + m
 
                 @pl.when(to >= 0)
                 def _():
                     query = lax.div(to, retrieved)
                     into = pl.ds(pl.multiple_of(lax.rem(to, retrieved) * PLEN, PLEN), PLEN)
-                    keys_at[query, into, :] = srcs[b][at, :, :HD]
-                    values_at[query, into, :] = srcs[b][at, :, HD:]
+                    keys_at[query, into, :] = srcs[b][m, :, :HD]
+                    values_at[query, into, :] = srcs[b][m, :, HD:]
 
     for g in range(group):
         q_st[pl.ds(g * HD, HD), :] = q_ref[:, g * HD : (g + 1) * HD]
@@ -289,9 +286,9 @@
         ds_t[:, cols] = (w * (gw - delta)).astype(BF)
     d_v = jnp.dot(p_t[...], do_st[...], preferred_element_type=F32)
     d_k = jnp.dot(ds_t[...], q_st[...], preferred_element_type=F32) * F32(scaling)
-    dq_t = lax.dot_general(k_all, ds_t[...], TN, preferred_element_type=F32) * F32(scaling)
+    d_q = lax.dot_general(ds_t[...], k_all, TN, preferred_element_type=F32) * F32(scaling)
     for g in range(group):
-        dq_ref[:, g * HD : (g + 1) * HD] = dq_t[:, g * HD : (g + 1) * HD].T.astype(BF)
+        dq_ref[:, g * HD : (g + 1) * HD] = d_q[g * HD : (g + 1) * HD].astype(BF)
 
     down_ref[:, :HD] = d_k[rows:].astype(BF)
     down_ref[:, HD:] = d_v[rows:].astype(BF)
@@ -349,26 +346,26 @@
 def pick_kernel(slot_of, *rest):
     ring, outs = rest[:SIDE], rest[SIDE:]
     n = outs[0].shape[0]
-    for k in range(SIDE):
+    for k in range(2 * SIDE):
         for m in range(n):
-            outs[k][m] = ring[(m // 2) % SIDE][jnp.maximum(slot_of[k * n + m], 0)]
+            outs[k][m] = ring[m // 2][jnp.maximum(slot_of[k * n + m], 0)]
 
 
 def pick(slot_of, ring):
-    n = slot_of.shape[0] // SIDE
+    n = slot_of.shape[0] // (2 * SIDE)
     whole = pl.BlockSpec(memory_space=pltpu.VMEM)
     shape = jax.ShapeDtypeStruct((n,) + ring[0].shape[1:], BF)
     return pl.pallas_call(
         pick_kernel,
-        out_shape=[shape] * SIDE,
+        out_shape=[shape] * (2 * SIDE),
         grid_spec=pltpu.PrefetchScalarGridSpec(
             num_scalar_prefetch=1,
             in_specs=[whole] * SIDE,
-            out_specs=[whole] * SIDE,
+            out_specs=[whole] * (2 * SIDE),
         ),
         compiler_params=pltpu.CompilerParams(vmem_limit_bytes=16 * 2**20),
         cost_estimate=pl.CostEstimate(
-            flops=0, bytes_accessed=8 * SIDE * n * PLEN * HD, transcendentals=0
+            flops=0, bytes_accessed=16 * SIDE * n * PLEN * HD, transcendentals=0
         ),
         name="pick",
     )(slot_of, *ring)
@@ -513,18 +510,23 @@
     places = own_places(flat_device, ranking, capacity)
     served = slots_served(tables, owners, capacity)
 
-    parts = project(passage_hidden, weights)
-    own = [reduce_heads(parts[n : n + 2 * SIDE]) for n in (0, 2 * SIDE)]
-    own = jnp.concatenate(own, axis=0).reshape(passages_here, PLEN, local_width)
+    *lower, weights = project(passage_hidden, weights, 0)
+    upper = project(passage_hidden, [weights], 2)
+    own = jnp.concatenate([reduce_heads(lower), reduce_heads(upper)], axis=0)
+    own = own.reshape(passages_here, PLEN, local_width)
     wanted = pick(served, ring_gather(own, send_first))
-    got = [wanted[0]] + [send_second(wanted[k], k) for k in (1, 2, 3)]
+    same, other = wanted[::2], wanted[1::2]
+    other = [other[0]] + [send_second(other[k], k) for k in (1, 3, 2)]
+    same = [same[0]] + [send_second(same[k], k) for k in (1, 3, 2)]
+    for blocks in (other, same):
+        blocks[2], blocks[3] = blocks[3], blocks[2]
     hidden_theirs = swap_cores(passage_hidden)
     half = SIDE * capacity
     grad_queries, own_grads, *grads = attention(
         queries,
         out_grad,
         query_kv,
-        got + [swap_cores(g) for g in got],
+        same + [swap_cores(g) for g in other],
         [half] * SIDE + [SIDE * half],
         places,
         queries_here,

time: 269 us -> 257 us (0.955)
  waiting for transfers between devices: 139 us -> 128 us
  Pallas kernels: 42.7 us -> 38.2 us
  starting transfers between devices: 75.8 us -> 79.1 us
    ppermute x12, waiting for transfers between devices: 11.7 us -> 7.35 us  [swap_cores(): return lax.ppermute(x, 'pas', [(i, i ^ 1) for i in range(2 * SIDE * SIDE)])]
    pallas_call x1, Pallas kernels: 26.5 us -> 22.4 us  [attention(): pl.pallas_call(functools.partial(attention_kernel, len(sources), len(out_...]
    ppermute x18 -> x21, waiting for transfers between devices: 65.6 us -> 62.2 us  [send_second(): return lax.ppermute(x, 'pas', ring_pairs(1, k))]
    ppermute x18 -> x21, starting transfers between devices: 23.2 us -> 26.4 us  [send_second(): return lax.ppermute(x, 'pas', ring_pairs(1, k))]
    ppermute x20, waiting for transfers between devices: 28.6 us -> 25.7 us  [send_tp(): return lax.ppermute(x, 'tp', [(i, (i + k) % SIDE) for i in range(SIDE)])]
    pallas_call x2 -> x3, Pallas kernels: 7.16 us -> 6.7 us  [the longest x2 5.88 us: project(): pl.pallas_call(functools.partial(project_kernel, first, len(pieces)), out...]
  transfers between devices with their start and end apart: 62 -> 65, of which waited for: 38 -> 36; matrix products, arithmetic and copies ran while one was open for 2% -> 2% of each run, Pallas kernels for 11% -> 11%
where the time goes in v2:
time: 257 us
  waiting for transfers between devices  128 us (50%)
  starting transfers between devices  79.1 us (31%)
  Pallas kernels  38.2 us (15%)
  local copies, waits for them, and re-layouts  6.04 us (2%)
  other arithmetic  4.47 us (2%)
    ppermute x21, waiting for transfers between devices, send_second(): return lax.ppermute(x, 'pas', ring_pairs(1, k))  62.2 us
    ppermute x20, starting transfers between devices, send_tp(): return lax.ppermute(x, 'tp', [(i, (i + k) % SIDE) for i in range(SIDE)])  33.9 us
    ppermute x12, waiting for transfers between devices, send_first(): return lax.ppermute(x, 'pas', ring_pairs(0, k))  33.2 us
    ppermute x21, starting transfers between devices, send_second(): return lax.ppermute(x, 'pas', ring_pairs(1, k))  26.4 us
    ppermute x20, waiting for transfers between devices, send_tp(): return lax.ppermute(x, 'tp', [(i, (i + k) % SIDE) for i in range(SIDE)])  25.7 us
    pallas_call x1, Pallas kernels, attention(): pl.pallas_call(functools.partial(attention_kernel, len(sources), len(out_...  22.4 us
    ppermute x12, starting transfers between devices, send_first(): return lax.ppermute(x, 'pas', ring_pairs(0, k))  16.9 us
    ppermute x12, waiting for transfers between devices, swap_cores(): return lax.ppermute(x, 'pas', [(i, i ^ 1) for i in range(2 * SIDE * SIDE)])  7.35 us
  transfers between devices with their start and end apart: 65, of which 36 were waited for; matrix products, arithmetic and copies ran while one was open for 2% of the time, Pallas kernels for 11%

profile of v2, /device:TPU:0, one launch (start us, length us, event | category | flops | bytes accessed | tf_op | source)
XLA Modules:
  0.0 257.3 jit_solution(6590900718775678301)
XLA Ops:
  0.6 4.0 %collective-permute-start.1 = (bf16[32,2048]{1,0:T(8,128)(2,1)}, bf16[32,2048]{1,0:T(8,128)(2,1)S(1)}, u32[]{:S(2)}, u32[]{:S(2)}) collective-permute-start(bf16[32,2048]{1,0:T(8,128)(2,1)} %param.8), channel_id=1, source_target_pairs={{0,16},{4,68},{8,24},{12,76},{16,0},{20,84},{24,8},{28,92},{32,48}... | collective-permute-start | bytes 393224 | tf_op jit(solution)/shard_map/ppermute | solution.py:39
  5.7 2.2 collective-permute-start.2
  12.0 3.1 %collective-permute-start.9 = (bf16[128,2048]{1,0:T(8,128)(2,1)S(1)}, bf16[128,2048]{1,0:T(8,128)(2,1)S(1)}, u32[]{:S(2)}, u32[]{:S(2)}) collective-permute-start(bf16[128,2048]{1,0:T(8,128)(2,1)S(1)} %pad_maximum_fusion.rest_0_), channel_id=1, source_target_pairs={{0,96},{4,28},{8,104},{12,4},{16,112},{20,12},{24,120},{28,20},{32... | collective-permute-start | bytes 1572872 | tf_op jit(solution)/shard_map/ppermute | solution.py:43
  16.7 10.7 %collective-permute-done.9.rest_3_ = bf16[128,2048]{1,0:T(8,128)(2,1)S(1)} collective-permute-done((bf16[128,2048]{1,0:T(8,128)(2,1)S(1)}, bf16[128,2048]{1,0:T(8,128)(2,1)S(1)}, u32[]{:S(2)}, u32[]{:S(2)}) %collective-permute-start.9) | collective-permute-done | bytes 524320 | tf_op jit(solution)/shard_map/ppermute | solution.py:43
  27.9 3.5 %collective-permute-done.7.rest_1_ = bf16[128,2048]{1,0:T(8,128)(2,1)S(1)} collective-permute-done((bf16[128,2048]{1,0:T(8,128)(2,1)S(1)}, bf16[128,2048]{1,0:T(8,128)(2,1)S(1)}, u32[]{:S(2)}, u32[]{:S(2)}) %collective-permute-start.7) | collective-permute-done | bytes 524320 | tf_op jit(solution)/shard_map/ppermute | solution.py:43
  33.3 2.2 copy-done
  35.5 3.2 %project.2 = (f32[256,256]{1,0:T(8,128)S(1)}, f32[256,256]{1,0:T(8,128)S(1)}, f32[256,256]{1,0:T(8,128)S(1)}, f32[256,256]{1,0:T(8,128)S(1)}, f32[256,256]{1,0:T...) custom-call(bf16[1024,2048]{1,0:T(8,128)(2,1)S(1)} %copy-done, ...), custom_call_target="tpu_custom_call" | custom-call | flops 2147483648 | bytes 8388608 | tf_op jit(solution)/shard_map/project/pallas_call | solution.py:135
  42.0 2.7 %project.3 = (f32[256,256]{1,0:T(8,128)S(1)}, f32[256,256]{1,0:T(8,128)S(1)}, f32[256,256]{1,0:T(8,128)S(1)}, f32[256,256]{1,0:T(8,128)S(1)}, f32[256,256]{1,0:T...) custom-call(bf16[1024,2048]{1,0:T(8,128)(2,1)S(1)} %copy-done, ...), custom_call_target="tpu_custom_call" | custom-call | flops 2147483648 | bytes 8388608 | tf_op jit(solution)/shard_map/project/pallas_call | solution.py:135
  45.1 3.0 %collective-permute-start.23 = (f32[256,256]{1,0:T(8,128)S(1)}, f32[256,256]{1,0:T(8,128)S(1)}, u32[]{:S(2)}, u32[]{:S(2)}) collective-permute-start(f32[256,256]{1,0:T(8,128)S(1)} %get-tuple-element.62), channel_id=1, source_target_pairs={{0,3},{1,0},{2,1},{3,2},{4,7},{5,4},{6,5},{7,6},{8,11},{9,8},{10,9... | collective-permute-start | bytes 786440 | tf_op jit(solution)/shard_map/ppermute | solution.py:47
  49.5 2.3 collective-permute-start.18
  51.9 3.4 %collective-permute-done.20 = f32[256,256]{1,0:T(8,128)S(1)} collective-permute-done((f32[256,256]{1,0:T(8,128)S(1)}, f32[256,256]{1,0:T(8,128)S(1)}, u32[]{:S(2)}, u32[]{:S(2)}) %collective-permute-start.20) | collective-permute-done | bytes 262176 | tf_op jit(solution)/shard_map/ppermute | solution.py:47
  55.4 3.3 %collective-permute-start.24 = (f32[256,256]{1,0:T(8,128)S(1)}, f32[256,256]{1,0:T(8,128)S(1)}, u32[]{:S(2)}, u32[]{:S(2)}) collective-permute-start(f32[256,256]{1,0:T(8,128)S(1)} %add.314), channel_id=1, source_target_pairs={{0,3},{1,0},{2,1},{3,2},{4,7},{5,4},{6,5},{7,6},{8,11},{9,8},{10,9... | collective-permute-start | bytes 786440 | tf_op jit(solution)/shard_map/ppermute | solution.py:47
  58.7 2.2 collective-permute-done.15
  61.0 3.3 %collective-permute-start.19 = (f32[256,256]{1,0:T(8,128)S(1)}, f32[256,256]{1,0:T(8,128)S(1)}, u32[]{:S(2)}, u32[]{:S(2)}) collective-permute-start(f32[256,256]{1,0:T(8,128)S(1)} %add.309), channel_id=1, source_target_pairs={{0,3},{1,0},{2,1},{3,2},{4,7},{5,4},{6,5},{7,6},{8,11},{9,8},{10,9... | collective-permute-start | bytes 786440 | tf_op jit(solution)/shard_map/ppermute | solution.py:47
  64.3 2.1 collective-permute-done.21
  66.6 3.3 %collective-permute-start.25 = (f32[256,256]{1,0:T(8,128)S(1)}, f32[256,256]{1,0:T(8,128)S(1)}, u32[]{:S(2)}, u32[]{:S(2)}) collective-permute-start(f32[256,256]{1,0:T(8,128)S(1)} %add.315), channel_id=1, source_target_pairs={{0,3},{1,0},{2,1},{3,2},{4,7},{5,4},{6,5},{7,6},{8,11},{9,8},{10,9... | collective-permute-start | bytes 786440 | tf_op jit(solution)/shard_map/ppermute | solution.py:47
  69.9 2.2 collective-permute-done.16
  72.2 4.2 %collective-permute-done.22 = f32[256,256]{1,0:T(8,128)S(1)} collective-permute-done((f32[256,256]{1,0:T(8,128)S(1)}, f32[256,256]{1,0:T(8,128)S(1)}, u32[]{:S(2)}, u32[]{:S(2)}) %collective-permute-start.22) | collective-permute-done | bytes 262176 | tf_op jit(solution)/shard_map/ppermute | solution.py:47
  76.5 3.3 %collective-permute-start.28 = (bf16[8,128,256]{2,1,0:T(8,128)(2,1)S(1)}, bf16[8,128,256]{2,1,0:T(8,128)(2,1)S(1)}, u32[]{:S(2)}, u32[]{:S(2)}) collective-permute-start(bf16[8,128,256]{2,1,0:T(8,128)(2,1)S(1)} %bitcast.19), channel_id=1, source_target_pairs={{0,24},{4,100},{8,0},{12,108},{16,8},{20,116},{24,16},{28,124},{32... | collective-permute-start | bytes 1572872 | tf_op jit(solution)/shard_map/ppermute | solution.py:39
  82.1 2.7 %collective-permute-start.5 = (s32[64,2]{0,1:T(2,128)S(1)}, s32[64,2]{0,1:T(2,128)S(1)}, u32[]{:S(2)}, u32[]{:S(2)}) collective-permute-start(s32[64,2]{0,1:T(2,128)S(1)} %pad_add_fusion.1), channel_id=1, source_target_pairs={{0,64},{4,20},{8,72},{12,28},{16,80},{20,4},{24,88},{28,12},{32,96... | collective-permute-start | bytes 1544 | tf_op jit(solution)/shard_map/ppermute | solution.py:43
  84.8 2.1 collective-permute-done.6
  87.3 3.2 %collective-permute-done.4 = s32[64,2]{0,1:T(2,128)S(1)} collective-permute-done((s32[64,2]{0,1:T(2,128)S(1)}, s32[64,2]{0,1:T(2,128)S(1)}, u32[]{:S(2)}, u32[]{:S(2)}) %collective-permute-start.4) | collective-permute-done | bytes 544 | tf_op jit(solution)/shard_map/ppermute | solution.py:43
  92.2 3.7 %collective-permute-done.26.rest_1_ = bf16[8,128,256]{2,1,0:T(8,128)(2,1)S(1)} collective-permute-done((bf16[8,128,256]{2,1,0:T(8,128)(2,1)S(1)}, bf16[8,128,256]{2,1,0:T(8,128)(2,1)S(1)}, u32[]{:S(2)}, u32[]{:S(2)}) %collective-permute-start.26) | collective-permute-done | bytes 524320 | tf_op jit(solution)/shard_map/ppermute | solution.py:39
  96.8 2.7 %collective-permute-start.30 = (bf16[8,128,256]{2,1,0:T(8,128)(2,1)S(1)}, bf16[8,128,256]{2,1,0:T(8,128)(2,1)S(1)}, u32[]{:S(2)}, u32[]{:S(2)}) collective-permute-start(bf16[8,128,256]{2,1,0:T(8,128)(2,1)S(1)} %get-tuple-element.68), channel_id=1, source_target_pairs={{0,64},{4,20},{8,72},{12,28},{16,80},{20,4},{24,88},{28,12},{32,96... | collective-permute-start | bytes 1572872 | tf_op jit(solution)/shard_map/ppermute | solution.py:43
  101.5 2.0 collective-permute-start.37
  103.6 9.2 %collective-permute-done.29.rest_1_ = bf16[8,128,256]{2,1,0:T(8,128)(2,1)S(1)} collective-permute-done((bf16[8,128,256]{2,1,0:T(8,128)(2,1)S(1)}, bf16[8,128,256]{2,1,0:T(8,128)(2,1)S(1)}, u32[]{:S(2)}, u32[]{:S(2)}) %collective-permute-start.29) | collective-permute-done | bytes 524320 | tf_op jit(solution)/shard_map/ppermute | solution.py:43
  112.8 11.2 %collective-permute-done.33 = bf16[8,128,256]{2,1,0:T(8,128)(2,1)S(1)} collective-permute-done((bf16[8,128,256]{2,1,0:T(8,128)(2,1)S(1)}, bf16[8,128,256]{2,1,0:T(8,128)(2,1)S(1)}, u32[]{:S(2)}, u32[]{:S(2)}) %collective-permute-start.33) | collective-permute-done | bytes 524320 | tf_op jit(solution)/shard_map/ppermute | solution.py:43
  129.4 22.4 %attention.1 = (bf16[512,1024]{1,0:T(8,128)(2,1)}, bf16[512,256]{1,0:T(8,128)(2,1)}, bf16[8,128,256]{2,1,0:T(8,128)(2,1)S(1)}, bf16[8,128,256]{2,1,0:T(8,128)(2,...) custom-call(s32[64]{0:T(128)S(1)} %select_reduce_fusion.taken_by, ...), custom_call_target="tpu_custom_call" | custom-call | flops 6039797760 | bytes 8912896 | tf_op jit(solution)/shard_map/attention/pallas_call | solution.py:315
  154.2 2.0 collective-permute-done.39
  156.5 4.8 %collective-permute-done.40.rest_2_ = bf16[8,128,256]{2,1,0:T(8,128)(2,1)S(1)} collective-permute-done((bf16[8,128,256]{2,1,0:T(8,128)(2,1)S(1)}, bf16[8,128,256]{2,1,0:T(8,128)(2,1)S(1)}, u32[]{:S(2)}, u32[]{:S(2)}) %collective-permute-start.40) | collective-permute-done | bytes 524320 | tf_op jit(solution)/shard_map/ppermute | solution.py:43
  163.0 6.6 %collective-permute-start.41 = (bf16[8,128,256]{2,1,0:T(8,128)(2,1)S(1)}, bf16[8,128,256]{2,1,0:T(8,128)(2,1)S(1)}, u32[]{:S(2)}, u32[]{:S(2)}) collective-permute-start(bf16[8,128,256]{2,1,0:T(8,128)(2,1)S(1)} %get-tuple-element.99), channel_id=1, source_target_pairs={{0,96},{4,28},{8,104},{12,4},{16,112},{20,12},{24,120},{28,20},{32... | collective-permute-start | bytes 1572872 | tf_op jit(solution)/shard_map/ppermute | solution.py:43
  169.6 4.5 %collective-permute-done.45.rest_7_ = bf16[8,128,256]{2,1,0:T(8,128)(2,1)S(1)} collective-permute-done((bf16[8,128,256]{2,1,0:T(8,128)(2,1)S(1)}, bf16[8,128,256]{2,1,0:T(8,128)(2,1)S(1)}, u32[]{:S(2)}, u32[]{:S(2)}) %collective-permute-start.45) | collective-permute-done | bytes 524320 | tf_op jit(solution)/shard_map/ppermute | solution.py:43
  174.2 5.7 %collective-permute-done.43.rest_5_ = bf16[8,128,256]{2,1,0:T(8,128)(2,1)S(1)} collective-permute-done((bf16[8,128,256]{2,1,0:T(8,128)(2,1)S(1)}, bf16[8,128,256]{2,1,0:T(8,128)(2,1)S(1)}, u32[]{:S(2)}, u32[]{:S(2)}) %collective-permute-start.43) | collective-permute-done | bytes 524320 | tf_op jit(solution)/shard_map/ppermute | solution.py:43
  179.8 2.5 add_blocks.1
  184.4 7.2 %collective-permute-done.46.left_ref = bf16[8,128,256]{2,1,0:T(8,128)(2,1)S(1)} collective-permute-done((bf16[8,128,256]{2,1,0:T(8,128)(2,1)S(1)}, bf16[8,128,256]{2,1,0:T(8,128)(2,1)S(1)}, u32[]{:S(2)}, u32[]{:S(2)}) %collective-permute-start.46) | collective-permute-done | bytes 524320 | tf_op jit(solution)/shard_map/ppermute | solution.py:39
  191.6 2.6 collective-permute-done.47.far_ref
  194.1 5.5 %collective-permute-done.48.right_ref = bf16[8,128,256]{2,1,0:T(8,128)(2,1)S(1)} collective-permute-done((bf16[8,128,256]{2,1,0:T(8,128)(2,1)S(1)}, bf16[8,128,256]{2,1,0:T(8,128)(2,1)S(1)}, u32[]{:S(2)}, u32[]{:S(2)}) %collective-permute-start.48) | collective-permute-done | bytes 524320 | tf_op jit(solution)/shard_map/ppermute | solution.py:39
  200.1 3.0 %collective-permute-start.51 = (bf16[128,1024]{1,0:T(8,128)(2,1)S(1)}, bf16[128,1024]{1,0:T(8,128)(2,1)S(1)}, u32[]{:S(2)}, u32[]{:S(2)}) collective-permute-start(bf16[128,1024]{1,0:T(8,128)(2,1)S(1)} %get-tuple-element.85.refs_0_), channel_id=1, source_target_pairs={{0,3},{1,0},{2,1},{3,2},{4,7},{5,4},{6,5},{7,6},{8,11},{9,8},{10,9... | collective-permute-start | bytes 786440 | tf_op jit(solution)/shard_map/ppermute | solution.py:47
  203.1 3.2 %collective-permute-start.56 = (bf16[128,1024]{1,0:T(8,128)(2,1)S(1)}, bf16[128,1024]{1,0:T(8,128)(2,1)S(1)}, u32[]{:S(2)}, u32[]{:S(2)}) collective-permute-start(bf16[128,1024]{1,0:T(8,128)(2,1)S(1)} %collective-permute-done.53.refs_5_), channel_id=1, source_target_pairs={{0,3},{1,0},{2,1},{3,2},{4,7},{5,4},{6,5},{7,6},{8,11},{9,8},{10,9... | collective-permute-start | bytes 786440 | tf_op jit(solution)/shard_map/ppermute | solution.py:47
  206.4 3.4 %collective-permute-done.51.refs_4_ = bf16[128,1024]{1,0:T(8,128)(2,1)S(1)} collective-permute-done((bf16[128,1024]{1,0:T(8,128)(2,1)S(1)}, bf16[128,1024]{1,0:T(8,128)(2,1)S(1)}, u32[]{:S(2)}, u32[]{:S(2)}) %collective-permute-start.51) | collective-permute-done | bytes 262176 | tf_op jit(solution)/shard_map/ppermute | solution.py:47
  209.8 3.8 %collective-permute-start.52 = (bf16[64,1024]{1,0:T(8,128)(2,1)S(1)}, bf16[64,1024]{1,0:T(8,128)(2,1)S(1)}, u32[]{:S(2)}, u32[]{:S(2)}) collective-permute-start(bf16[64,1024]{1,0:T(8,128)(2,1)S(1)} %slice.60), channel_id=1, source_target_pairs={{0,3},{1,0},{2,1},{3,2},{4,7},{5,4},{6,5},{7,6},{8,11},{9,8},{10,9... | collective-permute-start | bytes 393224 | tf_op jit(solution)/shard_map/ppermute | solution.py:47
  215.4 3.8 %collective-permute-start.57 = (bf16[64,1024]{1,0:T(8,128)(2,1)S(1)}, bf16[64,1024]{1,0:T(8,128)(2,1)S(1)}, u32[]{:S(2)}, u32[]{:S(2)}) collective-permute-start(bf16[64,1024]{1,0:T(8,128)(2,1)S(1)} %slice.62), channel_id=1, source_target_pairs={{0,3},{1,0},{2,1},{3,2},{4,7},{5,4},{6,5},{7,6},{8,11},{9,8},{10,9... | collective-permute-start | bytes 393224 | tf_op jit(solution)/shard_map/ppermute | solution.py:47
  221.7 3.7 %collective-permute-done.55.refs_7_ = bf16[64,1024]{1,0:T(8,128)(2,1)S(1)} collective-permute-done((bf16[64,1024]{1,0:T(8,128)(2,1)S(1)}, bf16[64,1024]{1,0:T(8,128)(2,1)S(1)}, u32[]{:S(2)}, u32[]{:S(2)}) %collective-permute-start.55) | collective-permute-done | bytes 131104 | tf_op jit(solution)/shard_map/ppermute | solution.py:47
  225.4 6.2 %weight_product.1 = (f32[4,32,2048]{2,1,0:T(8,128)S(1)}, bf16[4,32,2048]{2,1,0:T(8,128)(2,1)S(1)}, bf16[4,32,2048]{2,1,0:T(8,128)(2,1)S(1)}, bf16[4,32,2048]{2,1,0:T(8,128)(2,1)S(1)}) custom-call(bf16[128,1024]{1,0:T(8,128)(2,1)S(1)} %get-tuple-element.85.refs_0_, bf16[128,1024]{1,0:T(8,128)(2,1)S(1)} %collective-permute-done.49.refs_1_, ...), custom_call_target="tpu_custom_call" | custom-call | flops 4294967296 | bytes 12582912 | tf_op jit(solution)/shard_map/weight_product/pallas_call | solution.py:199
  231.6 3.2 %collective-permute-start.60 = (bf16[4,32,2048]{2,1,0:T(8,128)(2,1)S(1)}, bf16[4,32,2048]{2,1,0:T(8,128)(2,1)S(1)}, u32[]{:S(2)}, u32[]{:S(2)}) collective-permute-start(bf16[4,32,2048]{2,1,0:T(8,128)(2,1)S(1)} %get-tuple-element.89), channel_id=1, source_target_pairs={{0,24},{4,100},{8,0},{12,108},{16,8},{20,116},{24,16},{28,124},{32... | collective-permute-start | bytes 1572872 | tf_op jit(solution)/shard_map/ppermute | solution.py:39
  234.9 12.8 %collective-permute-done.59 = bf16[4,32,2048]{2,1,0:T(8,128)(2,1)S(1)} collective-permute-done((bf16[4,32,2048]{2,1,0:T(8,128)(2,1)S(1)}, bf16[4,32,2048]{2,1,0:T(8,128)(2,1)S(1)}, u32[]{:S(2)}, u32[]{:S(2)}) %collective-permute-start.59) | collective-permute-done | bytes 524320 | tf_op jit(solution)/shard_map/ppermute | solution.py:39
  248.1 2.2 collective-permute-start.64
  251.3 4.3 %collective-permute-done.62 = bf16[32,2048]{1,0:T(8,128)(2,1)S(1)} collective-permute-done((bf16[32,2048]{1,0:T(8,128)(2,1)S(1)}, bf16[32,2048]{1,0:T(8,128)(2,1)S(1)}, u32[]{:S(2)}, u32[]{:S(2)}) %collective-permute-start.62) | collective-permute-done | bytes 131104 | tf_op jit(solution)/shard_map/ppermute | solution.py:43
  (142 shorter events, 42.1 us)
Async XLA Ops:
  0.6 9.6 %collective-permute-start.1 = (bf16[32,2048]{1,0:T(8,128)(2,1)}, bf16[32,2048]{1,0:T(8,128)(2,1)S(1)}, u32[]{:S(2)}, u32[]{:S(2)}) collective-permute-start(bf16[32,2048]{1,0:T(8,128)(2,1)} %param.8), channel_id=1, source_target_pairs={{0,16},{4,68},{8,24},{12,76},{16,0},{20,84},{24,8},{28,92},{32,48}... | collective-permute-start | bytes 393224 | tf_op jit(solution)/shard_map/ppermute | solution.py:39
  12.0 15.4 %collective-permute-start.9 = (bf16[128,2048]{1,0:T(8,128)(2,1)S(1)}, bf16[128,2048]{1,0:T(8,128)(2,1)S(1)}, u32[]{:S(2)}, u32[]{:S(2)}) collective-permute-start(bf16[128,2048]{1,0:T(8,128)(2,1)S(1)} %pad_maximum_fusion.rest_0_), channel_id=1, source_target_pairs={{0,96},{4,28},{8,104},{12,4},{16,112},{20,12},{24,120},{28,20},{32... | collective-permute-start | bytes 1572872 | tf_op jit(solution)/shard_map/ppermute | solution.py:43
  15.1 12.3 %collective-permute-start.8 = (bf16[128,2048]{1,0:T(8,128)(2,1)S(1)}, bf16[128,2048]{1,0:T(8,128)(2,1)S(1)}, u32[]{:S(2)}, u32[]{:S(2)}) collective-permute-start(bf16[128,2048]{1,0:T(8,128)(2,1)S(1)} %pad_maximum_fusion.rest_0_), channel_id=1, source_target_pairs={{0,64},{4,20},{8,72},{12,28},{16,80},{20,4},{24,88},{28,12},{32,96... | collective-permute-start | bytes 1572872 | tf_op jit(solution)/shard_map/ppermute | solution.py:43
  15.7 15.7 %collective-permute-start.7 = (bf16[128,2048]{1,0:T(8,128)(2,1)S(1)}, bf16[128,2048]{1,0:T(8,128)(2,1)S(1)}, u32[]{:S(2)}, u32[]{:S(2)}) collective-permute-start(bf16[128,2048]{1,0:T(8,128)(2,1)S(1)} %pad_maximum_fusion.rest_0_), channel_id=1, source_target_pairs={{0,32},{4,12},{8,40},{12,20},{16,48},{20,28},{24,56},{28,4},{32,64... | collective-permute-start | bytes 1572872 | tf_op jit(solution)/shard_map/ppermute | solution.py:43
  16.7 14.7 %collective-permute-start.10 = (bf16[128,2048]{1,0:T(8,128)(2,1)S(1)}, bf16[128,2048]{1,0:T(8,128)(2,1)S(1)}, u32[]{:S(2)}, u32[]{:S(2)}) collective-permute-start(bf16[128,2048]{1,0:T(8,128)(2,1)S(1)} %pad_maximum_fusion.rest_0_), channel_id=1, source_target_pairs={{0,4},{4,0},{8,12},{12,8},{16,20},{20,16},{24,28},{28,24},{32,36},... | collective-permute-start | bytes 1572872 | tf_op jit(solution)/shard_map/ppermute | solution.py:51
  38.7 9.7 %collective-permute-start.14 = (f32[256,256]{1,0:T(8,128)S(1)}, f32[256,256]{1,0:T(8,128)S(1)}, u32[]{:S(2)}, u32[]{:S(2)}) collective-permute-start(f32[256,256]{1,0:T(8,128)S(1)} %get-tuple-element.49), channel_id=1, source_target_pairs={{0,1},{1,2},{2,3},{3,0},{4,5},{5,6},{6,7},{7,4},{8,9},{9,10},{10,1... | collective-permute-start | bytes 786440 | tf_op jit(solution)/shard_map/ppermute | solution.py:47
  40.3 9.3 %collective-permute-start.17 = (f32[256,256]{1,0:T(8,128)S(1)}, f32[256,256]{1,0:T(8,128)S(1)}, u32[]{:S(2)}, u32[]{:S(2)}) collective-permute-start(f32[256,256]{1,0:T(8,128)S(1)} %get-tuple-element.53), channel_id=1, source_target_pairs={{0,3},{1,0},{2,1},{3,2},{4,7},{5,4},{6,5},{7,6},{8,11},{9,8},{10,9... | collective-permute-start | bytes 786440 | tf_op jit(solution)/shard_map/ppermute | solution.py:47
  44.7 10.5 %collective-permute-start.20 = (f32[256,256]{1,0:T(8,128)S(1)}, f32[256,256]{1,0:T(8,128)S(1)}, u32[]{:S(2)}, u32[]{:S(2)}) collective-permute-start(f32[256,256]{1,0:T(8,128)S(1)} %get-tuple-element.58), channel_id=1, source_target_pairs={{0,1},{1,2},{2,3},{3,0},{4,5},{5,6},{6,7},{7,4},{8,9},{9,10},{10,1... | collective-permute-start | bytes 786440 | tf_op jit(solution)/shard_map/ppermute | solution.py:47
  45.1 10.3 %collective-permute-start.23 = (f32[256,256]{1,0:T(8,128)S(1)}, f32[256,256]{1,0:T(8,128)S(1)}, u32[]{:S(2)}, u32[]{:S(2)}) collective-permute-start(f32[256,256]{1,0:T(8,128)S(1)} %get-tuple-element.62), channel_id=1, source_target_pairs={{0,3},{1,0},{2,1},{3,2},{4,7},{5,4},{6,5},{7,6},{8,11},{9,8},{10,9... | collective-permute-start | bytes 786440 | tf_op jit(solution)/shard_map/ppermute | solution.py:47
  48.4 12.4 %collective-permute-start.15 = (f32[256,256]{1,0:T(8,128)S(1)}, f32[256,256]{1,0:T(8,128)S(1)}, u32[]{:S(2)}, u32[]{:S(2)}) collective-permute-start(f32[256,256]{1,0:T(8,128)S(1)} %add.305), channel_id=1, source_target_pairs={{0,1},{1,2},{2,3},{3,0},{4,5},{5,6},{6,7},{7,4},{8,9},{9,10},{10,1... | collective-permute-start | bytes 786440 | tf_op jit(solution)/shard_map/ppermute | solution.py:47
  49.5 11.4 %collective-permute-start.18 = (f32[256,256]{1,0:T(8,128)S(1)}, f32[256,256]{1,0:T(8,128)S(1)}, u32[]{:S(2)}, u32[]{:S(2)}) collective-permute-start(f32[256,256]{1,0:T(8,128)S(1)} %add.308), channel_id=1, source_target_pairs={{0,3},{1,0},{2,1},{3,2},{4,7},{5,4},{6,5},{7,6},{8,11},{9,8},{10,9... | collective-permute-start | bytes 786440 | tf_op jit(solution)/shard_map/ppermute | solution.py:47
  55.3 11.2 %collective-permute-start.21 = (f32[256,256]{1,0:T(8,128)S(1)}, f32[256,256]{1,0:T(8,128)S(1)}, u32[]{:S(2)}, u32[]{:S(2)}) collective-permute-start(f32[256,256]{1,0:T(8,128)S(1)} %add.311), channel_id=1, source_target_pairs={{0,1},{1,2},{2,3},{3,0},{4,5},{5,6},{6,7},{7,4},{8,9},{9,10},{10,1... | collective-permute-start | bytes 786440 | tf_op jit(solution)/shard_map/ppermute | solution.py:47
  55.4 11.2 %collective-permute-start.24 = (f32[256,256]{1,0:T(8,128)S(1)}, f32[256,256]{1,0:T(8,128)S(1)}, u32[]{:S(2)}, u32[]{:S(2)}) collective-permute-start(f32[256,256]{1,0:T(8,128)S(1)} %add.314), channel_id=1, source_target_pairs={{0,3},{1,0},{2,1},{3,2},{4,7},{5,4},{6,5},{7,6},{8,11},{9,8},{10,9... | collective-permute-start | bytes 786440 | tf_op jit(solution)/shard_map/ppermute | solution.py:47
  60.9 11.2 %collective-permute-start.16 = (f32[256,256]{1,0:T(8,128)S(1)}, f32[256,256]{1,0:T(8,128)S(1)}, u32[]{:S(2)}, u32[]{:S(2)}) collective-permute-start(f32[256,256]{1,0:T(8,128)S(1)} %add.306), channel_id=1, source_target_pairs={{0,1},{1,2},{2,3},{3,0},{4,5},{5,6},{6,7},{7,4},{8,9},{9,10},{10,1... | collective-permute-start | bytes 786440 | tf_op jit(solution)/shard_map/ppermute | solution.py:47
  61.0 11.1 %collective-permute-start.19 = (f32[256,256]{1,0:T(8,128)S(1)}, f32[256,256]{1,0:T(8,128)S(1)}, u32[]{:S(2)}, u32[]{:S(2)}) collective-permute-start(f32[256,256]{1,0:T(8,128)S(1)} %add.309), channel_id=1, source_target_pairs={{0,3},{1,0},{2,1},{3,2},{4,7},{5,4},{6,5},{7,6},{8,11},{9,8},{10,9... | collective-permute-start | bytes 786440 | tf_op jit(solution)/shard_map/ppermute | solution.py:47
  66.5 9.9 %collective-permute-start.22 = (f32[256,256]{1,0:T(8,128)S(1)}, f32[256,256]{1,0:T(8,128)S(1)}, u32[]{:S(2)}, u32[]{:S(2)}) collective-permute-start(f32[256,256]{1,0:T(8,128)S(1)} %add.312), channel_id=1, source_target_pairs={{0,1},{1,2},{2,3},{3,0},{4,5},{5,6},{6,7},{7,4},{8,9},{9,10},{10,1... | collective-permute-start | bytes 786440 | tf_op jit(solution)/shard_map/ppermute | solution.py:47
  66.6 9.8 %collective-permute-start.25 = (f32[256,256]{1,0:T(8,128)S(1)}, f32[256,256]{1,0:T(8,128)S(1)}, u32[]{:S(2)}, u32[]{:S(2)}) collective-permute-start(f32[256,256]{1,0:T(8,128)S(1)} %add.315), channel_id=1, source_target_pairs={{0,3},{1,0},{2,1},{3,2},{4,7},{5,4},{6,5},{7,6},{8,11},{9,8},{10,9... | collective-permute-start | bytes 786440 | tf_op jit(solution)/shard_map/ppermute | solution.py:47
  76.5 15.6 %collective-permute-start.28 = (bf16[8,128,256]{2,1,0:T(8,128)(2,1)S(1)}, bf16[8,128,256]{2,1,0:T(8,128)(2,1)S(1)}, u32[]{:S(2)}, u32[]{:S(2)}) collective-permute-start(bf16[8,128,256]{2,1,0:T(8,128)(2,1)S(1)} %bitcast.19), channel_id=1, source_target_pairs={{0,24},{4,100},{8,0},{12,108},{16,8},{20,116},{24,16},{28,124},{32... | collective-permute-start | bytes 1572872 | tf_op jit(solution)/shard_map/ppermute | solution.py:39
  79.9 12.3 %collective-permute-start.27 = (bf16[8,128,256]{2,1,0:T(8,128)(2,1)S(1)}, bf16[8,128,256]{2,1,0:T(8,128)(2,1)S(1)}, u32[]{:S(2)}, u32[]{:S(2)}) collective-permute-start(bf16[8,128,256]{2,1,0:T(8,128)(2,1)S(1)} %bitcast.20), channel_id=1, source_target_pairs={{0,16},{4,68},{8,24},{12,76},{16,0},{20,84},{24,8},{28,92},{32,48}... | collective-permute-start | bytes 1572872 | tf_op jit(solution)/shard_map/ppermute | solution.py:39
  79.9 16.0 %collective-permute-start.26 = (bf16[8,128,256]{2,1,0:T(8,128)(2,1)S(1)}, bf16[8,128,256]{2,1,0:T(8,128)(2,1)S(1)}, u32[]{:S(2)}, u32[]{:S(2)}) collective-permute-start(bf16[8,128,256]{2,1,0:T(8,128)(2,1)S(1)} %bitcast.21), channel_id=1, source_target_pairs={{0,8},{4,36},{8,16},{12,44},{16,24},{20,52},{24,0},{28,60},{32,40}... | collective-permute-start | bytes 1572872 | tf_op jit(solution)/shard_map/ppermute | solution.py:39
  96.7 16.1 %collective-permute-start.29 = (bf16[8,128,256]{2,1,0:T(8,128)(2,1)S(1)}, bf16[8,128,256]{2,1,0:T(8,128)(2,1)S(1)}, u32[]{:S(2)}, u32[]{:S(2)}) collective-permute-start(bf16[8,128,256]{2,1,0:T(8,128)(2,1)S(1)} %get-tuple-element.67), channel_id=1, source_target_pairs={{0,32},{4,12},{8,40},{12,20},{16,48},{20,28},{24,56},{28,4},{32,64... | collective-permute-start | bytes 1572872 | tf_op jit(solution)/shard_map/ppermute | solution.py:43
  96.8 16.0 %collective-permute-start.30 = (bf16[8,128,256]{2,1,0:T(8,128)(2,1)S(1)}, bf16[8,128,256]{2,1,0:T(8,128)(2,1)S(1)}, u32[]{:S(2)}, u32[]{:S(2)}) collective-permute-start(bf16[8,128,256]{2,1,0:T(8,128)(2,1)S(1)} %get-tuple-element.68), channel_id=1, source_target_pairs={{0,64},{4,20},{8,72},{12,28},{16,80},{20,4},{24,88},{28,12},{32,96... | collective-permute-start | bytes 1572872 | tf_op jit(solution)/shard_map/ppermute | solution.py:43
  99.4 24.6 %collective-permute-start.33 = (bf16[8,128,256]{2,1,0:T(8,128)(2,1)S(1)}, bf16[8,128,256]{2,1,0:T(8,128)(2,1)S(1)}, u32[]{:S(2)}, u32[]{:S(2)}) collective-permute-start(bf16[8,128,256]{2,1,0:T(8,128)(2,1)S(1)} %get-tuple-element.71), channel_id=1, source_target_pairs={{0,32},{4,12},{8,40},{12,20},{16,48},{20,28},{24,56},{28,4},{32,64... | collective-permute-start | bytes 1572872 | tf_op jit(solution)/shard_map/ppermute | solution.py:43
  100.9 23.2 %collective-permute-start.35 = (bf16[8,128,256]{2,1,0:T(8,128)(2,1)S(1)}, bf16[8,128,256]{2,1,0:T(8,128)(2,1)S(1)}, u32[]{:S(2)}, u32[]{:S(2)}) collective-permute-start(bf16[8,128,256]{2,1,0:T(8,128)(2,1)S(1)} %get-tuple-element.72), channel_id=1, source_target_pairs={{0,64},{4,20},{8,72},{12,28},{16,80},{20,4},{24,88},{28,12},{32,96... | collective-permute-start | bytes 1572872 | tf_op jit(solution)/shard_map/ppermute | solution.py:43
  101.5 23.0 %collective-permute-start.37 = (bf16[8,128,256]{2,1,0:T(8,128)(2,1)S(1)}, bf16[8,128,256]{2,1,0:T(8,128)(2,1)S(1)}, u32[]{:S(2)}, u32[]{:S(2)}) collective-permute-start(bf16[8,128,256]{2,1,0:T(8,128)(2,1)S(1)} %get-tuple-element.73), channel_id=1, source_target_pairs={{0,96},{4,28},{8,104},{12,4},{16,112},{20,12},{24,120},{28,20},{32... | collective-permute-start | bytes 1572872 | tf_op jit(solution)/shard_map/ppermute | solution.py:43
  112.8 12.6 %collective-permute-start.31 = (bf16[8,128,256]{2,1,0:T(8,128)(2,1)S(1)}, bf16[8,128,256]{2,1,0:T(8,128)(2,1)S(1)}, u32[]{:S(2)}, u32[]{:S(2)}) collective-permute-start(bf16[8,128,256]{2,1,0:T(8,128)(2,1)S(1)} %get-tuple-element.69), channel_id=1, source_target_pairs={{0,96},{4,28},{8,104},{12,4},{16,112},{20,12},{24,120},{28,20},{32... | collective-permute-start | bytes 1572872 | tf_op jit(solution)/shard_map/ppermute | solution.py:43
  112.8 13.1 %collective-permute-start.32 = (bf16[8,128,256]{2,1,0:T(8,128)(2,1)S(1)}, bf16[8,128,256]{2,1,0:T(8,128)(2,1)S(1)}, u32[]{:S(2)}, u32[]{:S(2)}) collective-permute-start(bf16[8,128,256]{2,1,0:T(8,128)(2,1)S(1)} %get-tuple-element.70), channel_id=1, source_target_pairs={{0,4},{4,0},{8,12},{12,8},{16,20},{20,16},{24,28},{28,24},{32,36},... | collective-permute-start | bytes 1572872 | tf_op jit(solution)/shard_map/ppermute | solution.py:51
  125.4 93.8 %collective-permute-start.58 = (bf16[1024,2048]{1,0:T(8,128)(2,1)}, bf16[1024,2048]{1,0:T(8,128)(2,1)S(1)}, u32[]{:S(2)}, u32[]{:S(2)}) collective-permute-start(bf16[1024,2048]{1,0:T(8,128)(2,1)} %refs_10_.1), channel_id=1, source_target_pairs={{0,4},{4,0},{8,12},{12,8},{16,20},{20,16},{24,28},{28,24},{32,36},... | collective-permute-start | bytes 12582920 | tf_op jit(solution)/shard_map/ppermute | solution.py:51
  152.0 9.3 %collective-permute-start.40 = (bf16[8,128,256]{2,1,0:T(8,128)(2,1)S(1)}, bf16[8,128,256]{2,1,0:T(8,128)(2,1)S(1)}, u32[]{:S(2)}, u32[]{:S(2)}) collective-permute-start(bf16[8,128,256]{2,1,0:T(8,128)(2,1)S(1)} %get-tuple-element.78), channel_id=1, source_target_pairs={{0,96},{4,28},{8,104},{12,4},{16,112},{20,12},{24,120},{28,20},{32... | collective-permute-start | bytes 1572872 | tf_op jit(solution)/shard_map/ppermute | solution.py:43
  152.2 10.9 %collective-permute-start.42 = (bf16[8,128,256]{2,1,0:T(8,128)(2,1)S(1)}, bf16[8,128,256]{2,1,0:T(8,128)(2,1)S(1)}, u32[]{:S(2)}, u32[]{:S(2)}) collective-permute-start(bf16[8,128,256]{2,1,0:T(8,128)(2,1)S(1)} %get-tuple-element.79), channel_id=1, source_target_pairs={{0,64},{4,20},{8,72},{12,28},{16,80},{20,4},{24,88},{28,12},{32,96... | collective-permute-start | bytes 1572872 | tf_op jit(solution)/shard_map/ppermute | solution.py:43
  152.2 17.4 %collective-permute-start.44 = (bf16[8,128,256]{2,1,0:T(8,128)(2,1)S(1)}, bf16[8,128,256]{2,1,0:T(8,128)(2,1)S(1)}, u32[]{:S(2)}, u32[]{:S(2)}) collective-permute-start(bf16[8,128,256]{2,1,0:T(8,128)(2,1)S(1)} %get-tuple-element.80), channel_id=1, source_target_pairs={{0,32},{4,12},{8,40},{12,20},{16,48},{20,28},{24,56},{28,4},{32,64... | collective-permute-start | bytes 1572872 | tf_op jit(solution)/shard_map/ppermute | solution.py:43
  156.4 17.7 %collective-permute-start.45 = (bf16[8,128,256]{2,1,0:T(8,128)(2,1)S(1)}, bf16[8,128,256]{2,1,0:T(8,128)(2,1)S(1)}, u32[]{:S(2)}, u32[]{:S(2)}) collective-permute-start(bf16[8,128,256]{2,1,0:T(8,128)(2,1)S(1)} %get-tuple-element.97), channel_id=1, source_target_pairs={{0,32},{4,12},{8,40},{12,20},{16,48},{20,28},{24,56},{28,4},{32,64... | collective-permute-start | bytes 1572872 | tf_op jit(solution)/shard_map/ppermute | solution.py:43
  161.3 18.5 %collective-permute-start.43 = (bf16[8,128,256]{2,1,0:T(8,128)(2,1)S(1)}, bf16[8,128,256]{2,1,0:T(8,128)(2,1)S(1)}, u32[]{:S(2)}, u32[]{:S(2)}) collective-permute-start(bf16[8,128,256]{2,1,0:T(8,128)(2,1)S(1)} %get-tuple-element.98), channel_id=1, source_target_pairs={{0,64},{4,20},{8,72},{12,28},{16,80},{20,4},{24,88},{28,12},{32,96... | collective-permute-start | bytes 1572872 | tf_op jit(solution)/shard_map/ppermute | solution.py:43
  163.0 16.8 %collective-permute-start.41 = (bf16[8,128,256]{2,1,0:T(8,128)(2,1)S(1)}, bf16[8,128,256]{2,1,0:T(8,128)(2,1)S(1)}, u32[]{:S(2)}, u32[]{:S(2)}) collective-permute-start(bf16[8,128,256]{2,1,0:T(8,128)(2,1)S(1)} %get-tuple-element.99), channel_id=1, source_target_pairs={{0,96},{4,28},{8,104},{12,4},{16,112},{20,12},{24,120},{28,20},{32... | collective-permute-start | bytes 1572872 | tf_op jit(solution)/shard_map/ppermute | solution.py:43
  182.3 9.3 %collective-permute-start.46 = (bf16[8,128,256]{2,1,0:T(8,128)(2,1)S(1)}, bf16[8,128,256]{2,1,0:T(8,128)(2,1)S(1)}, u32[]{:S(2)}, u32[]{:S(2)}) collective-permute-start(bf16[8,128,256]{2,1,0:T(8,128)(2,1)S(1)} %get-tuple-element.82), channel_id=1, source_target_pairs={{0,24},{4,100},{8,0},{12,108},{16,8},{20,116},{24,16},{28,124},{32... | collective-permute-start | bytes 1572872 | tf_op jit(solution)/shard_map/ppermute | solution.py:39
  183.3 10.8 %collective-permute-start.47 = (bf16[8,128,256]{2,1,0:T(8,128)(2,1)S(1)}, bf16[8,128,256]{2,1,0:T(8,128)(2,1)S(1)}, u32[]{:S(2)}, u32[]{:S(2)}) collective-permute-start(bf16[8,128,256]{2,1,0:T(8,128)(2,1)S(1)} %get-tuple-element.83), channel_id=1, source_target_pairs={{0,16},{4,68},{8,24},{12,76},{16,0},{20,84},{24,8},{28,92},{32,48}... | collective-permute-start | bytes 1572872 | tf_op jit(solution)/shard_map/ppermute | solution.py:39
  183.3 16.3 %collective-permute-start.48 = (bf16[8,128,256]{2,1,0:T(8,128)(2,1)S(1)}, bf16[8,128,256]{2,1,0:T(8,128)(2,1)S(1)}, u32[]{:S(2)}, u32[]{:S(2)}) collective-permute-start(bf16[8,128,256]{2,1,0:T(8,128)(2,1)S(1)} %get-tuple-element.84), channel_id=1, source_target_pairs={{0,8},{4,36},{8,16},{12,44},{16,24},{20,52},{24,0},{28,60},{32,40}... | collective-permute-start | bytes 1572872 | tf_op jit(solution)/shard_map/ppermute | solution.py:39
  200.1 9.6 %collective-permute-start.51 = (bf16[128,1024]{1,0:T(8,128)(2,1)S(1)}, bf16[128,1024]{1,0:T(8,128)(2,1)S(1)}, u32[]{:S(2)}, u32[]{:S(2)}) collective-permute-start(bf16[128,1024]{1,0:T(8,128)(2,1)S(1)} %get-tuple-element.85.refs_0_), channel_id=1, source_target_pairs={{0,3},{1,0},{2,1},{3,2},{4,7},{5,4},{6,5},{7,6},{8,11},{9,8},{10,9... | collective-permute-start | bytes 786440 | tf_op jit(solution)/shard_map/ppermute | solution.py:47
  203.1 10.4 %collective-permute-start.49 = (bf16[128,1024]{1,0:T(8,128)(2,1)S(1)}, bf16[128,1024]{1,0:T(8,128)(2,1)S(1)}, u32[]{:S(2)}, u32[]{:S(2)}) collective-permute-start(bf16[128,1024]{1,0:T(8,128)(2,1)S(1)} %get-tuple-element.85.refs_0_), channel_id=1, source_target_pairs={{0,1},{1,2},{2,3},{3,0},{4,5},{5,6},{6,7},{7,4},{8,9},{9,10},{10,1... | collective-permute-start | bytes 786440 | tf_op jit(solution)/shard_map/ppermute | solution.py:47
  203.1 12.2 %collective-permute-start.56 = (bf16[128,1024]{1,0:T(8,128)(2,1)S(1)}, bf16[128,1024]{1,0:T(8,128)(2,1)S(1)}, u32[]{:S(2)}, u32[]{:S(2)}) collective-permute-start(bf16[128,1024]{1,0:T(8,128)(2,1)S(1)} %collective-permute-done.53.refs_5_), channel_id=1, source_target_pairs={{0,3},{1,0},{2,1},{3,2},{4,7},{5,4},{6,5},{7,6},{8,11},{9,8},{10,9... | collective-permute-start | bytes 786440 | tf_op jit(solution)/shard_map/ppermute | solution.py:47
  206.3 12.8 %collective-permute-start.54 = (bf16[128,1024]{1,0:T(8,128)(2,1)S(1)}, bf16[128,1024]{1,0:T(8,128)(2,1)S(1)}, u32[]{:S(2)}, u32[]{:S(2)}) collective-permute-start(bf16[128,1024]{1,0:T(8,128)(2,1)S(1)} %collective-permute-done.53.refs_5_), channel_id=1, source_target_pairs={{0,1},{1,2},{2,3},{3,0},{4,5},{5,6},{6,7},{7,4},{8,9},{9,10},{10,1... | collective-permute-start | bytes 786440 | tf_op jit(solution)/shard_map/ppermute | solution.py:47
  209.8 9.5 %collective-permute-start.52 = (bf16[64,1024]{1,0:T(8,128)(2,1)S(1)}, bf16[64,1024]{1,0:T(8,128)(2,1)S(1)}, u32[]{:S(2)}, u32[]{:S(2)}) collective-permute-start(bf16[64,1024]{1,0:T(8,128)(2,1)S(1)} %slice.60), channel_id=1, source_target_pairs={{0,3},{1,0},{2,1},{3,2},{4,7},{5,4},{6,5},{7,6},{8,11},{9,8},{10,9... | collective-permute-start | bytes 393224 | tf_op jit(solution)/shard_map/ppermute | solution.py:47
  213.5 7.6 %collective-permute-start.50 = (bf16[64,1024]{1,0:T(8,128)(2,1)S(1)}, bf16[64,1024]{1,0:T(8,128)(2,1)S(1)}, u32[]{:S(2)}, u32[]{:S(2)}) collective-permute-start(bf16[64,1024]{1,0:T(8,128)(2,1)S(1)} %slice.59), channel_id=1, source_target_pairs={{0,1},{1,2},{2,3},{3,0},{4,5},{5,6},{6,7},{7,4},{8,9},{9,10},{10,1... | collective-permute-start | bytes 393224 | tf_op jit(solution)/shard_map/ppermute | solution.py:47
  231.6 16.1 %collective-permute-start.59 = (bf16[4,32,2048]{2,1,0:T(8,128)(2,1)S(1)}, bf16[4,32,2048]{2,1,0:T(8,128)(2,1)S(1)}, u32[]{:S(2)}, u32[]{:S(2)}) collective-permute-start(bf16[4,32,2048]{2,1,0:T(8,128)(2,1)S(1)} %get-tuple-element.88), channel_id=1, source_target_pairs={{0,8},{4,36},{8,16},{12,44},{16,24},{20,52},{24,0},{28,60},{32,40}... | collective-permute-start | bytes 1572872 | tf_op jit(solution)/shard_map/ppermute | solution.py:39
  231.6 16.0 %collective-permute-start.60 = (bf16[4,32,2048]{2,1,0:T(8,128)(2,1)S(1)}, bf16[4,32,2048]{2,1,0:T(8,128)(2,1)S(1)}, u32[]{:S(2)}, u32[]{:S(2)}) collective-permute-start(bf16[4,32,2048]{2,1,0:T(8,128)(2,1)S(1)} %get-tuple-element.89), channel_id=1, source_target_pairs={{0,24},{4,100},{8,0},{12,108},{16,8},{20,116},{24,16},{28,124},{32... | collective-permute-start | bytes 1572872 | tf_op jit(solution)/shard_map/ppermute | solution.py:39
  234.9 12.8 %collective-permute-start.61 = (bf16[4,32,2048]{2,1,0:T(8,128)(2,1)S(1)}, bf16[4,32,2048]{2,1,0:T(8,128)(2,1)S(1)}, u32[]{:S(2)}, u32[]{:S(2)}) collective-permute-start(bf16[4,32,2048]{2,1,0:T(8,128)(2,1)S(1)} %get-tuple-element.90), channel_id=1, source_target_pairs={{0,16},{4,68},{8,24},{12,76},{16,0},{20,84},{24,8},{28,92},{32,48}... | collective-permute-start | bytes 1572872 | tf_op jit(solution)/shard_map/ppermute | solution.py:39
  248.0 7.7 %collective-permute-start.62 = (bf16[32,2048]{1,0:T(8,128)(2,1)S(1)}, bf16[32,2048]{1,0:T(8,128)(2,1)S(1)}, u32[]{:S(2)}, u32[]{:S(2)}) collective-permute-start(bf16[32,2048]{1,0:T(8,128)(2,1)S(1)} %get-tuple-element.101), channel_id=1, source_target_pairs={{0,32},{4,12},{8,40},{12,20},{16,48},{20,28},{24,56},{28,4},{32,64... | collective-permute-start | bytes 393224 | tf_op jit(solution)/shard_map/ppermute | solution.py:43
  248.1 7.6 %collective-permute-start.64 = (bf16[32,2048]{1,0:T(8,128)(2,1)S(1)}, bf16[32,2048]{1,0:T(8,128)(2,1)S(1)}, u32[]{:S(2)}, u32[]{:S(2)}) collective-permute-start(bf16[32,2048]{1,0:T(8,128)(2,1)S(1)} %get-tuple-element.102), channel_id=1, source_target_pairs={{0,64},{4,20},{8,72},{12,28},{16,80},{20,4},{24,88},{28,12},{32,96... | collective-permute-start | bytes 393224 | tf_op jit(solution)/shard_map/ppermute | solution.py:43
  (23 other events, 278.1 us)

commit v3 on v2

--- a/solution.py
+++ b/solution.py
@@ -15,6 +15,7 @@
 NT = (((1,), (1,)), ((), ()))
 TN = (((0,), (0,)), ((), ()))
 SIDE = 4
+SENT_FIRST = (3, 1)
 OUT_ROWS = 32
 
 
@@ -81,6 +82,13 @@
 
 def ring_mod(n):
     return lax.rem(n + 2 * SIDE, SIDE)
+
+
+def pack(keys, values, out_ref):
+    high = keys.astype(BF)
+    out_ref[:, :HD] = high
+    out_ref[:, HD : 2 * HD] = (keys - high.astype(F32)).astype(BF)
+    out_ref[:, 2 * HD :] = values.astype(BF)
 
 
 def gather_rows(pieces, weights):
@@ -120,7 +128,11 @@
         @pl.when(step == i)
         def _():
             for j in range(SIDE):
-                outs[i * SIDE + j][...] = product[:, j * head : (j + 1) * head]
+                part = product[:, j * head : (j + 1) * head]
+                if j == SENT_FIRST[i]:
+                    pack(part[:, :HD], part[:, HD:], outs[i * SIDE + j])
+                else:
+                    outs[i * SIDE + j][...] = part
 
 
 def project(hidden, pieces, first):
@@ -130,6 +142,8 @@
     head = columns // SIDE
     whole = pl.BlockSpec(memory_space=pltpu.VMEM)
     outs = [jax.ShapeDtypeStruct((block, head), F32)] * (2 * SIDE)
+    for i in range(2):
+        outs[i * SIDE + SENT_FIRST[i]] = jax.ShapeDtypeStruct((block, 3 * HD), BF)
     if first == 0:
         outs += [jax.ShapeDtypeStruct((columns, depth), BF)]
     return pl.pallas_call(
@@ -138,7 +152,7 @@
         grid=(2,),
         in_specs=[whole] * (1 + len(pieces)),
         out_specs=[whole] * len(outs),
-        compiler_params=pltpu.CompilerParams(vmem_limit_bytes=20 * 2**20),
+        compiler_params=pltpu.CompilerParams(vmem_limit_bytes=10 * 2**20),
         cost_estimate=pl.CostEstimate(
             flops=rows * columns * depth,
             bytes_accessed=(rows + 2 * columns) * depth + 2 * rows * columns,
@@ -148,12 +162,43 @@
     )(hidden, *pieces)
 
 
+def relay_kernel(got_ref, part_ref, out_ref):
+    keys = (part_ref[:, :HD] + got_ref[:, :HD].astype(F32)) + got_ref[:, HD : 2 * HD].astype(F32)
+    pack(keys, part_ref[:, HD:] + got_ref[:, 2 * HD :].astype(F32), out_ref)
+
+
+def finish_kernel(*refs):
+    n = (len(refs) - 1) // 2
+    out_ref = refs[-1]
+    for i in range(n):
+        got_ref, part_ref = refs[i], refs[n + i]
+        rows = slice(i * part_ref.shape[0], (i + 1) * part_ref.shape[0])
+        keys = part_ref[:, :HD] + got_ref[:, :HD].astype(F32)
+        out_ref[rows, :HD] = (keys + got_ref[:, HD : 2 * HD].astype(F32)).astype(BF)
+        out_ref[rows, HD:] = (part_ref[:, HD:] + got_ref[:, 2 * HD :].astype(F32)).astype(BF)
+
+
+def small_kernel(kernel, name, shape, *args):
+    whole = pl.BlockSpec(memory_space=pltpu.VMEM)
+    return pl.pallas_call(
+        kernel,
+        out_shape=jax.ShapeDtypeStruct(shape, BF),
+        in_specs=[whole] * len(args),
+        out_specs=whole,
+        compiler_params=pltpu.CompilerParams(vmem_limit_bytes=2 * 2**20),
+        cost_estimate=pl.CostEstimate(
+            flops=4 * math.prod(shape), bytes_accessed=8 * math.prod(shape), transcendentals=0
+        ),
+        name=name,
+    )(*args)
+
+
 def reduce_heads(parts):
     down, up = parts[3], parts[SIDE + 1]
-    for first, second in ((2, 2), (1, 3), (0, 0)):
-        down = send_tp(down, 1) + parts[first]
-        up = send_tp(up, -1) + parts[SIDE + second]
-    return jnp.concatenate([down.astype(BF), up.astype(BF)], axis=0)
+    for first, second in ((2, 2), (1, 3)):
+        down = small_kernel(relay_kernel, "relay", down.shape, send_tp(down, 1), parts[first])
+        up = small_kernel(relay_kernel, "relay", up.shape, send_tp(up, -1), parts[SIDE + second])
+    return [send_tp(down, 1), send_tp(up, -1)], [parts[0], parts[SIDE]]
 
 
 def weight_kernel(*refs):
@@ -207,7 +252,7 @@
             pltpu.VMEM((heads_rows, 2 * rows), BF),
             pltpu.VMEM((heads_rows, tile), F32),
         ],
-        compiler_params=pltpu.CompilerParams(vmem_limit_bytes=40 * 2**20),
+        compiler_params=pltpu.CompilerParams(vmem_limit_bytes=16 * 2**20),
         cost_estimate=pl.CostEstimate(
             flops=4 * heads_rows * rows * depth,
             bytes_accessed=4 * rows * depth + 4 * heads_rows * depth,
@@ -333,7 +378,7 @@
                 pltpu.VMEM((keys, width), BF),
             ],
         ),
-        compiler_params=pltpu.CompilerParams(vmem_limit_bytes=44 * 2**20),
+        compiler_params=pltpu.CompilerParams(vmem_limit_bytes=26 * 2**20),
         cost_estimate=pl.CostEstimate(
             flops=10 * n_query * keys * qlen * width,
             bytes_accessed=8 * rows * width + 4 * n_query * keys * local,
@@ -363,7 +408,7 @@
             in_specs=[whole] * SIDE,
             out_specs=[whole] * (2 * SIDE),
         ),
-        compiler_params=pltpu.CompilerParams(vmem_limit_bytes=16 * 2**20),
+        compiler_params=pltpu.CompilerParams(vmem_limit_bytes=2 * 2**20),
         cost_estimate=pl.CostEstimate(
             flops=0, bytes_accessed=16 * SIDE * n * PLEN * HD, transcendentals=0
         ),
@@ -403,7 +448,7 @@
             out_specs=[whole] * SIDE,
             scratch_shapes=[pltpu.VMEM((SIDE,) + shape, F32)],
         ),
-        compiler_params=pltpu.CompilerParams(vmem_limit_bytes=32 * 2**20),
+        compiler_params=pltpu.CompilerParams(vmem_limit_bytes=9 * 2**20),
         cost_estimate=pl.CostEstimate(
             flops=8 * parts[0].size, bytes_accessed=32 * parts[0].size, transcendentals=0
         ),
@@ -434,7 +479,7 @@
         in_specs=[whole] * SIDE,
         out_specs=(whole, whole),
         scratch_shapes=[pltpu.VMEM((width, passages * length), BF)],
-        compiler_params=pltpu.CompilerParams(vmem_limit_bytes=32 * 2**20),
+        compiler_params=pltpu.CompilerParams(vmem_limit_bytes=5 * 2**20),
         cost_estimate=pl.CostEstimate(
             flops=4 * parts[0].size, bytes_accessed=12 * parts[0].size, transcendentals=0
         ),
@@ -512,7 +557,17 @@
 
     *lower, weights = project(passage_hidden, weights, 0)
     upper = project(passage_hidden, [weights], 2)
-    own = jnp.concatenate([reduce_heads(lower), reduce_heads(upper)], axis=0)
+    lower_got, lower_own = reduce_heads(lower)
+    upper_got, upper_own = reduce_heads(upper)
+    own = small_kernel(
+        finish_kernel,
+        "finish",
+        (rows_local, local_width),
+        *lower_got,
+        *upper_got,
+        *lower_own,
+        *upper_own,
+    )
     own = own.reshape(passages_here, PLEN, local_width)
     wanted = pick(served, ring_gather(own, send_first))
     same, other = wanted[::2], wanted[1::2]
@@ -533,9 +588,9 @@
     )
     mine, theirs = grads[:SIDE], swap_cores(grads[SIDE])
     theirs = [theirs[k * half : (k + 1) * half] for k in range(SIDE)]
-    parts = [mine[0], theirs[0]]
-    for k in range(1, SIDE):
-        parts += [send_second(mine[k], -k), send_second(theirs[k], -k)]
+    mine[1:] = [send_second(mine[k], -k) for k in range(1, SIDE)]
+    theirs[1:] = [send_second(theirs[k], -k) for k in range(1, SIDE)]
+    parts = [blocks for pair in zip(mine, theirs) for blocks in pair]
     sums = add_blocks(served, parts, passages_here)
     mine, theirs = add_owners([sums[0]] + [send_first(sums[j], -j) for j in range(1, SIDE)])
     mine_heads = ring_gather_halves(mine, send_tp)

time: 257 us -> 250 us (0.973)
  waiting for transfers between devices: 128 us -> 121 us
    ppermute x20, waiting for transfers between devices: 25.7 us -> 18.5 us  [send_tp(): return lax.ppermute(x, 'tp', [(i, (i + k) % SIDE) for i in range(SIDE)])]
  transfers between devices with their start and end apart: 65 -> 65, of which waited for: 36 -> 35; matrix products, arithmetic and copies ran while one was open for 2% -> 2% of each run, Pallas kernels for 11% -> 11%
where the time goes in v3:
time: 250 us
  waiting for transfers between devices  121 us (48%)
  starting transfers between devices  80 us (32%)
  Pallas kernels  38 us (15%)
  local copies, waits for them, and re-layouts  6.04 us (2%)
  other arithmetic  3.98 us (2%)
    ppermute x21, waiting for transfers between devices, send_second(): return lax.ppermute(x, 'pas', ring_pairs(1, k))  62.1 us
    ppermute x20, starting transfers between devices, send_tp(): return lax.ppermute(x, 'tp', [(i, (i + k) % SIDE) for i in range(SIDE)])  34.7 us
    ppermute x12, waiting for transfers between devices, send_first(): return lax.ppermute(x, 'pas', ring_pairs(0, k))  32.9 us
    ppermute x21, starting transfers between devices, send_second(): return lax.ppermute(x, 'pas', ring_pairs(1, k))  26.3 us
    pallas_call x1, Pallas kernels, attention(): pl.pallas_call(functools.partial(attention_kernel, len(sources), len(out_...  21.7 us
    ppermute x20, waiting for transfers between devices, send_tp(): return lax.ppermute(x, 'tp', [(i, (i + k) % SIDE) for i in range(SIDE)])  18.5 us
    ppermute x12, starting transfers between devices, send_first(): return lax.ppermute(x, 'pas', ring_pairs(0, k))  17.1 us
    ppermute x12, waiting for transfers between devices, swap_cores(): return lax.ppermute(x, 'pas', [(i, i ^ 1) for i in range(2 * SIDE * SIDE)])  7.31 us
  transfers between devices with their start and end apart: 65, of which 35 were waited for; matrix products, arithmetic and copies ran while one was open for 2% of the time, Pallas kernels for 11%

profile of v3, /device:TPU:0, one launch (start us, length us, event | category | flops | bytes accessed | tf_op | source)
XLA Modules:
  0.0 249.9 jit_solution(15249764802948492156)
XLA Ops:
  0.6 4.0 %collective-permute-start.1 = (bf16[32,2048]{1,0:T(8,128)(2,1)}, bf16[32,2048]{1,0:T(8,128)(2,1)S(1)}, u32[]{:S(2)}, u32[]{:S(2)}) collective-permute-start(bf16[32,2048]{1,0:T(8,128)(2,1)} %param.8), channel_id=1, source_target_pairs={{0,16},{4,68},{8,24},{12,76},{16,0},{20,84},{24,8},{28,92},{32,48}... | collective-permute-start | bytes 393224 | tf_op jit(solution)/shard_map/ppermute | solution.py:40
  5.7 2.2 collective-permute-start.2
  12.0 3.1 %collective-permute-start.9 = (bf16[128,2048]{1,0:T(8,128)(2,1)S(1)}, bf16[128,2048]{1,0:T(8,128)(2,1)S(1)}, u32[]{:S(2)}, u32[]{:S(2)}) collective-permute-start(bf16[128,2048]{1,0:T(8,128)(2,1)S(1)} %pad_maximum_fusion.rest_0_), channel_id=1, source_target_pairs={{0,96},{4,28},{8,104},{12,4},{16,112},{20,12},{24,120},{28,20},{32... | collective-permute-start | bytes 1572872 | tf_op jit(solution)/shard_map/ppermute | solution.py:44
  16.7 10.7 %collective-permute-done.9.rest_3_ = bf16[128,2048]{1,0:T(8,128)(2,1)S(1)} collective-permute-done((bf16[128,2048]{1,0:T(8,128)(2,1)S(1)}, bf16[128,2048]{1,0:T(8,128)(2,1)S(1)}, u32[]{:S(2)}, u32[]{:S(2)}) %collective-permute-start.9) | collective-permute-done | bytes 524320 | tf_op jit(solution)/shard_map/ppermute | solution.py:44
  27.9 3.5 %collective-permute-done.7.rest_1_ = bf16[128,2048]{1,0:T(8,128)(2,1)S(1)} collective-permute-done((bf16[128,2048]{1,0:T(8,128)(2,1)S(1)}, bf16[128,2048]{1,0:T(8,128)(2,1)S(1)}, u32[]{:S(2)}, u32[]{:S(2)}) %collective-permute-start.7) | collective-permute-done | bytes 524320 | tf_op jit(solution)/shard_map/ppermute | solution.py:44
  31.4 1.9 collective-permute-done.11.rest_5_
  33.3 2.2 copy-done
  35.5 3.2 %project.2 = (f32[256,256]{1,0:T(8,128)S(1)}, f32[256,256]{1,0:T(8,128)S(1)}, f32[256,256]{1,0:T(8,128)S(1)}, bf16[256,384]{1,0:T(8,128)(2,1)S(1)}, f32[256,256]...) custom-call(bf16[1024,2048]{1,0:T(8,128)(2,1)S(1)} %copy-done, ...), custom_call_target="tpu_custom_call" | custom-call | flops 2147483648 | bytes 8388608 | tf_op jit(solution)/shard_map/project/pallas_call | solution.py:149
  42.0 2.7 %project.3 = (f32[256,256]{1,0:T(8,128)S(1)}, f32[256,256]{1,0:T(8,128)S(1)}, f32[256,256]{1,0:T(8,128)S(1)}, bf16[256,384]{1,0:T(8,128)(2,1)S(1)}, f32[256,256]...) custom-call(bf16[1024,2048]{1,0:T(8,128)(2,1)S(1)} %copy-done, ...), custom_call_target="tpu_custom_call" | custom-call | flops 2147483648 | bytes 8388608 | tf_op jit(solution)/shard_map/project/pallas_call | solution.py:149
  45.1 3.0 %collective-permute-start.23 = (bf16[256,384]{1,0:T(8,128)(2,1)S(1)}, bf16[256,384]{1,0:T(8,128)(2,1)S(1)}, u32[]{:S(2)}, u32[]{:S(2)}) collective-permute-start(bf16[256,384]{1,0:T(8,128)(2,1)S(1)} %get-tuple-element.59), channel_id=1, source_target_pairs={{0,3},{1,0},{2,1},{3,2},{4,7},{5,4},{6,5},{7,6},{8,11},{9,8},{10,9... | collective-permute-start | bytes 589832 | tf_op jit(solution)/shard_map/ppermute | solution.py:48
  48.3 3.3 %collective-permute-start.18 = (bf16[256,384]{1,0:T(8,128)(2,1)S(1)}, bf16[256,384]{1,0:T(8,128)(2,1)S(1)}, u32[]{:S(2)}, u32[]{:S(2)}) collective-permute-start(bf16[256,384]{1,0:T(8,128)(2,1)S(1)} %relay.10), channel_id=1, source_target_pairs={{0,3},{1,0},{2,1},{3,2},{4,7},{5,4},{6,5},{7,6},{8,11},{9,8},{10,9... | collective-permute-start | bytes 589832 | tf_op jit(solution)/shard_map/ppermute | solution.py:48
  51.6 2.2 collective-permute-done.20.got_ref
  54.0 3.3 %collective-permute-start.24 = (bf16[256,384]{1,0:T(8,128)(2,1)S(1)}, bf16[256,384]{1,0:T(8,128)(2,1)S(1)}, u32[]{:S(2)}, u32[]{:S(2)}) collective-permute-start(bf16[256,384]{1,0:T(8,128)(2,1)S(1)} %relay.14), channel_id=1, source_target_pairs={{0,3},{1,0},{2,1},{3,2},{4,7},{5,4},{6,5},{7,6},{8,11},{9,8},{10,9... | collective-permute-start | bytes 589832 | tf_op jit(solution)/shard_map/ppermute | solution.py:48
  58.2 3.3 %collective-permute-start.19 = (bf16[256,384]{1,0:T(8,128)(2,1)S(1)}, bf16[256,384]{1,0:T(8,128)(2,1)S(1)}, u32[]{:S(2)}, u32[]{:S(2)}) collective-permute-start(bf16[256,384]{1,0:T(8,128)(2,1)S(1)} %relay.11), channel_id=1, source_target_pairs={{0,3},{1,0},{2,1},{3,2},{4,7},{5,4},{6,5},{7,6},{8,11},{9,8},{10,9... | collective-permute-start | bytes 589832 | tf_op jit(solution)/shard_map/ppermute | solution.py:48
  62.6 3.5 %collective-permute-start.25 = (bf16[256,384]{1,0:T(8,128)(2,1)S(1)}, bf16[256,384]{1,0:T(8,128)(2,1)S(1)}, u32[]{:S(2)}, u32[]{:S(2)}) collective-permute-start(bf16[256,384]{1,0:T(8,128)(2,1)S(1)} %relay.15), channel_id=1, source_target_pairs={{0,3},{1,0},{2,1},{3,2},{4,7},{5,4},{6,5},{7,6},{8,11},{9,8},{10,9... | collective-permute-start | bytes 589832 | tf_op jit(solution)/shard_map/ppermute | solution.py:48
  67.2 2.3 collective-permute-done.22.refs_2_
  69.6 3.3 %collective-permute-start.28 = (bf16[8,128,256]{2,1,0:T(8,128)(2,1)S(1)}, bf16[8,128,256]{2,1,0:T(8,128)(2,1)S(1)}, u32[]{:S(2)}, u32[]{:S(2)}) collective-permute-start(bf16[8,128,256]{2,1,0:T(8,128)(2,1)S(1)} %bitcast.19), channel_id=1, source_target_pairs={{0,24},{4,100},{8,0},{12,108},{16,8},{20,116},{24,16},{28,124},{32... | collective-permute-start | bytes 1572872 | tf_op jit(solution)/shard_map/ppermute | solution.py:40
  75.3 2.7 %collective-permute-start.5 = (s32[64,2]{0,1:T(2,128)S(1)}, s32[64,2]{0,1:T(2,128)S(1)}, u32[]{:S(2)}, u32[]{:S(2)}) collective-permute-start(s32[64,2]{0,1:T(2,128)S(1)} %pad_add_fusion.1), channel_id=1, source_target_pairs={{0,64},{4,20},{8,72},{12,28},{16,80},{20,4},{24,88},{28,12},{32,96... | collective-permute-start | bytes 1544 | tf_op jit(solution)/shard_map/ppermute | solution.py:44
  78.0 2.1 collective-permute-done.6
  80.5 3.2 %collective-permute-done.4 = s32[64,2]{0,1:T(2,128)S(1)} collective-permute-done((s32[64,2]{0,1:T(2,128)S(1)}, s32[64,2]{0,1:T(2,128)S(1)}, u32[]{:S(2)}, u32[]{:S(2)}) %collective-permute-start.4) | collective-permute-done | bytes 544 | tf_op jit(solution)/shard_map/ppermute | solution.py:44
  85.2 3.7 %collective-permute-done.26.rest_1_ = bf16[8,128,256]{2,1,0:T(8,128)(2,1)S(1)} collective-permute-done((bf16[8,128,256]{2,1,0:T(8,128)(2,1)S(1)}, bf16[8,128,256]{2,1,0:T(8,128)(2,1)S(1)}, u32[]{:S(2)}, u32[]{:S(2)}) %collective-permute-start.26) | collective-permute-done | bytes 524320 | tf_op jit(solution)/shard_map/ppermute | solution.py:40
  89.8 2.7 %collective-permute-start.30 = (bf16[8,128,256]{2,1,0:T(8,128)(2,1)S(1)}, bf16[8,128,256]{2,1,0:T(8,128)(2,1)S(1)}, u32[]{:S(2)}, u32[]{:S(2)}) collective-permute-start(bf16[8,128,256]{2,1,0:T(8,128)(2,1)S(1)} %get-tuple-element.68), channel_id=1, source_target_pairs={{0,64},{4,20},{8,72},{12,28},{16,80},{20,4},{24,88},{28,12},{32,96... | collective-permute-start | bytes 1572872 | tf_op jit(solution)/shard_map/ppermute | solution.py:44
  94.5 2.0 collective-permute-start.37
  96.6 9.2 %collective-permute-done.29.rest_1_ = bf16[8,128,256]{2,1,0:T(8,128)(2,1)S(1)} collective-permute-done((bf16[8,128,256]{2,1,0:T(8,128)(2,1)S(1)}, bf16[8,128,256]{2,1,0:T(8,128)(2,1)S(1)}, u32[]{:S(2)}, u32[]{:S(2)}) %collective-permute-start.29) | collective-permute-done | bytes 524320 | tf_op jit(solution)/shard_map/ppermute | solution.py:44
  105.8 11.2 %collective-permute-done.33 = bf16[8,128,256]{2,1,0:T(8,128)(2,1)S(1)} collective-permute-done((bf16[8,128,256]{2,1,0:T(8,128)(2,1)S(1)}, bf16[8,128,256]{2,1,0:T(8,128)(2,1)S(1)}, u32[]{:S(2)}, u32[]{:S(2)}) %collective-permute-start.33) | collective-permute-done | bytes 524320 | tf_op jit(solution)/shard_map/ppermute | solution.py:44
  122.4 21.7 %attention.1 = (bf16[512,1024]{1,0:T(8,128)(2,1)}, bf16[512,256]{1,0:T(8,128)(2,1)}, bf16[8,128,256]{2,1,0:T(8,128)(2,1)S(1)}, bf16[8,128,256]{2,1,0:T(8,128)(2,...) custom-call(s32[64]{0:T(128)S(1)} %select_reduce_fusion.taken_by, ...), custom_call_target="tpu_custom_call" | custom-call | flops 6039797760 | bytes 8912896 | tf_op jit(solution)/shard_map/attention/pallas_call | solution.py:360
  144.3 2.0 collective-permute-start.44
  146.3 2.0 collective-permute-done.39
  148.6 4.8 %collective-permute-done.40.rest_2_ = bf16[8,128,256]{2,1,0:T(8,128)(2,1)S(1)} collective-permute-done((bf16[8,128,256]{2,1,0:T(8,128)(2,1)S(1)}, bf16[8,128,256]{2,1,0:T(8,128)(2,1)S(1)}, u32[]{:S(2)}, u32[]{:S(2)}) %collective-permute-start.40) | collective-permute-done | bytes 524320 | tf_op jit(solution)/shard_map/ppermute | solution.py:44
  155.1 6.7 %collective-permute-start.41 = (bf16[8,128,256]{2,1,0:T(8,128)(2,1)S(1)}, bf16[8,128,256]{2,1,0:T(8,128)(2,1)S(1)}, u32[]{:S(2)}, u32[]{:S(2)}) collective-permute-start(bf16[8,128,256]{2,1,0:T(8,128)(2,1)S(1)} %get-tuple-element.99), channel_id=1, source_target_pairs={{0,96},{4,28},{8,104},{12,4},{16,112},{20,12},{24,120},{28,20},{32... | collective-permute-start | bytes 1572872 | tf_op jit(solution)/shard_map/ppermute | solution.py:44
  161.8 4.4 %collective-permute-done.45.rest_7_ = bf16[8,128,256]{2,1,0:T(8,128)(2,1)S(1)} collective-permute-done((bf16[8,128,256]{2,1,0:T(8,128)(2,1)S(1)}, bf16[8,128,256]{2,1,0:T(8,128)(2,1)S(1)}, u32[]{:S(2)}, u32[]{:S(2)}) %collective-permute-start.45) | collective-permute-done | bytes 524320 | tf_op jit(solution)/shard_map/ppermute | solution.py:44
  166.2 5.7 %collective-permute-done.43.rest_5_ = bf16[8,128,256]{2,1,0:T(8,128)(2,1)S(1)} collective-permute-done((bf16[8,128,256]{2,1,0:T(8,128)(2,1)S(1)}, bf16[8,128,256]{2,1,0:T(8,128)(2,1)S(1)}, u32[]{:S(2)}, u32[]{:S(2)}) %collective-permute-start.43) | collective-permute-done | bytes 524320 | tf_op jit(solution)/shard_map/ppermute | solution.py:44
  171.9 2.4 add_blocks.1
  176.4 7.2 %collective-permute-done.46.left_ref = bf16[8,128,256]{2,1,0:T(8,128)(2,1)S(1)} collective-permute-done((bf16[8,128,256]{2,1,0:T(8,128)(2,1)S(1)}, bf16[8,128,256]{2,1,0:T(8,128)(2,1)S(1)}, u32[]{:S(2)}, u32[]{:S(2)}) %collective-permute-start.46) | collective-permute-done | bytes 524320 | tf_op jit(solution)/shard_map/ppermute | solution.py:40
  183.5 2.5 collective-permute-done.47.far_ref
  186.0 5.5 %collective-permute-done.48.right_ref = bf16[8,128,256]{2,1,0:T(8,128)(2,1)S(1)} collective-permute-done((bf16[8,128,256]{2,1,0:T(8,128)(2,1)S(1)}, bf16[8,128,256]{2,1,0:T(8,128)(2,1)S(1)}, u32[]{:S(2)}, u32[]{:S(2)}) %collective-permute-start.48) | collective-permute-done | bytes 524320 | tf_op jit(solution)/shard_map/ppermute | solution.py:40
  192.0 3.6 %collective-permute-start.51 = (bf16[128,1024]{1,0:T(8,128)(2,1)S(1)}, bf16[128,1024]{1,0:T(8,128)(2,1)S(1)}, u32[]{:S(2)}, u32[]{:S(2)}) collective-permute-start(bf16[128,1024]{1,0:T(8,128)(2,1)S(1)} %get-tuple-element.85.refs_0_), channel_id=1, source_target_pairs={{0,3},{1,0},{2,1},{3,2},{4,7},{5,4},{6,5},{7,6},{8,11},{9,8},{10,9... | collective-permute-start | bytes 786440 | tf_op jit(solution)/shard_map/ppermute | solution.py:48
  195.7 3.2 %collective-permute-start.56 = (bf16[128,1024]{1,0:T(8,128)(2,1)S(1)}, bf16[128,1024]{1,0:T(8,128)(2,1)S(1)}, u32[]{:S(2)}, u32[]{:S(2)}) collective-permute-start(bf16[128,1024]{1,0:T(8,128)(2,1)S(1)} %collective-permute-done.53.refs_5_), channel_id=1, source_target_pairs={{0,3},{1,0},{2,1},{3,2},{4,7},{5,4},{6,5},{7,6},{8,11},{9,8},{10,9... | collective-permute-start | bytes 786440 | tf_op jit(solution)/shard_map/ppermute | solution.py:48
  198.9 3.4 %collective-permute-done.51.refs_4_ = bf16[128,1024]{1,0:T(8,128)(2,1)S(1)} collective-permute-done((bf16[128,1024]{1,0:T(8,128)(2,1)S(1)}, bf16[128,1024]{1,0:T(8,128)(2,1)S(1)}, u32[]{:S(2)}, u32[]{:S(2)}) %collective-permute-start.51) | collective-permute-done | bytes 262176 | tf_op jit(solution)/shard_map/ppermute | solution.py:48
  202.3 3.8 %collective-permute-start.52 = (bf16[64,1024]{1,0:T(8,128)(2,1)S(1)}, bf16[64,1024]{1,0:T(8,128)(2,1)S(1)}, u32[]{:S(2)}, u32[]{:S(2)}) collective-permute-start(bf16[64,1024]{1,0:T(8,128)(2,1)S(1)} %slice.60), channel_id=1, source_target_pairs={{0,3},{1,0},{2,1},{3,2},{4,7},{5,4},{6,5},{7,6},{8,11},{9,8},{10,9... | collective-permute-start | bytes 393224 | tf_op jit(solution)/shard_map/ppermute | solution.py:48
  207.9 3.8 %collective-permute-start.57 = (bf16[64,1024]{1,0:T(8,128)(2,1)S(1)}, bf16[64,1024]{1,0:T(8,128)(2,1)S(1)}, u32[]{:S(2)}, u32[]{:S(2)}) collective-permute-start(bf16[64,1024]{1,0:T(8,128)(2,1)S(1)} %slice.62), channel_id=1, source_target_pairs={{0,3},{1,0},{2,1},{3,2},{4,7},{5,4},{6,5},{7,6},{8,11},{9,8},{10,9... | collective-permute-start | bytes 393224 | tf_op jit(solution)/shard_map/ppermute | solution.py:48
  211.8 1.9 collective-permute-done.50.refs_2_
  214.2 3.7 %collective-permute-done.55.refs_7_ = bf16[64,1024]{1,0:T(8,128)(2,1)S(1)} collective-permute-done((bf16[64,1024]{1,0:T(8,128)(2,1)S(1)}, bf16[64,1024]{1,0:T(8,128)(2,1)S(1)}, u32[]{:S(2)}, u32[]{:S(2)}) %collective-permute-start.55) | collective-permute-done | bytes 131104 | tf_op jit(solution)/shard_map/ppermute | solution.py:48
  218.0 6.2 %weight_product.1 = (f32[4,32,2048]{2,1,0:T(8,128)S(1)}, bf16[4,32,2048]{2,1,0:T(8,128)(2,1)S(1)}, bf16[4,32,2048]{2,1,0:T(8,128)(2,1)S(1)}, bf16[4,32,2048]{2,1,0:T(8,128)(2,1)S(1)}) custom-call(bf16[128,1024]{1,0:T(8,128)(2,1)S(1)} %get-tuple-element.85.refs_0_, bf16[128,1024]{1,0:T(8,128)(2,1)S(1)} %collective-permute-done.49.refs_1_, ...), custom_call_target="tpu_custom_call" | custom-call | flops 4294967296 | bytes 12582912 | tf_op jit(solution)/shard_map/weight_product/pallas_call | solution.py:244
  224.2 3.2 %collective-permute-start.60 = (bf16[4,32,2048]{2,1,0:T(8,128)(2,1)S(1)}, bf16[4,32,2048]{2,1,0:T(8,128)(2,1)S(1)}, u32[]{:S(2)}, u32[]{:S(2)}) collective-permute-start(bf16[4,32,2048]{2,1,0:T(8,128)(2,1)S(1)} %get-tuple-element.89), channel_id=1, source_target_pairs={{0,24},{4,100},{8,0},{12,108},{16,8},{20,116},{24,16},{28,124},{32... | collective-permute-start | bytes 1572872 | tf_op jit(solution)/shard_map/ppermute | solution.py:40
  227.4 12.8 %collective-permute-done.59 = bf16[4,32,2048]{2,1,0:T(8,128)(2,1)S(1)} collective-permute-done((bf16[4,32,2048]{2,1,0:T(8,128)(2,1)S(1)}, bf16[4,32,2048]{2,1,0:T(8,128)(2,1)S(1)}, u32[]{:S(2)}, u32[]{:S(2)}) %collective-permute-start.59) | collective-permute-done | bytes 524320 | tf_op jit(solution)/shard_map/ppermute | solution.py:40
  240.7 2.5 collective-permute-start.64
  243.9 4.3 %collective-permute-done.62 = bf16[32,2048]{1,0:T(8,128)(2,1)S(1)} collective-permute-done((bf16[32,2048]{1,0:T(8,128)(2,1)S(1)}, bf16[32,2048]{1,0:T(8,128)(2,1)S(1)}, u32[]{:S(2)}, u32[]{:S(2)}) %collective-permute-start.62) | collective-permute-done | bytes 131104 | tf_op jit(solution)/shard_map/ppermute | solution.py:44
  (138 shorter events, 37.2 us)
Async XLA Ops:
  0.6 9.6 %collective-permute-start.1 = (bf16[32,2048]{1,0:T(8,128)(2,1)}, bf16[32,2048]{1,0:T(8,128)(2,1)S(1)}, u32[]{:S(2)}, u32[]{:S(2)}) collective-permute-start(bf16[32,2048]{1,0:T(8,128)(2,1)} %param.8), channel_id=1, source_target_pairs={{0,16},{4,68},{8,24},{12,76},{16,0},{20,84},{24,8},{28,92},{32,48}... | collective-permute-start | bytes 393224 | tf_op jit(solution)/shard_map/ppermute | solution.py:40
  12.0 15.4 %collective-permute-start.9 = (bf16[128,2048]{1,0:T(8,128)(2,1)S(1)}, bf16[128,2048]{1,0:T(8,128)(2,1)S(1)}, u32[]{:S(2)}, u32[]{:S(2)}) collective-permute-start(bf16[128,2048]{1,0:T(8,128)(2,1)S(1)} %pad_maximum_fusion.rest_0_), channel_id=1, source_target_pairs={{0,96},{4,28},{8,104},{12,4},{16,112},{20,12},{24,120},{28,20},{32... | collective-permute-start | bytes 1572872 | tf_op jit(solution)/shard_map/ppermute | solution.py:44
  15.1 12.3 %collective-permute-start.8 = (bf16[128,2048]{1,0:T(8,128)(2,1)S(1)}, bf16[128,2048]{1,0:T(8,128)(2,1)S(1)}, u32[]{:S(2)}, u32[]{:S(2)}) collective-permute-start(bf16[128,2048]{1,0:T(8,128)(2,1)S(1)} %pad_maximum_fusion.rest_0_), channel_id=1, source_target_pairs={{0,64},{4,20},{8,72},{12,28},{16,80},{20,4},{24,88},{28,12},{32,96... | collective-permute-start | bytes 1572872 | tf_op jit(solution)/shard_map/ppermute | solution.py:44
  15.7 15.7 %collective-permute-start.7 = (bf16[128,2048]{1,0:T(8,128)(2,1)S(1)}, bf16[128,2048]{1,0:T(8,128)(2,1)S(1)}, u32[]{:S(2)}, u32[]{:S(2)}) collective-permute-start(bf16[128,2048]{1,0:T(8,128)(2,1)S(1)} %pad_maximum_fusion.rest_0_), channel_id=1, source_target_pairs={{0,32},{4,12},{8,40},{12,20},{16,48},{20,28},{24,56},{28,4},{32,64... | collective-permute-start | bytes 1572872 | tf_op jit(solution)/shard_map/ppermute | solution.py:44
  16.7 14.7 %collective-permute-start.10 = (bf16[128,2048]{1,0:T(8,128)(2,1)S(1)}, bf16[128,2048]{1,0:T(8,128)(2,1)S(1)}, u32[]{:S(2)}, u32[]{:S(2)}) collective-permute-start(bf16[128,2048]{1,0:T(8,128)(2,1)S(1)} %pad_maximum_fusion.rest_0_), channel_id=1, source_target_pairs={{0,4},{4,0},{8,12},{12,8},{16,20},{20,16},{24,28},{28,24},{32,36},... | collective-permute-start | bytes 1572872 | tf_op jit(solution)/shard_map/ppermute | solution.py:52
  38.7 9.4 %collective-permute-start.14 = (bf16[256,384]{1,0:T(8,128)(2,1)S(1)}, bf16[256,384]{1,0:T(8,128)(2,1)S(1)}, u32[]{:S(2)}, u32[]{:S(2)}) collective-permute-start(bf16[256,384]{1,0:T(8,128)(2,1)S(1)} %get-tuple-element.49), channel_id=1, source_target_pairs={{0,1},{1,2},{2,3},{3,0},{4,5},{5,6},{6,7},{7,4},{8,9},{9,10},{10,1... | collective-permute-start | bytes 589832 | tf_op jit(solution)/shard_map/ppermute | solution.py:48
  40.3 7.9 %collective-permute-start.17 = (bf16[256,384]{1,0:T(8,128)(2,1)S(1)}, bf16[256,384]{1,0:T(8,128)(2,1)S(1)}, u32[]{:S(2)}, u32[]{:S(2)}) collective-permute-start(bf16[256,384]{1,0:T(8,128)(2,1)S(1)} %get-tuple-element.52), channel_id=1, source_target_pairs={{0,3},{1,0},{2,1},{3,2},{4,7},{5,4},{6,5},{7,6},{8,11},{9,8},{10,9... | collective-permute-start | bytes 589832 | tf_op jit(solution)/shard_map/ppermute | solution.py:48
  44.8 9.0 %collective-permute-start.20 = (bf16[256,384]{1,0:T(8,128)(2,1)S(1)}, bf16[256,384]{1,0:T(8,128)(2,1)S(1)}, u32[]{:S(2)}, u32[]{:S(2)}) collective-permute-start(bf16[256,384]{1,0:T(8,128)(2,1)S(1)} %get-tuple-element.56), channel_id=1, source_target_pairs={{0,1},{1,2},{2,3},{3,0},{4,5},{5,6},{6,7},{7,4},{8,9},{9,10},{10,1... | collective-permute-start | bytes 589832 | tf_op jit(solution)/shard_map/ppermute | solution.py:48
  45.1 8.8 %collective-permute-start.23 = (bf16[256,384]{1,0:T(8,128)(2,1)S(1)}, bf16[256,384]{1,0:T(8,128)(2,1)S(1)}, u32[]{:S(2)}, u32[]{:S(2)}) collective-permute-start(bf16[256,384]{1,0:T(8,128)(2,1)S(1)} %get-tuple-element.59), channel_id=1, source_target_pairs={{0,3},{1,0},{2,1},{3,2},{4,7},{5,4},{6,5},{7,6},{8,11},{9,8},{10,9... | collective-permute-start | bytes 589832 | tf_op jit(solution)/shard_map/ppermute | solution.py:48
  48.1 9.9 %collective-permute-start.15 = (bf16[256,384]{1,0:T(8,128)(2,1)S(1)}, bf16[256,384]{1,0:T(8,128)(2,1)S(1)}, u32[]{:S(2)}, u32[]{:S(2)}) collective-permute-start(bf16[256,384]{1,0:T(8,128)(2,1)S(1)} %relay.8), channel_id=1, source_target_pairs={{0,1},{1,2},{2,3},{3,0},{4,5},{5,6},{6,7},{7,4},{8,9},{9,10},{10,1... | collective-permute-start | bytes 589832 | tf_op jit(solution)/shard_map/ppermute | solution.py:48
  48.3 9.9 %collective-permute-start.18 = (bf16[256,384]{1,0:T(8,128)(2,1)S(1)}, bf16[256,384]{1,0:T(8,128)(2,1)S(1)}, u32[]{:S(2)}, u32[]{:S(2)}) collective-permute-start(bf16[256,384]{1,0:T(8,128)(2,1)S(1)} %relay.10), channel_id=1, source_target_pairs={{0,3},{1,0},{2,1},{3,2},{4,7},{5,4},{6,5},{7,6},{8,11},{9,8},{10,9... | collective-permute-start | bytes 589832 | tf_op jit(solution)/shard_map/ppermute | solution.py:48
  53.8 8.6 %collective-permute-start.21 = (bf16[256,384]{1,0:T(8,128)(2,1)S(1)}, bf16[256,384]{1,0:T(8,128)(2,1)S(1)}, u32[]{:S(2)}, u32[]{:S(2)}) collective-permute-start(bf16[256,384]{1,0:T(8,128)(2,1)S(1)} %relay.12), channel_id=1, source_target_pairs={{0,1},{1,2},{2,3},{3,0},{4,5},{5,6},{6,7},{7,4},{8,9},{9,10},{10,1... | collective-permute-start | bytes 589832 | tf_op jit(solution)/shard_map/ppermute | solution.py:48
  54.0 8.6 %collective-permute-start.24 = (bf16[256,384]{1,0:T(8,128)(2,1)S(1)}, bf16[256,384]{1,0:T(8,128)(2,1)S(1)}, u32[]{:S(2)}, u32[]{:S(2)}) collective-permute-start(bf16[256,384]{1,0:T(8,128)(2,1)S(1)} %relay.14), channel_id=1, source_target_pairs={{0,3},{1,0},{2,1},{3,2},{4,7},{5,4},{6,5},{7,6},{8,11},{9,8},{10,9... | collective-permute-start | bytes 589832 | tf_op jit(solution)/shard_map/ppermute | solution.py:48
  58.0 9.1 %collective-permute-start.16 = (bf16[256,384]{1,0:T(8,128)(2,1)S(1)}, bf16[256,384]{1,0:T(8,128)(2,1)S(1)}, u32[]{:S(2)}, u32[]{:S(2)}) collective-permute-start(bf16[256,384]{1,0:T(8,128)(2,1)S(1)} %relay.9), channel_id=1, source_target_pairs={{0,1},{1,2},{2,3},{3,0},{4,5},{5,6},{6,7},{7,4},{8,9},{9,10},{10,1... | collective-permute-start | bytes 589832 | tf_op jit(solution)/shard_map/ppermute | solution.py:48
  58.2 9.0 %collective-permute-start.19 = (bf16[256,384]{1,0:T(8,128)(2,1)S(1)}, bf16[256,384]{1,0:T(8,128)(2,1)S(1)}, u32[]{:S(2)}, u32[]{:S(2)}) collective-permute-start(bf16[256,384]{1,0:T(8,128)(2,1)S(1)} %relay.11), channel_id=1, source_target_pairs={{0,3},{1,0},{2,1},{3,2},{4,7},{5,4},{6,5},{7,6},{8,11},{9,8},{10,9... | collective-permute-start | bytes 589832 | tf_op jit(solution)/shard_map/ppermute | solution.py:48
  62.5 6.9 %collective-permute-start.22 = (bf16[256,384]{1,0:T(8,128)(2,1)S(1)}, bf16[256,384]{1,0:T(8,128)(2,1)S(1)}, u32[]{:S(2)}, u32[]{:S(2)}) collective-permute-start(bf16[256,384]{1,0:T(8,128)(2,1)S(1)} %relay.13), channel_id=1, source_target_pairs={{0,1},{1,2},{2,3},{3,0},{4,5},{5,6},{6,7},{7,4},{8,9},{9,10},{10,1... | collective-permute-start | bytes 589832 | tf_op jit(solution)/shard_map/ppermute | solution.py:48
  62.6 6.8 %collective-permute-start.25 = (bf16[256,384]{1,0:T(8,128)(2,1)S(1)}, bf16[256,384]{1,0:T(8,128)(2,1)S(1)}, u32[]{:S(2)}, u32[]{:S(2)}) collective-permute-start(bf16[256,384]{1,0:T(8,128)(2,1)S(1)} %relay.15), channel_id=1, source_target_pairs={{0,3},{1,0},{2,1},{3,2},{4,7},{5,4},{6,5},{7,6},{8,11},{9,8},{10,9... | collective-permute-start | bytes 589832 | tf_op jit(solution)/shard_map/ppermute | solution.py:48
  69.6 15.6 %collective-permute-start.28 = (bf16[8,128,256]{2,1,0:T(8,128)(2,1)S(1)}, bf16[8,128,256]{2,1,0:T(8,128)(2,1)S(1)}, u32[]{:S(2)}, u32[]{:S(2)}) collective-permute-start(bf16[8,128,256]{2,1,0:T(8,128)(2,1)S(1)} %bitcast.19), channel_id=1, source_target_pairs={{0,24},{4,100},{8,0},{12,108},{16,8},{20,116},{24,16},{28,124},{32... | collective-permute-start | bytes 1572872 | tf_op jit(solution)/shard_map/ppermute | solution.py:40
  72.9 12.3 %collective-permute-start.27 = (bf16[8,128,256]{2,1,0:T(8,128)(2,1)S(1)}, bf16[8,128,256]{2,1,0:T(8,128)(2,1)S(1)}, u32[]{:S(2)}, u32[]{:S(2)}) collective-permute-start(bf16[8,128,256]{2,1,0:T(8,128)(2,1)S(1)} %bitcast.20), channel_id=1, source_target_pairs={{0,16},{4,68},{8,24},{12,76},{16,0},{20,84},{24,8},{28,92},{32,48}... | collective-permute-start | bytes 1572872 | tf_op jit(solution)/shard_map/ppermute | solution.py:40
  72.9 16.0 %collective-permute-start.26 = (bf16[8,128,256]{2,1,0:T(8,128)(2,1)S(1)}, bf16[8,128,256]{2,1,0:T(8,128)(2,1)S(1)}, u32[]{:S(2)}, u32[]{:S(2)}) collective-permute-start(bf16[8,128,256]{2,1,0:T(8,128)(2,1)S(1)} %bitcast.21), channel_id=1, source_target_pairs={{0,8},{4,36},{8,16},{12,44},{16,24},{20,52},{24,0},{28,60},{32,40}... | collective-permute-start | bytes 1572872 | tf_op jit(solution)/shard_map/ppermute | solution.py:40
  89.7 16.1 %collective-permute-start.29 = (bf16[8,128,256]{2,1,0:T(8,128)(2,1)S(1)}, bf16[8,128,256]{2,1,0:T(8,128)(2,1)S(1)}, u32[]{:S(2)}, u32[]{:S(2)}) collective-permute-start(bf16[8,128,256]{2,1,0:T(8,128)(2,1)S(1)} %get-tuple-element.67), channel_id=1, source_target_pairs={{0,32},{4,12},{8,40},{12,20},{16,48},{20,28},{24,56},{28,4},{32,64... | collective-permute-start | bytes 1572872 | tf_op jit(solution)/shard_map/ppermute | solution.py:44
  89.8 16.0 %collective-permute-start.30 = (bf16[8,128,256]{2,1,0:T(8,128)(2,1)S(1)}, bf16[8,128,256]{2,1,0:T(8,128)(2,1)S(1)}, u32[]{:S(2)}, u32[]{:S(2)}) collective-permute-start(bf16[8,128,256]{2,1,0:T(8,128)(2,1)S(1)} %get-tuple-element.68), channel_id=1, source_target_pairs={{0,64},{4,20},{8,72},{12,28},{16,80},{20,4},{24,88},{28,12},{32,96... | collective-permute-start | bytes 1572872 | tf_op jit(solution)/shard_map/ppermute | solution.py:44
  92.5 24.6 %collective-permute-start.33 = (bf16[8,128,256]{2,1,0:T(8,128)(2,1)S(1)}, bf16[8,128,256]{2,1,0:T(8,128)(2,1)S(1)}, u32[]{:S(2)}, u32[]{:S(2)}) collective-permute-start(bf16[8,128,256]{2,1,0:T(8,128)(2,1)S(1)} %get-tuple-element.71), channel_id=1, source_target_pairs={{0,32},{4,12},{8,40},{12,20},{16,48},{20,28},{24,56},{28,4},{32,64... | collective-permute-start | bytes 1572872 | tf_op jit(solution)/shard_map/ppermute | solution.py:44
  93.9 23.2 %collective-permute-start.35 = (bf16[8,128,256]{2,1,0:T(8,128)(2,1)S(1)}, bf16[8,128,256]{2,1,0:T(8,128)(2,1)S(1)}, u32[]{:S(2)}, u32[]{:S(2)}) collective-permute-start(bf16[8,128,256]{2,1,0:T(8,128)(2,1)S(1)} %get-tuple-element.72), channel_id=1, source_target_pairs={{0,64},{4,20},{8,72},{12,28},{16,80},{20,4},{24,88},{28,12},{32,96... | collective-permute-start | bytes 1572872 | tf_op jit(solution)/shard_map/ppermute | solution.py:44
  94.5 23.0 %collective-permute-start.37 = (bf16[8,128,256]{2,1,0:T(8,128)(2,1)S(1)}, bf16[8,128,256]{2,1,0:T(8,128)(2,1)S(1)}, u32[]{:S(2)}, u32[]{:S(2)}) collective-permute-start(bf16[8,128,256]{2,1,0:T(8,128)(2,1)S(1)} %get-tuple-element.73), channel_id=1, source_target_pairs={{0,96},{4,28},{8,104},{12,4},{16,112},{20,12},{24,120},{28,20},{32... | collective-permute-start | bytes 1572872 | tf_op jit(solution)/shard_map/ppermute | solution.py:44
  105.8 12.6 %collective-permute-start.31 = (bf16[8,128,256]{2,1,0:T(8,128)(2,1)S(1)}, bf16[8,128,256]{2,1,0:T(8,128)(2,1)S(1)}, u32[]{:S(2)}, u32[]{:S(2)}) collective-permute-start(bf16[8,128,256]{2,1,0:T(8,128)(2,1)S(1)} %get-tuple-element.69), channel_id=1, source_target_pairs={{0,96},{4,28},{8,104},{12,4},{16,112},{20,12},{24,120},{28,20},{32... | collective-permute-start | bytes 1572872 | tf_op jit(solution)/shard_map/ppermute | solution.py:44
  105.8 13.1 %collective-permute-start.32 = (bf16[8,128,256]{2,1,0:T(8,128)(2,1)S(1)}, bf16[8,128,256]{2,1,0:T(8,128)(2,1)S(1)}, u32[]{:S(2)}, u32[]{:S(2)}) collective-permute-start(bf16[8,128,256]{2,1,0:T(8,128)(2,1)S(1)} %get-tuple-element.70), channel_id=1, source_target_pairs={{0,4},{4,0},{8,12},{12,8},{16,20},{20,16},{24,28},{28,24},{32,36},... | collective-permute-start | bytes 1572872 | tf_op jit(solution)/shard_map/ppermute | solution.py:52
  118.4 93.4 %collective-permute-start.58 = (bf16[1024,2048]{1,0:T(8,128)(2,1)}, bf16[1024,2048]{1,0:T(8,128)(2,1)S(1)}, u32[]{:S(2)}, u32[]{:S(2)}) collective-permute-start(bf16[1024,2048]{1,0:T(8,128)(2,1)} %refs_10_.1), channel_id=1, source_target_pairs={{0,4},{4,0},{8,12},{12,8},{16,20},{20,16},{24,28},{28,24},{32,36},... | collective-permute-start | bytes 12582920 | tf_op jit(solution)/shard_map/ppermute | solution.py:52
  144.3 9.2 %collective-permute-start.40 = (bf16[8,128,256]{2,1,0:T(8,128)(2,1)S(1)}, bf16[8,128,256]{2,1,0:T(8,128)(2,1)S(1)}, u32[]{:S(2)}, u32[]{:S(2)}) collective-permute-start(bf16[8,128,256]{2,1,0:T(8,128)(2,1)S(1)} %get-tuple-element.78), channel_id=1, source_target_pairs={{0,96},{4,28},{8,104},{12,4},{16,112},{20,12},{24,120},{28,20},{32... | collective-permute-start | bytes 1572872 | tf_op jit(solution)/shard_map/ppermute | solution.py:44
  144.3 10.8 %collective-permute-start.42 = (bf16[8,128,256]{2,1,0:T(8,128)(2,1)S(1)}, bf16[8,128,256]{2,1,0:T(8,128)(2,1)S(1)}, u32[]{:S(2)}, u32[]{:S(2)}) collective-permute-start(bf16[8,128,256]{2,1,0:T(8,128)(2,1)S(1)} %get-tuple-element.79), channel_id=1, source_target_pairs={{0,64},{4,20},{8,72},{12,28},{16,80},{20,4},{24,88},{28,12},{32,96... | collective-permute-start | bytes 1572872 | tf_op jit(solution)/shard_map/ppermute | solution.py:44
  144.3 17.5 %collective-permute-start.44 = (bf16[8,128,256]{2,1,0:T(8,128)(2,1)S(1)}, bf16[8,128,256]{2,1,0:T(8,128)(2,1)S(1)}, u32[]{:S(2)}, u32[]{:S(2)}) collective-permute-start(bf16[8,128,256]{2,1,0:T(8,128)(2,1)S(1)} %get-tuple-element.80), channel_id=1, source_target_pairs={{0,32},{4,12},{8,40},{12,20},{16,48},{20,28},{24,56},{28,4},{32,64... | collective-permute-start | bytes 1572872 | tf_op jit(solution)/shard_map/ppermute | solution.py:44
  148.5 17.7 %collective-permute-start.45 = (bf16[8,128,256]{2,1,0:T(8,128)(2,1)S(1)}, bf16[8,128,256]{2,1,0:T(8,128)(2,1)S(1)}, u32[]{:S(2)}, u32[]{:S(2)}) collective-permute-start(bf16[8,128,256]{2,1,0:T(8,128)(2,1)S(1)} %get-tuple-element.97), channel_id=1, source_target_pairs={{0,32},{4,12},{8,40},{12,20},{16,48},{20,28},{24,56},{28,4},{32,64... | collective-permute-start | bytes 1572872 | tf_op jit(solution)/shard_map/ppermute | solution.py:44
  153.5 18.4 %collective-permute-start.43 = (bf16[8,128,256]{2,1,0:T(8,128)(2,1)S(1)}, bf16[8,128,256]{2,1,0:T(8,128)(2,1)S(1)}, u32[]{:S(2)}, u32[]{:S(2)}) collective-permute-start(bf16[8,128,256]{2,1,0:T(8,128)(2,1)S(1)} %get-tuple-element.98), channel_id=1, source_target_pairs={{0,64},{4,20},{8,72},{12,28},{16,80},{20,4},{24,88},{28,12},{32,96... | collective-permute-start | bytes 1572872 | tf_op jit(solution)/shard_map/ppermute | solution.py:44
  155.1 16.8 %collective-permute-start.41 = (bf16[8,128,256]{2,1,0:T(8,128)(2,1)S(1)}, bf16[8,128,256]{2,1,0:T(8,128)(2,1)S(1)}, u32[]{:S(2)}, u32[]{:S(2)}) collective-permute-start(bf16[8,128,256]{2,1,0:T(8,128)(2,1)S(1)} %get-tuple-element.99), channel_id=1, source_target_pairs={{0,96},{4,28},{8,104},{12,4},{16,112},{20,12},{24,120},{28,20},{32... | collective-permute-start | bytes 1572872 | tf_op jit(solution)/shard_map/ppermute | solution.py:44
  174.3 9.3 %collective-permute-start.46 = (bf16[8,128,256]{2,1,0:T(8,128)(2,1)S(1)}, bf16[8,128,256]{2,1,0:T(8,128)(2,1)S(1)}, u32[]{:S(2)}, u32[]{:S(2)}) collective-permute-start(bf16[8,128,256]{2,1,0:T(8,128)(2,1)S(1)} %get-tuple-element.82), channel_id=1, source_target_pairs={{0,24},{4,100},{8,0},{12,108},{16,8},{20,116},{24,16},{28,124},{32... | collective-permute-start | bytes 1572872 | tf_op jit(solution)/shard_map/ppermute | solution.py:40
  175.2 10.8 %collective-permute-start.47 = (bf16[8,128,256]{2,1,0:T(8,128)(2,1)S(1)}, bf16[8,128,256]{2,1,0:T(8,128)(2,1)S(1)}, u32[]{:S(2)}, u32[]{:S(2)}) collective-permute-start(bf16[8,128,256]{2,1,0:T(8,128)(2,1)S(1)} %get-tuple-element.83), channel_id=1, source_target_pairs={{0,16},{4,68},{8,24},{12,76},{16,0},{20,84},{24,8},{28,92},{32,48}... | collective-permute-start | bytes 1572872 | tf_op jit(solution)/shard_map/ppermute | solution.py:40
  175.2 16.3 %collective-permute-start.48 = (bf16[8,128,256]{2,1,0:T(8,128)(2,1)S(1)}, bf16[8,128,256]{2,1,0:T(8,128)(2,1)S(1)}, u32[]{:S(2)}, u32[]{:S(2)}) collective-permute-start(bf16[8,128,256]{2,1,0:T(8,128)(2,1)S(1)} %get-tuple-element.84), channel_id=1, source_target_pairs={{0,8},{4,36},{8,16},{12,44},{16,24},{20,52},{24,0},{28,60},{32,40}... | collective-permute-start | bytes 1572872 | tf_op jit(solution)/shard_map/ppermute | solution.py:40
  192.0 10.3 %collective-permute-start.51 = (bf16[128,1024]{1,0:T(8,128)(2,1)S(1)}, bf16[128,1024]{1,0:T(8,128)(2,1)S(1)}, u32[]{:S(2)}, u32[]{:S(2)}) collective-permute-start(bf16[128,1024]{1,0:T(8,128)(2,1)S(1)} %get-tuple-element.85.refs_0_), channel_id=1, source_target_pairs={{0,3},{1,0},{2,1},{3,2},{4,7},{5,4},{6,5},{7,6},{8,11},{9,8},{10,9... | collective-permute-start | bytes 786440 | tf_op jit(solution)/shard_map/ppermute | solution.py:48
  195.7 10.4 %collective-permute-start.49 = (bf16[128,1024]{1,0:T(8,128)(2,1)S(1)}, bf16[128,1024]{1,0:T(8,128)(2,1)S(1)}, u32[]{:S(2)}, u32[]{:S(2)}) collective-permute-start(bf16[128,1024]{1,0:T(8,128)(2,1)S(1)} %get-tuple-element.85.refs_0_), channel_id=1, source_target_pairs={{0,1},{1,2},{2,3},{3,0},{4,5},{5,6},{6,7},{7,4},{8,9},{9,10},{10,1... | collective-permute-start | bytes 786440 | tf_op jit(solution)/shard_map/ppermute | solution.py:48
  195.7 12.2 %collective-permute-start.56 = (bf16[128,1024]{1,0:T(8,128)(2,1)S(1)}, bf16[128,1024]{1,0:T(8,128)(2,1)S(1)}, u32[]{:S(2)}, u32[]{:S(2)}) collective-permute-start(bf16[128,1024]{1,0:T(8,128)(2,1)S(1)} %collective-permute-done.53.refs_5_), channel_id=1, source_target_pairs={{0,3},{1,0},{2,1},{3,2},{4,7},{5,4},{6,5},{7,6},{8,11},{9,8},{10,9... | collective-permute-start | bytes 786440 | tf_op jit(solution)/shard_map/ppermute | solution.py:48
  198.9 12.8 %collective-permute-start.54 = (bf16[128,1024]{1,0:T(8,128)(2,1)S(1)}, bf16[128,1024]{1,0:T(8,128)(2,1)S(1)}, u32[]{:S(2)}, u32[]{:S(2)}) collective-permute-start(bf16[128,1024]{1,0:T(8,128)(2,1)S(1)} %collective-permute-done.53.refs_5_), channel_id=1, source_target_pairs={{0,1},{1,2},{2,3},{3,0},{4,5},{5,6},{6,7},{7,4},{8,9},{9,10},{10,1... | collective-permute-start | bytes 786440 | tf_op jit(solution)/shard_map/ppermute | solution.py:48
  202.3 9.5 %collective-permute-start.52 = (bf16[64,1024]{1,0:T(8,128)(2,1)S(1)}, bf16[64,1024]{1,0:T(8,128)(2,1)S(1)}, u32[]{:S(2)}, u32[]{:S(2)}) collective-permute-start(bf16[64,1024]{1,0:T(8,128)(2,1)S(1)} %slice.60), channel_id=1, source_target_pairs={{0,3},{1,0},{2,1},{3,2},{4,7},{5,4},{6,5},{7,6},{8,11},{9,8},{10,9... | collective-permute-start | bytes 393224 | tf_op jit(solution)/shard_map/ppermute | solution.py:48
  206.1 7.6 %collective-permute-start.50 = (bf16[64,1024]{1,0:T(8,128)(2,1)S(1)}, bf16[64,1024]{1,0:T(8,128)(2,1)S(1)}, u32[]{:S(2)}, u32[]{:S(2)}) collective-permute-start(bf16[64,1024]{1,0:T(8,128)(2,1)S(1)} %slice.59), channel_id=1, source_target_pairs={{0,1},{1,2},{2,3},{3,0},{4,5},{5,6},{6,7},{7,4},{8,9},{9,10},{10,1... | collective-permute-start | bytes 393224 | tf_op jit(solution)/shard_map/ppermute | solution.py:48
  224.1 16.1 %collective-permute-start.59 = (bf16[4,32,2048]{2,1,0:T(8,128)(2,1)S(1)}, bf16[4,32,2048]{2,1,0:T(8,128)(2,1)S(1)}, u32[]{:S(2)}, u32[]{:S(2)}) collective-permute-start(bf16[4,32,2048]{2,1,0:T(8,128)(2,1)S(1)} %get-tuple-element.88), channel_id=1, source_target_pairs={{0,8},{4,36},{8,16},{12,44},{16,24},{20,52},{24,0},{28,60},{32,40}... | collective-permute-start | bytes 1572872 | tf_op jit(solution)/shard_map/ppermute | solution.py:40
  224.2 16.0 %collective-permute-start.60 = (bf16[4,32,2048]{2,1,0:T(8,128)(2,1)S(1)}, bf16[4,32,2048]{2,1,0:T(8,128)(2,1)S(1)}, u32[]{:S(2)}, u32[]{:S(2)}) collective-permute-start(bf16[4,32,2048]{2,1,0:T(8,128)(2,1)S(1)} %get-tuple-element.89), channel_id=1, source_target_pairs={{0,24},{4,100},{8,0},{12,108},{16,8},{20,116},{24,16},{28,124},{32... | collective-permute-start | bytes 1572872 | tf_op jit(solution)/shard_map/ppermute | solution.py:40
  227.4 12.8 %collective-permute-start.61 = (bf16[4,32,2048]{2,1,0:T(8,128)(2,1)S(1)}, bf16[4,32,2048]{2,1,0:T(8,128)(2,1)S(1)}, u32[]{:S(2)}, u32[]{:S(2)}) collective-permute-start(bf16[4,32,2048]{2,1,0:T(8,128)(2,1)S(1)} %get-tuple-element.90), channel_id=1, source_target_pairs={{0,16},{4,68},{8,24},{12,76},{16,0},{20,84},{24,8},{28,92},{32,48}... | collective-permute-start | bytes 1572872 | tf_op jit(solution)/shard_map/ppermute | solution.py:40
  240.6 7.7 %collective-permute-start.62 = (bf16[32,2048]{1,0:T(8,128)(2,1)S(1)}, bf16[32,2048]{1,0:T(8,128)(2,1)S(1)}, u32[]{:S(2)}, u32[]{:S(2)}) collective-permute-start(bf16[32,2048]{1,0:T(8,128)(2,1)S(1)} %get-tuple-element.101), channel_id=1, source_target_pairs={{0,32},{4,12},{8,40},{12,20},{16,48},{20,28},{24,56},{28,4},{32,64... | collective-permute-start | bytes 393224 | tf_op jit(solution)/shard_map/ppermute | solution.py:44
  240.7 7.6 %collective-permute-start.64 = (bf16[32,2048]{1,0:T(8,128)(2,1)S(1)}, bf16[32,2048]{1,0:T(8,128)(2,1)S(1)}, u32[]{:S(2)}, u32[]{:S(2)}) collective-permute-start(bf16[32,2048]{1,0:T(8,128)(2,1)S(1)} %get-tuple-element.102), channel_id=1, source_target_pairs={{0,64},{4,20},{8,72},{12,28},{16,80},{20,4},{24,88},{28,12},{32,96... | collective-permute-start | bytes 393224 | tf_op jit(solution)/shard_map/ppermute | solution.py:44
  (23 other events, 279.0 us)

commit v4 on v3

--- a/solution.py
+++ b/solution.py
@@ -201,25 +201,43 @@
     return [send_tp(down, 1), send_tp(up, -1)], [parts[0], parts[SIDE]]
 
 
-def weight_kernel(*refs):
-    mine, theirs = refs[:5], refs[5:10]
-    h_mine, h_theirs = refs[10:12]
-    outs = refs[12 : 12 + SIDE]
-    left, result = refs[12 + SIDE :]
-    y, z, core, tp = here_in_kernel()
-    rows = mine[0].shape[1]
+def stack_heads(pieces, left):
+    at = 0
+    for piece in pieces:
+        left[pl.ds(at, piece.shape[0]), :] = piece[...]
+        at += piece.shape[0]
+
+
+def columns_of_step(tile):
+    return pl.ds(pl.multiple_of(pl.program_id(0) * tile, tile), tile)
+
+
+def first_weight_kernel(*refs):
+    h_ref, out_ref, left = refs[5:]
 
     @pl.when(pl.program_id(0) == 0)
     def _():
-        for half, refs_of in enumerate((mine, theirs)):
-            at = 0
-            for piece in refs_of:
-                left[pl.ds(at, piece.shape[0]), half * rows : (half + 1) * rows] = piece[...]
-                at += piece.shape[0]
-
-    result[...] = jnp.dot(
-        left[:, :rows], h_mine[...], preferred_element_type=F32
-    ) + jnp.dot(left[:, rows:], h_theirs[...], preferred_element_type=F32)
+        stack_heads(refs[:5], left)
+
+    out_ref[:, columns_of_step(h_ref.shape[1])] = jnp.dot(
+        left[...], h_ref[...], preferred_element_type=F32
+    )
+
+
+def second_weight_kernel(*refs):
+    h_ref, so_far = refs[5:7]
+    outs = refs[7 : 7 + SIDE]
+    left, result = refs[7 + SIDE :]
+    y, z, core, tp = here_in_kernel()
+    columns = columns_of_step(h_ref.shape[1])
+
+    @pl.when(pl.program_id(0) == 0)
+    def _():
+        stack_heads(refs[:5], left)
+
+    result[...] = so_far[:, columns] + jnp.dot(
+        left[...], h_ref[...], preferred_element_type=F32
+    )
 
     def block(ja, jb):
         a_z, a_y = ring_mod(z + ja), ring_mod(y + ja)
@@ -229,8 +247,6 @@
         at = ring_mod(tp - y_of) * SIDE * OUT_ROWS + z_of * OUT_ROWS
         return result[pl.ds(pl.multiple_of(at, OUT_ROWS), OUT_ROWS), :]
 
-    tile = result.shape[1]
-    columns = pl.ds(pl.multiple_of(pl.program_id(0) * tile, tile), tile)
     for ja in range(SIDE):
         for jb in range(SIDE):
             outs[ja][jb, :, columns] = block(ja, jb).astype(outs[ja].dtype)
@@ -241,25 +257,36 @@
     tile = 512
     heads_rows = SIDE * SIDE * OUT_ROWS
     whole = pl.BlockSpec(memory_space=pltpu.VMEM)
+    left = pltpu.VMEM((heads_rows, rows), BF)
+    common = dict(
+        grid=(depth // tile,),
+        compiler_params=pltpu.CompilerParams(vmem_limit_bytes=12 * 2**20),
+        cost_estimate=pl.CostEstimate(
+            flops=2 * heads_rows * rows * depth,
+            bytes_accessed=2 * rows * depth + 4 * heads_rows * depth,
+            transcendentals=0,
+        ),
+    )
+    in_specs = [whole] * 5 + [pl.BlockSpec((rows, tile), lambda i: (0, i))]
+    so_far = pl.pallas_call(
+        first_weight_kernel,
+        out_shape=jax.ShapeDtypeStruct((heads_rows, depth), F32),
+        in_specs=in_specs,
+        out_specs=whole,
+        scratch_shapes=[left],
+        name="first_weight_product",
+        **common,
+    )(*mine, h_mine)
     return pl.pallas_call(
-        weight_kernel,
+        second_weight_kernel,
         out_shape=[jax.ShapeDtypeStruct((SIDE, OUT_ROWS, depth), F32)]
         + [jax.ShapeDtypeStruct((SIDE, OUT_ROWS, depth), BF)] * (SIDE - 1),
-        grid=(depth // tile,),
-        in_specs=[whole] * 10 + [pl.BlockSpec((rows, tile), lambda i: (0, i))] * 2,
+        in_specs=in_specs + [whole],
         out_specs=[whole] * SIDE,
-        scratch_shapes=[
-            pltpu.VMEM((heads_rows, 2 * rows), BF),
-            pltpu.VMEM((heads_rows, tile), F32),
-        ],
-        compiler_params=pltpu.CompilerParams(vmem_limit_bytes=16 * 2**20),
-        cost_estimate=pl.CostEstimate(
-            flops=4 * heads_rows * rows * depth,
-            bytes_accessed=4 * rows * depth + 4 * heads_rows * depth,
-            transcendentals=0,
-        ),
-        name="weight_product",
-    )(*mine, *theirs, h_mine, h_theirs)
+        scratch_shapes=[left, pltpu.VMEM((heads_rows, tile), F32)],
+        name="second_weight_product",
+        **common,
+    )(*theirs, h_theirs, so_far)
 
 
 def reduce_owners(blocks):
@@ -378,7 +405,7 @@
                 pltpu.VMEM((keys, width), BF),
             ],
         ),
-        compiler_params=pltpu.CompilerParams(vmem_limit_bytes=26 * 2**20),
+        compiler_params=pltpu.CompilerParams(vmem_limit_bytes=22 * 2**20),
         cost_estimate=pl.CostEstimate(
             flops=10 * n_query * keys * qlen * width,
             bytes_accessed=8 * rows * width + 4 * n_query * keys * local,
@@ -388,32 +415,33 @@
     )(*places, queries, out_grad, query_kv, *sources)
 
 
-def pick_kernel(slot_of, *rest):
-    ring, outs = rest[:SIDE], rest[SIDE:]
+def pick_kernel(other, slot_of, *rest):
+    ring, outs = rest[:SIDE], rest[-SIDE:]
     n = outs[0].shape[0]
-    for k in range(2 * SIDE):
+    for k in range(SIDE):
         for m in range(n):
-            outs[k][m] = ring[m // 2][jnp.maximum(slot_of[k * n + m], 0)]
-
-
-def pick(slot_of, ring):
+            at = (2 * k + other) * n + m
+            outs[k][m] = ring[m // 2][jnp.maximum(slot_of[at], 0)]
+
+
+def pick(slot_of, ring, other, *earlier):
     n = slot_of.shape[0] // (2 * SIDE)
     whole = pl.BlockSpec(memory_space=pltpu.VMEM)
     shape = jax.ShapeDtypeStruct((n,) + ring[0].shape[1:], BF)
     return pl.pallas_call(
-        pick_kernel,
-        out_shape=[shape] * (2 * SIDE),
+        functools.partial(pick_kernel, other),
+        out_shape=[shape] * SIDE,
         grid_spec=pltpu.PrefetchScalarGridSpec(
             num_scalar_prefetch=1,
-            in_specs=[whole] * SIDE,
-            out_specs=[whole] * (2 * SIDE),
+            in_specs=[whole] * (SIDE + len(earlier)),
+            out_specs=[whole] * SIDE,
         ),
         compiler_params=pltpu.CompilerParams(vmem_limit_bytes=2 * 2**20),
         cost_estimate=pl.CostEstimate(
-            flops=0, bytes_accessed=16 * SIDE * n * PLEN * HD, transcendentals=0
+            flops=0, bytes_accessed=8 * SIDE * n * PLEN * HD, transcendentals=0
         ),
         name="pick",
-    )(slot_of, *ring)
+    )(slot_of, *ring, *earlier)
 
 
 def add_blocks_kernel(slot_of, *rest):
@@ -569,19 +597,18 @@
         *upper_own,
     )
     own = own.reshape(passages_here, PLEN, local_width)
-    wanted = pick(served, ring_gather(own, send_first))
-    same, other = wanted[::2], wanted[1::2]
-    other = [other[0]] + [send_second(other[k], k) for k in (1, 3, 2)]
-    same = [same[0]] + [send_second(same[k], k) for k in (1, 3, 2)]
-    for blocks in (other, same):
-        blocks[2], blocks[3] = blocks[3], blocks[2]
+    ring = ring_gather(own, send_first)
+    other = pick(served, ring, 1, places[0])
+    swapped = [swap_cores(other[0])] + [swap_cores(send_second(other[k], k)) for k in range(1, SIDE)]
+    same = pick(served, ring, 0, swapped[0])
+    same = [same[0]] + [send_second(same[k], k) for k in range(1, SIDE)]
     hidden_theirs = swap_cores(passage_hidden)
     half = SIDE * capacity
     grad_queries, own_grads, *grads = attention(
         queries,
         out_grad,
         query_kv,
-        same + [swap_cores(g) for g in other],
+        same + swapped,
         [half] * SIDE + [SIDE * half],
         places,
         queries_here,

time: 250 us -> 248 us (level)
  waiting for transfers between devices: 121 us -> 116 us
    ppermute x20, waiting for transfers between devices: 18.5 us -> 15.2 us  [send_tp(): return lax.ppermute(x, 'tp', [(i, (i + k) % SIDE) for i in range(SIDE)])]
    ppermute x12, waiting for transfers between devices: 7.31 us -> 4.53 us  [swap_cores(): return lax.ppermute(x, 'pas', [(i, i ^ 1) for i in range(2 * SIDE * SIDE)])]
    pallas_call x2 -> x4, Pallas kernels: 6.97 us -> 8.22 us  [the longest x1 3.6 us: weight_product(): pl.pallas_call(second_weight_kernel, out_shape=[jax.ShapeDtypeStruct((SID...]
  transfers between devices with their start and end apart: 65 -> 65, of which waited for: 35 -> 34; matrix products, arithmetic and copies ran while one was open for 2% -> 2% of each run, Pallas kernels for 11% -> 13%
where the time goes in v4:
time: 248 us
  waiting for transfers between devices  116 us (47%)
  starting transfers between devices  79.9 us (32%)
  Pallas kernels  40.2 us (16%)
  local copies, waits for them, and re-layouts  7.12 us (3%)
  other arithmetic  3.32 us (1%)
    ppermute x21, waiting for transfers between devices, send_second(): return lax.ppermute(x, 'pas', ring_pairs(1, k))  63.3 us
    ppermute x20, starting transfers between devices, send_tp(): return lax.ppermute(x, 'tp', [(i, (i + k) % SIDE) for i in range(SIDE)])  34.5 us
    ppermute x12, waiting for transfers between devices, send_first(): return lax.ppermute(x, 'pas', ring_pairs(0, k))  33 us
    ppermute x21, starting transfers between devices, send_second(): return lax.ppermute(x, 'pas', ring_pairs(1, k))  26.9 us
    pallas_call x1, Pallas kernels, attention(): pl.pallas_call(functools.partial(attention_kernel, len(sources), len(out_...  21.5 us
    ppermute x12, starting transfers between devices, send_first(): return lax.ppermute(x, 'pas', ring_pairs(0, k))  17.1 us
    ppermute x20, waiting for transfers between devices, send_tp(): return lax.ppermute(x, 'tp', [(i, (i + k) % SIDE) for i in range(SIDE)])  15.2 us
    pallas_call x2, Pallas kernels, project(): pl.pallas_call(functools.partial(project_kernel, first, len(pieces)), out...  7.15 us
  transfers between devices with their start and end apart: 65, of which 34 were waited for; matrix products, arithmetic and copies ran while one was open for 2% of the time, Pallas kernels for 13%

profile of v4, /device:TPU:0, one launch (start us, length us, event | category | flops | bytes accessed | tf_op | source)
XLA Modules:
  0.0 247.7 jit_solution(15661840049233278224)
XLA Ops:
  0.6 4.0 %collective-permute-start.1 = (bf16[32,2048]{1,0:T(8,128)(2,1)}, bf16[32,2048]{1,0:T(8,128)(2,1)S(1)}, u32[]{:S(2)}, u32[]{:S(2)}) collective-permute-start(bf16[32,2048]{1,0:T(8,128)(2,1)} %param.8), channel_id=1, source_target_pairs={{0,16},{4,68},{8,24},{12,76},{16,0},{20,84},{24,8},{28,92},{32,48}... | collective-permute-start | bytes 393224 | tf_op jit(solution)/shard_map/ppermute | solution.py:40
  5.7 2.2 collective-permute-start.2
  12.0 3.1 %collective-permute-start.9 = (bf16[128,2048]{1,0:T(8,128)(2,1)S(1)}, bf16[128,2048]{1,0:T(8,128)(2,1)S(1)}, u32[]{:S(2)}, u32[]{:S(2)}) collective-permute-start(bf16[128,2048]{1,0:T(8,128)(2,1)S(1)} %pad_maximum_fusion.rest_0_), channel_id=1, source_target_pairs={{0,96},{4,28},{8,104},{12,4},{16,112},{20,12},{24,120},{28,20},{32... | collective-permute-start | bytes 1572872 | tf_op jit(solution)/shard_map/ppermute | solution.py:44
  16.7 10.7 %collective-permute-done.9.rest_3_ = bf16[128,2048]{1,0:T(8,128)(2,1)S(1)} collective-permute-done((bf16[128,2048]{1,0:T(8,128)(2,1)S(1)}, bf16[128,2048]{1,0:T(8,128)(2,1)S(1)}, u32[]{:S(2)}, u32[]{:S(2)}) %collective-permute-start.9) | collective-permute-done | bytes 524320 | tf_op jit(solution)/shard_map/ppermute | solution.py:44
  27.9 3.5 %collective-permute-done.7.rest_1_ = bf16[128,2048]{1,0:T(8,128)(2,1)S(1)} collective-permute-done((bf16[128,2048]{1,0:T(8,128)(2,1)S(1)}, bf16[128,2048]{1,0:T(8,128)(2,1)S(1)}, u32[]{:S(2)}, u32[]{:S(2)}) %collective-permute-start.7) | collective-permute-done | bytes 524320 | tf_op jit(solution)/shard_map/ppermute | solution.py:44
  31.4 2.0 collective-permute-done.11.rest_5_
  33.4 2.2 copy-done
  35.6 4.4 %project.2 = (f32[256,256]{1,0:T(8,128)S(1)}, f32[256,256]{1,0:T(8,128)S(1)}, f32[256,256]{1,0:T(8,128)S(1)}, bf16[256,384]{1,0:T(8,128)(2,1)S(1)}, f32[256,256]...) custom-call(bf16[1024,2048]{1,0:T(8,128)(2,1)S(1)} %copy-done, ...), custom_call_target="tpu_custom_call" | custom-call | flops 2147483648 | bytes 8388608 | tf_op jit(solution)/shard_map/project/pallas_call | solution.py:149
  41.6 1.7 collective-permute-start.17
  43.4 2.7 %project.3 = (f32[256,256]{1,0:T(8,128)S(1)}, f32[256,256]{1,0:T(8,128)S(1)}, f32[256,256]{1,0:T(8,128)S(1)}, bf16[256,384]{1,0:T(8,128)(2,1)S(1)}, f32[256,256]...) custom-call(bf16[1024,2048]{1,0:T(8,128)(2,1)S(1)} %copy-done, ...), custom_call_target="tpu_custom_call" | custom-call | flops 2147483648 | bytes 8388608 | tf_op jit(solution)/shard_map/project/pallas_call | solution.py:149
  46.5 3.0 %collective-permute-start.23 = (bf16[256,384]{1,0:T(8,128)(2,1)S(1)}, bf16[256,384]{1,0:T(8,128)(2,1)S(1)}, u32[]{:S(2)}, u32[]{:S(2)}) collective-permute-start(bf16[256,384]{1,0:T(8,128)(2,1)S(1)} %get-tuple-element.59), channel_id=1, source_target_pairs={{0,3},{1,0},{2,1},{3,2},{4,7},{5,4},{6,5},{7,6},{8,11},{9,8},{10,9... | collective-permute-start | bytes 589832 | tf_op jit(solution)/shard_map/ppermute | solution.py:48
  49.7 3.3 %collective-permute-start.18 = (bf16[256,384]{1,0:T(8,128)(2,1)S(1)}, bf16[256,384]{1,0:T(8,128)(2,1)S(1)}, u32[]{:S(2)}, u32[]{:S(2)}) collective-permute-start(bf16[256,384]{1,0:T(8,128)(2,1)S(1)} %relay.10), channel_id=1, source_target_pairs={{0,3},{1,0},{2,1},{3,2},{4,7},{5,4},{6,5},{7,6},{8,11},{9,8},{10,9... | collective-permute-start | bytes 589832 | tf_op jit(solution)/shard_map/ppermute | solution.py:48
  52.9 2.1 collective-permute-done.20.got_ref
  55.3 3.3 %collective-permute-start.24 = (bf16[256,384]{1,0:T(8,128)(2,1)S(1)}, bf16[256,384]{1,0:T(8,128)(2,1)S(1)}, u32[]{:S(2)}, u32[]{:S(2)}) collective-permute-start(bf16[256,384]{1,0:T(8,128)(2,1)S(1)} %relay.14), channel_id=1, source_target_pairs={{0,3},{1,0},{2,1},{3,2},{4,7},{5,4},{6,5},{7,6},{8,11},{9,8},{10,9... | collective-permute-start | bytes 589832 | tf_op jit(solution)/shard_map/ppermute | solution.py:48
  59.5 3.3 %collective-permute-start.19 = (bf16[256,384]{1,0:T(8,128)(2,1)S(1)}, bf16[256,384]{1,0:T(8,128)(2,1)S(1)}, u32[]{:S(2)}, u32[]{:S(2)}) collective-permute-start(bf16[256,384]{1,0:T(8,128)(2,1)S(1)} %relay.11), channel_id=1, source_target_pairs={{0,3},{1,0},{2,1},{3,2},{4,7},{5,4},{6,5},{7,6},{8,11},{9,8},{10,9... | collective-permute-start | bytes 589832 | tf_op jit(solution)/shard_map/ppermute | solution.py:48
  63.9 3.3 %collective-permute-start.25 = (bf16[256,384]{1,0:T(8,128)(2,1)S(1)}, bf16[256,384]{1,0:T(8,128)(2,1)S(1)}, u32[]{:S(2)}, u32[]{:S(2)}) collective-permute-start(bf16[256,384]{1,0:T(8,128)(2,1)S(1)} %relay.15), channel_id=1, source_target_pairs={{0,3},{1,0},{2,1},{3,2},{4,7},{5,4},{6,5},{7,6},{8,11},{9,8},{10,9... | collective-permute-start | bytes 589832 | tf_op jit(solution)/shard_map/ppermute | solution.py:48
  68.5 2.2 collective-permute-done.22.refs_2_
  70.9 3.5 %collective-permute-start.28 = (bf16[8,128,256]{2,1,0:T(8,128)(2,1)S(1)}, bf16[8,128,256]{2,1,0:T(8,128)(2,1)S(1)}, u32[]{:S(2)}, u32[]{:S(2)}) collective-permute-start(bf16[8,128,256]{2,1,0:T(8,128)(2,1)S(1)} %bitcast.19), channel_id=1, source_target_pairs={{0,24},{4,100},{8,0},{12,108},{16,8},{20,116},{24,16},{28,124},{32... | collective-permute-start | bytes 1572872 | tf_op jit(solution)/shard_map/ppermute | solution.py:40
  75.5 2.7 %collective-permute-start.5 = (s32[64,2]{0,1:T(2,128)S(1)}, s32[64,2]{0,1:T(2,128)S(1)}, u32[]{:S(2)}, u32[]{:S(2)}) collective-permute-start(s32[64,2]{0,1:T(2,128)S(1)} %pad_add_fusion.1), channel_id=1, source_target_pairs={{0,64},{4,20},{8,72},{12,28},{16,80},{20,4},{24,88},{28,12},{32,96... | collective-permute-start | bytes 1544 | tf_op jit(solution)/shard_map/ppermute | solution.py:44
  78.3 2.1 collective-permute-done.6
  80.8 3.1 %collective-permute-done.4 = s32[64,2]{0,1:T(2,128)S(1)} collective-permute-done((s32[64,2]{0,1:T(2,128)S(1)}, s32[64,2]{0,1:T(2,128)S(1)}, u32[]{:S(2)}, u32[]{:S(2)}) %collective-permute-start.4) | collective-permute-done | bytes 544 | tf_op jit(solution)/shard_map/ppermute | solution.py:44
  86.7 3.7 %collective-permute-done.26.rest_1_ = bf16[8,128,256]{2,1,0:T(8,128)(2,1)S(1)} collective-permute-done((bf16[8,128,256]{2,1,0:T(8,128)(2,1)S(1)}, bf16[8,128,256]{2,1,0:T(8,128)(2,1)S(1)}, u32[]{:S(2)}, u32[]{:S(2)}) %collective-permute-start.26) | collective-permute-done | bytes 524320 | tf_op jit(solution)/shard_map/ppermute | solution.py:40
  91.2 2.7 %collective-permute-start.35 = (bf16[8,128,256]{2,1,0:T(8,128)(2,1)S(1)}, bf16[8,128,256]{2,1,0:T(8,128)(2,1)S(1)}, u32[]{:S(2)}, u32[]{:S(2)}) collective-permute-start(bf16[8,128,256]{2,1,0:T(8,128)(2,1)S(1)} %get-tuple-element.72), channel_id=1, source_target_pairs={{0,64},{4,20},{8,72},{12,28},{16,80},{20,4},{24,88},{28,12},{32,96... | collective-permute-start | bytes 1572872 | tf_op jit(solution)/shard_map/ppermute | solution.py:44
  98.2 9.0 %collective-permute-done.33 = bf16[8,128,256]{2,1,0:T(8,128)(2,1)S(1)} collective-permute-done((bf16[8,128,256]{2,1,0:T(8,128)(2,1)S(1)}, bf16[8,128,256]{2,1,0:T(8,128)(2,1)S(1)}, u32[]{:S(2)}, u32[]{:S(2)}) %collective-permute-start.33) | collective-permute-done | bytes 524320 | tf_op jit(solution)/shard_map/ppermute | solution.py:44
  108.1 10.3 %collective-permute-done.30.rest_1_ = bf16[8,128,256]{2,1,0:T(8,128)(2,1)S(1)} collective-permute-done((bf16[8,128,256]{2,1,0:T(8,128)(2,1)S(1)}, bf16[8,128,256]{2,1,0:T(8,128)(2,1)S(1)}, u32[]{:S(2)}, u32[]{:S(2)}) %collective-permute-start.30) | collective-permute-done | bytes 524320 | tf_op jit(solution)/shard_map/ppermute | solution.py:44
  121.6 21.5 %attention.1 = (bf16[512,1024]{1,0:T(8,128)(2,1)}, bf16[512,256]{1,0:T(8,128)(2,1)}, bf16[8,128,256]{2,1,0:T(8,128)(2,1)S(1)}, bf16[8,128,256]{2,1,0:T(8,128)(2,...) custom-call(s32[64]{0:T(128)S(1)} %select_reduce_fusion.rest_4_.taken_, ...), custom_call_target="tpu_custom_call" | custom-call | flops 6039797760 | bytes 8912896 | tf_op jit(solution)/shard_map/attention/pallas_call | solution.py:387
  148.5 3.9 %collective-permute-done.40.rest_2_ = bf16[8,128,256]{2,1,0:T(8,128)(2,1)S(1)} collective-permute-done((bf16[8,128,256]{2,1,0:T(8,128)(2,1)S(1)}, bf16[8,128,256]{2,1,0:T(8,128)(2,1)S(1)}, u32[]{:S(2)}, u32[]{:S(2)}) %collective-permute-start.40) | collective-permute-done | bytes 524320 | tf_op jit(solution)/shard_map/ppermute | solution.py:44
  153.4 2.2 collective-permute-done.42.rest_4_
  155.6 5.2 %collective-permute-start.41 = (bf16[8,128,256]{2,1,0:T(8,128)(2,1)S(1)}, bf16[8,128,256]{2,1,0:T(8,128)(2,1)S(1)}, u32[]{:S(2)}, u32[]{:S(2)}) collective-permute-start(bf16[8,128,256]{2,1,0:T(8,128)(2,1)S(1)} %get-tuple-element.99), channel_id=1, source_target_pairs={{0,96},{4,28},{8,104},{12,4},{16,112},{20,12},{24,120},{28,20},{32... | collective-permute-start | bytes 1572872 | tf_op jit(solution)/shard_map/ppermute | solution.py:44
  160.8 5.6 %collective-permute-done.45.rest_7_ = bf16[8,128,256]{2,1,0:T(8,128)(2,1)S(1)} collective-permute-done((bf16[8,128,256]{2,1,0:T(8,128)(2,1)S(1)}, bf16[8,128,256]{2,1,0:T(8,128)(2,1)S(1)}, u32[]{:S(2)}, u32[]{:S(2)}) %collective-permute-start.45) | collective-permute-done | bytes 524320 | tf_op jit(solution)/shard_map/ppermute | solution.py:44
  166.4 6.0 %collective-permute-done.43.rest_5_ = bf16[8,128,256]{2,1,0:T(8,128)(2,1)S(1)} collective-permute-done((bf16[8,128,256]{2,1,0:T(8,128)(2,1)S(1)}, bf16[8,128,256]{2,1,0:T(8,128)(2,1)S(1)}, u32[]{:S(2)}, u32[]{:S(2)}) %collective-permute-start.43) | collective-permute-done | bytes 524320 | tf_op jit(solution)/shard_map/ppermute | solution.py:44
  172.4 2.4 add_blocks.1
  176.9 7.2 %collective-permute-done.46.left_ref = bf16[8,128,256]{2,1,0:T(8,128)(2,1)S(1)} collective-permute-done((bf16[8,128,256]{2,1,0:T(8,128)(2,1)S(1)}, bf16[8,128,256]{2,1,0:T(8,128)(2,1)S(1)}, u32[]{:S(2)}, u32[]{:S(2)}) %collective-permute-start.46) | collective-permute-done | bytes 524320 | tf_op jit(solution)/shard_map/ppermute | solution.py:40
  184.0 2.5 %collective-permute-done.47.far_ref = bf16[8,128,256]{2,1,0:T(8,128)(2,1)S(1)} collective-permute-done((bf16[8,128,256]{2,1,0:T(8,128)(2,1)S(1)}, bf16[8,128,256]{2,1,0:T(8,128)(2,1)S(1)}, u32[]{:S(2)}, u32[]{:S(2)}) %collective-permute-start.47) | collective-permute-done | bytes 524320 | tf_op jit(solution)/shard_map/ppermute | solution.py:40
  186.5 5.5 %collective-permute-done.48.right_ref = bf16[8,128,256]{2,1,0:T(8,128)(2,1)S(1)} collective-permute-done((bf16[8,128,256]{2,1,0:T(8,128)(2,1)S(1)}, bf16[8,128,256]{2,1,0:T(8,128)(2,1)S(1)}, u32[]{:S(2)}, u32[]{:S(2)}) %collective-permute-start.48) | collective-permute-done | bytes 524320 | tf_op jit(solution)/shard_map/ppermute | solution.py:40
  192.5 3.5 %collective-permute-start.57 = (bf16[128,1024]{1,0:T(8,128)(2,1)S(1)}, bf16[128,1024]{1,0:T(8,128)(2,1)S(1)}, u32[]{:S(2)}, u32[]{:S(2)}) collective-permute-start(bf16[128,1024]{1,0:T(8,128)(2,1)S(1)} %get-tuple-element.86.refs_0_), channel_id=1, source_target_pairs={{0,3},{1,0},{2,1},{3,2},{4,7},{5,4},{6,5},{7,6},{8,11},{9,8},{10,9... | collective-permute-start | bytes 786440 | tf_op jit(solution)/shard_map/ppermute | solution.py:48
  196.1 3.2 %collective-permute-start.52 = (bf16[128,1024]{1,0:T(8,128)(2,1)S(1)}, bf16[128,1024]{1,0:T(8,128)(2,1)S(1)}, u32[]{:S(2)}, u32[]{:S(2)}) collective-permute-start(bf16[128,1024]{1,0:T(8,128)(2,1)S(1)} %collective-permute-done.49.refs_0_), channel_id=1, source_target_pairs={{0,3},{1,0},{2,1},{3,2},{4,7},{5,4},{6,5},{7,6},{8,11},{9,8},{10,9... | collective-permute-start | bytes 786440 | tf_op jit(solution)/shard_map/ppermute | solution.py:48
  199.3 3.4 %collective-permute-done.57.refs_4_ = bf16[128,1024]{1,0:T(8,128)(2,1)S(1)} collective-permute-done((bf16[128,1024]{1,0:T(8,128)(2,1)S(1)}, bf16[128,1024]{1,0:T(8,128)(2,1)S(1)}, u32[]{:S(2)}, u32[]{:S(2)}) %collective-permute-start.57) | collective-permute-done | bytes 262176 | tf_op jit(solution)/shard_map/ppermute | solution.py:48
  202.7 3.8 %collective-permute-start.58 = (bf16[64,1024]{1,0:T(8,128)(2,1)S(1)}, bf16[64,1024]{1,0:T(8,128)(2,1)S(1)}, u32[]{:S(2)}, u32[]{:S(2)}) collective-permute-start(bf16[64,1024]{1,0:T(8,128)(2,1)S(1)} %slice.62), channel_id=1, source_target_pairs={{0,3},{1,0},{2,1},{3,2},{4,7},{5,4},{6,5},{7,6},{8,11},{9,8},{10,9... | collective-permute-start | bytes 393224 | tf_op jit(solution)/shard_map/ppermute | solution.py:48
  206.6 1.7 collective-permute-done.52.refs_4_
  208.3 3.8 %collective-permute-start.53 = (bf16[64,1024]{1,0:T(8,128)(2,1)S(1)}, bf16[64,1024]{1,0:T(8,128)(2,1)S(1)}, u32[]{:S(2)}, u32[]{:S(2)}) collective-permute-start(bf16[64,1024]{1,0:T(8,128)(2,1)S(1)} %slice.60), channel_id=1, source_target_pairs={{0,3},{1,0},{2,1},{3,2},{4,7},{5,4},{6,5},{7,6},{8,11},{9,8},{10,9... | collective-permute-start | bytes 393224 | tf_op jit(solution)/shard_map/ppermute | solution.py:48
  212.2 1.9 collective-permute-done.56.refs_2_
  214.1 3.3 %first_weight_product.1.refs_6_ = f32[512,2048]{1,0:T(8,128)S(1)} custom-call(bf16[128,1024]{1,0:T(8,128)(2,1)S(1)} %get-tuple-element.86.refs_0_, bf16[128,1024]{1,0:T(8,128)(2,1)S(1)} %collective-permute-done.55.refs_1_, bf16[64,1024]{1,0:T(8,128)(2,1)S(1)} %collective-permute-done.56.refs_2_, bf16[64,1024]{1,0:T(8,128)(2,1)S(1)} %collective-permute-done.58.refs_3_, ...), custom_call_target="tpu_custom_call" | custom-call | flops 2147483648 | bytes 8388608 | tf_op jit(solution)/shard_map/first_weight_product/pallas_call | solution.py:271
  218.4 3.6 %second_weight_product.1 = (f32[4,32,2048]{2,1,0:T(8,128)S(1)}, bf16[4,32,2048]{2,1,0:T(8,128)(2,1)S(1)}, bf16[4,32,2048]{2,1,0:T(8,128)(2,1)S(1)}, bf16[4,32,2048]{2,1,0:T(8,128)(2,1)S(1)}) custom-call(bf16[128,1024]{1,0:T(8,128)(2,1)S(1)} %collective-permute-done.49.refs_0_, bf16[128,1024]{1,0:T(8,128)(2,1)S(1)} %collective-permute-done.50.refs_1_, ...), custom_call_target="tpu_custom_call" | custom-call | flops 2147483648 | bytes 8388608 | tf_op jit(solution)/shard_map/second_weight_product/pallas_call | solution.py:280
  222.0 3.2 %collective-permute-start.60 = (bf16[4,32,2048]{2,1,0:T(8,128)(2,1)S(1)}, bf16[4,32,2048]{2,1,0:T(8,128)(2,1)S(1)}, u32[]{:S(2)}, u32[]{:S(2)}) collective-permute-start(bf16[4,32,2048]{2,1,0:T(8,128)(2,1)S(1)} %get-tuple-element.89), channel_id=1, source_target_pairs={{0,24},{4,100},{8,0},{12,108},{16,8},{20,116},{24,16},{28,124},{32... | collective-permute-start | bytes 1572872 | tf_op jit(solution)/shard_map/ppermute | solution.py:40
  225.3 12.8 %collective-permute-done.59 = bf16[4,32,2048]{2,1,0:T(8,128)(2,1)S(1)} collective-permute-done((bf16[4,32,2048]{2,1,0:T(8,128)(2,1)S(1)}, bf16[4,32,2048]{2,1,0:T(8,128)(2,1)S(1)}, u32[]{:S(2)}, u32[]{:S(2)}) %collective-permute-start.59) | collective-permute-done | bytes 524320 | tf_op jit(solution)/shard_map/ppermute | solution.py:40
  239.5 2.2 collective-permute-start.63
  241.7 4.3 %collective-permute-done.62 = bf16[32,2048]{1,0:T(8,128)(2,1)S(1)} collective-permute-done((bf16[32,2048]{1,0:T(8,128)(2,1)S(1)}, bf16[32,2048]{1,0:T(8,128)(2,1)S(1)}, u32[]{:S(2)}, u32[]{:S(2)}) %collective-permute-start.62) | collective-permute-done | bytes 131104 | tf_op jit(solution)/shard_map/ppermute | solution.py:44
  (138 shorter events, 39.9 us)
Async XLA Ops:
  0.6 9.2 %collective-permute-start.1 = (bf16[32,2048]{1,0:T(8,128)(2,1)}, bf16[32,2048]{1,0:T(8,128)(2,1)S(1)}, u32[]{:S(2)}, u32[]{:S(2)}) collective-permute-start(bf16[32,2048]{1,0:T(8,128)(2,1)} %param.8), channel_id=1, source_target_pairs={{0,16},{4,68},{8,24},{12,76},{16,0},{20,84},{24,8},{28,92},{32,48}... | collective-permute-start | bytes 393224 | tf_op jit(solution)/shard_map/ppermute | solution.py:40
  12.0 15.4 %collective-permute-start.9 = (bf16[128,2048]{1,0:T(8,128)(2,1)S(1)}, bf16[128,2048]{1,0:T(8,128)(2,1)S(1)}, u32[]{:S(2)}, u32[]{:S(2)}) collective-permute-start(bf16[128,2048]{1,0:T(8,128)(2,1)S(1)} %pad_maximum_fusion.rest_0_), channel_id=1, source_target_pairs={{0,96},{4,28},{8,104},{12,4},{16,112},{20,12},{24,120},{28,20},{32... | collective-permute-start | bytes 1572872 | tf_op jit(solution)/shard_map/ppermute | solution.py:44
  15.1 12.3 %collective-permute-start.8 = (bf16[128,2048]{1,0:T(8,128)(2,1)S(1)}, bf16[128,2048]{1,0:T(8,128)(2,1)S(1)}, u32[]{:S(2)}, u32[]{:S(2)}) collective-permute-start(bf16[128,2048]{1,0:T(8,128)(2,1)S(1)} %pad_maximum_fusion.rest_0_), channel_id=1, source_target_pairs={{0,64},{4,20},{8,72},{12,28},{16,80},{20,4},{24,88},{28,12},{32,96... | collective-permute-start | bytes 1572872 | tf_op jit(solution)/shard_map/ppermute | solution.py:44
  15.7 15.7 %collective-permute-start.7 = (bf16[128,2048]{1,0:T(8,128)(2,1)S(1)}, bf16[128,2048]{1,0:T(8,128)(2,1)S(1)}, u32[]{:S(2)}, u32[]{:S(2)}) collective-permute-start(bf16[128,2048]{1,0:T(8,128)(2,1)S(1)} %pad_maximum_fusion.rest_0_), channel_id=1, source_target_pairs={{0,32},{4,12},{8,40},{12,20},{16,48},{20,28},{24,56},{28,4},{32,64... | collective-permute-start | bytes 1572872 | tf_op jit(solution)/shard_map/ppermute | solution.py:44
  16.7 14.7 %collective-permute-start.10 = (bf16[128,2048]{1,0:T(8,128)(2,1)S(1)}, bf16[128,2048]{1,0:T(8,128)(2,1)S(1)}, u32[]{:S(2)}, u32[]{:S(2)}) collective-permute-start(bf16[128,2048]{1,0:T(8,128)(2,1)S(1)} %pad_maximum_fusion.rest_0_), channel_id=1, source_target_pairs={{0,4},{4,0},{8,12},{12,8},{16,20},{20,16},{24,28},{28,24},{32,36},... | collective-permute-start | bytes 1572872 | tf_op jit(solution)/shard_map/ppermute | solution.py:52
  40.1 9.4 %collective-permute-start.14 = (bf16[256,384]{1,0:T(8,128)(2,1)S(1)}, bf16[256,384]{1,0:T(8,128)(2,1)S(1)}, u32[]{:S(2)}, u32[]{:S(2)}) collective-permute-start(bf16[256,384]{1,0:T(8,128)(2,1)S(1)} %get-tuple-element.49), channel_id=1, source_target_pairs={{0,1},{1,2},{2,3},{3,0},{4,5},{5,6},{6,7},{7,4},{8,9},{9,10},{10,1... | collective-permute-start | bytes 589832 | tf_op jit(solution)/shard_map/ppermute | solution.py:48
  41.6 8.0 %collective-permute-start.17 = (bf16[256,384]{1,0:T(8,128)(2,1)S(1)}, bf16[256,384]{1,0:T(8,128)(2,1)S(1)}, u32[]{:S(2)}, u32[]{:S(2)}) collective-permute-start(bf16[256,384]{1,0:T(8,128)(2,1)S(1)} %get-tuple-element.52), channel_id=1, source_target_pairs={{0,3},{1,0},{2,1},{3,2},{4,7},{5,4},{6,5},{7,6},{8,11},{9,8},{10,9... | collective-permute-start | bytes 589832 | tf_op jit(solution)/shard_map/ppermute | solution.py:48
  46.1 9.0 %collective-permute-start.20 = (bf16[256,384]{1,0:T(8,128)(2,1)S(1)}, bf16[256,384]{1,0:T(8,128)(2,1)S(1)}, u32[]{:S(2)}, u32[]{:S(2)}) collective-permute-start(bf16[256,384]{1,0:T(8,128)(2,1)S(1)} %get-tuple-element.56), channel_id=1, source_target_pairs={{0,1},{1,2},{2,3},{3,0},{4,5},{5,6},{6,7},{7,4},{8,9},{9,10},{10,1... | collective-permute-start | bytes 589832 | tf_op jit(solution)/shard_map/ppermute | solution.py:48
  46.5 8.8 %collective-permute-start.23 = (bf16[256,384]{1,0:T(8,128)(2,1)S(1)}, bf16[256,384]{1,0:T(8,128)(2,1)S(1)}, u32[]{:S(2)}, u32[]{:S(2)}) collective-permute-start(bf16[256,384]{1,0:T(8,128)(2,1)S(1)} %get-tuple-element.59), channel_id=1, source_target_pairs={{0,3},{1,0},{2,1},{3,2},{4,7},{5,4},{6,5},{7,6},{8,11},{9,8},{10,9... | collective-permute-start | bytes 589832 | tf_op jit(solution)/shard_map/ppermute | solution.py:48
  49.5 9.8 %collective-permute-start.15 = (bf16[256,384]{1,0:T(8,128)(2,1)S(1)}, bf16[256,384]{1,0:T(8,128)(2,1)S(1)}, u32[]{:S(2)}, u32[]{:S(2)}) collective-permute-start(bf16[256,384]{1,0:T(8,128)(2,1)S(1)} %relay.8), channel_id=1, source_target_pairs={{0,1},{1,2},{2,3},{3,0},{4,5},{5,6},{6,7},{7,4},{8,9},{9,10},{10,1... | collective-permute-start | bytes 589832 | tf_op jit(solution)/shard_map/ppermute | solution.py:48
  49.7 9.8 %collective-permute-start.18 = (bf16[256,384]{1,0:T(8,128)(2,1)S(1)}, bf16[256,384]{1,0:T(8,128)(2,1)S(1)}, u32[]{:S(2)}, u32[]{:S(2)}) collective-permute-start(bf16[256,384]{1,0:T(8,128)(2,1)S(1)} %relay.10), channel_id=1, source_target_pairs={{0,3},{1,0},{2,1},{3,2},{4,7},{5,4},{6,5},{7,6},{8,11},{9,8},{10,9... | collective-permute-start | bytes 589832 | tf_op jit(solution)/shard_map/ppermute | solution.py:48
  55.1 8.6 %collective-permute-start.21 = (bf16[256,384]{1,0:T(8,128)(2,1)S(1)}, bf16[256,384]{1,0:T(8,128)(2,1)S(1)}, u32[]{:S(2)}, u32[]{:S(2)}) collective-permute-start(bf16[256,384]{1,0:T(8,128)(2,1)S(1)} %relay.12), channel_id=1, source_target_pairs={{0,1},{1,2},{2,3},{3,0},{4,5},{5,6},{6,7},{7,4},{8,9},{9,10},{10,1... | collective-permute-start | bytes 589832 | tf_op jit(solution)/shard_map/ppermute | solution.py:48
  55.3 8.6 %collective-permute-start.24 = (bf16[256,384]{1,0:T(8,128)(2,1)S(1)}, bf16[256,384]{1,0:T(8,128)(2,1)S(1)}, u32[]{:S(2)}, u32[]{:S(2)}) collective-permute-start(bf16[256,384]{1,0:T(8,128)(2,1)S(1)} %relay.14), channel_id=1, source_target_pairs={{0,3},{1,0},{2,1},{3,2},{4,7},{5,4},{6,5},{7,6},{8,11},{9,8},{10,9... | collective-permute-start | bytes 589832 | tf_op jit(solution)/shard_map/ppermute | solution.py:48
  59.3 9.1 %collective-permute-start.16 = (bf16[256,384]{1,0:T(8,128)(2,1)S(1)}, bf16[256,384]{1,0:T(8,128)(2,1)S(1)}, u32[]{:S(2)}, u32[]{:S(2)}) collective-permute-start(bf16[256,384]{1,0:T(8,128)(2,1)S(1)} %relay.9), channel_id=1, source_target_pairs={{0,1},{1,2},{2,3},{3,0},{4,5},{5,6},{6,7},{7,4},{8,9},{9,10},{10,1... | collective-permute-start | bytes 589832 | tf_op jit(solution)/shard_map/ppermute | solution.py:48
  59.5 9.0 %collective-permute-start.19 = (bf16[256,384]{1,0:T(8,128)(2,1)S(1)}, bf16[256,384]{1,0:T(8,128)(2,1)S(1)}, u32[]{:S(2)}, u32[]{:S(2)}) collective-permute-start(bf16[256,384]{1,0:T(8,128)(2,1)S(1)} %relay.11), channel_id=1, source_target_pairs={{0,3},{1,0},{2,1},{3,2},{4,7},{5,4},{6,5},{7,6},{8,11},{9,8},{10,9... | collective-permute-start | bytes 589832 | tf_op jit(solution)/shard_map/ppermute | solution.py:48
  67.3 8.1 %collective-permute-start.3 = (s32[32,2]{0,1:T(2,128)S(1)}, s32[32,2]{0,1:T(2,128)S(1)}, u32[]{:S(2)}, u32[]{:S(2)}) collective-permute-start(s32[32,2]{0,1:T(2,128)S(1)} %broadcast_add_fusion.1), channel_id=1, source_target_pairs={{0,4},{4,0},{8,12},{12,8},{16,20},{20,16},{24,28},{28,24},{32,36},... | collective-permute-start | bytes 776 | tf_op jit(solution)/shard_map/ppermute | solution.py:52
  70.9 15.8 %collective-permute-start.28 = (bf16[8,128,256]{2,1,0:T(8,128)(2,1)S(1)}, bf16[8,128,256]{2,1,0:T(8,128)(2,1)S(1)}, u32[]{:S(2)}, u32[]{:S(2)}) collective-permute-start(bf16[8,128,256]{2,1,0:T(8,128)(2,1)S(1)} %bitcast.19), channel_id=1, source_target_pairs={{0,24},{4,100},{8,0},{12,108},{16,8},{20,116},{24,16},{28,124},{32... | collective-permute-start | bytes 1572872 | tf_op jit(solution)/shard_map/ppermute | solution.py:40
  74.3 12.3 %collective-permute-start.27 = (bf16[8,128,256]{2,1,0:T(8,128)(2,1)S(1)}, bf16[8,128,256]{2,1,0:T(8,128)(2,1)S(1)}, u32[]{:S(2)}, u32[]{:S(2)}) collective-permute-start(bf16[8,128,256]{2,1,0:T(8,128)(2,1)S(1)} %bitcast.20), channel_id=1, source_target_pairs={{0,16},{4,68},{8,24},{12,76},{16,0},{20,84},{24,8},{28,92},{32,48}... | collective-permute-start | bytes 1572872 | tf_op jit(solution)/shard_map/ppermute | solution.py:40
  74.3 16.0 %collective-permute-start.26 = (bf16[8,128,256]{2,1,0:T(8,128)(2,1)S(1)}, bf16[8,128,256]{2,1,0:T(8,128)(2,1)S(1)}, u32[]{:S(2)}, u32[]{:S(2)}) collective-permute-start(bf16[8,128,256]{2,1,0:T(8,128)(2,1)S(1)} %bitcast.21), channel_id=1, source_target_pairs={{0,8},{4,36},{8,16},{12,44},{16,24},{20,52},{24,0},{28,60},{32,40}... | collective-permute-start | bytes 1572872 | tf_op jit(solution)/shard_map/ppermute | solution.py:40
  91.1 16.1 %collective-permute-start.33 = (bf16[8,128,256]{2,1,0:T(8,128)(2,1)S(1)}, bf16[8,128,256]{2,1,0:T(8,128)(2,1)S(1)}, u32[]{:S(2)}, u32[]{:S(2)}) collective-permute-start(bf16[8,128,256]{2,1,0:T(8,128)(2,1)S(1)} %get-tuple-element.71), channel_id=1, source_target_pairs={{0,32},{4,12},{8,40},{12,20},{16,48},{20,28},{24,56},{28,4},{32,64... | collective-permute-start | bytes 1572872 | tf_op jit(solution)/shard_map/ppermute | solution.py:44
  91.2 16.0 %collective-permute-start.35 = (bf16[8,128,256]{2,1,0:T(8,128)(2,1)S(1)}, bf16[8,128,256]{2,1,0:T(8,128)(2,1)S(1)}, u32[]{:S(2)}, u32[]{:S(2)}) collective-permute-start(bf16[8,128,256]{2,1,0:T(8,128)(2,1)S(1)} %get-tuple-element.72), channel_id=1, source_target_pairs={{0,64},{4,20},{8,72},{12,28},{16,80},{20,4},{24,88},{28,12},{32,96... | collective-permute-start | bytes 1572872 | tf_op jit(solution)/shard_map/ppermute | solution.py:44
  93.9 14.2 %collective-permute-start.37 = (bf16[8,128,256]{2,1,0:T(8,128)(2,1)S(1)}, bf16[8,128,256]{2,1,0:T(8,128)(2,1)S(1)}, u32[]{:S(2)}, u32[]{:S(2)}) collective-permute-start(bf16[8,128,256]{2,1,0:T(8,128)(2,1)S(1)} %get-tuple-element.73), channel_id=1, source_target_pairs={{0,96},{4,28},{8,104},{12,4},{16,112},{20,12},{24,120},{28,20},{32... | collective-permute-start | bytes 1572872 | tf_op jit(solution)/shard_map/ppermute | solution.py:44
  95.2 23.3 %collective-permute-start.30 = (bf16[8,128,256]{2,1,0:T(8,128)(2,1)S(1)}, bf16[8,128,256]{2,1,0:T(8,128)(2,1)S(1)}, u32[]{:S(2)}, u32[]{:S(2)}) collective-permute-start(bf16[8,128,256]{2,1,0:T(8,128)(2,1)S(1)} %get-tuple-element.68), channel_id=1, source_target_pairs={{0,32},{4,12},{8,40},{12,20},{16,48},{20,28},{24,56},{28,4},{32,64... | collective-permute-start | bytes 1572872 | tf_op jit(solution)/shard_map/ppermute | solution.py:44
  96.7 21.8 %collective-permute-start.31 = (bf16[8,128,256]{2,1,0:T(8,128)(2,1)S(1)}, bf16[8,128,256]{2,1,0:T(8,128)(2,1)S(1)}, u32[]{:S(2)}, u32[]{:S(2)}) collective-permute-start(bf16[8,128,256]{2,1,0:T(8,128)(2,1)S(1)} %get-tuple-element.69), channel_id=1, source_target_pairs={{0,64},{4,20},{8,72},{12,28},{16,80},{20,4},{24,88},{28,12},{32,96... | collective-permute-start | bytes 1572872 | tf_op jit(solution)/shard_map/ppermute | solution.py:44
  107.2 12.2 %collective-permute-start.32 = (bf16[8,128,256]{2,1,0:T(8,128)(2,1)S(1)}, bf16[8,128,256]{2,1,0:T(8,128)(2,1)S(1)}, u32[]{:S(2)}, u32[]{:S(2)}) collective-permute-start(bf16[8,128,256]{2,1,0:T(8,128)(2,1)S(1)} %get-tuple-element.70), channel_id=1, source_target_pairs={{0,96},{4,28},{8,104},{12,4},{16,112},{20,12},{24,120},{28,20},{32... | collective-permute-start | bytes 1572872 | tf_op jit(solution)/shard_map/ppermute | solution.py:44
  107.2 12.2 %collective-permute-start.34 = (bf16[8,128,256]{2,1,0:T(8,128)(2,1)S(1)}, bf16[8,128,256]{2,1,0:T(8,128)(2,1)S(1)}, u32[]{:S(2)}, u32[]{:S(2)}) collective-permute-start(bf16[8,128,256]{2,1,0:T(8,128)(2,1)S(1)} %collective-permute-done.33), channel_id=1, source_target_pairs={{0,4},{4,0},{8,12},{12,8},{16,20},{20,16},{24,28},{28,24},{32,36},... | collective-permute-start | bytes 1572872 | tf_op jit(solution)/shard_map/ppermute | solution.py:52
  108.1 11.3 %collective-permute-start.36 = (bf16[8,128,256]{2,1,0:T(8,128)(2,1)S(1)}, bf16[8,128,256]{2,1,0:T(8,128)(2,1)S(1)}, u32[]{:S(2)}, u32[]{:S(2)}) collective-permute-start(bf16[8,128,256]{2,1,0:T(8,128)(2,1)S(1)} %collective-permute-done.35), channel_id=1, source_target_pairs={{0,4},{4,0},{8,12},{12,8},{16,20},{20,16},{24,28},{28,24},{32,36},... | collective-permute-start | bytes 1572872 | tf_op jit(solution)/shard_map/ppermute | solution.py:52
  118.5 98.9 %collective-permute-start.54 = (bf16[1024,2048]{1,0:T(8,128)(2,1)S(1)}, bf16[1024,2048]{1,0:T(8,128)(2,1)S(1)}, u32[]{:S(2)}, u32[]{:S(2)}) collective-permute-start(bf16[1024,2048]{1,0:T(8,128)(2,1)S(1)} %copy-done.1), channel_id=1, source_target_pairs={{0,4},{4,0},{8,12},{12,8},{16,20},{20,16},{24,28},{28,24},{32,36},... | collective-permute-start | bytes 12582920 | tf_op jit(solution)/shard_map/ppermute | solution.py:52
  143.2 9.2 %collective-permute-start.40 = (bf16[8,128,256]{2,1,0:T(8,128)(2,1)S(1)}, bf16[8,128,256]{2,1,0:T(8,128)(2,1)S(1)}, u32[]{:S(2)}, u32[]{:S(2)}) collective-permute-start(bf16[8,128,256]{2,1,0:T(8,128)(2,1)S(1)} %get-tuple-element.78), channel_id=1, source_target_pairs={{0,96},{4,28},{8,104},{12,4},{16,112},{20,12},{24,120},{28,20},{32... | collective-permute-start | bytes 1572872 | tf_op jit(solution)/shard_map/ppermute | solution.py:44
  144.8 10.8 %collective-permute-start.42 = (bf16[8,128,256]{2,1,0:T(8,128)(2,1)S(1)}, bf16[8,128,256]{2,1,0:T(8,128)(2,1)S(1)}, u32[]{:S(2)}, u32[]{:S(2)}) collective-permute-start(bf16[8,128,256]{2,1,0:T(8,128)(2,1)S(1)} %get-tuple-element.79), channel_id=1, source_target_pairs={{0,64},{4,20},{8,72},{12,28},{16,80},{20,4},{24,88},{28,12},{32,96... | collective-permute-start | bytes 1572872 | tf_op jit(solution)/shard_map/ppermute | solution.py:44
  144.8 16.0 %collective-permute-start.44 = (bf16[8,128,256]{2,1,0:T(8,128)(2,1)S(1)}, bf16[8,128,256]{2,1,0:T(8,128)(2,1)S(1)}, u32[]{:S(2)}, u32[]{:S(2)}) collective-permute-start(bf16[8,128,256]{2,1,0:T(8,128)(2,1)S(1)} %get-tuple-element.80), channel_id=1, source_target_pairs={{0,32},{4,12},{8,40},{12,20},{16,48},{20,28},{24,56},{28,4},{32,64... | collective-permute-start | bytes 1572872 | tf_op jit(solution)/shard_map/ppermute | solution.py:44
  147.4 19.0 %collective-permute-start.45 = (bf16[8,128,256]{2,1,0:T(8,128)(2,1)S(1)}, bf16[8,128,256]{2,1,0:T(8,128)(2,1)S(1)}, u32[]{:S(2)}, u32[]{:S(2)}) collective-permute-start(bf16[8,128,256]{2,1,0:T(8,128)(2,1)S(1)} %get-tuple-element.97), channel_id=1, source_target_pairs={{0,32},{4,12},{8,40},{12,20},{16,48},{20,28},{24,56},{28,4},{32,64... | collective-permute-start | bytes 1572872 | tf_op jit(solution)/shard_map/ppermute | solution.py:44
  152.4 20.0 %collective-permute-start.43 = (bf16[8,128,256]{2,1,0:T(8,128)(2,1)S(1)}, bf16[8,128,256]{2,1,0:T(8,128)(2,1)S(1)}, u32[]{:S(2)}, u32[]{:S(2)}) collective-permute-start(bf16[8,128,256]{2,1,0:T(8,128)(2,1)S(1)} %get-tuple-element.98), channel_id=1, source_target_pairs={{0,64},{4,20},{8,72},{12,28},{16,80},{20,4},{24,88},{28,12},{32,96... | collective-permute-start | bytes 1572872 | tf_op jit(solution)/shard_map/ppermute | solution.py:44
  155.6 16.8 %collective-permute-start.41 = (bf16[8,128,256]{2,1,0:T(8,128)(2,1)S(1)}, bf16[8,128,256]{2,1,0:T(8,128)(2,1)S(1)}, u32[]{:S(2)}, u32[]{:S(2)}) collective-permute-start(bf16[8,128,256]{2,1,0:T(8,128)(2,1)S(1)} %get-tuple-element.99), channel_id=1, source_target_pairs={{0,96},{4,28},{8,104},{12,4},{16,112},{20,12},{24,120},{28,20},{32... | collective-permute-start | bytes 1572872 | tf_op jit(solution)/shard_map/ppermute | solution.py:44
  174.8 9.3 %collective-permute-start.46 = (bf16[8,128,256]{2,1,0:T(8,128)(2,1)S(1)}, bf16[8,128,256]{2,1,0:T(8,128)(2,1)S(1)}, u32[]{:S(2)}, u32[]{:S(2)}) collective-permute-start(bf16[8,128,256]{2,1,0:T(8,128)(2,1)S(1)} %get-tuple-element.82), channel_id=1, source_target_pairs={{0,24},{4,100},{8,0},{12,108},{16,8},{20,116},{24,16},{28,124},{32... | collective-permute-start | bytes 1572872 | tf_op jit(solution)/shard_map/ppermute | solution.py:40
  175.7 10.8 %collective-permute-start.47 = (bf16[8,128,256]{2,1,0:T(8,128)(2,1)S(1)}, bf16[8,128,256]{2,1,0:T(8,128)(2,1)S(1)}, u32[]{:S(2)}, u32[]{:S(2)}) collective-permute-start(bf16[8,128,256]{2,1,0:T(8,128)(2,1)S(1)} %get-tuple-element.83), channel_id=1, source_target_pairs={{0,16},{4,68},{8,24},{12,76},{16,0},{20,84},{24,8},{28,92},{32,48}... | collective-permute-start | bytes 1572872 | tf_op jit(solution)/shard_map/ppermute | solution.py:40
  175.8 16.3 %collective-permute-start.48 = (bf16[8,128,256]{2,1,0:T(8,128)(2,1)S(1)}, bf16[8,128,256]{2,1,0:T(8,128)(2,1)S(1)}, u32[]{:S(2)}, u32[]{:S(2)}) collective-permute-start(bf16[8,128,256]{2,1,0:T(8,128)(2,1)S(1)} %get-tuple-element.84), channel_id=1, source_target_pairs={{0,8},{4,36},{8,16},{12,44},{16,24},{20,52},{24,0},{28,60},{32,40}... | collective-permute-start | bytes 1572872 | tf_op jit(solution)/shard_map/ppermute | solution.py:40
  192.5 10.2 %collective-permute-start.57 = (bf16[128,1024]{1,0:T(8,128)(2,1)S(1)}, bf16[128,1024]{1,0:T(8,128)(2,1)S(1)}, u32[]{:S(2)}, u32[]{:S(2)}) collective-permute-start(bf16[128,1024]{1,0:T(8,128)(2,1)S(1)} %get-tuple-element.86.refs_0_), channel_id=1, source_target_pairs={{0,3},{1,0},{2,1},{3,2},{4,7},{5,4},{6,5},{7,6},{8,11},{9,8},{10,9... | collective-permute-start | bytes 786440 | tf_op jit(solution)/shard_map/ppermute | solution.py:48
  196.1 10.4 %collective-permute-start.55 = (bf16[128,1024]{1,0:T(8,128)(2,1)S(1)}, bf16[128,1024]{1,0:T(8,128)(2,1)S(1)}, u32[]{:S(2)}, u32[]{:S(2)}) collective-permute-start(bf16[128,1024]{1,0:T(8,128)(2,1)S(1)} %get-tuple-element.86.refs_0_), channel_id=1, source_target_pairs={{0,1},{1,2},{2,3},{3,0},{4,5},{5,6},{6,7},{7,4},{8,9},{9,10},{10,1... | collective-permute-start | bytes 786440 | tf_op jit(solution)/shard_map/ppermute | solution.py:48
  196.1 12.2 %collective-permute-start.52 = (bf16[128,1024]{1,0:T(8,128)(2,1)S(1)}, bf16[128,1024]{1,0:T(8,128)(2,1)S(1)}, u32[]{:S(2)}, u32[]{:S(2)}) collective-permute-start(bf16[128,1024]{1,0:T(8,128)(2,1)S(1)} %collective-permute-done.49.refs_0_), channel_id=1, source_target_pairs={{0,3},{1,0},{2,1},{3,2},{4,7},{5,4},{6,5},{7,6},{8,11},{9,8},{10,9... | collective-permute-start | bytes 786440 | tf_op jit(solution)/shard_map/ppermute | solution.py:48
  199.3 12.8 %collective-permute-start.50 = (bf16[128,1024]{1,0:T(8,128)(2,1)S(1)}, bf16[128,1024]{1,0:T(8,128)(2,1)S(1)}, u32[]{:S(2)}, u32[]{:S(2)}) collective-permute-start(bf16[128,1024]{1,0:T(8,128)(2,1)S(1)} %collective-permute-done.49.refs_0_), channel_id=1, source_target_pairs={{0,1},{1,2},{2,3},{3,0},{4,5},{5,6},{6,7},{7,4},{8,9},{9,10},{10,1... | collective-permute-start | bytes 786440 | tf_op jit(solution)/shard_map/ppermute | solution.py:48
  202.7 9.5 %collective-permute-start.58 = (bf16[64,1024]{1,0:T(8,128)(2,1)S(1)}, bf16[64,1024]{1,0:T(8,128)(2,1)S(1)}, u32[]{:S(2)}, u32[]{:S(2)}) collective-permute-start(bf16[64,1024]{1,0:T(8,128)(2,1)S(1)} %slice.62), channel_id=1, source_target_pairs={{0,3},{1,0},{2,1},{3,2},{4,7},{5,4},{6,5},{7,6},{8,11},{9,8},{10,9... | collective-permute-start | bytes 393224 | tf_op jit(solution)/shard_map/ppermute | solution.py:48
  206.5 7.6 %collective-permute-start.56 = (bf16[64,1024]{1,0:T(8,128)(2,1)S(1)}, bf16[64,1024]{1,0:T(8,128)(2,1)S(1)}, u32[]{:S(2)}, u32[]{:S(2)}) collective-permute-start(bf16[64,1024]{1,0:T(8,128)(2,1)S(1)} %slice.61), channel_id=1, source_target_pairs={{0,1},{1,2},{2,3},{3,0},{4,5},{5,6},{6,7},{7,4},{8,9},{9,10},{10,1... | collective-permute-start | bytes 393224 | tf_op jit(solution)/shard_map/ppermute | solution.py:48
  208.3 9.0 %collective-permute-start.53 = (bf16[64,1024]{1,0:T(8,128)(2,1)S(1)}, bf16[64,1024]{1,0:T(8,128)(2,1)S(1)}, u32[]{:S(2)}, u32[]{:S(2)}) collective-permute-start(bf16[64,1024]{1,0:T(8,128)(2,1)S(1)} %slice.60), channel_id=1, source_target_pairs={{0,3},{1,0},{2,1},{3,2},{4,7},{5,4},{6,5},{7,6},{8,11},{9,8},{10,9... | collective-permute-start | bytes 393224 | tf_op jit(solution)/shard_map/ppermute | solution.py:48
  222.0 16.1 %collective-permute-start.59 = (bf16[4,32,2048]{2,1,0:T(8,128)(2,1)S(1)}, bf16[4,32,2048]{2,1,0:T(8,128)(2,1)S(1)}, u32[]{:S(2)}, u32[]{:S(2)}) collective-permute-start(bf16[4,32,2048]{2,1,0:T(8,128)(2,1)S(1)} %get-tuple-element.88), channel_id=1, source_target_pairs={{0,8},{4,36},{8,16},{12,44},{16,24},{20,52},{24,0},{28,60},{32,40}... | collective-permute-start | bytes 1572872 | tf_op jit(solution)/shard_map/ppermute | solution.py:40
  222.0 16.0 %collective-permute-start.60 = (bf16[4,32,2048]{2,1,0:T(8,128)(2,1)S(1)}, bf16[4,32,2048]{2,1,0:T(8,128)(2,1)S(1)}, u32[]{:S(2)}, u32[]{:S(2)}) collective-permute-start(bf16[4,32,2048]{2,1,0:T(8,128)(2,1)S(1)} %get-tuple-element.89), channel_id=1, source_target_pairs={{0,24},{4,100},{8,0},{12,108},{16,8},{20,116},{24,16},{28,124},{32... | collective-permute-start | bytes 1572872 | tf_op jit(solution)/shard_map/ppermute | solution.py:40
  225.3 12.8 %collective-permute-start.61 = (bf16[4,32,2048]{2,1,0:T(8,128)(2,1)S(1)}, bf16[4,32,2048]{2,1,0:T(8,128)(2,1)S(1)}, u32[]{:S(2)}, u32[]{:S(2)}) collective-permute-start(bf16[4,32,2048]{2,1,0:T(8,128)(2,1)S(1)} %get-tuple-element.90), channel_id=1, source_target_pairs={{0,16},{4,68},{8,24},{12,76},{16,0},{20,84},{24,8},{28,92},{32,48}... | collective-permute-start | bytes 1572872 | tf_op jit(solution)/shard_map/ppermute | solution.py:40
  238.4 7.7 %collective-permute-start.62 = (bf16[32,2048]{1,0:T(8,128)(2,1)S(1)}, bf16[32,2048]{1,0:T(8,128)(2,1)S(1)}, u32[]{:S(2)}, u32[]{:S(2)}) collective-permute-start(bf16[32,2048]{1,0:T(8,128)(2,1)S(1)} %get-tuple-element.101), channel_id=1, source_target_pairs={{0,32},{4,12},{8,40},{12,20},{16,48},{20,28},{24,56},{28,4},{32,64... | collective-permute-start | bytes 393224 | tf_op jit(solution)/shard_map/ppermute | solution.py:44
  (22 other events, 231.9 us)

commit v5 on v4

--- a/solution.py
+++ b/solution.py
@@ -328,8 +328,9 @@
                 def _():
                     query = lax.div(to, retrieved)
                     into = pl.ds(pl.multiple_of(lax.rem(to, retrieved) * PLEN, PLEN), PLEN)
-                    keys_at[query, into, :] = srcs[b][m, :, :HD]
-                    values_at[query, into, :] = srcs[b][m, :, HD:]
+                    at = slots + m if b == 2 else m
+                    keys_at[query, into, :] = srcs[b][at, :, :HD]
+                    values_at[query, into, :] = srcs[b][at, :, HD:]
 
     for g in range(group):
         q_st[pl.ds(g * HD, HD), :] = q_ref[:, g * HD : (g + 1) * HD]
@@ -415,26 +416,29 @@
     )(*places, queries, out_grad, query_kv, *sources)
 
 
-def pick_kernel(other, slot_of, *rest):
-    ring, outs = rest[:SIDE], rest[-SIDE:]
-    n = outs[0].shape[0]
-    for k in range(SIDE):
-        for m in range(n):
-            at = (2 * k + other) * n + m
-            outs[k][m] = ring[m // 2][jnp.maximum(slot_of[at], 0)]
-
-
-def pick(slot_of, ring, other, *earlier):
+def pick_kernel(groups, slot_of, *rest):
+    ring, outs = rest[:SIDE], rest[-len(groups) :]
+    n = slot_of.shape[0] // (2 * SIDE)
+    for group, out in zip(groups, outs):
+        for i, (k, other) in enumerate(group):
+            for m in range(n):
+                place = jnp.maximum(slot_of[(2 * k + other) * n + m], 0)
+                out[i * n + m] = ring[m // 2][place]
+
+
+def pick(slot_of, ring, groups, *earlier):
     n = slot_of.shape[0] // (2 * SIDE)
     whole = pl.BlockSpec(memory_space=pltpu.VMEM)
-    shape = jax.ShapeDtypeStruct((n,) + ring[0].shape[1:], BF)
+    shapes = [
+        jax.ShapeDtypeStruct((len(group) * n,) + ring[0].shape[1:], BF) for group in groups
+    ]
     return pl.pallas_call(
-        functools.partial(pick_kernel, other),
-        out_shape=[shape] * SIDE,
+        functools.partial(pick_kernel, groups),
+        out_shape=shapes,
         grid_spec=pltpu.PrefetchScalarGridSpec(
             num_scalar_prefetch=1,
             in_specs=[whole] * (SIDE + len(earlier)),
-            out_specs=[whole] * SIDE,
+            out_specs=[whole] * len(groups),
         ),
         compiler_params=pltpu.CompilerParams(vmem_limit_bytes=2 * 2**20),
         cost_estimate=pl.CostEstimate(
@@ -445,18 +449,21 @@
 
 
 def add_blocks_kernel(slot_of, *rest):
-    parts, outs, total = rest[: 2 * SIDE], rest[2 * SIDE : 3 * SIDE], rest[3 * SIDE]
-    n = parts[0].shape[0]
+    parts, outs, total = rest[: -SIDE - 1], rest[-SIDE - 1 : -1], rest[-1]
+    owners = SIDE * 2
     total[...] = jnp.zeros_like(total)
-    for p, part in enumerate(parts):
-
-        @pl.loop(0, n)
+    first = 0
+    for part in parts:
+
+        @pl.loop(0, part.shape[0])
         def _(m):
-            place = slot_of[p * n + m]
+            place = slot_of[first + m]
 
             @pl.when(place >= 0)
             def _():
-                total[lax.div(m, 2), place] += part[m].astype(F32)
+                total[lax.div(lax.rem(m, owners), 2), place] += part[m].astype(F32)
+
+        first += part.shape[0]
 
     outs[0][...] = total[0]
     for j in range(1, SIDE):
@@ -472,7 +479,7 @@
         + [jax.ShapeDtypeStruct(shape, BF)] * (SIDE - 1),
         grid_spec=pltpu.PrefetchScalarGridSpec(
             num_scalar_prefetch=1,
-            in_specs=[whole] * (2 * SIDE),
+            in_specs=[whole] * len(parts),
             out_specs=[whole] * SIDE,
             scratch_shapes=[pltpu.VMEM((SIDE,) + shape, F32)],
         ),
@@ -598,10 +605,16 @@
     )
     own = own.reshape(passages_here, PLEN, local_width)
     ring = ring_gather(own, send_first)
-    other = pick(served, ring, 1, places[0])
-    swapped = [swap_cores(other[0])] + [swap_cores(send_second(other[k], k)) for k in range(1, SIDE)]
-    same = pick(served, ring, 0, swapped[0])
-    same = [same[0]] + [send_second(same[k], k) for k in range(1, SIDE)]
+    both, *other = pick(served, ring, [[(2, 1), (2, 0)], [(0, 1)], [(1, 1)], [(3, 1)]])
+    both = send_second(both, 2)
+    swapped = [
+        swap_cores(other[0]),
+        swap_cores(send_second(other[1], 1)),
+        swap_cores(both),
+        swap_cores(send_second(other[2], 3)),
+    ]
+    same = pick(served, ring, [[(0, 0)], [(1, 0)], [(3, 0)]], swapped[0])
+    same = [same[0], send_second(same[1], 1), both, send_second(same[2], 3)]
     hidden_theirs = swap_cores(passage_hidden)
     half = SIDE * capacity
     grad_queries, own_grads, *grads = attention(

time: 248 us -> 249 us (level)
    ppermute x21 -> x20, waiting for transfers between devices: 63.3 us -> 65.5 us  [send_second(): return lax.ppermute(x, 'pas', ring_pairs(1, k))]
    ppermute x21 -> x20, starting transfers between devices: 26.9 us -> 28.4 us  [send_second(): return lax.ppermute(x, 'pas', ring_pairs(1, k))]
  transfers between devices with their start and end apart: 65 -> 64, of which waited for: 34 -> 34; matrix products, arithmetic and copies ran while one was open for 2% -> 2% of each run, Pallas kernels for 13% -> 13%
where the time goes in v5:
time: 249 us
  waiting for transfers between devices  117 us (47%)
  starting transfers between devices  81.8 us (33%)
  Pallas kernels  39.4 us (16%)
  local copies, waits for them, and re-layouts  5.96 us (2%)
  other arithmetic  3.96 us (2%)
    ppermute x20, waiting for transfers between devices, send_second(): return lax.ppermute(x, 'pas', ring_pairs(1, k))  65.5 us
    ppermute x20, starting transfers between devices, send_tp(): return lax.ppermute(x, 'tp', [(i, (i + k) % SIDE) for i in range(SIDE)])  34.7 us
    ppermute x12, waiting for transfers between devices, send_first(): return lax.ppermute(x, 'pas', ring_pairs(0, k))  32.9 us
    ppermute x20, starting transfers between devices, send_second(): return lax.ppermute(x, 'pas', ring_pairs(1, k))  28.4 us
    pallas_call x1, Pallas kernels, attention(): pl.pallas_call(functools.partial(attention_kernel, len(sources), len(out_...  21.7 us
    ppermute x12, starting transfers between devices, send_first(): return lax.ppermute(x, 'pas', ring_pairs(0, k))  17.1 us
    ppermute x20, waiting for transfers between devices, send_tp(): return lax.ppermute(x, 'tp', [(i, (i + k) % SIDE) for i in range(SIDE)])  15.2 us
    pallas_call x2, Pallas kernels, project(): pl.pallas_call(functools.partial(project_kernel, first, len(pieces)), out...  5.93 us
  transfers between devices with their start and end apart: 64, of which 34 were waited for; matrix products, arithmetic and copies ran while one was open for 2% of the time, Pallas kernels for 13%

profile of v5, /device:TPU:0, one launch (start us, length us, event | category | flops | bytes accessed | tf_op | source)
XLA Modules:
  0.0 249.0 jit_solution(18238712624831051165)
XLA Ops:
  0.6 4.0 %collective-permute-start.1 = (bf16[32,2048]{1,0:T(8,128)(2,1)}, bf16[32,2048]{1,0:T(8,128)(2,1)S(1)}, u32[]{:S(2)}, u32[]{:S(2)}) collective-permute-start(bf16[32,2048]{1,0:T(8,128)(2,1)} %param.8), channel_id=1, source_target_pairs={{0,16},{4,68},{8,24},{12,76},{16,0},{20,84},{24,8},{28,92},{32,48}... | collective-permute-start | bytes 393224 | tf_op jit(solution)/shard_map/ppermute | solution.py:40
  5.7 2.2 collective-permute-start.2
  12.0 3.1 %collective-permute-start.9 = (bf16[128,2048]{1,0:T(8,128)(2,1)S(1)}, bf16[128,2048]{1,0:T(8,128)(2,1)S(1)}, u32[]{:S(2)}, u32[]{:S(2)}) collective-permute-start(bf16[128,2048]{1,0:T(8,128)(2,1)S(1)} %pad_maximum_fusion.rest_0_), channel_id=1, source_target_pairs={{0,96},{4,28},{8,104},{12,4},{16,112},{20,12},{24,120},{28,20},{32... | collective-permute-start | bytes 1572872 | tf_op jit(solution)/shard_map/ppermute | solution.py:44
  16.7 10.7 %collective-permute-done.9.rest_3_ = bf16[128,2048]{1,0:T(8,128)(2,1)S(1)} collective-permute-done((bf16[128,2048]{1,0:T(8,128)(2,1)S(1)}, bf16[128,2048]{1,0:T(8,128)(2,1)S(1)}, u32[]{:S(2)}, u32[]{:S(2)}) %collective-permute-start.9) | collective-permute-done | bytes 524320 | tf_op jit(solution)/shard_map/ppermute | solution.py:44
  27.9 3.5 %collective-permute-done.7.rest_1_ = bf16[128,2048]{1,0:T(8,128)(2,1)S(1)} collective-permute-done((bf16[128,2048]{1,0:T(8,128)(2,1)S(1)}, bf16[128,2048]{1,0:T(8,128)(2,1)S(1)}, u32[]{:S(2)}, u32[]{:S(2)}) %collective-permute-start.7) | collective-permute-done | bytes 524320 | tf_op jit(solution)/shard_map/ppermute | solution.py:44
  31.4 1.9 collective-permute-done.11.rest_5_
  33.3 2.2 copy-done
  35.5 3.2 %project.2 = (f32[256,256]{1,0:T(8,128)S(1)}, f32[256,256]{1,0:T(8,128)S(1)}, f32[256,256]{1,0:T(8,128)S(1)}, bf16[256,384]{1,0:T(8,128)(2,1)S(1)}, f32[256,256]...) custom-call(bf16[1024,2048]{1,0:T(8,128)(2,1)S(1)} %copy-done, ...), custom_call_target="tpu_custom_call" | custom-call | flops 2147483648 | bytes 8388608 | tf_op jit(solution)/shard_map/project/pallas_call | solution.py:149
  42.0 2.7 %project.3 = (f32[256,256]{1,0:T(8,128)S(1)}, f32[256,256]{1,0:T(8,128)S(1)}, f32[256,256]{1,0:T(8,128)S(1)}, bf16[256,384]{1,0:T(8,128)(2,1)S(1)}, f32[256,256]...) custom-call(bf16[1024,2048]{1,0:T(8,128)(2,1)S(1)} %copy-done, ...), custom_call_target="tpu_custom_call" | custom-call | flops 2147483648 | bytes 8388608 | tf_op jit(solution)/shard_map/project/pallas_call | solution.py:149
  45.1 3.0 %collective-permute-start.23 = (bf16[256,384]{1,0:T(8,128)(2,1)S(1)}, bf16[256,384]{1,0:T(8,128)(2,1)S(1)}, u32[]{:S(2)}, u32[]{:S(2)}) collective-permute-start(bf16[256,384]{1,0:T(8,128)(2,1)S(1)} %get-tuple-element.58), channel_id=1, source_target_pairs={{0,3},{1,0},{2,1},{3,2},{4,7},{5,4},{6,5},{7,6},{8,11},{9,8},{10,9... | collective-permute-start | bytes 589832 | tf_op jit(solution)/shard_map/ppermute | solution.py:48
  48.3 3.3 %collective-permute-start.18 = (bf16[256,384]{1,0:T(8,128)(2,1)S(1)}, bf16[256,384]{1,0:T(8,128)(2,1)S(1)}, u32[]{:S(2)}, u32[]{:S(2)}) collective-permute-start(bf16[256,384]{1,0:T(8,128)(2,1)S(1)} %relay.10), channel_id=1, source_target_pairs={{0,3},{1,0},{2,1},{3,2},{4,7},{5,4},{6,5},{7,6},{8,11},{9,8},{10,9... | collective-permute-start | bytes 589832 | tf_op jit(solution)/shard_map/ppermute | solution.py:48
  51.6 2.2 collective-permute-done.20.got_ref
  54.0 3.3 %collective-permute-start.24 = (bf16[256,384]{1,0:T(8,128)(2,1)S(1)}, bf16[256,384]{1,0:T(8,128)(2,1)S(1)}, u32[]{:S(2)}, u32[]{:S(2)}) collective-permute-start(bf16[256,384]{1,0:T(8,128)(2,1)S(1)} %relay.14), channel_id=1, source_target_pairs={{0,3},{1,0},{2,1},{3,2},{4,7},{5,4},{6,5},{7,6},{8,11},{9,8},{10,9... | collective-permute-start | bytes 589832 | tf_op jit(solution)/shard_map/ppermute | solution.py:48
  58.2 3.3 %collective-permute-start.19 = (bf16[256,384]{1,0:T(8,128)(2,1)S(1)}, bf16[256,384]{1,0:T(8,128)(2,1)S(1)}, u32[]{:S(2)}, u32[]{:S(2)}) collective-permute-start(bf16[256,384]{1,0:T(8,128)(2,1)S(1)} %relay.11), channel_id=1, source_target_pairs={{0,3},{1,0},{2,1},{3,2},{4,7},{5,4},{6,5},{7,6},{8,11},{9,8},{10,9... | collective-permute-start | bytes 589832 | tf_op jit(solution)/shard_map/ppermute | solution.py:48
  62.6 3.4 %collective-permute-start.25 = (bf16[256,384]{1,0:T(8,128)(2,1)S(1)}, bf16[256,384]{1,0:T(8,128)(2,1)S(1)}, u32[]{:S(2)}, u32[]{:S(2)}) collective-permute-start(bf16[256,384]{1,0:T(8,128)(2,1)S(1)} %relay.15), channel_id=1, source_target_pairs={{0,3},{1,0},{2,1},{3,2},{4,7},{5,4},{6,5},{7,6},{8,11},{9,8},{10,9... | collective-permute-start | bytes 589832 | tf_op jit(solution)/shard_map/ppermute | solution.py:48
  67.2 2.3 collective-permute-done.22.refs_2_
  69.6 3.3 %collective-permute-start.28 = (bf16[8,128,256]{2,1,0:T(8,128)(2,1)S(1)}, bf16[8,128,256]{2,1,0:T(8,128)(2,1)S(1)}, u32[]{:S(2)}, u32[]{:S(2)}) collective-permute-start(bf16[8,128,256]{2,1,0:T(8,128)(2,1)S(1)} %bitcast.19), channel_id=1, source_target_pairs={{0,24},{4,100},{8,0},{12,108},{16,8},{20,116},{24,16},{28,124},{32... | collective-permute-start | bytes 1572872 | tf_op jit(solution)/shard_map/ppermute | solution.py:40
  75.3 2.7 %collective-permute-start.5 = (s32[64,2]{0,1:T(2,128)S(1)}, s32[64,2]{0,1:T(2,128)S(1)}, u32[]{:S(2)}, u32[]{:S(2)}) collective-permute-start(s32[64,2]{0,1:T(2,128)S(1)} %pad_add_fusion.1), channel_id=1, source_target_pairs={{0,64},{4,20},{8,72},{12,28},{16,80},{20,4},{24,88},{28,12},{32,96... | collective-permute-start | bytes 1544 | tf_op jit(solution)/shard_map/ppermute | solution.py:44
  78.0 2.1 collective-permute-done.6
  80.5 3.2 %collective-permute-done.4 = s32[64,2]{0,1:T(2,128)S(1)} collective-permute-done((s32[64,2]{0,1:T(2,128)S(1)}, s32[64,2]{0,1:T(2,128)S(1)}, u32[]{:S(2)}, u32[]{:S(2)}) %collective-permute-start.4) | collective-permute-done | bytes 544 | tf_op jit(solution)/shard_map/ppermute | solution.py:44
  85.2 3.7 %collective-permute-done.26.rest_1_ = bf16[8,128,256]{2,1,0:T(8,128)(2,1)S(1)} collective-permute-done((bf16[8,128,256]{2,1,0:T(8,128)(2,1)S(1)}, bf16[8,128,256]{2,1,0:T(8,128)(2,1)S(1)}, u32[]{:S(2)}, u32[]{:S(2)}) %collective-permute-start.26) | collective-permute-done | bytes 524320 | tf_op jit(solution)/shard_map/ppermute | solution.py:40
  93.6 12.5 %collective-permute-done.31.rest_2_ = bf16[16,128,256]{2,1,0:T(8,128)(2,1)S(1)} collective-permute-done((bf16[16,128,256]{2,1,0:T(8,128)(2,1)S(1)}, bf16[16,128,256]{2,1,0:T(8,128)(2,1)S(1)}, u32[]{:S(2)}, u32[]{:S(2)}) %collective-permute-start.31) | collective-permute-done | bytes 1048608 | tf_op jit(solution)/shard_map/ppermute | solution.py:44
  106.9 3.2 %collective-permute-start.32 = (bf16[8,128,256]{2,1,0:T(8,128)(2,1)S(1)}, bf16[8,128,256]{2,1,0:T(8,128)(2,1)S(1)}, u32[]{:S(2)}, u32[]{:S(2)}) collective-permute-start(bf16[8,128,256]{2,1,0:T(8,128)(2,1)S(1)} %get-tuple-element.69), channel_id=1, source_target_pairs={{0,96},{4,28},{8,104},{12,4},{16,112},{20,12},{24,120},{28,20},{32... | collective-permute-start | bytes 1572872 | tf_op jit(solution)/shard_map/ppermute | solution.py:44
  112.9 4.4 %collective-permute-done.30.rest_1_ = bf16[8,128,256]{2,1,0:T(8,128)(2,1)S(1)} collective-permute-done((bf16[8,128,256]{2,1,0:T(8,128)(2,1)S(1)}, bf16[8,128,256]{2,1,0:T(8,128)(2,1)S(1)}, u32[]{:S(2)}, u32[]{:S(2)}) %collective-permute-start.30) | collective-permute-done | bytes 524320 | tf_op jit(solution)/shard_map/ppermute | solution.py:44
  118.6 21.7 %attention.1 = (bf16[512,1024]{1,0:T(8,128)(2,1)}, bf16[512,256]{1,0:T(8,128)(2,1)}, bf16[8,128,256]{2,1,0:T(8,128)(2,1)S(1)}, bf16[8,128,256]{2,1,0:T(8,128)(2,...) custom-call(s32[64]{0:T(128)S(1)} %select_reduce_fusion.taken_by, ...), custom_call_target="tpu_custom_call" | custom-call | flops 6039797760 | bytes 8912896 | tf_op jit(solution)/shard_map/attention/pallas_call | solution.py:388
  140.8 2.7 %collective-permute-start.39 = (bf16[8,128,256]{2,1,0:T(8,128)(2,1)S(1)}, bf16[8,128,256]{2,1,0:T(8,128)(2,1)S(1)}, u32[]{:S(2)}, u32[]{:S(2)}) collective-permute-start(bf16[8,128,256]{2,1,0:T(8,128)(2,1)S(1)} %get-tuple-element.76), channel_id=1, source_target_pairs={{0,96},{4,28},{8,104},{12,4},{16,112},{20,12},{24,120},{28,20},{32... | collective-permute-start | bytes 1572872 | tf_op jit(solution)/shard_map/ppermute | solution.py:44
  144.7 2.5 %collective-permute-start.44 = (bf16[8,128,256]{2,1,0:T(8,128)(2,1)S(1)}, bf16[8,128,256]{2,1,0:T(8,128)(2,1)S(1)}, u32[]{:S(2)}, u32[]{:S(2)}) collective-permute-start(bf16[8,128,256]{2,1,0:T(8,128)(2,1)S(1)} %get-tuple-element.95), channel_id=1, source_target_pairs={{0,32},{4,12},{8,40},{12,20},{16,48},{20,28},{24,56},{28,4},{32,64... | collective-permute-start | bytes 1572872 | tf_op jit(solution)/shard_map/ppermute | solution.py:44
  147.2 8.6 %collective-permute-done.39.rest_2_ = bf16[8,128,256]{2,1,0:T(8,128)(2,1)S(1)} collective-permute-done((bf16[8,128,256]{2,1,0:T(8,128)(2,1)S(1)}, bf16[8,128,256]{2,1,0:T(8,128)(2,1)S(1)}, u32[]{:S(2)}, u32[]{:S(2)}) %collective-permute-start.39) | collective-permute-done | bytes 524320 | tf_op jit(solution)/shard_map/ppermute | solution.py:44
  155.8 3.7 %collective-permute-start.40 = (bf16[8,128,256]{2,1,0:T(8,128)(2,1)S(1)}, bf16[8,128,256]{2,1,0:T(8,128)(2,1)S(1)}, u32[]{:S(2)}, u32[]{:S(2)}) collective-permute-start(bf16[8,128,256]{2,1,0:T(8,128)(2,1)S(1)} %get-tuple-element.97), channel_id=1, source_target_pairs={{0,96},{4,28},{8,104},{12,4},{16,112},{20,12},{24,120},{28,20},{32... | collective-permute-start | bytes 1572872 | tf_op jit(solution)/shard_map/ppermute | solution.py:44
  159.5 5.6 %collective-permute-done.44.rest_7_ = bf16[8,128,256]{2,1,0:T(8,128)(2,1)S(1)} collective-permute-done((bf16[8,128,256]{2,1,0:T(8,128)(2,1)S(1)}, bf16[8,128,256]{2,1,0:T(8,128)(2,1)S(1)}, u32[]{:S(2)}, u32[]{:S(2)}) %collective-permute-start.44) | collective-permute-done | bytes 524320 | tf_op jit(solution)/shard_map/ppermute | solution.py:44
  165.1 6.0 %collective-permute-done.42.rest_5_ = bf16[8,128,256]{2,1,0:T(8,128)(2,1)S(1)} collective-permute-done((bf16[8,128,256]{2,1,0:T(8,128)(2,1)S(1)}, bf16[8,128,256]{2,1,0:T(8,128)(2,1)S(1)}, u32[]{:S(2)}, u32[]{:S(2)}) %collective-permute-start.42) | collective-permute-done | bytes 524320 | tf_op jit(solution)/shard_map/ppermute | solution.py:44
  171.1 2.1 collective-permute-done.40.rest_3_
  173.2 2.5 %add_blocks.1 = (f32[8,128,256]{2,1,0:T(8,128)S(1)}, bf16[8,128,256]{2,1,0:T(8,128)(2,1)S(1)}, bf16[8,128,256]{2,1,0:T(8,128)(2,1)S(1)}, bf16[8,128,256]{2,1,0:T(8,128)(2,1)S(1)}) custom-call(s32[64]{0:T(128)S(1)} %gather_fusion, bf16[8,128,256]{2,1,0:T(8,128)(2,1)S(1)} %get-tuple-element.74.rest_0_, bf16[8,128,256]{2,1,0:T(8,128)(2,1)S(1)} %get-tuple-element.98.rest_1_, ...), custom_call_target="tpu_custom_call" | custom-call | flops 2097152 | bytes 8388608 | tf_op jit(solution)/shard_map/add_blocks/pallas_call | solution.py:476
  177.8 7.2 %collective-permute-done.45.left_ref = bf16[8,128,256]{2,1,0:T(8,128)(2,1)S(1)} collective-permute-done((bf16[8,128,256]{2,1,0:T(8,128)(2,1)S(1)}, bf16[8,128,256]{2,1,0:T(8,128)(2,1)S(1)}, u32[]{:S(2)}, u32[]{:S(2)}) %collective-permute-start.45) | collective-permute-done | bytes 524320 | tf_op jit(solution)/shard_map/ppermute | solution.py:40
  185.0 2.5 collective-permute-done.46.far_ref
  187.4 5.5 %collective-permute-done.47.right_ref = bf16[8,128,256]{2,1,0:T(8,128)(2,1)S(1)} collective-permute-done((bf16[8,128,256]{2,1,0:T(8,128)(2,1)S(1)}, bf16[8,128,256]{2,1,0:T(8,128)(2,1)S(1)}, u32[]{:S(2)}, u32[]{:S(2)}) %collective-permute-start.47) | collective-permute-done | bytes 524320 | tf_op jit(solution)/shard_map/ppermute | solution.py:40
  193.5 3.6 %collective-permute-start.56 = (bf16[128,1024]{1,0:T(8,128)(2,1)S(1)}, bf16[128,1024]{1,0:T(8,128)(2,1)S(1)}, u32[]{:S(2)}, u32[]{:S(2)}) collective-permute-start(bf16[128,1024]{1,0:T(8,128)(2,1)S(1)} %get-tuple-element.84.refs_0_), channel_id=1, source_target_pairs={{0,3},{1,0},{2,1},{3,2},{4,7},{5,4},{6,5},{7,6},{8,11},{9,8},{10,9... | collective-permute-start | bytes 786440 | tf_op jit(solution)/shard_map/ppermute | solution.py:48
  197.1 3.2 %collective-permute-start.51 = (bf16[128,1024]{1,0:T(8,128)(2,1)S(1)}, bf16[128,1024]{1,0:T(8,128)(2,1)S(1)}, u32[]{:S(2)}, u32[]{:S(2)}) collective-permute-start(bf16[128,1024]{1,0:T(8,128)(2,1)S(1)} %collective-permute-done.48.refs_0_), channel_id=1, source_target_pairs={{0,3},{1,0},{2,1},{3,2},{4,7},{5,4},{6,5},{7,6},{8,11},{9,8},{10,9... | collective-permute-start | bytes 786440 | tf_op jit(solution)/shard_map/ppermute | solution.py:48
  200.3 3.4 %collective-permute-done.56.refs_4_ = bf16[128,1024]{1,0:T(8,128)(2,1)S(1)} collective-permute-done((bf16[128,1024]{1,0:T(8,128)(2,1)S(1)}, bf16[128,1024]{1,0:T(8,128)(2,1)S(1)}, u32[]{:S(2)}, u32[]{:S(2)}) %collective-permute-start.56) | collective-permute-done | bytes 262176 | tf_op jit(solution)/shard_map/ppermute | solution.py:48
  203.7 3.8 %collective-permute-start.57 = (bf16[64,1024]{1,0:T(8,128)(2,1)S(1)}, bf16[64,1024]{1,0:T(8,128)(2,1)S(1)}, u32[]{:S(2)}, u32[]{:S(2)}) collective-permute-start(bf16[64,1024]{1,0:T(8,128)(2,1)S(1)} %slice.62), channel_id=1, source_target_pairs={{0,3},{1,0},{2,1},{3,2},{4,7},{5,4},{6,5},{7,6},{8,11},{9,8},{10,9... | collective-permute-start | bytes 393224 | tf_op jit(solution)/shard_map/ppermute | solution.py:48
  209.3 3.8 %collective-permute-start.52 = (bf16[64,1024]{1,0:T(8,128)(2,1)S(1)}, bf16[64,1024]{1,0:T(8,128)(2,1)S(1)}, u32[]{:S(2)}, u32[]{:S(2)}) collective-permute-start(bf16[64,1024]{1,0:T(8,128)(2,1)S(1)} %slice.60), channel_id=1, source_target_pairs={{0,3},{1,0},{2,1},{3,2},{4,7},{5,4},{6,5},{7,6},{8,11},{9,8},{10,9... | collective-permute-start | bytes 393224 | tf_op jit(solution)/shard_map/ppermute | solution.py:48
  215.1 3.3 %first_weight_product.1.refs_6_ = f32[512,2048]{1,0:T(8,128)S(1)} custom-call(bf16[128,1024]{1,0:T(8,128)(2,1)S(1)} %get-tuple-element.84.refs_0_, bf16[128,1024]{1,0:T(8,128)(2,1)S(1)} %collective-permute-done.54.refs_1_, bf16[64,1024]{1,0:T(8,128)(2,1)S(1)} %collective-permute-done.55.refs_2_, bf16[64,1024]{1,0:T(8,128)(2,1)S(1)} %collective-permute-done.57.refs_3_, ...), custom_call_target="tpu_custom_call" | custom-call | flops 2147483648 | bytes 8388608 | tf_op jit(solution)/shard_map/first_weight_product/pallas_call | solution.py:271
  219.4 3.6 %second_weight_product.1 = (f32[4,32,2048]{2,1,0:T(8,128)S(1)}, bf16[4,32,2048]{2,1,0:T(8,128)(2,1)S(1)}, bf16[4,32,2048]{2,1,0:T(8,128)(2,1)S(1)}, bf16[4,32,2048]{2,1,0:T(8,128)(2,1)S(1)}) custom-call(bf16[128,1024]{1,0:T(8,128)(2,1)S(1)} %collective-permute-done.48.refs_0_, bf16[128,1024]{1,0:T(8,128)(2,1)S(1)} %collective-permute-done.49.refs_1_, ...), custom_call_target="tpu_custom_call" | custom-call | flops 2147483648 | bytes 8388608 | tf_op jit(solution)/shard_map/second_weight_product/pallas_call | solution.py:280
  223.1 3.2 %collective-permute-start.59 = (bf16[4,32,2048]{2,1,0:T(8,128)(2,1)S(1)}, bf16[4,32,2048]{2,1,0:T(8,128)(2,1)S(1)}, u32[]{:S(2)}, u32[]{:S(2)}) collective-permute-start(bf16[4,32,2048]{2,1,0:T(8,128)(2,1)S(1)} %get-tuple-element.87), channel_id=1, source_target_pairs={{0,24},{4,100},{8,0},{12,108},{16,8},{20,116},{24,16},{28,124},{32... | collective-permute-start | bytes 1572872 | tf_op jit(solution)/shard_map/ppermute | solution.py:40
  226.3 12.8 %collective-permute-done.58 = bf16[4,32,2048]{2,1,0:T(8,128)(2,1)S(1)} collective-permute-done((bf16[4,32,2048]{2,1,0:T(8,128)(2,1)S(1)}, bf16[4,32,2048]{2,1,0:T(8,128)(2,1)S(1)}, u32[]{:S(2)}, u32[]{:S(2)}) %collective-permute-start.58) | collective-permute-done | bytes 524320 | tf_op jit(solution)/shard_map/ppermute | solution.py:40
  239.5 3.8 %collective-permute-start.63 = (bf16[32,2048]{1,0:T(8,128)(2,1)S(1)}, bf16[32,2048]{1,0:T(8,128)(2,1)S(1)}, u32[]{:S(2)}, u32[]{:S(2)}) collective-permute-start(bf16[32,2048]{1,0:T(8,128)(2,1)S(1)} %get-tuple-element.100), channel_id=1, source_target_pairs={{0,64},{4,20},{8,72},{12,28},{16,80},{20,4},{24,88},{28,12},{32,96... | collective-permute-start | bytes 393224 | tf_op jit(solution)/shard_map/ppermute | solution.py:44
  243.3 2.4 collective-permute-done.61
  245.6 2.0 collective-permute-done.63
  (138 shorter events, 39.3 us)
Async XLA Ops:
  0.6 9.6 %collective-permute-start.1 = (bf16[32,2048]{1,0:T(8,128)(2,1)}, bf16[32,2048]{1,0:T(8,128)(2,1)S(1)}, u32[]{:S(2)}, u32[]{:S(2)}) collective-permute-start(bf16[32,2048]{1,0:T(8,128)(2,1)} %param.8), channel_id=1, source_target_pairs={{0,16},{4,68},{8,24},{12,76},{16,0},{20,84},{24,8},{28,92},{32,48}... | collective-permute-start | bytes 393224 | tf_op jit(solution)/shard_map/ppermute | solution.py:40
  12.0 15.4 %collective-permute-start.9 = (bf16[128,2048]{1,0:T(8,128)(2,1)S(1)}, bf16[128,2048]{1,0:T(8,128)(2,1)S(1)}, u32[]{:S(2)}, u32[]{:S(2)}) collective-permute-start(bf16[128,2048]{1,0:T(8,128)(2,1)S(1)} %pad_maximum_fusion.rest_0_), channel_id=1, source_target_pairs={{0,96},{4,28},{8,104},{12,4},{16,112},{20,12},{24,120},{28,20},{32... | collective-permute-start | bytes 1572872 | tf_op jit(solution)/shard_map/ppermute | solution.py:44
  15.1 12.3 %collective-permute-start.8 = (bf16[128,2048]{1,0:T(8,128)(2,1)S(1)}, bf16[128,2048]{1,0:T(8,128)(2,1)S(1)}, u32[]{:S(2)}, u32[]{:S(2)}) collective-permute-start(bf16[128,2048]{1,0:T(8,128)(2,1)S(1)} %pad_maximum_fusion.rest_0_), channel_id=1, source_target_pairs={{0,64},{4,20},{8,72},{12,28},{16,80},{20,4},{24,88},{28,12},{32,96... | collective-permute-start | bytes 1572872 | tf_op jit(solution)/shard_map/ppermute | solution.py:44
  15.7 15.7 %collective-permute-start.7 = (bf16[128,2048]{1,0:T(8,128)(2,1)S(1)}, bf16[128,2048]{1,0:T(8,128)(2,1)S(1)}, u32[]{:S(2)}, u32[]{:S(2)}) collective-permute-start(bf16[128,2048]{1,0:T(8,128)(2,1)S(1)} %pad_maximum_fusion.rest_0_), channel_id=1, source_target_pairs={{0,32},{4,12},{8,40},{12,20},{16,48},{20,28},{24,56},{28,4},{32,64... | collective-permute-start | bytes 1572872 | tf_op jit(solution)/shard_map/ppermute | solution.py:44
  16.7 14.7 %collective-permute-start.10 = (bf16[128,2048]{1,0:T(8,128)(2,1)S(1)}, bf16[128,2048]{1,0:T(8,128)(2,1)S(1)}, u32[]{:S(2)}, u32[]{:S(2)}) collective-permute-start(bf16[128,2048]{1,0:T(8,128)(2,1)S(1)} %pad_maximum_fusion.rest_0_), channel_id=1, source_target_pairs={{0,4},{4,0},{8,12},{12,8},{16,20},{20,16},{24,28},{28,24},{32,36},... | collective-permute-start | bytes 1572872 | tf_op jit(solution)/shard_map/ppermute | solution.py:52
  38.7 9.4 %collective-permute-start.14 = (bf16[256,384]{1,0:T(8,128)(2,1)S(1)}, bf16[256,384]{1,0:T(8,128)(2,1)S(1)}, u32[]{:S(2)}, u32[]{:S(2)}) collective-permute-start(bf16[256,384]{1,0:T(8,128)(2,1)S(1)} %get-tuple-element.48), channel_id=1, source_target_pairs={{0,1},{1,2},{2,3},{3,0},{4,5},{5,6},{6,7},{7,4},{8,9},{9,10},{10,1... | collective-permute-start | bytes 589832 | tf_op jit(solution)/shard_map/ppermute | solution.py:48
  40.3 7.9 %collective-permute-start.17 = (bf16[256,384]{1,0:T(8,128)(2,1)S(1)}, bf16[256,384]{1,0:T(8,128)(2,1)S(1)}, u32[]{:S(2)}, u32[]{:S(2)}) collective-permute-start(bf16[256,384]{1,0:T(8,128)(2,1)S(1)} %get-tuple-element.51), channel_id=1, source_target_pairs={{0,3},{1,0},{2,1},{3,2},{4,7},{5,4},{6,5},{7,6},{8,11},{9,8},{10,9... | collective-permute-start | bytes 589832 | tf_op jit(solution)/shard_map/ppermute | solution.py:48
  44.8 9.0 %collective-permute-start.20 = (bf16[256,384]{1,0:T(8,128)(2,1)S(1)}, bf16[256,384]{1,0:T(8,128)(2,1)S(1)}, u32[]{:S(2)}, u32[]{:S(2)}) collective-permute-start(bf16[256,384]{1,0:T(8,128)(2,1)S(1)} %get-tuple-element.55), channel_id=1, source_target_pairs={{0,1},{1,2},{2,3},{3,0},{4,5},{5,6},{6,7},{7,4},{8,9},{9,10},{10,1... | collective-permute-start | bytes 589832 | tf_op jit(solution)/shard_map/ppermute | solution.py:48
  45.1 8.8 %collective-permute-start.23 = (bf16[256,384]{1,0:T(8,128)(2,1)S(1)}, bf16[256,384]{1,0:T(8,128)(2,1)S(1)}, u32[]{:S(2)}, u32[]{:S(2)}) collective-permute-start(bf16[256,384]{1,0:T(8,128)(2,1)S(1)} %get-tuple-element.58), channel_id=1, source_target_pairs={{0,3},{1,0},{2,1},{3,2},{4,7},{5,4},{6,5},{7,6},{8,11},{9,8},{10,9... | collective-permute-start | bytes 589832 | tf_op jit(solution)/shard_map/ppermute | solution.py:48
  48.1 9.9 %collective-permute-start.15 = (bf16[256,384]{1,0:T(8,128)(2,1)S(1)}, bf16[256,384]{1,0:T(8,128)(2,1)S(1)}, u32[]{:S(2)}, u32[]{:S(2)}) collective-permute-start(bf16[256,384]{1,0:T(8,128)(2,1)S(1)} %relay.8), channel_id=1, source_target_pairs={{0,1},{1,2},{2,3},{3,0},{4,5},{5,6},{6,7},{7,4},{8,9},{9,10},{10,1... | collective-permute-start | bytes 589832 | tf_op jit(solution)/shard_map/ppermute | solution.py:48
  48.3 9.9 %collective-permute-start.18 = (bf16[256,384]{1,0:T(8,128)(2,1)S(1)}, bf16[256,384]{1,0:T(8,128)(2,1)S(1)}, u32[]{:S(2)}, u32[]{:S(2)}) collective-permute-start(bf16[256,384]{1,0:T(8,128)(2,1)S(1)} %relay.10), channel_id=1, source_target_pairs={{0,3},{1,0},{2,1},{3,2},{4,7},{5,4},{6,5},{7,6},{8,11},{9,8},{10,9... | collective-permute-start | bytes 589832 | tf_op jit(solution)/shard_map/ppermute | solution.py:48
  53.8 8.6 %collective-permute-start.21 = (bf16[256,384]{1,0:T(8,128)(2,1)S(1)}, bf16[256,384]{1,0:T(8,128)(2,1)S(1)}, u32[]{:S(2)}, u32[]{:S(2)}) collective-permute-start(bf16[256,384]{1,0:T(8,128)(2,1)S(1)} %relay.12), channel_id=1, source_target_pairs={{0,1},{1,2},{2,3},{3,0},{4,5},{5,6},{6,7},{7,4},{8,9},{9,10},{10,1... | collective-permute-start | bytes 589832 | tf_op jit(solution)/shard_map/ppermute | solution.py:48
  54.0 8.6 %collective-permute-start.24 = (bf16[256,384]{1,0:T(8,128)(2,1)S(1)}, bf16[256,384]{1,0:T(8,128)(2,1)S(1)}, u32[]{:S(2)}, u32[]{:S(2)}) collective-permute-start(bf16[256,384]{1,0:T(8,128)(2,1)S(1)} %relay.14), channel_id=1, source_target_pairs={{0,3},{1,0},{2,1},{3,2},{4,7},{5,4},{6,5},{7,6},{8,11},{9,8},{10,9... | collective-permute-start | bytes 589832 | tf_op jit(solution)/shard_map/ppermute | solution.py:48
  58.0 9.1 %collective-permute-start.16 = (bf16[256,384]{1,0:T(8,128)(2,1)S(1)}, bf16[256,384]{1,0:T(8,128)(2,1)S(1)}, u32[]{:S(2)}, u32[]{:S(2)}) collective-permute-start(bf16[256,384]{1,0:T(8,128)(2,1)S(1)} %relay.9), channel_id=1, source_target_pairs={{0,1},{1,2},{2,3},{3,0},{4,5},{5,6},{6,7},{7,4},{8,9},{9,10},{10,1... | collective-permute-start | bytes 589832 | tf_op jit(solution)/shard_map/ppermute | solution.py:48
  58.2 9.0 %collective-permute-start.19 = (bf16[256,384]{1,0:T(8,128)(2,1)S(1)}, bf16[256,384]{1,0:T(8,128)(2,1)S(1)}, u32[]{:S(2)}, u32[]{:S(2)}) collective-permute-start(bf16[256,384]{1,0:T(8,128)(2,1)S(1)} %relay.11), channel_id=1, source_target_pairs={{0,3},{1,0},{2,1},{3,2},{4,7},{5,4},{6,5},{7,6},{8,11},{9,8},{10,9... | collective-permute-start | bytes 589832 | tf_op jit(solution)/shard_map/ppermute | solution.py:48
  62.5 6.9 %collective-permute-start.22 = (bf16[256,384]{1,0:T(8,128)(2,1)S(1)}, bf16[256,384]{1,0:T(8,128)(2,1)S(1)}, u32[]{:S(2)}, u32[]{:S(2)}) collective-permute-start(bf16[256,384]{1,0:T(8,128)(2,1)S(1)} %relay.13), channel_id=1, source_target_pairs={{0,1},{1,2},{2,3},{3,0},{4,5},{5,6},{6,7},{7,4},{8,9},{9,10},{10,1... | collective-permute-start | bytes 589832 | tf_op jit(solution)/shard_map/ppermute | solution.py:48
  62.6 6.8 %collective-permute-start.25 = (bf16[256,384]{1,0:T(8,128)(2,1)S(1)}, bf16[256,384]{1,0:T(8,128)(2,1)S(1)}, u32[]{:S(2)}, u32[]{:S(2)}) collective-permute-start(bf16[256,384]{1,0:T(8,128)(2,1)S(1)} %relay.15), channel_id=1, source_target_pairs={{0,3},{1,0},{2,1},{3,2},{4,7},{5,4},{6,5},{7,6},{8,11},{9,8},{10,9... | collective-permute-start | bytes 589832 | tf_op jit(solution)/shard_map/ppermute | solution.py:48
  69.6 15.6 %collective-permute-start.28 = (bf16[8,128,256]{2,1,0:T(8,128)(2,1)S(1)}, bf16[8,128,256]{2,1,0:T(8,128)(2,1)S(1)}, u32[]{:S(2)}, u32[]{:S(2)}) collective-permute-start(bf16[8,128,256]{2,1,0:T(8,128)(2,1)S(1)} %bitcast.19), channel_id=1, source_target_pairs={{0,24},{4,100},{8,0},{12,108},{16,8},{20,116},{24,16},{28,124},{32... | collective-permute-start | bytes 1572872 | tf_op jit(solution)/shard_map/ppermute | solution.py:40
  72.9 12.3 %collective-permute-start.27 = (bf16[8,128,256]{2,1,0:T(8,128)(2,1)S(1)}, bf16[8,128,256]{2,1,0:T(8,128)(2,1)S(1)}, u32[]{:S(2)}, u32[]{:S(2)}) collective-permute-start(bf16[8,128,256]{2,1,0:T(8,128)(2,1)S(1)} %bitcast.20), channel_id=1, source_target_pairs={{0,16},{4,68},{8,24},{12,76},{16,0},{20,84},{24,8},{28,92},{32,48}... | collective-permute-start | bytes 1572872 | tf_op jit(solution)/shard_map/ppermute | solution.py:40
  72.9 16.0 %collective-permute-start.26 = (bf16[8,128,256]{2,1,0:T(8,128)(2,1)S(1)}, bf16[8,128,256]{2,1,0:T(8,128)(2,1)S(1)}, u32[]{:S(2)}, u32[]{:S(2)}) collective-permute-start(bf16[8,128,256]{2,1,0:T(8,128)(2,1)S(1)} %bitcast.21), channel_id=1, source_target_pairs={{0,8},{4,36},{8,16},{12,44},{16,24},{20,52},{24,0},{28,60},{32,40}... | collective-permute-start | bytes 1572872 | tf_op jit(solution)/shard_map/ppermute | solution.py:40
  89.6 16.5 %collective-permute-start.31 = (bf16[16,128,256]{2,1,0:T(8,128)(2,1)S(1)}, bf16[16,128,256]{2,1,0:T(8,128)(2,1)S(1)}, u32[]{:S(2)}, u32[]{:S(2)}) collective-permute-start(bf16[16,128,256]{2,1,0:T(8,128)(2,1)S(1)} %get-tuple-element.68), channel_id=1, source_target_pairs={{0,64},{4,20},{8,72},{12,28},{16,80},{20,4},{24,88},{28,12},{32,96... | collective-permute-start | bytes 3145736 | tf_op jit(solution)/shard_map/ppermute | solution.py:44
  90.3 15.8 %collective-permute-start.29 = (bf16[8,128,256]{2,1,0:T(8,128)(2,1)S(1)}, bf16[8,128,256]{2,1,0:T(8,128)(2,1)S(1)}, u32[]{:S(2)}, u32[]{:S(2)}) collective-permute-start(bf16[8,128,256]{2,1,0:T(8,128)(2,1)S(1)} %get-tuple-element.65), channel_id=1, source_target_pairs={{0,4},{4,0},{8,12},{12,8},{16,20},{20,16},{24,28},{28,24},{32,36},... | collective-permute-start | bytes 1572872 | tf_op jit(solution)/shard_map/ppermute | solution.py:52
  90.3 21.3 %collective-permute-start.33 = (bf16[8,128,256]{2,1,0:T(8,128)(2,1)S(1)}, bf16[8,128,256]{2,1,0:T(8,128)(2,1)S(1)}, u32[]{:S(2)}, u32[]{:S(2)}) collective-permute-start(bf16[8,128,256]{2,1,0:T(8,128)(2,1)S(1)} %get-tuple-element.70), channel_id=1, source_target_pairs={{0,32},{4,12},{8,40},{12,20},{16,48},{20,28},{24,56},{28,4},{32,64... | collective-permute-start | bytes 1572872 | tf_op jit(solution)/shard_map/ppermute | solution.py:44
  91.8 19.9 %collective-permute-start.36 = (bf16[8,128,256]{2,1,0:T(8,128)(2,1)S(1)}, bf16[8,128,256]{2,1,0:T(8,128)(2,1)S(1)}, u32[]{:S(2)}, u32[]{:S(2)}) collective-permute-start(bf16[8,128,256]{2,1,0:T(8,128)(2,1)S(1)} %get-tuple-element.71), channel_id=1, source_target_pairs={{0,96},{4,28},{8,104},{12,4},{16,112},{20,12},{24,120},{28,20},{32... | collective-permute-start | bytes 1572872 | tf_op jit(solution)/shard_map/ppermute | solution.py:44
  106.1 11.2 %collective-permute-start.35 = (bf16[16,128,256]{2,1,0:T(8,128)(2,1)S(1)}, bf16[16,128,256]{2,1,0:T(8,128)(2,1)S(1)}, u32[]{:S(2)}, u32[]{:S(2)}) collective-permute-start(bf16[16,128,256]{2,1,0:T(8,128)(2,1)S(1)} %collective-permute-done.31.rest_2_), channel_id=1, source_target_pairs={{0,4},{4,0},{8,12},{12,8},{16,20},{20,16},{24,28},{28,24},{32,36},... | collective-permute-start | bytes 3145736 | tf_op jit(solution)/shard_map/ppermute | solution.py:52
  106.8 10.5 %collective-permute-start.30 = (bf16[8,128,256]{2,1,0:T(8,128)(2,1)S(1)}, bf16[8,128,256]{2,1,0:T(8,128)(2,1)S(1)}, u32[]{:S(2)}, u32[]{:S(2)}) collective-permute-start(bf16[8,128,256]{2,1,0:T(8,128)(2,1)S(1)} %get-tuple-element.67), channel_id=1, source_target_pairs={{0,32},{4,12},{8,40},{12,20},{16,48},{20,28},{24,56},{28,4},{32,64... | collective-permute-start | bytes 1572872 | tf_op jit(solution)/shard_map/ppermute | solution.py:44
  106.9 10.4 %collective-permute-start.32 = (bf16[8,128,256]{2,1,0:T(8,128)(2,1)S(1)}, bf16[8,128,256]{2,1,0:T(8,128)(2,1)S(1)}, u32[]{:S(2)}, u32[]{:S(2)}) collective-permute-start(bf16[8,128,256]{2,1,0:T(8,128)(2,1)S(1)} %get-tuple-element.69), channel_id=1, source_target_pairs={{0,96},{4,28},{8,104},{12,4},{16,112},{20,12},{24,120},{28,20},{32... | collective-permute-start | bytes 1572872 | tf_op jit(solution)/shard_map/ppermute | solution.py:44
  117.3 101.1 %collective-permute-start.53 = (bf16[1024,2048]{1,0:T(8,128)(2,1)S(1)}, bf16[1024,2048]{1,0:T(8,128)(2,1)S(1)}, u32[]{:S(2)}, u32[]{:S(2)}) collective-permute-start(bf16[1024,2048]{1,0:T(8,128)(2,1)S(1)} %copy-done.1), channel_id=1, source_target_pairs={{0,4},{4,0},{8,12},{12,8},{16,20},{20,16},{24,28},{28,24},{32,36},... | collective-permute-start | bytes 12582920 | tf_op jit(solution)/shard_map/ppermute | solution.py:52
  140.8 15.1 %collective-permute-start.39 = (bf16[8,128,256]{2,1,0:T(8,128)(2,1)S(1)}, bf16[8,128,256]{2,1,0:T(8,128)(2,1)S(1)}, u32[]{:S(2)}, u32[]{:S(2)}) collective-permute-start(bf16[8,128,256]{2,1,0:T(8,128)(2,1)S(1)} %get-tuple-element.76), channel_id=1, source_target_pairs={{0,96},{4,28},{8,104},{12,4},{16,112},{20,12},{24,120},{28,20},{32... | collective-permute-start | bytes 1572872 | tf_op jit(solution)/shard_map/ppermute | solution.py:44
  143.5 12.4 %collective-permute-start.41 = (bf16[8,128,256]{2,1,0:T(8,128)(2,1)S(1)}, bf16[8,128,256]{2,1,0:T(8,128)(2,1)S(1)}, u32[]{:S(2)}, u32[]{:S(2)}) collective-permute-start(bf16[8,128,256]{2,1,0:T(8,128)(2,1)S(1)} %get-tuple-element.77), channel_id=1, source_target_pairs={{0,64},{4,20},{8,72},{12,28},{16,80},{20,4},{24,88},{28,12},{32,96... | collective-permute-start | bytes 1572872 | tf_op jit(solution)/shard_map/ppermute | solution.py:44
  143.5 16.0 %collective-permute-start.43 = (bf16[8,128,256]{2,1,0:T(8,128)(2,1)S(1)}, bf16[8,128,256]{2,1,0:T(8,128)(2,1)S(1)}, u32[]{:S(2)}, u32[]{:S(2)}) collective-permute-start(bf16[8,128,256]{2,1,0:T(8,128)(2,1)S(1)} %get-tuple-element.78), channel_id=1, source_target_pairs={{0,32},{4,12},{8,40},{12,20},{16,48},{20,28},{24,56},{28,4},{32,64... | collective-permute-start | bytes 1572872 | tf_op jit(solution)/shard_map/ppermute | solution.py:44
  144.7 20.4 %collective-permute-start.44 = (bf16[8,128,256]{2,1,0:T(8,128)(2,1)S(1)}, bf16[8,128,256]{2,1,0:T(8,128)(2,1)S(1)}, u32[]{:S(2)}, u32[]{:S(2)}) collective-permute-start(bf16[8,128,256]{2,1,0:T(8,128)(2,1)S(1)} %get-tuple-element.95), channel_id=1, source_target_pairs={{0,32},{4,12},{8,40},{12,20},{16,48},{20,28},{24,56},{28,4},{32,64... | collective-permute-start | bytes 1572872 | tf_op jit(solution)/shard_map/ppermute | solution.py:44
  155.8 15.2 %collective-permute-start.42 = (bf16[8,128,256]{2,1,0:T(8,128)(2,1)S(1)}, bf16[8,128,256]{2,1,0:T(8,128)(2,1)S(1)}, u32[]{:S(2)}, u32[]{:S(2)}) collective-permute-start(bf16[8,128,256]{2,1,0:T(8,128)(2,1)S(1)} %get-tuple-element.96), channel_id=1, source_target_pairs={{0,64},{4,20},{8,72},{12,28},{16,80},{20,4},{24,88},{28,12},{32,96... | collective-permute-start | bytes 1572872 | tf_op jit(solution)/shard_map/ppermute | solution.py:44
  155.8 17.3 %collective-permute-start.40 = (bf16[8,128,256]{2,1,0:T(8,128)(2,1)S(1)}, bf16[8,128,256]{2,1,0:T(8,128)(2,1)S(1)}, u32[]{:S(2)}, u32[]{:S(2)}) collective-permute-start(bf16[8,128,256]{2,1,0:T(8,128)(2,1)S(1)} %get-tuple-element.97), channel_id=1, source_target_pairs={{0,96},{4,28},{8,104},{12,4},{16,112},{20,12},{24,120},{28,20},{32... | collective-permute-start | bytes 1572872 | tf_op jit(solution)/shard_map/ppermute | solution.py:44
  175.7 9.3 %collective-permute-start.45 = (bf16[8,128,256]{2,1,0:T(8,128)(2,1)S(1)}, bf16[8,128,256]{2,1,0:T(8,128)(2,1)S(1)}, u32[]{:S(2)}, u32[]{:S(2)}) collective-permute-start(bf16[8,128,256]{2,1,0:T(8,128)(2,1)S(1)} %get-tuple-element.80), channel_id=1, source_target_pairs={{0,24},{4,100},{8,0},{12,108},{16,8},{20,116},{24,16},{28,124},{32... | collective-permute-start | bytes 1572872 | tf_op jit(solution)/shard_map/ppermute | solution.py:40
  176.6 10.8 %collective-permute-start.46 = (bf16[8,128,256]{2,1,0:T(8,128)(2,1)S(1)}, bf16[8,128,256]{2,1,0:T(8,128)(2,1)S(1)}, u32[]{:S(2)}, u32[]{:S(2)}) collective-permute-start(bf16[8,128,256]{2,1,0:T(8,128)(2,1)S(1)} %get-tuple-element.81), channel_id=1, source_target_pairs={{0,16},{4,68},{8,24},{12,76},{16,0},{20,84},{24,8},{28,92},{32,48}... | collective-permute-start | bytes 1572872 | tf_op jit(solution)/shard_map/ppermute | solution.py:40
  176.6 16.3 %collective-permute-start.47 = (bf16[8,128,256]{2,1,0:T(8,128)(2,1)S(1)}, bf16[8,128,256]{2,1,0:T(8,128)(2,1)S(1)}, u32[]{:S(2)}, u32[]{:S(2)}) collective-permute-start(bf16[8,128,256]{2,1,0:T(8,128)(2,1)S(1)} %get-tuple-element.82), channel_id=1, source_target_pairs={{0,8},{4,36},{8,16},{12,44},{16,24},{20,52},{24,0},{28,60},{32,40}... | collective-permute-start | bytes 1572872 | tf_op jit(solution)/shard_map/ppermute | solution.py:40
  193.5 10.2 %collective-permute-start.56 = (bf16[128,1024]{1,0:T(8,128)(2,1)S(1)}, bf16[128,1024]{1,0:T(8,128)(2,1)S(1)}, u32[]{:S(2)}, u32[]{:S(2)}) collective-permute-start(bf16[128,1024]{1,0:T(8,128)(2,1)S(1)} %get-tuple-element.84.refs_0_), channel_id=1, source_target_pairs={{0,3},{1,0},{2,1},{3,2},{4,7},{5,4},{6,5},{7,6},{8,11},{9,8},{10,9... | collective-permute-start | bytes 786440 | tf_op jit(solution)/shard_map/ppermute | solution.py:48
  197.1 10.4 %collective-permute-start.54 = (bf16[128,1024]{1,0:T(8,128)(2,1)S(1)}, bf16[128,1024]{1,0:T(8,128)(2,1)S(1)}, u32[]{:S(2)}, u32[]{:S(2)}) collective-permute-start(bf16[128,1024]{1,0:T(8,128)(2,1)S(1)} %get-tuple-element.84.refs_0_), channel_id=1, source_target_pairs={{0,1},{1,2},{2,3},{3,0},{4,5},{5,6},{6,7},{7,4},{8,9},{9,10},{10,1... | collective-permute-start | bytes 786440 | tf_op jit(solution)/shard_map/ppermute | solution.py:48
  197.1 12.2 %collective-permute-start.51 = (bf16[128,1024]{1,0:T(8,128)(2,1)S(1)}, bf16[128,1024]{1,0:T(8,128)(2,1)S(1)}, u32[]{:S(2)}, u32[]{:S(2)}) collective-permute-start(bf16[128,1024]{1,0:T(8,128)(2,1)S(1)} %collective-permute-done.48.refs_0_), channel_id=1, source_target_pairs={{0,3},{1,0},{2,1},{3,2},{4,7},{5,4},{6,5},{7,6},{8,11},{9,8},{10,9... | collective-permute-start | bytes 786440 | tf_op jit(solution)/shard_map/ppermute | solution.py:48
  200.3 12.8 %collective-permute-start.49 = (bf16[128,1024]{1,0:T(8,128)(2,1)S(1)}, bf16[128,1024]{1,0:T(8,128)(2,1)S(1)}, u32[]{:S(2)}, u32[]{:S(2)}) collective-permute-start(bf16[128,1024]{1,0:T(8,128)(2,1)S(1)} %collective-permute-done.48.refs_0_), channel_id=1, source_target_pairs={{0,1},{1,2},{2,3},{3,0},{4,5},{5,6},{6,7},{7,4},{8,9},{9,10},{10,1... | collective-permute-start | bytes 786440 | tf_op jit(solution)/shard_map/ppermute | solution.py:48
  203.7 9.5 %collective-permute-start.57 = (bf16[64,1024]{1,0:T(8,128)(2,1)S(1)}, bf16[64,1024]{1,0:T(8,128)(2,1)S(1)}, u32[]{:S(2)}, u32[]{:S(2)}) collective-permute-start(bf16[64,1024]{1,0:T(8,128)(2,1)S(1)} %slice.62), channel_id=1, source_target_pairs={{0,3},{1,0},{2,1},{3,2},{4,7},{5,4},{6,5},{7,6},{8,11},{9,8},{10,9... | collective-permute-start | bytes 393224 | tf_op jit(solution)/shard_map/ppermute | solution.py:48
  207.5 7.6 %collective-permute-start.55 = (bf16[64,1024]{1,0:T(8,128)(2,1)S(1)}, bf16[64,1024]{1,0:T(8,128)(2,1)S(1)}, u32[]{:S(2)}, u32[]{:S(2)}) collective-permute-start(bf16[64,1024]{1,0:T(8,128)(2,1)S(1)} %slice.61), channel_id=1, source_target_pairs={{0,1},{1,2},{2,3},{3,0},{4,5},{5,6},{6,7},{7,4},{8,9},{9,10},{10,1... | collective-permute-start | bytes 393224 | tf_op jit(solution)/shard_map/ppermute | solution.py:48
  209.3 9.0 %collective-permute-start.52 = (bf16[64,1024]{1,0:T(8,128)(2,1)S(1)}, bf16[64,1024]{1,0:T(8,128)(2,1)S(1)}, u32[]{:S(2)}, u32[]{:S(2)}) collective-permute-start(bf16[64,1024]{1,0:T(8,128)(2,1)S(1)} %slice.60), channel_id=1, source_target_pairs={{0,3},{1,0},{2,1},{3,2},{4,7},{5,4},{6,5},{7,6},{8,11},{9,8},{10,9... | collective-permute-start | bytes 393224 | tf_op jit(solution)/shard_map/ppermute | solution.py:48
  223.0 16.1 %collective-permute-start.58 = (bf16[4,32,2048]{2,1,0:T(8,128)(2,1)S(1)}, bf16[4,32,2048]{2,1,0:T(8,128)(2,1)S(1)}, u32[]{:S(2)}, u32[]{:S(2)}) collective-permute-start(bf16[4,32,2048]{2,1,0:T(8,128)(2,1)S(1)} %get-tuple-element.86), channel_id=1, source_target_pairs={{0,8},{4,36},{8,16},{12,44},{16,24},{20,52},{24,0},{28,60},{32,40}... | collective-permute-start | bytes 1572872 | tf_op jit(solution)/shard_map/ppermute | solution.py:40
  223.1 16.0 %collective-permute-start.59 = (bf16[4,32,2048]{2,1,0:T(8,128)(2,1)S(1)}, bf16[4,32,2048]{2,1,0:T(8,128)(2,1)S(1)}, u32[]{:S(2)}, u32[]{:S(2)}) collective-permute-start(bf16[4,32,2048]{2,1,0:T(8,128)(2,1)S(1)} %get-tuple-element.87), channel_id=1, source_target_pairs={{0,24},{4,100},{8,0},{12,108},{16,8},{20,116},{24,16},{28,124},{32... | collective-permute-start | bytes 1572872 | tf_op jit(solution)/shard_map/ppermute | solution.py:40
  226.3 12.8 %collective-permute-start.60 = (bf16[4,32,2048]{2,1,0:T(8,128)(2,1)S(1)}, bf16[4,32,2048]{2,1,0:T(8,128)(2,1)S(1)}, u32[]{:S(2)}, u32[]{:S(2)}) collective-permute-start(bf16[4,32,2048]{2,1,0:T(8,128)(2,1)S(1)} %get-tuple-element.88), channel_id=1, source_target_pairs={{0,16},{4,68},{8,24},{12,76},{16,0},{20,84},{24,8},{28,92},{32,48}... | collective-permute-start | bytes 1572872 | tf_op jit(solution)/shard_map/ppermute | solution.py:40
  239.5 8.2 %collective-permute-start.63 = (bf16[32,2048]{1,0:T(8,128)(2,1)S(1)}, bf16[32,2048]{1,0:T(8,128)(2,1)S(1)}, u32[]{:S(2)}, u32[]{:S(2)}) collective-permute-start(bf16[32,2048]{1,0:T(8,128)(2,1)S(1)} %get-tuple-element.100), channel_id=1, source_target_pairs={{0,64},{4,20},{8,72},{12,28},{16,80},{20,4},{24,88},{28,12},{32,96... | collective-permute-start | bytes 393224 | tf_op jit(solution)/shard_map/ppermute | solution.py:44
  (22 other events, 219.2 us)

commit v6 on v4

--- a/solution.py
+++ b/solution.py
@@ -598,9 +598,9 @@
     )
     own = own.reshape(passages_here, PLEN, local_width)
     ring = ring_gather(own, send_first)
-    other = pick(served, ring, 1, places[0])
+    other = pick(served, ring, 1)
     swapped = [swap_cores(other[0])] + [swap_cores(send_second(other[k], k)) for k in range(1, SIDE)]
-    same = pick(served, ring, 0, swapped[0])
+    same = pick(served, ring, 0, swapped[0], places[0])
     same = [same[0]] + [send_second(same[k], k) for k in range(1, SIDE)]
     hidden_theirs = swap_cores(passage_hidden)
     half = SIDE * capacity

time: 248 us -> 248 us (level)
  transfers between devices with their start and end apart: 65 -> 65, of which waited for: 34 -> 35; matrix products, arithmetic and copies ran while one was open for 2% -> 1% of each run, Pallas kernels for 13% -> 13%
where the time goes in v6:
time: 248 us
  waiting for transfers between devices  117 us (47%)
  starting transfers between devices  80.2 us (32%)
  Pallas kernels  39.2 us (16%)
  local copies, waits for them, and re-layouts  6.55 us (3%)
  other arithmetic  3.32 us (1%)
    ppermute x21, waiting for transfers between devices, send_second(): return lax.ppermute(x, 'pas', ring_pairs(1, k))  63.3 us
    ppermute x20, starting transfers between devices, send_tp(): return lax.ppermute(x, 'tp', [(i, (i + k) % SIDE) for i in range(SIDE)])  34.7 us
    ppermute x12, waiting for transfers between devices, send_first(): return lax.ppermute(x, 'pas', ring_pairs(0, k))  33.3 us
    ppermute x21, starting transfers between devices, send_second(): return lax.ppermute(x, 'pas', ring_pairs(1, k))  26.9 us
    pallas_call x1, Pallas kernels, attention(): pl.pallas_call(functools.partial(attention_kernel, len(sources), len(out_...  21.5 us
    ppermute x12, starting transfers between devices, send_first(): return lax.ppermute(x, 'pas', ring_pairs(0, k))  17.1 us
    ppermute x20, waiting for transfers between devices, send_tp(): return lax.ppermute(x, 'tp', [(i, (i + k) % SIDE) for i in range(SIDE)])  15.2 us
    pallas_call x2, Pallas kernels, project(): pl.pallas_call(functools.partial(project_kernel, first, len(pieces)), out...  5.93 us
  transfers between devices with their start and end apart: 65, of which 35 were waited for; matrix products, arithmetic and copies ran while one was open for 1% of the time, Pallas kernels for 13%

profile of v6, /device:TPU:0, one launch (start us, length us, event | category | flops | bytes accessed | tf_op | source)
XLA Modules:
  0.0 247.6 jit_solution(15342102403338441058)
XLA Ops:
  0.6 4.0 %collective-permute-start.1 = (bf16[32,2048]{1,0:T(8,128)(2,1)}, bf16[32,2048]{1,0:T(8,128)(2,1)S(1)}, u32[]{:S(2)}, u32[]{:S(2)}) collective-permute-start(bf16[32,2048]{1,0:T(8,128)(2,1)} %param.8), channel_id=1, source_target_pairs={{0,16},{4,68},{8,24},{12,76},{16,0},{20,84},{24,8},{28,92},{32,48}... | collective-permute-start | bytes 393224 | tf_op jit(solution)/shard_map/ppermute | solution.py:40
  5.7 2.2 collective-permute-start.2
  12.0 3.1 %collective-permute-start.9 = (bf16[128,2048]{1,0:T(8,128)(2,1)S(1)}, bf16[128,2048]{1,0:T(8,128)(2,1)S(1)}, u32[]{:S(2)}, u32[]{:S(2)}) collective-permute-start(bf16[128,2048]{1,0:T(8,128)(2,1)S(1)} %pad_maximum_fusion.rest_0_), channel_id=1, source_target_pairs={{0,96},{4,28},{8,104},{12,4},{16,112},{20,12},{24,120},{28,20},{32... | collective-permute-start | bytes 1572872 | tf_op jit(solution)/shard_map/ppermute | solution.py:44
  16.7 10.7 %collective-permute-done.9.rest_3_ = bf16[128,2048]{1,0:T(8,128)(2,1)S(1)} collective-permute-done((bf16[128,2048]{1,0:T(8,128)(2,1)S(1)}, bf16[128,2048]{1,0:T(8,128)(2,1)S(1)}, u32[]{:S(2)}, u32[]{:S(2)}) %collective-permute-start.9) | collective-permute-done | bytes 524320 | tf_op jit(solution)/shard_map/ppermute | solution.py:44
  27.9 3.5 %collective-permute-done.7.rest_1_ = bf16[128,2048]{1,0:T(8,128)(2,1)S(1)} collective-permute-done((bf16[128,2048]{1,0:T(8,128)(2,1)S(1)}, bf16[128,2048]{1,0:T(8,128)(2,1)S(1)}, u32[]{:S(2)}, u32[]{:S(2)}) %collective-permute-start.7) | collective-permute-done | bytes 524320 | tf_op jit(solution)/shard_map/ppermute | solution.py:44
  31.4 1.9 collective-permute-done.11.rest_5_
  33.3 2.2 copy-done
  35.5 3.2 %project.2 = (f32[256,256]{1,0:T(8,128)S(1)}, f32[256,256]{1,0:T(8,128)S(1)}, f32[256,256]{1,0:T(8,128)S(1)}, bf16[256,384]{1,0:T(8,128)(2,1)S(1)}, f32[256,256]...) custom-call(bf16[1024,2048]{1,0:T(8,128)(2,1)S(1)} %copy-done, ...), custom_call_target="tpu_custom_call" | custom-call | flops 2147483648 | bytes 8388608 | tf_op jit(solution)/shard_map/project/pallas_call | solution.py:149
  40.3 1.7 collective-permute-start.17
  42.0 2.7 %project.3 = (f32[256,256]{1,0:T(8,128)S(1)}, f32[256,256]{1,0:T(8,128)S(1)}, f32[256,256]{1,0:T(8,128)S(1)}, bf16[256,384]{1,0:T(8,128)(2,1)S(1)}, f32[256,256]...) custom-call(bf16[1024,2048]{1,0:T(8,128)(2,1)S(1)} %copy-done, ...), custom_call_target="tpu_custom_call" | custom-call | flops 2147483648 | bytes 8388608 | tf_op jit(solution)/shard_map/project/pallas_call | solution.py:149
  45.1 3.0 %collective-permute-start.23 = (bf16[256,384]{1,0:T(8,128)(2,1)S(1)}, bf16[256,384]{1,0:T(8,128)(2,1)S(1)}, u32[]{:S(2)}, u32[]{:S(2)}) collective-permute-start(bf16[256,384]{1,0:T(8,128)(2,1)S(1)} %get-tuple-element.59), channel_id=1, source_target_pairs={{0,3},{1,0},{2,1},{3,2},{4,7},{5,4},{6,5},{7,6},{8,11},{9,8},{10,9... | collective-permute-start | bytes 589832 | tf_op jit(solution)/shard_map/ppermute | solution.py:48
  48.3 3.3 %collective-permute-start.18 = (bf16[256,384]{1,0:T(8,128)(2,1)S(1)}, bf16[256,384]{1,0:T(8,128)(2,1)S(1)}, u32[]{:S(2)}, u32[]{:S(2)}) collective-permute-start(bf16[256,384]{1,0:T(8,128)(2,1)S(1)} %relay.10), channel_id=1, source_target_pairs={{0,3},{1,0},{2,1},{3,2},{4,7},{5,4},{6,5},{7,6},{8,11},{9,8},{10,9... | collective-permute-start | bytes 589832 | tf_op jit(solution)/shard_map/ppermute | solution.py:48
  51.5 2.2 collective-permute-done.20.got_ref
  54.0 3.3 %collective-permute-start.24 = (bf16[256,384]{1,0:T(8,128)(2,1)S(1)}, bf16[256,384]{1,0:T(8,128)(2,1)S(1)}, u32[]{:S(2)}, u32[]{:S(2)}) collective-permute-start(bf16[256,384]{1,0:T(8,128)(2,1)S(1)} %relay.14), channel_id=1, source_target_pairs={{0,3},{1,0},{2,1},{3,2},{4,7},{5,4},{6,5},{7,6},{8,11},{9,8},{10,9... | collective-permute-start | bytes 589832 | tf_op jit(solution)/shard_map/ppermute | solution.py:48
  58.2 3.3 %collective-permute-start.19 = (bf16[256,384]{1,0:T(8,128)(2,1)S(1)}, bf16[256,384]{1,0:T(8,128)(2,1)S(1)}, u32[]{:S(2)}, u32[]{:S(2)}) collective-permute-start(bf16[256,384]{1,0:T(8,128)(2,1)S(1)} %relay.11), channel_id=1, source_target_pairs={{0,3},{1,0},{2,1},{3,2},{4,7},{5,4},{6,5},{7,6},{8,11},{9,8},{10,9... | collective-permute-start | bytes 589832 | tf_op jit(solution)/shard_map/ppermute | solution.py:48
  62.6 3.5 %collective-permute-start.25 = (bf16[256,384]{1,0:T(8,128)(2,1)S(1)}, bf16[256,384]{1,0:T(8,128)(2,1)S(1)}, u32[]{:S(2)}, u32[]{:S(2)}) collective-permute-start(bf16[256,384]{1,0:T(8,128)(2,1)S(1)} %relay.15), channel_id=1, source_target_pairs={{0,3},{1,0},{2,1},{3,2},{4,7},{5,4},{6,5},{7,6},{8,11},{9,8},{10,9... | collective-permute-start | bytes 589832 | tf_op jit(solution)/shard_map/ppermute | solution.py:48
  67.1 2.3 collective-permute-done.22.refs_2_
  69.6 3.3 %collective-permute-start.28 = (bf16[8,128,256]{2,1,0:T(8,128)(2,1)S(1)}, bf16[8,128,256]{2,1,0:T(8,128)(2,1)S(1)}, u32[]{:S(2)}, u32[]{:S(2)}) collective-permute-start(bf16[8,128,256]{2,1,0:T(8,128)(2,1)S(1)} %bitcast.19), channel_id=1, source_target_pairs={{0,24},{4,100},{8,0},{12,108},{16,8},{20,116},{24,16},{28,124},{32... | collective-permute-start | bytes 1572872 | tf_op jit(solution)/shard_map/ppermute | solution.py:40
  75.4 2.7 %collective-permute-start.5 = (s32[64,2]{0,1:T(2,128)S(1)}, s32[64,2]{0,1:T(2,128)S(1)}, u32[]{:S(2)}, u32[]{:S(2)}) collective-permute-start(s32[64,2]{0,1:T(2,128)S(1)} %pad_add_fusion.1), channel_id=1, source_target_pairs={{0,64},{4,20},{8,72},{12,28},{16,80},{20,4},{24,88},{28,12},{32,96... | collective-permute-start | bytes 1544 | tf_op jit(solution)/shard_map/ppermute | solution.py:44
  78.1 2.1 collective-permute-done.6
  80.6 3.1 %collective-permute-done.4 = s32[64,2]{0,1:T(2,128)S(1)} collective-permute-done((s32[64,2]{0,1:T(2,128)S(1)}, s32[64,2]{0,1:T(2,128)S(1)}, u32[]{:S(2)}, u32[]{:S(2)}) %collective-permute-start.4) | collective-permute-done | bytes 544 | tf_op jit(solution)/shard_map/ppermute | solution.py:44
  85.2 3.7 %collective-permute-done.26.rest_1_ = bf16[8,128,256]{2,1,0:T(8,128)(2,1)S(1)} collective-permute-done((bf16[8,128,256]{2,1,0:T(8,128)(2,1)S(1)}, bf16[8,128,256]{2,1,0:T(8,128)(2,1)S(1)}, u32[]{:S(2)}, u32[]{:S(2)}) %collective-permute-start.26) | collective-permute-done | bytes 524320 | tf_op jit(solution)/shard_map/ppermute | solution.py:40
  89.9 2.7 %collective-permute-start.35 = (bf16[8,128,256]{2,1,0:T(8,128)(2,1)S(1)}, bf16[8,128,256]{2,1,0:T(8,128)(2,1)S(1)}, u32[]{:S(2)}, u32[]{:S(2)}) collective-permute-start(bf16[8,128,256]{2,1,0:T(8,128)(2,1)S(1)} %get-tuple-element.72), channel_id=1, source_target_pairs={{0,64},{4,20},{8,72},{12,28},{16,80},{20,4},{24,88},{28,12},{32,96... | collective-permute-start | bytes 1572872 | tf_op jit(solution)/shard_map/ppermute | solution.py:44
  96.9 9.0 %collective-permute-done.33 = bf16[8,128,256]{2,1,0:T(8,128)(2,1)S(1)} collective-permute-done((bf16[8,128,256]{2,1,0:T(8,128)(2,1)S(1)}, bf16[8,128,256]{2,1,0:T(8,128)(2,1)S(1)}, u32[]{:S(2)}, u32[]{:S(2)}) %collective-permute-start.33) | collective-permute-done | bytes 524320 | tf_op jit(solution)/shard_map/ppermute | solution.py:44
  106.8 10.3 %collective-permute-done.30.rest_1_ = bf16[8,128,256]{2,1,0:T(8,128)(2,1)S(1)} collective-permute-done((bf16[8,128,256]{2,1,0:T(8,128)(2,1)S(1)}, bf16[8,128,256]{2,1,0:T(8,128)(2,1)S(1)}, u32[]{:S(2)}, u32[]{:S(2)}) %collective-permute-start.30) | collective-permute-done | bytes 524320 | tf_op jit(solution)/shard_map/ppermute | solution.py:44
  121.2 21.5 %attention.1 = (bf16[512,1024]{1,0:T(8,128)(2,1)}, bf16[512,256]{1,0:T(8,128)(2,1)}, bf16[8,128,256]{2,1,0:T(8,128)(2,1)S(1)}, bf16[8,128,256]{2,1,0:T(8,128)(2,...) custom-call(s32[64]{0:T(128)S(1)} %select_reduce_fusion.rest_5_.taken_, ...), custom_call_target="tpu_custom_call" | custom-call | flops 6039797760 | bytes 8912896 | tf_op jit(solution)/shard_map/attention/pallas_call | solution.py:387
  148.2 3.8 %collective-permute-done.40.rest_2_ = bf16[8,128,256]{2,1,0:T(8,128)(2,1)S(1)} collective-permute-done((bf16[8,128,256]{2,1,0:T(8,128)(2,1)S(1)}, bf16[8,128,256]{2,1,0:T(8,128)(2,1)S(1)}, u32[]{:S(2)}, u32[]{:S(2)}) %collective-permute-start.40) | collective-permute-done | bytes 524320 | tf_op jit(solution)/shard_map/ppermute | solution.py:44
  153.0 2.2 collective-permute-done.42.rest_4_
  155.2 5.2 %collective-permute-start.41 = (bf16[8,128,256]{2,1,0:T(8,128)(2,1)S(1)}, bf16[8,128,256]{2,1,0:T(8,128)(2,1)S(1)}, u32[]{:S(2)}, u32[]{:S(2)}) collective-permute-start(bf16[8,128,256]{2,1,0:T(8,128)(2,1)S(1)} %get-tuple-element.99), channel_id=1, source_target_pairs={{0,96},{4,28},{8,104},{12,4},{16,112},{20,12},{24,120},{28,20},{32... | collective-permute-start | bytes 1572872 | tf_op jit(solution)/shard_map/ppermute | solution.py:44
  160.4 5.6 %collective-permute-done.45.rest_7_ = bf16[8,128,256]{2,1,0:T(8,128)(2,1)S(1)} collective-permute-done((bf16[8,128,256]{2,1,0:T(8,128)(2,1)S(1)}, bf16[8,128,256]{2,1,0:T(8,128)(2,1)S(1)}, u32[]{:S(2)}, u32[]{:S(2)}) %collective-permute-start.45) | collective-permute-done | bytes 524320 | tf_op jit(solution)/shard_map/ppermute | solution.py:44
  166.0 6.0 %collective-permute-done.43.rest_5_ = bf16[8,128,256]{2,1,0:T(8,128)(2,1)S(1)} collective-permute-done((bf16[8,128,256]{2,1,0:T(8,128)(2,1)S(1)}, bf16[8,128,256]{2,1,0:T(8,128)(2,1)S(1)}, u32[]{:S(2)}, u32[]{:S(2)}) %collective-permute-start.43) | collective-permute-done | bytes 524320 | tf_op jit(solution)/shard_map/ppermute | solution.py:44
  172.0 2.5 %add_blocks.1 = (f32[8,128,256]{2,1,0:T(8,128)S(1)}, bf16[8,128,256]{2,1,0:T(8,128)(2,1)S(1)}, bf16[8,128,256]{2,1,0:T(8,128)(2,1)S(1)}, bf16[8,128,256]{2,1,0:T(8,128)(2,1)S(1)}) custom-call(s32[64]{0:T(128)S(1)} %gather_fusion, bf16[8,128,256]{2,1,0:T(8,128)(2,1)S(1)} %get-tuple-element.76.rest_0_, bf16[8,128,256]{2,1,0:T(8,128)(2,1)S(1)} %get-tuple-element.100.rest_1_, ...), custom_call_target="tpu_custom_call" | custom-call | flops 2097152 | bytes 8388608 | tf_op jit(solution)/shard_map/add_blocks/pallas_call | solution.py:469
  176.6 7.2 %collective-permute-done.46.left_ref = bf16[8,128,256]{2,1,0:T(8,128)(2,1)S(1)} collective-permute-done((bf16[8,128,256]{2,1,0:T(8,128)(2,1)S(1)}, bf16[8,128,256]{2,1,0:T(8,128)(2,1)S(1)}, u32[]{:S(2)}, u32[]{:S(2)}) %collective-permute-start.46) | collective-permute-done | bytes 524320 | tf_op jit(solution)/shard_map/ppermute | solution.py:40
  183.8 2.5 %collective-permute-done.47.far_ref = bf16[8,128,256]{2,1,0:T(8,128)(2,1)S(1)} collective-permute-done((bf16[8,128,256]{2,1,0:T(8,128)(2,1)S(1)}, bf16[8,128,256]{2,1,0:T(8,128)(2,1)S(1)}, u32[]{:S(2)}, u32[]{:S(2)}) %collective-permute-start.47) | collective-permute-done | bytes 524320 | tf_op jit(solution)/shard_map/ppermute | solution.py:40
  186.3 5.5 %collective-permute-done.48.right_ref = bf16[8,128,256]{2,1,0:T(8,128)(2,1)S(1)} collective-permute-done((bf16[8,128,256]{2,1,0:T(8,128)(2,1)S(1)}, bf16[8,128,256]{2,1,0:T(8,128)(2,1)S(1)}, u32[]{:S(2)}, u32[]{:S(2)}) %collective-permute-start.48) | collective-permute-done | bytes 524320 | tf_op jit(solution)/shard_map/ppermute | solution.py:40
  192.3 3.6 %collective-permute-start.57 = (bf16[128,1024]{1,0:T(8,128)(2,1)S(1)}, bf16[128,1024]{1,0:T(8,128)(2,1)S(1)}, u32[]{:S(2)}, u32[]{:S(2)}) collective-permute-start(bf16[128,1024]{1,0:T(8,128)(2,1)S(1)} %get-tuple-element.86.refs_0_), channel_id=1, source_target_pairs={{0,3},{1,0},{2,1},{3,2},{4,7},{5,4},{6,5},{7,6},{8,11},{9,8},{10,9... | collective-permute-start | bytes 786440 | tf_op jit(solution)/shard_map/ppermute | solution.py:48
  195.9 3.2 %collective-permute-start.52 = (bf16[128,1024]{1,0:T(8,128)(2,1)S(1)}, bf16[128,1024]{1,0:T(8,128)(2,1)S(1)}, u32[]{:S(2)}, u32[]{:S(2)}) collective-permute-start(bf16[128,1024]{1,0:T(8,128)(2,1)S(1)} %collective-permute-done.49.refs_0_), channel_id=1, source_target_pairs={{0,3},{1,0},{2,1},{3,2},{4,7},{5,4},{6,5},{7,6},{8,11},{9,8},{10,9... | collective-permute-start | bytes 786440 | tf_op jit(solution)/shard_map/ppermute | solution.py:48
  199.2 3.4 %collective-permute-done.57.refs_4_ = bf16[128,1024]{1,0:T(8,128)(2,1)S(1)} collective-permute-done((bf16[128,1024]{1,0:T(8,128)(2,1)S(1)}, bf16[128,1024]{1,0:T(8,128)(2,1)S(1)}, u32[]{:S(2)}, u32[]{:S(2)}) %collective-permute-start.57) | collective-permute-done | bytes 262176 | tf_op jit(solution)/shard_map/ppermute | solution.py:48
  202.6 3.8 %collective-permute-start.58 = (bf16[64,1024]{1,0:T(8,128)(2,1)S(1)}, bf16[64,1024]{1,0:T(8,128)(2,1)S(1)}, u32[]{:S(2)}, u32[]{:S(2)}) collective-permute-start(bf16[64,1024]{1,0:T(8,128)(2,1)S(1)} %slice.62), channel_id=1, source_target_pairs={{0,3},{1,0},{2,1},{3,2},{4,7},{5,4},{6,5},{7,6},{8,11},{9,8},{10,9... | collective-permute-start | bytes 393224 | tf_op jit(solution)/shard_map/ppermute | solution.py:48
  206.4 1.7 collective-permute-done.52.refs_4_
  208.2 3.8 %collective-permute-start.53 = (bf16[64,1024]{1,0:T(8,128)(2,1)S(1)}, bf16[64,1024]{1,0:T(8,128)(2,1)S(1)}, u32[]{:S(2)}, u32[]{:S(2)}) collective-permute-start(bf16[64,1024]{1,0:T(8,128)(2,1)S(1)} %slice.60), channel_id=1, source_target_pairs={{0,3},{1,0},{2,1},{3,2},{4,7},{5,4},{6,5},{7,6},{8,11},{9,8},{10,9... | collective-permute-start | bytes 393224 | tf_op jit(solution)/shard_map/ppermute | solution.py:48
  212.1 1.9 collective-permute-done.56.refs_2_
  213.9 3.3 %first_weight_product.1.refs_6_ = f32[512,2048]{1,0:T(8,128)S(1)} custom-call(bf16[128,1024]{1,0:T(8,128)(2,1)S(1)} %get-tuple-element.86.refs_0_, bf16[128,1024]{1,0:T(8,128)(2,1)S(1)} %collective-permute-done.55.refs_1_, bf16[64,1024]{1,0:T(8,128)(2,1)S(1)} %collective-permute-done.56.refs_2_, bf16[64,1024]{1,0:T(8,128)(2,1)S(1)} %collective-permute-done.58.refs_3_, ...), custom_call_target="tpu_custom_call" | custom-call | flops 2147483648 | bytes 8388608 | tf_op jit(solution)/shard_map/first_weight_product/pallas_call | solution.py:271
  218.2 3.6 %second_weight_product.1 = (f32[4,32,2048]{2,1,0:T(8,128)S(1)}, bf16[4,32,2048]{2,1,0:T(8,128)(2,1)S(1)}, bf16[4,32,2048]{2,1,0:T(8,128)(2,1)S(1)}, bf16[4,32,2048]{2,1,0:T(8,128)(2,1)S(1)}) custom-call(bf16[128,1024]{1,0:T(8,128)(2,1)S(1)} %collective-permute-done.49.refs_0_, bf16[128,1024]{1,0:T(8,128)(2,1)S(1)} %collective-permute-done.50.refs_1_, ...), custom_call_target="tpu_custom_call" | custom-call | flops 2147483648 | bytes 8388608 | tf_op jit(solution)/shard_map/second_weight_product/pallas_call | solution.py:280
  221.9 3.2 %collective-permute-start.60 = (bf16[4,32,2048]{2,1,0:T(8,128)(2,1)S(1)}, bf16[4,32,2048]{2,1,0:T(8,128)(2,1)S(1)}, u32[]{:S(2)}, u32[]{:S(2)}) collective-permute-start(bf16[4,32,2048]{2,1,0:T(8,128)(2,1)S(1)} %get-tuple-element.89), channel_id=1, source_target_pairs={{0,24},{4,100},{8,0},{12,108},{16,8},{20,116},{24,16},{28,124},{32... | collective-permute-start | bytes 1572872 | tf_op jit(solution)/shard_map/ppermute | solution.py:40
  225.1 12.8 %collective-permute-done.59 = bf16[4,32,2048]{2,1,0:T(8,128)(2,1)S(1)} collective-permute-done((bf16[4,32,2048]{2,1,0:T(8,128)(2,1)S(1)}, bf16[4,32,2048]{2,1,0:T(8,128)(2,1)S(1)}, u32[]{:S(2)}, u32[]{:S(2)}) %collective-permute-start.59) | collective-permute-done | bytes 524320 | tf_op jit(solution)/shard_map/ppermute | solution.py:40
  239.2 2.4 collective-permute-start.63
  241.6 4.3 %collective-permute-done.62 = bf16[32,2048]{1,0:T(8,128)(2,1)S(1)} collective-permute-done((bf16[32,2048]{1,0:T(8,128)(2,1)S(1)}, bf16[32,2048]{1,0:T(8,128)(2,1)S(1)}, u32[]{:S(2)}, u32[]{:S(2)}) %collective-permute-start.62) | collective-permute-done | bytes 131104 | tf_op jit(solution)/shard_map/ppermute | solution.py:44
  (138 shorter events, 40.6 us)
Async XLA Ops:
  0.6 9.2 %collective-permute-start.1 = (bf16[32,2048]{1,0:T(8,128)(2,1)}, bf16[32,2048]{1,0:T(8,128)(2,1)S(1)}, u32[]{:S(2)}, u32[]{:S(2)}) collective-permute-start(bf16[32,2048]{1,0:T(8,128)(2,1)} %param.8), channel_id=1, source_target_pairs={{0,16},{4,68},{8,24},{12,76},{16,0},{20,84},{24,8},{28,92},{32,48}... | collective-permute-start | bytes 393224 | tf_op jit(solution)/shard_map/ppermute | solution.py:40
  12.0 15.4 %collective-permute-start.9 = (bf16[128,2048]{1,0:T(8,128)(2,1)S(1)}, bf16[128,2048]{1,0:T(8,128)(2,1)S(1)}, u32[]{:S(2)}, u32[]{:S(2)}) collective-permute-start(bf16[128,2048]{1,0:T(8,128)(2,1)S(1)} %pad_maximum_fusion.rest_0_), channel_id=1, source_target_pairs={{0,96},{4,28},{8,104},{12,4},{16,112},{20,12},{24,120},{28,20},{32... | collective-permute-start | bytes 1572872 | tf_op jit(solution)/shard_map/ppermute | solution.py:44
  15.1 12.3 %collective-permute-start.8 = (bf16[128,2048]{1,0:T(8,128)(2,1)S(1)}, bf16[128,2048]{1,0:T(8,128)(2,1)S(1)}, u32[]{:S(2)}, u32[]{:S(2)}) collective-permute-start(bf16[128,2048]{1,0:T(8,128)(2,1)S(1)} %pad_maximum_fusion.rest_0_), channel_id=1, source_target_pairs={{0,64},{4,20},{8,72},{12,28},{16,80},{20,4},{24,88},{28,12},{32,96... | collective-permute-start | bytes 1572872 | tf_op jit(solution)/shard_map/ppermute | solution.py:44
  15.7 15.7 %collective-permute-start.7 = (bf16[128,2048]{1,0:T(8,128)(2,1)S(1)}, bf16[128,2048]{1,0:T(8,128)(2,1)S(1)}, u32[]{:S(2)}, u32[]{:S(2)}) collective-permute-start(bf16[128,2048]{1,0:T(8,128)(2,1)S(1)} %pad_maximum_fusion.rest_0_), channel_id=1, source_target_pairs={{0,32},{4,12},{8,40},{12,20},{16,48},{20,28},{24,56},{28,4},{32,64... | collective-permute-start | bytes 1572872 | tf_op jit(solution)/shard_map/ppermute | solution.py:44
  16.7 14.7 %collective-permute-start.10 = (bf16[128,2048]{1,0:T(8,128)(2,1)S(1)}, bf16[128,2048]{1,0:T(8,128)(2,1)S(1)}, u32[]{:S(2)}, u32[]{:S(2)}) collective-permute-start(bf16[128,2048]{1,0:T(8,128)(2,1)S(1)} %pad_maximum_fusion.rest_0_), channel_id=1, source_target_pairs={{0,4},{4,0},{8,12},{12,8},{16,20},{20,16},{24,28},{28,24},{32,36},... | collective-permute-start | bytes 1572872 | tf_op jit(solution)/shard_map/ppermute | solution.py:52
  38.7 9.3 %collective-permute-start.14 = (bf16[256,384]{1,0:T(8,128)(2,1)S(1)}, bf16[256,384]{1,0:T(8,128)(2,1)S(1)}, u32[]{:S(2)}, u32[]{:S(2)}) collective-permute-start(bf16[256,384]{1,0:T(8,128)(2,1)S(1)} %get-tuple-element.49), channel_id=1, source_target_pairs={{0,1},{1,2},{2,3},{3,0},{4,5},{5,6},{6,7},{7,4},{8,9},{9,10},{10,1... | collective-permute-start | bytes 589832 | tf_op jit(solution)/shard_map/ppermute | solution.py:48
  40.3 7.9 %collective-permute-start.17 = (bf16[256,384]{1,0:T(8,128)(2,1)S(1)}, bf16[256,384]{1,0:T(8,128)(2,1)S(1)}, u32[]{:S(2)}, u32[]{:S(2)}) collective-permute-start(bf16[256,384]{1,0:T(8,128)(2,1)S(1)} %get-tuple-element.52), channel_id=1, source_target_pairs={{0,3},{1,0},{2,1},{3,2},{4,7},{5,4},{6,5},{7,6},{8,11},{9,8},{10,9... | collective-permute-start | bytes 589832 | tf_op jit(solution)/shard_map/ppermute | solution.py:48
  44.7 9.0 %collective-permute-start.20 = (bf16[256,384]{1,0:T(8,128)(2,1)S(1)}, bf16[256,384]{1,0:T(8,128)(2,1)S(1)}, u32[]{:S(2)}, u32[]{:S(2)}) collective-permute-start(bf16[256,384]{1,0:T(8,128)(2,1)S(1)} %get-tuple-element.56), channel_id=1, source_target_pairs={{0,1},{1,2},{2,3},{3,0},{4,5},{5,6},{6,7},{7,4},{8,9},{9,10},{10,1... | collective-permute-start | bytes 589832 | tf_op jit(solution)/shard_map/ppermute | solution.py:48
  45.1 8.8 %collective-permute-start.23 = (bf16[256,384]{1,0:T(8,128)(2,1)S(1)}, bf16[256,384]{1,0:T(8,128)(2,1)S(1)}, u32[]{:S(2)}, u32[]{:S(2)}) collective-permute-start(bf16[256,384]{1,0:T(8,128)(2,1)S(1)} %get-tuple-element.59), channel_id=1, source_target_pairs={{0,3},{1,0},{2,1},{3,2},{4,7},{5,4},{6,5},{7,6},{8,11},{9,8},{10,9... | collective-permute-start | bytes 589832 | tf_op jit(solution)/shard_map/ppermute | solution.py:48
  48.1 9.9 %collective-permute-start.15 = (bf16[256,384]{1,0:T(8,128)(2,1)S(1)}, bf16[256,384]{1,0:T(8,128)(2,1)S(1)}, u32[]{:S(2)}, u32[]{:S(2)}) collective-permute-start(bf16[256,384]{1,0:T(8,128)(2,1)S(1)} %relay.8), channel_id=1, source_target_pairs={{0,1},{1,2},{2,3},{3,0},{4,5},{5,6},{6,7},{7,4},{8,9},{9,10},{10,1... | collective-permute-start | bytes 589832 | tf_op jit(solution)/shard_map/ppermute | solution.py:48
  48.3 9.8 %collective-permute-start.18 = (bf16[256,384]{1,0:T(8,128)(2,1)S(1)}, bf16[256,384]{1,0:T(8,128)(2,1)S(1)}, u32[]{:S(2)}, u32[]{:S(2)}) collective-permute-start(bf16[256,384]{1,0:T(8,128)(2,1)S(1)} %relay.10), channel_id=1, source_target_pairs={{0,3},{1,0},{2,1},{3,2},{4,7},{5,4},{6,5},{7,6},{8,11},{9,8},{10,9... | collective-permute-start | bytes 589832 | tf_op jit(solution)/shard_map/ppermute | solution.py:48
  53.8 8.6 %collective-permute-start.21 = (bf16[256,384]{1,0:T(8,128)(2,1)S(1)}, bf16[256,384]{1,0:T(8,128)(2,1)S(1)}, u32[]{:S(2)}, u32[]{:S(2)}) collective-permute-start(bf16[256,384]{1,0:T(8,128)(2,1)S(1)} %relay.12), channel_id=1, source_target_pairs={{0,1},{1,2},{2,3},{3,0},{4,5},{5,6},{6,7},{7,4},{8,9},{9,10},{10,1... | collective-permute-start | bytes 589832 | tf_op jit(solution)/shard_map/ppermute | solution.py:48
  54.0 8.6 %collective-permute-start.24 = (bf16[256,384]{1,0:T(8,128)(2,1)S(1)}, bf16[256,384]{1,0:T(8,128)(2,1)S(1)}, u32[]{:S(2)}, u32[]{:S(2)}) collective-permute-start(bf16[256,384]{1,0:T(8,128)(2,1)S(1)} %relay.14), channel_id=1, source_target_pairs={{0,3},{1,0},{2,1},{3,2},{4,7},{5,4},{6,5},{7,6},{8,11},{9,8},{10,9... | collective-permute-start | bytes 589832 | tf_op jit(solution)/shard_map/ppermute | solution.py:48
  58.0 9.1 %collective-permute-start.16 = (bf16[256,384]{1,0:T(8,128)(2,1)S(1)}, bf16[256,384]{1,0:T(8,128)(2,1)S(1)}, u32[]{:S(2)}, u32[]{:S(2)}) collective-permute-start(bf16[256,384]{1,0:T(8,128)(2,1)S(1)} %relay.9), channel_id=1, source_target_pairs={{0,1},{1,2},{2,3},{3,0},{4,5},{5,6},{6,7},{7,4},{8,9},{9,10},{10,1... | collective-permute-start | bytes 589832 | tf_op jit(solution)/shard_map/ppermute | solution.py:48
  58.2 9.0 %collective-permute-start.19 = (bf16[256,384]{1,0:T(8,128)(2,1)S(1)}, bf16[256,384]{1,0:T(8,128)(2,1)S(1)}, u32[]{:S(2)}, u32[]{:S(2)}) collective-permute-start(bf16[256,384]{1,0:T(8,128)(2,1)S(1)} %relay.11), channel_id=1, source_target_pairs={{0,3},{1,0},{2,1},{3,2},{4,7},{5,4},{6,5},{7,6},{8,11},{9,8},{10,9... | collective-permute-start | bytes 589832 | tf_op jit(solution)/shard_map/ppermute | solution.py:48
  69.6 15.6 %collective-permute-start.28 = (bf16[8,128,256]{2,1,0:T(8,128)(2,1)S(1)}, bf16[8,128,256]{2,1,0:T(8,128)(2,1)S(1)}, u32[]{:S(2)}, u32[]{:S(2)}) collective-permute-start(bf16[8,128,256]{2,1,0:T(8,128)(2,1)S(1)} %bitcast.19), channel_id=1, source_target_pairs={{0,24},{4,100},{8,0},{12,108},{16,8},{20,116},{24,16},{28,124},{32... | collective-permute-start | bytes 1572872 | tf_op jit(solution)/shard_map/ppermute | solution.py:40
  72.9 12.3 %collective-permute-start.27 = (bf16[8,128,256]{2,1,0:T(8,128)(2,1)S(1)}, bf16[8,128,256]{2,1,0:T(8,128)(2,1)S(1)}, u32[]{:S(2)}, u32[]{:S(2)}) collective-permute-start(bf16[8,128,256]{2,1,0:T(8,128)(2,1)S(1)} %bitcast.20), channel_id=1, source_target_pairs={{0,16},{4,68},{8,24},{12,76},{16,0},{20,84},{24,8},{28,92},{32,48}... | collective-permute-start | bytes 1572872 | tf_op jit(solution)/shard_map/ppermute | solution.py:40
  72.9 16.0 %collective-permute-start.26 = (bf16[8,128,256]{2,1,0:T(8,128)(2,1)S(1)}, bf16[8,128,256]{2,1,0:T(8,128)(2,1)S(1)}, u32[]{:S(2)}, u32[]{:S(2)}) collective-permute-start(bf16[8,128,256]{2,1,0:T(8,128)(2,1)S(1)} %bitcast.21), channel_id=1, source_target_pairs={{0,8},{4,36},{8,16},{12,44},{16,24},{20,52},{24,0},{28,60},{32,40}... | collective-permute-start | bytes 1572872 | tf_op jit(solution)/shard_map/ppermute | solution.py:40
  89.8 16.1 %collective-permute-start.33 = (bf16[8,128,256]{2,1,0:T(8,128)(2,1)S(1)}, bf16[8,128,256]{2,1,0:T(8,128)(2,1)S(1)}, u32[]{:S(2)}, u32[]{:S(2)}) collective-permute-start(bf16[8,128,256]{2,1,0:T(8,128)(2,1)S(1)} %get-tuple-element.71), channel_id=1, source_target_pairs={{0,32},{4,12},{8,40},{12,20},{16,48},{20,28},{24,56},{28,4},{32,64... | collective-permute-start | bytes 1572872 | tf_op jit(solution)/shard_map/ppermute | solution.py:44
  89.9 16.0 %collective-permute-start.35 = (bf16[8,128,256]{2,1,0:T(8,128)(2,1)S(1)}, bf16[8,128,256]{2,1,0:T(8,128)(2,1)S(1)}, u32[]{:S(2)}, u32[]{:S(2)}) collective-permute-start(bf16[8,128,256]{2,1,0:T(8,128)(2,1)S(1)} %get-tuple-element.72), channel_id=1, source_target_pairs={{0,64},{4,20},{8,72},{12,28},{16,80},{20,4},{24,88},{28,12},{32,96... | collective-permute-start | bytes 1572872 | tf_op jit(solution)/shard_map/ppermute | solution.py:44
  92.5 14.2 %collective-permute-start.37 = (bf16[8,128,256]{2,1,0:T(8,128)(2,1)S(1)}, bf16[8,128,256]{2,1,0:T(8,128)(2,1)S(1)}, u32[]{:S(2)}, u32[]{:S(2)}) collective-permute-start(bf16[8,128,256]{2,1,0:T(8,128)(2,1)S(1)} %get-tuple-element.73), channel_id=1, source_target_pairs={{0,96},{4,28},{8,104},{12,4},{16,112},{20,12},{24,120},{28,20},{32... | collective-permute-start | bytes 1572872 | tf_op jit(solution)/shard_map/ppermute | solution.py:44
  93.8 23.3 %collective-permute-start.30 = (bf16[8,128,256]{2,1,0:T(8,128)(2,1)S(1)}, bf16[8,128,256]{2,1,0:T(8,128)(2,1)S(1)}, u32[]{:S(2)}, u32[]{:S(2)}) collective-permute-start(bf16[8,128,256]{2,1,0:T(8,128)(2,1)S(1)} %get-tuple-element.68), channel_id=1, source_target_pairs={{0,32},{4,12},{8,40},{12,20},{16,48},{20,28},{24,56},{28,4},{32,64... | collective-permute-start | bytes 1572872 | tf_op jit(solution)/shard_map/ppermute | solution.py:44
  95.3 21.8 %collective-permute-start.31 = (bf16[8,128,256]{2,1,0:T(8,128)(2,1)S(1)}, bf16[8,128,256]{2,1,0:T(8,128)(2,1)S(1)}, u32[]{:S(2)}, u32[]{:S(2)}) collective-permute-start(bf16[8,128,256]{2,1,0:T(8,128)(2,1)S(1)} %get-tuple-element.69), channel_id=1, source_target_pairs={{0,64},{4,20},{8,72},{12,28},{16,80},{20,4},{24,88},{28,12},{32,96... | collective-permute-start | bytes 1572872 | tf_op jit(solution)/shard_map/ppermute | solution.py:44
  105.9 12.2 %collective-permute-start.32 = (bf16[8,128,256]{2,1,0:T(8,128)(2,1)S(1)}, bf16[8,128,256]{2,1,0:T(8,128)(2,1)S(1)}, u32[]{:S(2)}, u32[]{:S(2)}) collective-permute-start(bf16[8,128,256]{2,1,0:T(8,128)(2,1)S(1)} %get-tuple-element.70), channel_id=1, source_target_pairs={{0,96},{4,28},{8,104},{12,4},{16,112},{20,12},{24,120},{28,20},{32... | collective-permute-start | bytes 1572872 | tf_op jit(solution)/shard_map/ppermute | solution.py:44
  105.9 12.2 %collective-permute-start.34 = (bf16[8,128,256]{2,1,0:T(8,128)(2,1)S(1)}, bf16[8,128,256]{2,1,0:T(8,128)(2,1)S(1)}, u32[]{:S(2)}, u32[]{:S(2)}) collective-permute-start(bf16[8,128,256]{2,1,0:T(8,128)(2,1)S(1)} %collective-permute-done.33), channel_id=1, source_target_pairs={{0,4},{4,0},{8,12},{12,8},{16,20},{20,16},{24,28},{28,24},{32,36},... | collective-permute-start | bytes 1572872 | tf_op jit(solution)/shard_map/ppermute | solution.py:52
  106.8 11.3 %collective-permute-start.36 = (bf16[8,128,256]{2,1,0:T(8,128)(2,1)S(1)}, bf16[8,128,256]{2,1,0:T(8,128)(2,1)S(1)}, u32[]{:S(2)}, u32[]{:S(2)}) collective-permute-start(bf16[8,128,256]{2,1,0:T(8,128)(2,1)S(1)} %collective-permute-done.35), channel_id=1, source_target_pairs={{0,4},{4,0},{8,12},{12,8},{16,20},{20,16},{24,28},{28,24},{32,36},... | collective-permute-start | bytes 1572872 | tf_op jit(solution)/shard_map/ppermute | solution.py:52
  117.1 100.1 %collective-permute-start.54 = (bf16[1024,2048]{1,0:T(8,128)(2,1)S(1)}, bf16[1024,2048]{1,0:T(8,128)(2,1)S(1)}, u32[]{:S(2)}, u32[]{:S(2)}) collective-permute-start(bf16[1024,2048]{1,0:T(8,128)(2,1)S(1)} %copy-done.1), channel_id=1, source_target_pairs={{0,4},{4,0},{8,12},{12,8},{16,20},{20,16},{24,28},{28,24},{32,36},... | collective-permute-start | bytes 12582920 | tf_op jit(solution)/shard_map/ppermute | solution.py:52
  142.8 9.2 %collective-permute-start.40 = (bf16[8,128,256]{2,1,0:T(8,128)(2,1)S(1)}, bf16[8,128,256]{2,1,0:T(8,128)(2,1)S(1)}, u32[]{:S(2)}, u32[]{:S(2)}) collective-permute-start(bf16[8,128,256]{2,1,0:T(8,128)(2,1)S(1)} %get-tuple-element.78), channel_id=1, source_target_pairs={{0,96},{4,28},{8,104},{12,4},{16,112},{20,12},{24,120},{28,20},{32... | collective-permute-start | bytes 1572872 | tf_op jit(solution)/shard_map/ppermute | solution.py:44
  144.4 10.8 %collective-permute-start.42 = (bf16[8,128,256]{2,1,0:T(8,128)(2,1)S(1)}, bf16[8,128,256]{2,1,0:T(8,128)(2,1)S(1)}, u32[]{:S(2)}, u32[]{:S(2)}) collective-permute-start(bf16[8,128,256]{2,1,0:T(8,128)(2,1)S(1)} %get-tuple-element.79), channel_id=1, source_target_pairs={{0,64},{4,20},{8,72},{12,28},{16,80},{20,4},{24,88},{28,12},{32,96... | collective-permute-start | bytes 1572872 | tf_op jit(solution)/shard_map/ppermute | solution.py:44
  144.4 16.0 %collective-permute-start.44 = (bf16[8,128,256]{2,1,0:T(8,128)(2,1)S(1)}, bf16[8,128,256]{2,1,0:T(8,128)(2,1)S(1)}, u32[]{:S(2)}, u32[]{:S(2)}) collective-permute-start(bf16[8,128,256]{2,1,0:T(8,128)(2,1)S(1)} %get-tuple-element.80), channel_id=1, source_target_pairs={{0,32},{4,12},{8,40},{12,20},{16,48},{20,28},{24,56},{28,4},{32,64... | collective-permute-start | bytes 1572872 | tf_op jit(solution)/shard_map/ppermute | solution.py:44
  147.1 19.0 %collective-permute-start.45 = (bf16[8,128,256]{2,1,0:T(8,128)(2,1)S(1)}, bf16[8,128,256]{2,1,0:T(8,128)(2,1)S(1)}, u32[]{:S(2)}, u32[]{:S(2)}) collective-permute-start(bf16[8,128,256]{2,1,0:T(8,128)(2,1)S(1)} %get-tuple-element.97), channel_id=1, source_target_pairs={{0,32},{4,12},{8,40},{12,20},{16,48},{20,28},{24,56},{28,4},{32,64... | collective-permute-start | bytes 1572872 | tf_op jit(solution)/shard_map/ppermute | solution.py:44
  152.0 20.0 %collective-permute-start.43 = (bf16[8,128,256]{2,1,0:T(8,128)(2,1)S(1)}, bf16[8,128,256]{2,1,0:T(8,128)(2,1)S(1)}, u32[]{:S(2)}, u32[]{:S(2)}) collective-permute-start(bf16[8,128,256]{2,1,0:T(8,128)(2,1)S(1)} %get-tuple-element.98), channel_id=1, source_target_pairs={{0,64},{4,20},{8,72},{12,28},{16,80},{20,4},{24,88},{28,12},{32,96... | collective-permute-start | bytes 1572872 | tf_op jit(solution)/shard_map/ppermute | solution.py:44
  155.2 16.8 %collective-permute-start.41 = (bf16[8,128,256]{2,1,0:T(8,128)(2,1)S(1)}, bf16[8,128,256]{2,1,0:T(8,128)(2,1)S(1)}, u32[]{:S(2)}, u32[]{:S(2)}) collective-permute-start(bf16[8,128,256]{2,1,0:T(8,128)(2,1)S(1)} %get-tuple-element.99), channel_id=1, source_target_pairs={{0,96},{4,28},{8,104},{12,4},{16,112},{20,12},{24,120},{28,20},{32... | collective-permute-start | bytes 1572872 | tf_op jit(solution)/shard_map/ppermute | solution.py:44
  174.5 9.3 %collective-permute-start.46 = (bf16[8,128,256]{2,1,0:T(8,128)(2,1)S(1)}, bf16[8,128,256]{2,1,0:T(8,128)(2,1)S(1)}, u32[]{:S(2)}, u32[]{:S(2)}) collective-permute-start(bf16[8,128,256]{2,1,0:T(8,128)(2,1)S(1)} %get-tuple-element.82), channel_id=1, source_target_pairs={{0,24},{4,100},{8,0},{12,108},{16,8},{20,116},{24,16},{28,124},{32... | collective-permute-start | bytes 1572872 | tf_op jit(solution)/shard_map/ppermute | solution.py:40
  175.5 10.8 %collective-permute-start.47 = (bf16[8,128,256]{2,1,0:T(8,128)(2,1)S(1)}, bf16[8,128,256]{2,1,0:T(8,128)(2,1)S(1)}, u32[]{:S(2)}, u32[]{:S(2)}) collective-permute-start(bf16[8,128,256]{2,1,0:T(8,128)(2,1)S(1)} %get-tuple-element.83), channel_id=1, source_target_pairs={{0,16},{4,68},{8,24},{12,76},{16,0},{20,84},{24,8},{28,92},{32,48}... | collective-permute-start | bytes 1572872 | tf_op jit(solution)/shard_map/ppermute | solution.py:40
  175.5 16.3 %collective-permute-start.48 = (bf16[8,128,256]{2,1,0:T(8,128)(2,1)S(1)}, bf16[8,128,256]{2,1,0:T(8,128)(2,1)S(1)}, u32[]{:S(2)}, u32[]{:S(2)}) collective-permute-start(bf16[8,128,256]{2,1,0:T(8,128)(2,1)S(1)} %get-tuple-element.84), channel_id=1, source_target_pairs={{0,8},{4,36},{8,16},{12,44},{16,24},{20,52},{24,0},{28,60},{32,40}... | collective-permute-start | bytes 1572872 | tf_op jit(solution)/shard_map/ppermute | solution.py:40
  192.3 10.2 %collective-permute-start.57 = (bf16[128,1024]{1,0:T(8,128)(2,1)S(1)}, bf16[128,1024]{1,0:T(8,128)(2,1)S(1)}, u32[]{:S(2)}, u32[]{:S(2)}) collective-permute-start(bf16[128,1024]{1,0:T(8,128)(2,1)S(1)} %get-tuple-element.86.refs_0_), channel_id=1, source_target_pairs={{0,3},{1,0},{2,1},{3,2},{4,7},{5,4},{6,5},{7,6},{8,11},{9,8},{10,9... | collective-permute-start | bytes 786440 | tf_op jit(solution)/shard_map/ppermute | solution.py:48
  195.9 10.4 %collective-permute-start.55 = (bf16[128,1024]{1,0:T(8,128)(2,1)S(1)}, bf16[128,1024]{1,0:T(8,128)(2,1)S(1)}, u32[]{:S(2)}, u32[]{:S(2)}) collective-permute-start(bf16[128,1024]{1,0:T(8,128)(2,1)S(1)} %get-tuple-element.86.refs_0_), channel_id=1, source_target_pairs={{0,1},{1,2},{2,3},{3,0},{4,5},{5,6},{6,7},{7,4},{8,9},{9,10},{10,1... | collective-permute-start | bytes 786440 | tf_op jit(solution)/shard_map/ppermute | solution.py:48
  195.9 12.2 %collective-permute-start.52 = (bf16[128,1024]{1,0:T(8,128)(2,1)S(1)}, bf16[128,1024]{1,0:T(8,128)(2,1)S(1)}, u32[]{:S(2)}, u32[]{:S(2)}) collective-permute-start(bf16[128,1024]{1,0:T(8,128)(2,1)S(1)} %collective-permute-done.49.refs_0_), channel_id=1, source_target_pairs={{0,3},{1,0},{2,1},{3,2},{4,7},{5,4},{6,5},{7,6},{8,11},{9,8},{10,9... | collective-permute-start | bytes 786440 | tf_op jit(solution)/shard_map/ppermute | solution.py:48
  199.2 12.8 %collective-permute-start.50 = (bf16[128,1024]{1,0:T(8,128)(2,1)S(1)}, bf16[128,1024]{1,0:T(8,128)(2,1)S(1)}, u32[]{:S(2)}, u32[]{:S(2)}) collective-permute-start(bf16[128,1024]{1,0:T(8,128)(2,1)S(1)} %collective-permute-done.49.refs_0_), channel_id=1, source_target_pairs={{0,1},{1,2},{2,3},{3,0},{4,5},{5,6},{6,7},{7,4},{8,9},{9,10},{10,1... | collective-permute-start | bytes 786440 | tf_op jit(solution)/shard_map/ppermute | solution.py:48
  202.6 9.5 %collective-permute-start.58 = (bf16[64,1024]{1,0:T(8,128)(2,1)S(1)}, bf16[64,1024]{1,0:T(8,128)(2,1)S(1)}, u32[]{:S(2)}, u32[]{:S(2)}) collective-permute-start(bf16[64,1024]{1,0:T(8,128)(2,1)S(1)} %slice.62), channel_id=1, source_target_pairs={{0,3},{1,0},{2,1},{3,2},{4,7},{5,4},{6,5},{7,6},{8,11},{9,8},{10,9... | collective-permute-start | bytes 393224 | tf_op jit(solution)/shard_map/ppermute | solution.py:48
  206.4 7.6 %collective-permute-start.56 = (bf16[64,1024]{1,0:T(8,128)(2,1)S(1)}, bf16[64,1024]{1,0:T(8,128)(2,1)S(1)}, u32[]{:S(2)}, u32[]{:S(2)}) collective-permute-start(bf16[64,1024]{1,0:T(8,128)(2,1)S(1)} %slice.61), channel_id=1, source_target_pairs={{0,1},{1,2},{2,3},{3,0},{4,5},{5,6},{6,7},{7,4},{8,9},{9,10},{10,1... | collective-permute-start | bytes 393224 | tf_op jit(solution)/shard_map/ppermute | solution.py:48
  208.2 9.0 %collective-permute-start.53 = (bf16[64,1024]{1,0:T(8,128)(2,1)S(1)}, bf16[64,1024]{1,0:T(8,128)(2,1)S(1)}, u32[]{:S(2)}, u32[]{:S(2)}) collective-permute-start(bf16[64,1024]{1,0:T(8,128)(2,1)S(1)} %slice.60), channel_id=1, source_target_pairs={{0,3},{1,0},{2,1},{3,2},{4,7},{5,4},{6,5},{7,6},{8,11},{9,8},{10,9... | collective-permute-start | bytes 393224 | tf_op jit(solution)/shard_map/ppermute | solution.py:48
  221.8 16.1 %collective-permute-start.59 = (bf16[4,32,2048]{2,1,0:T(8,128)(2,1)S(1)}, bf16[4,32,2048]{2,1,0:T(8,128)(2,1)S(1)}, u32[]{:S(2)}, u32[]{:S(2)}) collective-permute-start(bf16[4,32,2048]{2,1,0:T(8,128)(2,1)S(1)} %get-tuple-element.88), channel_id=1, source_target_pairs={{0,8},{4,36},{8,16},{12,44},{16,24},{20,52},{24,0},{28,60},{32,40}... | collective-permute-start | bytes 1572872 | tf_op jit(solution)/shard_map/ppermute | solution.py:40
  221.9 16.0 %collective-permute-start.60 = (bf16[4,32,2048]{2,1,0:T(8,128)(2,1)S(1)}, bf16[4,32,2048]{2,1,0:T(8,128)(2,1)S(1)}, u32[]{:S(2)}, u32[]{:S(2)}) collective-permute-start(bf16[4,32,2048]{2,1,0:T(8,128)(2,1)S(1)} %get-tuple-element.89), channel_id=1, source_target_pairs={{0,24},{4,100},{8,0},{12,108},{16,8},{20,116},{24,16},{28,124},{32... | collective-permute-start | bytes 1572872 | tf_op jit(solution)/shard_map/ppermute | solution.py:40
  225.1 12.8 %collective-permute-start.61 = (bf16[4,32,2048]{2,1,0:T(8,128)(2,1)S(1)}, bf16[4,32,2048]{2,1,0:T(8,128)(2,1)S(1)}, u32[]{:S(2)}, u32[]{:S(2)}) collective-permute-start(bf16[4,32,2048]{2,1,0:T(8,128)(2,1)S(1)} %get-tuple-element.90), channel_id=1, source_target_pairs={{0,16},{4,68},{8,24},{12,76},{16,0},{20,84},{24,8},{28,92},{32,48}... | collective-permute-start | bytes 1572872 | tf_op jit(solution)/shard_map/ppermute | solution.py:40
  238.3 7.7 %collective-permute-start.62 = (bf16[32,2048]{1,0:T(8,128)(2,1)S(1)}, bf16[32,2048]{1,0:T(8,128)(2,1)S(1)}, u32[]{:S(2)}, u32[]{:S(2)}) collective-permute-start(bf16[32,2048]{1,0:T(8,128)(2,1)S(1)} %get-tuple-element.101), channel_id=1, source_target_pairs={{0,32},{4,12},{8,40},{12,20},{16,48},{20,28},{24,56},{28,4},{32,64... | collective-permute-start | bytes 393224 | tf_op jit(solution)/shard_map/ppermute | solution.py:44
  239.2 7.7 %collective-permute-start.63 = (bf16[32,2048]{1,0:T(8,128)(2,1)S(1)}, bf16[32,2048]{1,0:T(8,128)(2,1)S(1)}, u32[]{:S(2)}, u32[]{:S(2)}) collective-permute-start(bf16[32,2048]{1,0:T(8,128)(2,1)S(1)} %get-tuple-element.103), channel_id=1, source_target_pairs={{0,96},{4,28},{8,104},{12,4},{16,112},{20,12},{24,120},{28,20},{32... | collective-permute-start | bytes 393224 | tf_op jit(solution)/shard_map/ppermute | solution.py:44
  (22 other events, 163.7 us)
